TPU v7x, 32 devices: a whole 2x2x4 slice. The times are simulated.
32 devices in a mesh: phase: 2 (over core), dp: 16 (over z, y, x).
Axes of the slice: x: 2, y: 2, z: 4, core: 2. Of those that a mesh axis runs over, the one named last changes fastest.
Arguments:
- char_ids: int32 [2, 16, 4096], P(None, 'dp'), may hold values from 0 to 255
- char_counts: int32 [2, 16, 256], P(None, 'dp'), may hold values from 1 to 16
- segment_ids: int32 [2, 16, 256], P(None, 'dp'), may hold values from 0 to 3, never falling along the last dimension, each value on 1 to 128 neighbouring positions
- out_cotangent: bfloat16 [2, 16, 256, 512], P(None, 'dp'), may hold values from -6 to 6
- char_table: bfloat16 [256, 256], replicated, may hold values from -6 to 6
- char_gain_one: bfloat16 [256], replicated, may hold values from 0.099609375 to 1.8984375
- char_query: bfloat16 [256, 256], replicated, may hold values from -0.375 to 0.375
- char_key: bfloat16 [256, 256], replicated, may hold values from -0.375 to 0.375
- char_value: bfloat16 [256, 256], replicated, may hold values from -0.375 to 0.375
- char_output: bfloat16 [256, 256], replicated, may hold values from -1 to 1
- char_gain_two: bfloat16 [256], replicated, may hold values from 0.099609375 to 1.8984375
- char_up: bfloat16 [256, 1024], replicated, may hold values from -0.375 to 0.375
- char_down: bfloat16 [1024, 256], replicated, may hold values from -0.25 to 0.25
- char_project: bfloat16 [256, 512], replicated, may hold values from -0.375 to 0.375
- word_gain_one: bfloat16 [512], replicated, may hold values from 0.099609375 to 1.8984375
- word_query: bfloat16 [512, 512], replicated, may hold values from -0.25 to 0.25
- word_key: bfloat16 [512, 512], replicated, may hold values from -0.25 to 0.25
- word_value: bfloat16 [512, 512], replicated, may hold values from -0.25 to 0.25
- word_output: bfloat16 [512, 512], replicated, may hold values from -1.5 to 1.5
- word_gain_two: bfloat16 [512], replicated, may hold values from 0.099609375 to 1.8984375
- word_up: bfloat16 [512, 2048], replicated, may hold values from -0.25 to 0.25
- word_down: bfloat16 [2048, 512], replicated, may hold values from -0.1875 to 0.1875
Outputs:
- word_out: bfloat16 [2, 16, 256, 512], P(None, 'dp', None, 'phase')
- gradient_char_table: float32 [256, 256], P('dp', 'phase')
- gradient_char_gain_one: float32 [256], P('dp')
- gradient_char_query: float32 [256, 256], P('dp', 'phase')
- gradient_char_key: float32 [256, 256], P('dp', 'phase')
- gradient_char_value: float32 [256, 256], P('dp', 'phase')
- gradient_char_output: float32 [256, 256], P('dp', 'phase')
- gradient_char_gain_two: float32 [256], P('dp')
- gradient_char_up: float32 [256, 1024], P('dp', 'phase')
- gradient_char_down: float32 [1024, 256], P('dp', 'phase')
- gradient_char_project: float32 [256, 512], P('dp', 'phase')
- gradient_word_gain_one: float32 [512], P('dp')
- gradient_word_query: float32 [512, 512], P('dp', 'phase')
- gradient_word_key: float32 [512, 512], P('dp', 'phase')
- gradient_word_value: float32 [512, 512], P('dp', 'phase')
- gradient_word_output: float32 [512, 512], P('dp', 'phase')
- gradient_word_gain_two: float32 [512], P('dp')
- gradient_word_up: float32 [512, 2048], P('dp', 'phase')
- gradient_word_down: float32 [2048, 512], P('dp', 'phase')
Inputs may be any that keep to these rules, and one draw needn't show every extreme that they name: `char_counts`: the number of characters of each word; slots past it are padding. `segment_ids`: segment numbers never fall along a row; each number names 1 to 128 consecutive words, and one names exactly 128.
All inputs are finite; a program needn't handle non-finite values.
Results may differ from a plain program's by a relative error of at most 0.023.
Values may be sent and summed in bfloat16 or wider, within the bound.
No kernel may reach another device: no remote copies, remote signals or barrier semaphores. Data moves between devices by JAX's collectives and lax.ppermute only.
A program may use at most 192 MiB of HBM per device.

v0:
```python
from functools import partial

import jax
import jax.numpy as jnp
from jax import lax
from jax.sharding import PartitionSpec as P

HEAD_DIM = 64
CHAR_HEADS = 4
CPW = 16
WORD_HEADS = 8
WD = 512


epsilon = 1e-06
half_root = 0.7071067811865476
density = 0.3989422804014327
floor_score = -1e30
score_scale = 0.125
gain_places = (1, 6, 10, 15)
char_forms = ("wqhd,wkhd->hqkw", "hqkw,wkhd->wqhd", "hqkw,wqhd->wkhd")
word_forms = ("qhd,khd->hqk", "hqk,khd->qhd", "hqk,qhd->khd")


def from_behind(value, axis, steps):
    count = lax.axis_size(axis)
    initial, last = (max(0, -steps), min(count, count - steps))
    return lax.ppermute(value, axis, [(source, source + steps) for source in range(initial, last)])


def for_sending(shard):
    return jax.tree.map(lambda a: a.astype(jnp.bfloat16) if a.dtype == jnp.float32 else a, shard)


def product(left, right):
    return jnp.dot(left, right, preferred_element_type=jnp.float32)


def product_left(left, right):
    return lax.dot_general(
        left, right, (((0,), (0,)), ((), ())), preferred_element_type=jnp.float32
    )


def product_right(left, right):
    return lax.dot_general(
        left, right, (((1,), (1,)), ((), ())), preferred_element_type=jnp.float32
    )


def rms_forward(values, scaling):
    inverse = lax.rsqrt(jnp.mean(values * values, axis=-1, keepdims=True) + epsilon)
    return (values * inverse * scaling, inverse)


def rms_backward(values, inverse, scaling, upstream):
    lifted = upstream * scaling
    scaling_delta = jnp.sum(upstream * values * inverse, axis=0)
    inner_mean = jnp.mean(lifted * values, axis=-1, keepdims=True)
    return (inverse * lifted - inverse * inverse * inverse * values * inner_mean, scaling_delta)


def gelu_value(values):
    return 0.5 * values * (1.0 + jax.scipy.special.erf(values * half_root))


def gelu_slope(values):
    return 0.5 * (1.0 + jax.scipy.special.erf(values * half_root)) + values * density * jnp.exp(
        -0.5 * values * values
    )


def softmax_masked(raw_scores, allowed):
    masked = jnp.where(allowed, raw_scores, floor_score)
    highest = jnp.max(masked, axis=2, keepdims=True)
    expanded = jnp.exp(masked - highest)
    return expanded / jnp.sum(expanded, axis=2, keepdims=True)


def heads_forward(query_low, key_low, value_low, setup):
    allowed, head_shape, einsum_forms = setup
    query_heads = query_low.reshape(head_shape)
    key_heads = key_low.reshape(head_shape)
    value_heads = value_low.reshape(head_shape)
    raw_scores = (
        jnp.einsum(einsum_forms[0], query_heads, key_heads, preferred_element_type=jnp.float32)
        * score_scale
    )
    soft_low = softmax_masked(raw_scores, allowed).astype(jnp.bfloat16)
    mixed = jnp.einsum(einsum_forms[1], soft_low, value_heads, preferred_element_type=jnp.float32)
    return mixed.reshape(query_low.shape)


def heads_backward(query_low, key_low, value_low, mixed_delta, setup):
    allowed, head_shape, einsum_forms = setup
    query_heads = query_low.reshape(head_shape)
    key_heads = key_low.reshape(head_shape)
    value_heads = value_low.reshape(head_shape)
    upstream = mixed_delta.reshape(head_shape)
    raw_scores = (
        jnp.einsum(einsum_forms[0], query_heads, key_heads, preferred_element_type=jnp.float32)
        * score_scale
    )
    soft = softmax_masked(raw_scores, allowed)
    soft_low = soft.astype(jnp.bfloat16)
    soft_delta = jnp.einsum(
        einsum_forms[0], upstream, value_heads, preferred_element_type=jnp.float32
    )
    centre = jnp.sum(soft * soft_delta, axis=2, keepdims=True)
    score_delta = (soft * (soft_delta - centre)).astype(jnp.bfloat16)
    query_delta = (
        jnp.einsum(einsum_forms[1], score_delta, key_heads, preferred_element_type=jnp.float32)
        * score_scale
    )
    key_delta = (
        jnp.einsum(einsum_forms[2], score_delta, query_heads, preferred_element_type=jnp.float32)
        * score_scale
    )
    value_delta = jnp.einsum(
        einsum_forms[2], soft_low, upstream, preferred_element_type=jnp.float32
    )
    width_shape = query_low.shape
    return (
        query_delta.reshape(width_shape),
        key_delta.reshape(width_shape),
        value_delta.reshape(width_shape),
    )


def layer_forward(inputs, weights, setup):
    gain_one, w_query, w_key, w_value, w_output, gain_two, w_up, w_down = weights
    normed, inverse_one = rms_forward(inputs, gain_one)
    normed_low = normed.astype(jnp.bfloat16)
    query_low = product(normed_low, w_query).astype(jnp.bfloat16)
    key_low = product(normed_low, w_key).astype(jnp.bfloat16)
    value_low = product(normed_low, w_value).astype(jnp.bfloat16)
    mixed_low = heads_forward(query_low, key_low, value_low, setup).astype(jnp.bfloat16)
    middle = inputs + product(mixed_low, w_output)
    normed_two, inverse_two = rms_forward(middle, gain_two)
    normed_two_low = normed_two.astype(jnp.bfloat16)
    before = product(normed_two_low, w_up)
    active_low = gelu_value(before).astype(jnp.bfloat16)
    result = middle + product(active_low, w_down)
    kept = (
        inputs,
        inverse_one,
        normed_low,
        query_low,
        key_low,
        value_low,
        mixed_low,
        middle,
        inverse_two,
        normed_two_low,
        before,
        active_low,
    )
    return (result, kept)


def layer_backward(kept, weights, setup, upstream):
    (
        inputs,
        inverse_one,
        normed_low,
        query_low,
        key_low,
        value_low,
        mixed_low,
        middle,
        inverse_two,
        normed_two_low,
        before,
        active_low,
    ) = kept
    gain_one, w_query, w_key, w_value, w_output, gain_two, w_up, w_down = weights
    upstream_low = upstream.astype(jnp.bfloat16)
    down_delta = product_left(active_low, upstream_low)
    active_delta = product_right(upstream_low, w_down)
    before_delta = (active_delta * gelu_slope(before)).astype(jnp.bfloat16)
    up_delta = product_left(normed_two_low, before_delta)
    normed_two_delta = product_right(before_delta, w_up)
    through_two, gain_two_delta = rms_backward(
        middle, inverse_two, gain_two.astype(jnp.float32), normed_two_delta
    )
    middle_delta = upstream + through_two
    middle_low = middle_delta.astype(jnp.bfloat16)
    output_delta = product_left(mixed_low, middle_low)
    mixed_delta = product_right(middle_low, w_output).astype(jnp.bfloat16)
    query_delta, key_delta, value_delta = heads_backward(
        query_low, key_low, value_low, mixed_delta, setup
    )
    query_back = query_delta.astype(jnp.bfloat16)
    key_back = key_delta.astype(jnp.bfloat16)
    value_back = value_delta.astype(jnp.bfloat16)
    query_weight_delta = product_left(normed_low, query_back)
    key_weight_delta = product_left(normed_low, key_back)
    value_weight_delta = product_left(normed_low, value_back)
    normed_delta = (
        product_right(query_back, w_query)
        + product_right(key_back, w_key)
        + product_right(value_back, w_value)
    )
    through_one, gain_one_delta = rms_backward(
        inputs, inverse_one, gain_one.astype(jnp.float32), normed_delta
    )
    deltas = (
        gain_one_delta,
        query_weight_delta,
        key_weight_delta,
        value_weight_delta,
        output_delta,
        gain_two_delta,
        up_delta,
        down_delta,
    )
    return (middle_delta + through_one, deltas)


def char_setup(counts):
    words = counts.shape[0]
    allowed = (lax.broadcasted_iota(jnp.int32, (CPW, words), 0) < counts[None, :])[None, None]
    return (allowed, (words, CPW, CHAR_HEADS, HEAD_DIM), char_forms)


def word_setup(segments):
    words = segments.shape[0]
    query_place = lax.broadcasted_iota(jnp.int32, (words, words), 0)
    key_place = lax.broadcasted_iota(jnp.int32, (words, words), 1)
    allowed = ((key_place <= query_place) & (segments[:, None] == segments[None, :]))[None]
    return (allowed, (words, WORD_HEADS, HEAD_DIM), word_forms)


def slot_presence(counts):
    words = counts.shape[0]
    return (lax.broadcasted_iota(jnp.int32, (words, CPW), 1) < counts[:, None]).astype(jnp.float32)


def char_forward(identifiers, counts, char_weights, char_table, char_project):
    words = counts.shape[0]
    embedded = jnp.take(char_table, identifiers, axis=0).astype(jnp.float32)
    result, kept = layer_forward(embedded, char_weights, char_setup(counts))
    present = slot_presence(counts)
    pooled = jnp.sum(
        result.reshape(words, CPW, result.shape[1]) * present[:, :, None], axis=1
    ) / counts[:, None].astype(jnp.float32)
    pooled_low = pooled.astype(jnp.bfloat16)
    vectors_low = product(pooled_low, char_project).astype(jnp.bfloat16)
    return (vectors_low, pooled_low, kept)


def vectors_only(identifiers, counts, char_weights, char_table, char_project):
    vectors_low, pooled_low, kept = char_forward(
        identifiers, counts, char_weights, char_table, char_project
    )
    return (vectors_low, pooled_low)


def char_backward(
    identifiers, counts, vector_delta, pooled_low, kept, char_weights, char_table, char_project
):
    words = counts.shape[0]
    project_delta = product_left(pooled_low, vector_delta)
    pooled_delta = product_right(vector_delta, char_project)
    present = slot_presence(counts)
    spread_delta = (pooled_delta / counts[:, None].astype(jnp.float32))[:, None, :] * present[
        :, :, None
    ]
    spread_delta = spread_delta.reshape(words * CPW, pooled_delta.shape[1])
    embedded_delta, layer_deltas = layer_backward(
        kept, char_weights, char_setup(counts), spread_delta
    )
    table_rows = char_table.shape[0]
    selector = (identifiers[:, None] == lax.broadcasted_iota(jnp.int32, (1, table_rows), 1)).astype(
        jnp.float32
    )
    table_delta = lax.dot_general(
        selector,
        embedded_delta,
        (((0,), (0,)), ((), ())),
        precision=lax.Precision.HIGHEST,
        preferred_element_type=jnp.float32,
    )
    return (table_delta,) + layer_deltas + (project_delta,)


def fresh_backward(identifiers, counts, vector_delta, char_weights, char_table, char_project):
    vectors_low, pooled_low, kept = char_forward(
        identifiers, counts, char_weights, char_table, char_project
    )
    return char_backward(
        identifiers, counts, vector_delta, pooled_low, kept, char_weights, char_table, char_project
    )


def word_pass(arrived, cotangent, segments, word_weights):
    setup = word_setup(segments)
    result, kept = layer_forward(arrived.astype(jnp.float32), word_weights, setup)
    inputs_delta, deltas = layer_backward(kept, word_weights, setup, cotangent.astype(jnp.float32))
    return (result.astype(jnp.bfloat16), inputs_delta.astype(jnp.bfloat16), deltas)


def zeros_of(compute):
    return jax.tree.map(jnp.zeros_like, compute())


def on_phase(flag, compute):
    return lax.cond(flag, compute, partial(zeros_of, compute))


def split_parts(deltas):
    matrices = tuple((member for place, member in enumerate(deltas) if place not in gain_places))
    gains = tuple((deltas[place] for place in gain_places))
    return (matrices, gains)


def join_parts(matrices, gains):
    joined = []
    matrix_place = 0
    gain_place = 0
    for place in range(len(matrices) + len(gains)):
        if place in gain_places:
            joined.append(gains[gain_place])
            gain_place += 1
        else:
            joined.append(matrices[matrix_place])
            matrix_place += 1
    return tuple(joined)


def body(
    char_ids,
    char_counts,
    segment_ids,
    out_cotangent,
    char_table,
    char_gain_one,
    char_query,
    char_key,
    char_value,
    char_output,
    char_gain_two,
    char_up,
    char_down,
    char_project,
    word_gain_one,
    word_query,
    word_key,
    word_value,
    word_output,
    word_gain_two,
    word_up,
    word_down,
):
    char_weights = (
        char_gain_one,
        char_query,
        char_key,
        char_value,
        char_output,
        char_gain_two,
        char_up,
        char_down,
    )
    word_weights = (
        word_gain_one,
        word_query,
        word_key,
        word_value,
        word_output,
        word_gain_two,
        word_up,
        word_down,
    )
    phase_index = lax.axis_index("phase")
    on_chars = phase_index == 0
    on_words = phase_index == 1
    batches = char_ids.shape[0]
    half_width = WD // 2
    stored = [
        on_phase(
            on_chars,
            partial(
                vectors_only,
                char_ids[batch_index, 0],
                char_counts[batch_index, 0],
                char_weights,
                char_table,
                char_project,
            ),
        )
        for batch_index in range(batches)
    ]
    outputs = []
    local_total = None
    for batch_index in range(batches):
        arrived = from_behind(stored[batch_index][0], "phase", 1)
        word_result, returned_delta, word_deltas = on_phase(
            on_words,
            partial(
                word_pass,
                arrived,
                out_cotangent[batch_index, 0],
                segment_ids[batch_index, 0],
                word_weights,
            ),
        )
        back_delta, front_half = from_behind(
            (returned_delta, word_result[:, :half_width]), "phase", -1
        )
        outputs.append(jnp.where(on_chars, front_half, word_result[:, half_width:]))
        char_deltas = on_phase(
            on_chars,
            partial(
                fresh_backward,
                char_ids[batch_index, 0],
                char_counts[batch_index, 0],
                back_delta,
                char_weights,
                char_table,
                char_project,
            ),
        )
        deltas = tuple(char_deltas) + tuple(word_deltas)
        local_total = deltas if local_total is None else jax.tree.map(jnp.add, local_total, deltas)
    row_totals = lax.psum_scatter(local_total, "dp", scatter_dimension=0, tiled=True)
    matrices, gains = split_parts(row_totals)
    matrix_totals = jax.tree.map(
        lambda part: part.astype(jnp.float32),
        lax.psum_scatter(for_sending(matrices), "phase", scatter_dimension=1, tiled=True),
    )
    gain_totals = lax.psum(gains, "phase")
    reduced = join_parts(matrix_totals, gain_totals)
    word_out = jnp.stack(outputs)[:, None]
    return (word_out,) + tuple(reduced)


def solution(mesh):
    return jax.shard_map(
        body,
        mesh=mesh,
        in_specs=(
            P(None, "dp", None),
            P(None, "dp", None),
            P(None, "dp", None),
            P(None, "dp", None, None),
            P(),
            P(),
            P(),
            P(),
            P(),
            P(),
            P(),
            P(),
            P(),
            P(),
            P(),
            P(),
            P(),
            P(),
            P(),
            P(),
            P(),
            P(),
        ),
        out_specs=(
            P(None, "dp", None, "phase"),
            P("dp", "phase"),
            P("dp"),
            P("dp", "phase"),
            P("dp", "phase"),
            P("dp", "phase"),
            P("dp", "phase"),
            P("dp"),
            P("dp", "phase"),
            P("dp", "phase"),
            P("dp", "phase"),
            P("dp"),
            P("dp", "phase"),
            P("dp", "phase"),
            P("dp", "phase"),
            P("dp", "phase"),
            P("dp"),
            P("dp", "phase"),
            P("dp", "phase"),
        ),
        check_vma=False,
    )
```

profile of v0, /device:TPU:0, one launch (start us, length us, event | category | flops | bytes accessed | tf_op | source)
XLA Modules:
  0.0 2011.8 jit_solution(15554365528703534111)
XLA Ops:
  9.9 107.7 %conditional.6 = (bf16[256,512]{1,0:T(8,128)(2,1)}) conditional(s32[]{:T(128)} %convert_element_type.619, () %tuple.54, (bf16[256,256]{1,0:T(8,128)(2,1)}, s32[4096]{0:T(1024)}, bf16[256]{0:T(256)(128)(2,1)}, bf16[256,256]{1,0:T(8,128)(2,1)}, s32[1,1,256]{2,1,0:T(1,128)}, /*index=5*/bf16[256,256]{1,0:T(8,128)(2,1)}, bf16[256,256]{1,0:T(8,128)(2,1)}, ...), branch_computations={%region_0.0_spmd, %region_1.8_spmd} | conditional | flops 6635123712 | bytes 80253344 | solution.py:308
  17.2 14.6 gather_fusion.2
  118.9 106.0 %conditional.8 = (bf16[256,512]{1,0:T(8,128)(2,1)}) conditional(s32[]{:T(128)} %convert_element_type.619, () %tuple.58, (bf16[256,256]{1,0:T(8,128)(2,1)}, s32[4096]{0:T(1024)S(1)}, bf16[256]{0:T(256)(128)(2,1)}, bf16[256,256]{1,0:T(8,128)(2,1)}, s32[1,1,256]{2,1,0:T(1,128)}, /*index=5*/bf16[256,256]{1,0:T(8,128)(2,1)}, ...), branch_computations={%region_18.20_spmd, %region_19.26_spmd} | conditional | flops 6635123712 | bytes 78033104 | solution.py:308
  122.5 14.6 gather_fusion.3
  241.2 252.3 %conditional.10 = (f32[256,256]{1,0:T(8,128)S(1)}, f32[256]{0:T(256)S(1)}, f32[256,256]{1,0:T(8,128)S(1)}, f32[256,256]{1,0:T(8,128)}, f32[256,256]{1,0:T(8,128)...) conditional(s32[]{:T(128)} %convert_element_type.619, () %tuple.61, ...), branch_computations={%region_36.38_spmd, %region_37.49_spmd} | conditional | flops 23022759936 | bytes 465890688 | solution.py:308
  250.1 14.6 gather_fusion
  351.9 12.2 fusion.174
  494.6 250.5 %conditional.11 = (f32[256,256]{1,0:T(8,128)}, f32[256]{0:T(256)}, f32[256,256]{1,0:T(8,128)}, f32[256,256]{1,0:T(8,128)}, f32[256,256]{1,0:T(8,128)}, /*index=5...) conditional(s32[]{:T(128)} %convert_element_type.619, () %tuple.63, ...), branch_computations={%region_48.50_spmd, %region_49.61_spmd} | conditional | flops 23022759936 | bytes 464592256 | solution.py:308
  501.9 14.6 gather_fusion.1
  605.0 12.2 fusion.247
  783.8 42.2 %reduce-scatter.49.cloned.1.call-done = f32[16,256]{1,0:T(8,128)} async-done(((f32[256,256]{1,0:T(8,128)}), f32[16,256]{1,0:T(8,128)}) %reduce-scatter.49.cloned.1.call-update) | async-done | bytes 16400 | tf_op jit(solution)/shard_map/reduce_scatter | solution.py:426
  827.5 73.3 %reduce-scatter.47.cloned.1.call-done = f32[16,256]{1,0:T(8,128)} async-done(((f32[256,256]{1,0:T(8,128)}), f32[16,256]{1,0:T(8,128)}) %reduce-scatter.47.cloned.1.call-update) | async-done | bytes 16400 | tf_op jit(solution)/shard_map/reduce_scatter | solution.py:426
  902.3 73.2 %reduce-scatter.45.cloned.1.call-done = f32[16,256]{1,0:T(8,128)} async-done(((f32[256,256]{1,0:T(8,128)}), f32[16,256]{1,0:T(8,128)}) %reduce-scatter.45.cloned.1.call-update) | async-done | bytes 16400 | tf_op jit(solution)/shard_map/reduce_scatter | solution.py:426
  977.1 73.2 %reduce-scatter.43.cloned.1.call-done = f32[16,256]{1,0:T(8,128)} async-done(((f32[256,256]{1,0:T(8,128)}), f32[16,256]{1,0:T(8,128)}) %reduce-scatter.43.cloned.1.call-update) | async-done | bytes 16400 | tf_op jit(solution)/shard_map/reduce_scatter | solution.py:426
  1051.8 73.6 %reduce-scatter.41.cloned.1.call-done = f32[16,256]{1,0:T(8,128)} async-done(((f32[256,256]{1,0:T(8,128)}), f32[16,256]{1,0:T(8,128)}) %reduce-scatter.41.cloned.1.call-update) | async-done | bytes 16400 | tf_op jit(solution)/shard_map/reduce_scatter | solution.py:426
  1126.9 73.6 %reduce-scatter.57.cloned.1.call-done = f32[16,512]{1,0:T(8,128)} async-done(((f32[256,512]{1,0:T(8,128)}), f32[16,512]{1,0:T(8,128)}) %reduce-scatter.57.cloned.1.call-update) | async-done | bytes 32784 | tf_op jit(solution)/shard_map/reduce_scatter | solution.py:426
  1202.0 74.8 %reduce-scatter.73.cloned.1.call-done = f32[32,512]{1,0:T(8,128)} async-done(((f32[512,512]{1,0:T(8,128)}), f32[32,512]{1,0:T(8,128)}) %reduce-scatter.73.cloned.1.call-update) | async-done | bytes 65552 | tf_op jit(solution)/shard_map/reduce_scatter | solution.py:426
  1278.3 75.0 %reduce-scatter.69.cloned.1.call-done = f32[32,512]{1,0:T(8,128)} async-done(((f32[512,512]{1,0:T(8,128)}), f32[32,512]{1,0:T(8,128)}) %reduce-scatter.69.cloned.1.call-update) | async-done | bytes 65552 | tf_op jit(solution)/shard_map/reduce_scatter | solution.py:426
  1354.8 74.9 %reduce-scatter.65.cloned.1.call-done = f32[32,512]{1,0:T(8,128)} async-done(((f32[512,512]{1,0:T(8,128)}), f32[32,512]{1,0:T(8,128)}) %reduce-scatter.65.cloned.1.call-update) | async-done | bytes 65552 | tf_op jit(solution)/shard_map/reduce_scatter | solution.py:426
  1431.3 74.6 %reduce-scatter.61.cloned.1.call-done = f32[32,512]{1,0:T(8,128)} async-done(((f32[512,512]{1,0:T(8,128)}), f32[32,512]{1,0:T(8,128)}) %reduce-scatter.61.cloned.1.call-update) | async-done | bytes 65552 | tf_op jit(solution)/shard_map/reduce_scatter | solution.py:426
  1507.4 75.1 %reduce-scatter.55.cloned.1.call-done = f32[64,256]{1,0:T(8,128)} async-done(((f32[1024,256]{1,0:T(8,128)}), f32[64,256]{1,0:T(8,128)}) %reduce-scatter.55.cloned.1.call-update) | async-done | bytes 65552 | tf_op jit(solution)/shard_map/reduce_scatter | solution.py:426
  1585.5 73.3 %reduce-scatter.51.cloned.1.call-done = f32[16,1024]{1,0:T(8,128)} async-done(((f32[256,1024]{1,0:T(8,128)}), f32[16,1024]{1,0:T(8,128)}) %reduce-scatter.51.cloned.1.call-update) | async-done | bytes 65552 | tf_op jit(solution)/shard_map/reduce_scatter | solution.py:426
  1660.3 92.3 %reduce-scatter.81.cloned.1.call-done = f32[128,512]{1,0:T(8,128)} async-done(((f32[2048,512]{1,0:T(8,128)}), f32[128,512]{1,0:T(8,128)}) %reduce-scatter.81.cloned.1.call-update) | async-done | bytes 262160 | tf_op jit(solution)/shard_map/reduce_scatter | solution.py:426
  1757.7 91.9 %reduce-scatter.77.cloned.1.call-done = f32[32,2048]{1,0:T(8,128)} async-done(((f32[512,2048]{1,0:T(8,128)}), f32[32,2048]{1,0:T(8,128)}) %reduce-scatter.77.cloned.1.call-update) | async-done | bytes 262160 | tf_op jit(solution)/shard_map/reduce_scatter | solution.py:426
  1853.3 40.6 %all-reduce.4 = (f32[256]{0:T(256)S(1)}, f32[256]{0:T(256)S(1)}, f32[512]{0:T(512)S(1)}, f32[512]{0:T(512)S(1)}) all-reduce(f32[256]{0:T(256)S(1)} %add.371, f32[256]{0:T(256)S(1)} %add.376, f32[512]{0:T(512)S(1)} %add.380, f32[512]{0:T(512)S(1)} %add.385), channel_id=4, replica_groups=mesh['phase'=2,'dp'=16] {'dp'}, use_global_device_ids=true, to_apply=%region_62.64.clone | all-reduce | flops 1536 | bytes 12288
  1914.1 10.1 reduce-scatter.75.cloned.1.call-done
  1925.5 10.0 reduce-scatter.71.cloned.1.call-done
  1936.9 10.0 reduce-scatter.67.cloned.1.call-done
  1948.2 9.9 reduce-scatter.63.cloned.1.call-done
  1970.5 9.7 reduce-scatter.53.cloned.1.call-done
  1981.5 10.0 reduce-scatter.83.cloned.1.call-done
  1993.0 10.0 reduce-scatter.79.cloned.1.call-done
  (650 shorter events, 762.6 us)
Async XLA Ops:
  7.2 818.8 %reduce-scatter.49.cloned.1.call-start = ((), (), s32[]{:S(2)}) async-start(), calls=%async_computation.32 | async-start | bytes 278528 | tf_op jit(solution)/shard_map/reduce_scatter | solution.py:426
  117.6 108.7 %collective-permute-start = (bf16[256,512]{1,0:T(8,128)(2,1)}, bf16[256,512]{1,0:T(8,128)(2,1)S(1)}, u32[]{:S(2)}, u32[]{:S(2)}) collective-permute-start(bf16[256,512]{1,0:T(8,128)(2,1)} %get-tuple-element.502), channel_id=1, source_target_pairs={{0,16},{1,17},{2,18},{3,19},{4,20},{5,21},{6,22},{7,23},{8,24},{9,... | collective-permute-start | bytes 786440 | tf_op jit(solution)/shard_map/ppermute | solution.py:28
  236.6 256.9 %collective-permute-start.5 = (bf16[256,512]{1,0:T(8,128)(2,1)}, bf16[256,512]{1,0:T(8,128)(2,1)}, u32[]{:S(2)}, u32[]{:S(2)}) collective-permute-start(bf16[256,512]{1,0:T(8,128)(2,1)} %get-tuple-element.298), channel_id=1, source_target_pairs={{16,0},{17,1},{18,2},{19,3},{20,4},{21,5},{22,6},{23,7},{24,8},{25... | collective-permute-start | bytes 786440 | tf_op jit(solution)/shard_map/ppermute | solution.py:28
  747.0 153.8 %reduce-scatter.47.cloned.1.call-start = ((), (), s32[]{:S(2)}) async-start(), calls=%async_computation.31 | async-start | bytes 278528 | tf_op jit(solution)/shard_map/reduce_scatter | solution.py:426
  748.9 226.7 %reduce-scatter.45.cloned.1.call-start = ((), (), s32[]{:S(2)}) async-start(), calls=%async_computation.30 | async-start | bytes 278528 | tf_op jit(solution)/shard_map/reduce_scatter | solution.py:426
  750.7 299.5 %reduce-scatter.43.cloned.1.call-start = ((), (), s32[]{:S(2)}) async-start(), calls=%async_computation.29 | async-start | bytes 278528 | tf_op jit(solution)/shard_map/reduce_scatter | solution.py:426
  752.7 372.7 %reduce-scatter.41.cloned.1.call-start = ((), (), s32[]{:S(2)}) async-start(), calls=%async_computation.28 | async-start | bytes 278528 | tf_op jit(solution)/shard_map/reduce_scatter | solution.py:426
  754.5 446.1 %reduce-scatter.57.cloned.1.call-start = ((), (), s32[]{:S(2)}) async-start(), calls=%async_computation.36 | async-start | bytes 557056 | tf_op jit(solution)/shard_map/reduce_scatter | solution.py:426
  756.5 520.3 %reduce-scatter.73.cloned.1.call-start = ((), (), s32[]{:S(2)}) async-start(), calls=%async_computation.44 | async-start | bytes 1114112 | tf_op jit(solution)/shard_map/reduce_scatter | solution.py:426
  759.0 594.3 %reduce-scatter.69.cloned.1.call-start = ((), (), s32[]{:S(2)}) async-start(), calls=%async_computation.42 | async-start | bytes 1114112 | tf_op jit(solution)/shard_map/reduce_scatter | solution.py:426
  761.6 668.1 %reduce-scatter.65.cloned.1.call-start = ((), (), s32[]{:S(2)}) async-start(), calls=%async_computation.40 | async-start | bytes 1114112 | tf_op jit(solution)/shard_map/reduce_scatter | solution.py:426
  764.2 741.7 %reduce-scatter.61.cloned.1.call-start = ((), (), s32[]{:S(2)}) async-start(), calls=%async_computation.38 | async-start | bytes 1114112 | tf_op jit(solution)/shard_map/reduce_scatter | solution.py:426
  765.5 817.0 %reduce-scatter.55.cloned.1.call-start = ((), (), s32[]{:S(2)}) async-start(), calls=%async_computation.35 | async-start | bytes 1114112 | tf_op jit(solution)/shard_map/reduce_scatter | solution.py:426
  768.0 890.8 %reduce-scatter.51.cloned.1.call-start = ((), (), s32[]{:S(2)}) async-start(), calls=%async_computation.33 | async-start | bytes 1114112 | tf_op jit(solution)/shard_map/reduce_scatter | solution.py:426
  770.4 982.2 %reduce-scatter.81.cloned.1.call-start = ((), (), s32[]{:S(2)}) async-start(), calls=%async_computation.48 | async-start | bytes 4456448 | tf_op jit(solution)/shard_map/reduce_scatter | solution.py:426
  777.0 1072.5 %reduce-scatter.77.cloned.1.call-start = ((), (), s32[]{:S(2)}) async-start(), calls=%async_computation.46 | async-start | bytes 4456448 | tf_op jit(solution)/shard_map/reduce_scatter | solution.py:426
  783.7 1113.4 %reduce-scatter.93.cloned.1.call-start = ((), (), s32[]{:S(2)}) async-start(), calls=%async_computation.54 | async-start | bytes 98304
  827.5 1071.1 %reduce-scatter.91.cloned.1.call-start = ((), (), s32[]{:S(2)}) async-start(), calls=%async_computation.53 | async-start | bytes 98304
  902.3 997.7 %reduce-scatter.89.cloned.1.call-start = ((), (), s32[]{:S(2)}) async-start(), calls=%async_computation.52 | async-start | bytes 98304
  977.0 924.4 %reduce-scatter.87.cloned.1.call-start = ((), (), s32[]{:S(2)}) async-start(), calls=%async_computation.51 | async-start | bytes 98304
  1051.7 851.2 %reduce-scatter.85.cloned.1.call-start = ((), (), s32[]{:S(2)}) async-start(), calls=%async_computation.50 | async-start | bytes 98304
  1126.9 785.9 %reduce-scatter.59.cloned.1.call-start = ((), (), s32[]{:S(2)}) async-start(), calls=%async_computation.37 | async-start | bytes 24576 | tf_op jit(solution)/shard_map/reduce_scatter | solution.py:430
  1201.9 722.2 %reduce-scatter.75.cloned.1.call-start = ((), (), s32[]{:S(2)}) async-start(), calls=%async_computation.45 | async-start | bytes 49152 | tf_op jit(solution)/shard_map/reduce_scatter | solution.py:430
  1278.3 657.2 %reduce-scatter.71.cloned.1.call-start = ((), (), s32[]{:S(2)}) async-start(), calls=%async_computation.43 | async-start | bytes 49152 | tf_op jit(solution)/shard_map/reduce_scatter | solution.py:430
  1354.8 592.1 %reduce-scatter.67.cloned.1.call-start = ((), (), s32[]{:S(2)}) async-start(), calls=%async_computation.41 | async-start | bytes 49152 | tf_op jit(solution)/shard_map/reduce_scatter | solution.py:430
  1431.2 526.9 %reduce-scatter.63.cloned.1.call-start = ((), (), s32[]{:S(2)}) async-start(), calls=%async_computation.39 | async-start | bytes 49152 | tf_op jit(solution)/shard_map/reduce_scatter | solution.py:430
  1507.4 461.6 %reduce-scatter.95.cloned.1.call-start = ((), (), s32[]{:S(2)}) async-start(), calls=%async_computation.55 | async-start | bytes 98304
  1584.1 396.1 %reduce-scatter.53.cloned.1.call-start = ((), (), s32[]{:S(2)}) async-start(), calls=%async_computation.34 | async-start | bytes 49152 | tf_op jit(solution)/shard_map/reduce_scatter | solution.py:430
  1584.2 173.5 %collective-permute-start.1 = (bf16[256,256]{1,0:T(8,128)(2,1)S(1)}, bf16[256,256]{1,0:T(8,128)(2,1)S(1)}, u32[]{:S(2)}, u32[]{:S(2)}) collective-permute-start(bf16[256,256]{1,0:T(8,128)(2,1)S(1)} %slice.46), channel_id=1, source_target_pairs={{16,0},{17,1},{18,2},{19,3},{20,4},{21,5},{22,6},{23,7},{24,8},{25... | collective-permute-start | bytes 393224 | tf_op jit(solution)/shard_map/ppermute | solution.py:28
  1660.2 331.3 %reduce-scatter.83.cloned.1.call-start = ((), (), s32[]{:S(2)}) async-start(), calls=%async_computation.49 | async-start | bytes 196608 | tf_op jit(solution)/shard_map/reduce_scatter | solution.py:430
  1754.3 248.7 %reduce-scatter.79.cloned.1.call-start = ((), (), s32[]{:S(2)}) async-start(), calls=%async_computation.47 | async-start | bytes 196608 | tf_op jit(solution)/shard_map/reduce_scatter | solution.py:430
  1756.3 94.9 %collective-permute-start.3 = (bf16[256,256]{1,0:T(8,128)(2,1)S(1)}, bf16[256,256]{1,0:T(8,128)(2,1)S(1)}, u32[]{:S(2)}, u32[]{:S(2)}) collective-permute-start(bf16[256,256]{1,0:T(8,128)(2,1)S(1)} %slice.50), channel_id=1, source_target_pairs={{16,0},{17,1},{18,2},{19,3},{20,4},{21,5},{22,6},{23,7},{24,8},{25... | collective-permute-start | bytes 393224 | tf_op jit(solution)/shard_map/ppermute | solution.py:28
  (155 other events, 10289.1 us)
Sparse Core Ops, SparseCore 0:
  747.2 78.7 reduce-scatter.48
  828.3 72.4 reduce-scatter.46
  903.1 72.4 reduce-scatter.44
  977.7 72.4 reduce-scatter.42
  1052.9 72.4 reduce-scatter.40
  1127.6 72.9 reduce-scatter.56
  1202.8 73.9 reduce-scatter.72
  1279.1 74.0 reduce-scatter.68
  1355.5 74.1 reduce-scatter.64
  1431.9 73.9 reduce-scatter.60
  1508.2 74.2 reduce-scatter.54
  1584.7 74.0 reduce-scatter.50
  1661.1 91.5 reduce-scatter.80
  1754.8 94.7 reduce-scatter.76
  1851.6 7.0 reduce-scatter.92
  1860.7 8.5 reduce-scatter.90
  1871.4 8.6 reduce-scatter.88
  1882.1 8.5 reduce-scatter.86
  1892.9 8.6 reduce-scatter.84
  1904.2 8.5 reduce-scatter.58
  1915.6 8.5 reduce-scatter.74
  1926.9 8.5 reduce-scatter.70
  1938.3 8.5 reduce-scatter.66
  1949.5 8.5 reduce-scatter.62
  1960.3 8.6 reduce-scatter.94
  1971.6 8.5 reduce-scatter.52
  1982.8 8.6 reduce-scatter.82
  1994.3 8.6 reduce-scatter.78
where the time goes:
time: 2030 us; the launch traced here: 2010 us
  waiting for transfers between devices  1130 us (56%)
  local copies, waits for them, and re-layouts  395 us (19%)
  matrix products  288 us (14%)
  other arithmetic  127 us (6%)
  blocking collectives  43.5 us (2%)
    reduce_scatter x14, waiting for transfers between devices, body(): lax.psum_scatter(local_total, 'dp', scatter_dimension=0, tiled=True)  1040 us
    dot_general x24, matrix products, product(): return jnp.dot(left, right, preferred_element_type=jnp.float32)  89.6 us
    reduce_scatter x8, waiting for transfers between devices, body(): lax.psum_scatter(for_sending(matrices), 'phase', scatter_dimension=1, til...  78.2 us
    gather x4, local copies, waits for them, and re-layouts, char_forward(): embedded = jnp.take(char_table, identifiers, axis=0).astype(jnp.float32)  58.4 us
    dot_general x14, matrix products, product_right(): lax.dot_general(left, right, (((1,), (1,)), ((), ())), preferred_element_...  47.1 us
    convert_element_type x8, local copies, waits for them, and re-layouts, layer_forward(): heads_forward(query_low, key_low, value_low, setup).astype(jnp.bfloat16)  44.6 us
  transfers between devices with their start and end apart: 34, of which 23 were waited for; matrix products, arithmetic and copies ran while one was open for 22% of the time, Pallas kernels for 0%

commit v1 on v0

v1 whole, which is shorter than its diff:
```python
from functools import partial

import jax
import jax.numpy as jnp
from jax import lax
from jax.experimental import pallas as pl
from jax.experimental.pallas import tpu as pltpu
from jax.sharding import PartitionSpec as P

F32 = jnp.float32
LOW = jnp.bfloat16

CD = 256
CFF = 1024
CPW = 16
CVOC = 256
CHAR_HEADS = 4
HEAD = 64
WD = 512
WFF = 2048
WORD_HEADS = 8
WORDS = 256

SPAN = 256
STEP = 240
BLOCKS = (WORDS * CPW - 1) // STEP + 1

epsilon = 1e-06
half_root = 0.7071067811865476
density = 0.3989422804014327
floor_score = -1e30

R_EMB, R_Q, R_K, R_V, R_P, R_MIX, R_SLOPE = 0, 256, 512, 768, 1024, 2048, 2304
KEPT_LOW = 3328
KEPT_F32 = 264

W_Q, W_K, W_V, W_O, W_UP, W_DOWN, W_CDOWN, W_PROJ = 0, 32, 64, 96, 128, 256, 384, 416
W_ROWS = 432
C_TABLE, C_Q, C_K, C_V, C_O, C_UP, C_GAIN = 0, 16, 32, 48, 64, 80, 144
C_ROWS = 160
SHARES = 16


def nn(left, right):
    return lax.dot_general(left, right, (((1,), (0,)), ((), ())), preferred_element_type=F32)


def nt(left, right):
    return lax.dot_general(left, right, (((1,), (1,)), ((), ())), preferred_element_type=F32)


def iota(shape, axis):
    return lax.broadcasted_iota(jnp.int32, shape, axis)


def eye(n):
    return iota((n, n), 0) == iota((n, n), 1)


def row_to_column(row):
    n = row.shape[1]
    return jnp.sum(jnp.where(eye(n), row, 0.0), axis=1, keepdims=True)


def gelu_pair(v):
    full = 0.5 + 0.5 * lax.erf(v * half_root)
    return v * full, full + v * (density * jnp.exp(-0.5 * v * v))


def share_order(d):
    return (d % 4) * 4 + d // 4


def membership(starts, counts, base):
    place = iota((1, SPAN), 1).astype(F32) + base
    own = jnp.where((starts >= base) & (starts < base + STEP), starts, 1e6)
    inside = (own <= place) & (place < own + counts)
    return jnp.where(inside, 1.0, 0.0).astype(LOW)


def word_starts(counts_row):
    earlier = iota((WORDS, WORDS), 1) < iota((WORDS, WORDS), 0)
    starts = jnp.sum(jnp.where(earlier, counts_row, 0.0), axis=1, keepdims=True)
    counts = row_to_column(counts_row)
    return starts, counts


def kernel_a(
    counts_ref, ids_ref, segs_ref, cot_hbm,
    table_ref, g1_ref, wq_ref, wk_ref, wv_ref, wo_ref, g2_ref, up_ref, down_ref, proj_ref,
    wg1_ref, wwq_hbm, wwk_hbm, wwv_hbm, wwo_hbm, wg2_ref, wup_hbm, wdown_hbm,
    keptl_hbm, keptf_hbm, gw_ref, keep_hbm, send_hbm, out_ref, gains_ref,
    cot, wwq, wwk, wwv, wwo, wup, wdown,
    tab_t, wqkv_t, wo_t, up_t, ids_t, slow, sf32, pa, pm, rowinfo,
    bundle, xs, midw, pw, actw, slopew,
    wsem, ksem, osem,
):
    phase = lax.axis_index("phase")
    loads = [
        pltpu.make_async_copy(src, dst, wsem.at[i])
        for i, (src, dst) in enumerate(
            ((wwq_hbm, wwq), (wwk_hbm, wwk), (wwv_hbm, wwv), (wwo_hbm, wwo),
             (wup_hbm, wup), (wdown_hbm, wdown), (cot_hbm.at[phase, 0], cot))
        )
    ]
    for load in loads:
        load.start()

    tab_t[...] = table_ref[...].T
    wqkv_t[0:CD] = (wq_ref[...] * 0.125).T
    wqkv_t[CD:2 * CD] = wk_ref[...].T
    wqkv_t[2 * CD:] = wv_ref[...].T
    wo_t[...] = wo_ref[...].T
    up_t[...] = up_ref[...].T
    g1 = row_to_column(g1_ref[...].astype(F32))
    g2 = row_to_column(g2_ref[...].astype(F32))
    counts_row = counts_ref[phase].astype(F32)
    starts, counts = word_starts(counts_row)
    last = jnp.max(starts)
    n_blocks = (last.astype(jnp.int32)) // STEP + 1
    ids = ids_ref[phase]
    ids_t[...] = jnp.concatenate(
        [ids[:, 128 * a:128 * a + 128] for a in range(32)], axis=0
    ).astype(F32).T.astype(LOW)
    starts_row = jnp.sum(
        jnp.where(iota((WORDS, WORDS), 0) < iota((WORDS, WORDS), 1), counts, 0.0), axis=0, keepdims=True
    )
    high = jnp.floor(starts_row * 0.0625)
    number = iota((1, WORDS), 1).astype(F32)
    rowinfo[...] = jnp.concatenate(
        [high, starts_row - 16.0 * high, number, jnp.ones((1, WORDS), F32), jnp.zeros((12, WORDS), F32)], axis=0
    ).astype(LOW)
    pa[...] = jnp.zeros_like(pa)
    pm[...] = jnp.zeros_like(pm)

    def kept_copies(b, slot):
        return (
            pltpu.make_async_copy(slow.at[slot], keptl_hbm.at[b], ksem.at[0, slot]),
            pltpu.make_async_copy(sf32.at[slot], keptf_hbm.at[b], ksem.at[1, slot]),
        )

    def block(b, carry):
        slot = lax.rem(b, 2)
        base = (b * STEP).astype(F32)

        @pl.when(b >= 2)
        def _():
            for c in kept_copies(b - 2, slot):
                c.wait()

        member = membership(starts, counts, base)
        info = nn(rowinfo[...], member)
        wid = info[2:3]
        valid = info[3:4] > 0.5
        place = iota((1, SPAN), 1).astype(F32) + base
        flat = (wid * 16.0 + place - (info[0:1] * 16.0 + info[1:2])).astype(jnp.int32)
        pick = jnp.where(iota((32, SPAN), 0) == (flat >> 7), 1.0, 0.0).astype(LOW)
        lanes = nn(ids_t[...], pick)
        ident = jnp.sum(jnp.where(iota((128, SPAN), 0) == (flat & 127), lanes, 0.0), axis=0, keepdims=True)
        ident = jnp.where(valid, ident, -1.0)
        hot = jnp.where(iota((CVOC, SPAN), 0).astype(F32) == ident, 1.0, 0.0).astype(LOW)
        emb = nn(tab_t[...], hot)
        inv1 = lax.rsqrt(jnp.mean(emb * emb, axis=0, keepdims=True) + epsilon)
        normed = (emb * inv1 * g1).astype(LOW)
        qkv = nn(wqkv_t[...], normed).astype(LOW)
        slow[slot, R_EMB:R_EMB + CD] = emb.astype(LOW)
        slow[slot, R_Q:R_Q + 2 * CD] = qkv[:2 * CD]
        key_rows = qkv[CD:2 * CD].T
        value_t = qkv[2 * CD:]
        slow[slot, R_V:R_V + SPAN] = value_t.T
        same = lax.dot_general(member, member, (((0,), (0,)), ((), ())), preferred_element_type=F32) > 0.5
        mixed = []
        for h in range(CHAR_HEADS):
            hs = slice(h * HEAD, (h + 1) * HEAD)
            s = nn(key_rows[:, hs], qkv[hs])
            s = jnp.where(same, s, floor_score)
            e = jnp.exp(s - jnp.max(s, axis=0, keepdims=True))
            p = (e * (1.0 / jnp.sum(e, axis=0, keepdims=True))).astype(LOW)
            slow[slot, R_P + h * SPAN:R_P + (h + 1) * SPAN] = p
            mixed.append(nn(value_t[hs], p).astype(LOW))
        mixed = jnp.concatenate(mixed, axis=0)
        slow[slot, R_MIX:R_MIX + CD] = mixed
        middle = emb + nn(wo_t[...], mixed)
        inv2 = lax.rsqrt(jnp.mean(middle * middle, axis=0, keepdims=True) + epsilon)
        sf32[slot, 0:CD] = middle
        sf32[slot, CD:] = jnp.concatenate([inv1, inv2, ident, jnp.zeros((5, SPAN), F32)], axis=0)
        normed_two = (middle * inv2 * g2).astype(LOW)
        for c in range(CFF // 256):
            cs = slice(c * 256, (c + 1) * 256)
            before = nn(up_t[cs], normed_two)
            act, slope = gelu_pair(before)
            slow[slot, R_SLOPE + c * 256:R_SLOPE + (c + 1) * 256] = slope.astype(LOW)
            pa[:, cs] += nt(member, act.astype(LOW))
        middle_hi = middle.astype(LOW)
        middle_lo = (middle - middle_hi.astype(F32)).astype(LOW)
        pm[...] += nt(member, middle_hi) + nt(member, middle_lo)
        for c in kept_copies(b, slot):
            c.start()
        return carry

    lax.fori_loop(0, n_blocks, block, 0)

    pa_hi = pa[...].astype(LOW)
    pa_lo = (pa[...] - pa_hi.astype(F32)).astype(LOW)
    per_count = 1.0 / counts
    pooled = (pm[...] + nn(pa_hi, down_ref[...]) + nn(pa_lo, down_ref[...])) * per_count
    pooled_low = pooled.astype(LOW)
    x = nn(pooled_low, proj_ref[...]).astype(LOW).astype(F32)
    xs[...] = x
    for load in loads:
        load.wait()
    wg1 = wg1_ref[...].astype(F32)
    wg2 = wg2_ref[...].astype(F32)
    winv1 = lax.rsqrt(jnp.mean(x * x, axis=1, keepdims=True) + epsilon)
    normed = (x * winv1 * wg1).astype(LOW)
    q = (nn(normed, wwq[...]) * 0.125).astype(LOW)
    k = nn(normed, wwk[...]).astype(LOW)
    v = nn(normed, wwv[...]).astype(LOW)
    seg_row = segs_ref[phase].astype(F32)
    seg_col = row_to_column(seg_row)
    allowed = (seg_row == seg_col) & (iota((WORDS, WORDS), 0) <= iota((WORDS, WORDS), 1))
    k_t = k.T
    v_t = v.T
    mixed_t = []
    for h in range(WORD_HEADS):
        hs = slice(h * HEAD, (h + 1) * HEAD)
        s = nt(k[:, hs], q[:, hs])
        s = jnp.where(allowed, s, floor_score)
        e = jnp.exp(s - jnp.max(s, axis=0, keepdims=True))
        p = (e * (1.0 / jnp.sum(e, axis=0, keepdims=True))).astype(LOW)
        pw[h] = p
        mixed_t.append(nn(v_t[hs], p).astype(LOW))
    mixed_t = jnp.concatenate(mixed_t, axis=0)
    middle = x + nn(mixed_t.T, wwo[...])
    midw[...] = middle
    winv2 = lax.rsqrt(jnp.mean(middle * middle, axis=1, keepdims=True) + epsilon)
    normed_two = (middle * winv2 * wg2).astype(LOW)
    result = middle
    for c in range(WFF // 512):
        cs = slice(c * 512, (c + 1) * 512)
        act, slope = gelu_pair(nn(normed_two, wup[:, cs]))
        act = act.astype(LOW)
        actw[:, cs] = act
        slopew[:, cs] = slope.astype(LOW)
        result = result + nn(act, wdown[cs, :])
    out_ref[...] = result.astype(LOW)

    mine = phase
    def place(row, value, width):
        n = value.shape[0] // SHARES
        low = value.astype(LOW)
        for half in range(2):
            side = jnp.bitwise_xor(mine, half)
            for piece in range(max(1, width // 256)):
                cols = low[:, half * width + piece * 256:half * width + piece * 256 + min(width, 256)]
                for d in range(SHARES):
                    part = cols[d * n:(d + 1) * n]
                    if width == 128:
                        part = jnp.concatenate([part[:n // 2], part[n // 2:]], axis=1)
                    m = part.shape[0]
                    bundle[side, share_order(d), row + piece * n:row + piece * n + m, :] = part

    cot_low = cot[...]
    n2d = jnp.zeros((WORDS, WD), F32)
    n2_t = normed_two.T
    for c in range(WFF // 512):
        cs = slice(c * 512, (c + 1) * 512)
        gd = nn(actw[:, cs].T, cot_low)
        low = gd.astype(LOW)
        for half in range(2):
            side = jnp.bitwise_xor(mine, half)
            for i in range(4):
                d = c * 4 + i
                bundle[side, share_order(d), W_DOWN:W_DOWN + 128, :] = low[i * 128:(i + 1) * 128, half * 256:half * 256 + 256]
        bd = (nt(cot_low, wdown[cs, :]) * slopew[:, cs].astype(F32)).astype(LOW)
        gu = nn(n2_t, bd).astype(LOW)
        half = c // 2
        side = jnp.bitwise_xor(mine, half)
        for piece in range(2):
            row = W_UP + ((c % 2) * 2 + piece) * 32
            for d in range(SHARES):
                bundle[side, share_order(d), row:row + 32, :] = gu[d * 32:(d + 1) * 32, piece * 256:piece * 256 + 256]
        n2d = n2d + nt(bd, wup[:, cs])
    middle = midw[...]
    vhat = middle * winv2
    gain2 = jnp.sum(n2d * vhat, axis=0, keepdims=True)
    lifted = n2d * wg2
    md = cot_low.astype(F32) + winv2 * (lifted - vhat * jnp.mean(lifted * vhat, axis=1, keepdims=True))
    md_low = md.astype(LOW)
    place(W_O, nn(mixed_t, md_low), 256)
    do = nt(md_low, wwo[...]).astype(LOW)
    dq_t, dk, dv = [], [], []
    for h in range(WORD_HEADS):
        hs = slice(h * HEAD, (h + 1) * HEAD)
        p = pw[h]
        pf = p.astype(F32)
        dp = nt(v[:, hs], do[:, hs])
        ds = (pf * (dp - jnp.sum(pf * dp, axis=0, keepdims=True))).astype(LOW)
        dq_t.append(nn(k_t[hs], ds))
        dk.append(nn(ds, q[:, hs]))
        dv.append(nn(p, do[:, hs]))
    dq = (jnp.concatenate(dq_t, axis=0) * 0.125).astype(LOW).T
    dk = jnp.concatenate(dk, axis=1).astype(LOW)
    dv = jnp.concatenate(dv, axis=1).astype(LOW)
    normed_t = normed.T
    place(W_Q, nn(normed_t, dq), 256)
    place(W_K, nn(normed_t, dk), 256)
    place(W_V, nn(normed_t, dv), 256)
    nd = nt(dq, wwq[...]) + nt(dk, wwk[...]) + nt(dv, wwv[...])
    vhat = xs[...] * winv1
    gain1 = jnp.sum(nd * vhat, axis=0, keepdims=True)
    lifted = nd * wg1
    xd = md + winv1 * (lifted - vhat * jnp.mean(lifted * vhat, axis=1, keepdims=True))
    vd = xd.astype(LOW)
    place(W_PROJ, nn(pooled_low.T, vd), 256)
    gw = (nt(vd, proj_ref[...]) * per_count).astype(LOW)
    gw_ref[...] = gw.T
    place(W_CDOWN, nn(pa_hi.T, gw), 128)
    gains_ref[...] = jnp.concatenate([gain1, gain2, jnp.zeros((6, WD), F32)], axis=0)
    stores = [
        pltpu.make_async_copy(bundle.at[0], keep_hbm, osem.at[0]),
        pltpu.make_async_copy(bundle.at[1], send_hbm, osem.at[1]),
    ]
    for s in stores:
        s.start()

    def drain(b, carry):
        for c in kept_copies(b, lax.rem(b, 2)):
            c.wait()
        return carry

    lax.fori_loop(jnp.maximum(n_blocks - 2, 0), n_blocks, drain, 0)
    for s in stores:
        s.wait()


def kernel_b(
    counts_ref, gw_ref, wgains_ref, g1_ref, wq_ref, wk_ref, wv_ref, wo_ref, g2_ref, up_ref, down_ref,
    keptl_hbm, keptf_hbm,
    keep_hbm, send_hbm,
    slow, sf32, wqkv, aup, aqkv, ao, atab, ag1, ag2, bundle, ksem, osem,
):
    phase = lax.axis_index("phase")
    counts_row = counts_ref[phase].astype(F32)
    starts, counts = word_starts(counts_row)
    n_blocks = jnp.max(starts).astype(jnp.int32) // STEP + 1

    def kept_copies(b, slot):
        return (
            pltpu.make_async_copy(keptl_hbm.at[b], slow.at[slot], ksem.at[0, slot]),
            pltpu.make_async_copy(keptf_hbm.at[b], sf32.at[slot], ksem.at[1, slot]),
        )

    for c in kept_copies(0, 0):
        c.start()
    g1 = row_to_column(g1_ref[...].astype(F32))
    g2 = row_to_column(g2_ref[...].astype(F32))
    for i, w in enumerate((wq_ref, wk_ref, wv_ref)):
        wqkv[:, i * CD:(i + 1) * CD] = w[...]
    for acc in (aup, aqkv, ao, atab, ag1, ag2):
        acc[...] = jnp.zeros_like(acc)

    def block(b, carry):
        slot = lax.rem(b, 2)
        base = (b * STEP).astype(F32)

        @pl.when(b + 1 < n_blocks)
        def _():
            for c in kept_copies(b + 1, 1 - slot):
                c.start()

        for c in kept_copies(b, slot):
            c.wait()
        member = membership(starts, counts, base)
        middle = sf32[slot, 0:CD]
        inv1 = sf32[slot, CD:CD + 1]
        inv2 = sf32[slot, CD + 1:CD + 2]
        ident = sf32[slot, CD + 2:CD + 3]
        g_low = nn(gw_ref[...], member).astype(LOW)
        vhat = middle * inv2
        normed_two = (vhat * g2).astype(LOW)
        n2d = jnp.zeros((CD, SPAN), F32)
        for c in range(CFF // 256):
            cs = slice(c * 256, (c + 1) * 256)
            slope = slow[slot, R_SLOPE + c * 256:R_SLOPE + (c + 1) * 256].astype(F32)
            bd = (nn(down_ref[cs, :], g_low) * slope).astype(LOW)
            aup[:, cs] += nt(normed_two, bd)
            n2d = n2d + nn(up_ref[:, cs], bd)
        ag2[...] += n2d * vhat
        lifted = n2d * g2
        md = g_low.astype(F32) + inv2 * (lifted - vhat * jnp.mean(lifted * vhat, axis=0, keepdims=True))
        md_low = md.astype(LOW)
        ao[...] += nt(slow[slot, R_MIX:R_MIX + CD], md_low)
        do = nn(wo_ref[...], md_low).astype(LOW)
        dq, dk, dv = [], [], []
        v = slow[slot, R_V:R_V + SPAN]
        for h in range(CHAR_HEADS):
            hs = slice(h * HEAD, (h + 1) * HEAD)
            p = slow[slot, R_P + h * SPAN:R_P + (h + 1) * SPAN]
            pf = p.astype(F32)
            dp = nn(v[:, hs], do[hs])
            ds = (pf * (dp - jnp.sum(pf * dp, axis=0, keepdims=True))).astype(LOW)
            dq.append((nn(slow[slot, R_K + h * HEAD:R_K + (h + 1) * HEAD], ds) * 0.125).astype(LOW))
            dk.append(nt(slow[slot, R_Q + h * HEAD:R_Q + (h + 1) * HEAD], ds).astype(LOW))
            dv.append(nt(do[hs], p).astype(LOW))
        dqkv = jnp.concatenate(dq + dk + dv, axis=0)
        emb = slow[slot, R_EMB:R_EMB + CD].astype(F32)
        ehat = emb * inv1
        normed = (ehat * g1).astype(LOW)
        aqkv[...] += nt(normed, dqkv)
        nd = nn(wqkv[...], dqkv)
        ag1[...] += nd * ehat
        lifted = nd * g1
        ed = md + inv1 * (lifted - ehat * jnp.mean(lifted * ehat, axis=0, keepdims=True))
        hot = jnp.where(iota((CVOC, SPAN), 0).astype(F32) == ident, 1.0, 0.0).astype(LOW)
        atab[...] += nt(hot, ed.astype(LOW))
        return carry

    lax.fori_loop(0, n_blocks, block, 0)

    def place(row, value, width):
        n = value.shape[0] // SHARES
        low = value.astype(LOW)
        for half in range(2):
            side = jnp.bitwise_xor(phase, half)
            for piece in range(width // 128):
                cols = low[:, half * width + piece * 128:half * width + piece * 128 + 128]
                for d in range(SHARES):
                    bundle[side, share_order(d), row + piece * n:row + piece * n + n, :] = cols[d * n:(d + 1) * n]

    place(C_TABLE, atab[...], 128)
    place(C_Q, aqkv[:, 0:CD], 128)
    place(C_K, aqkv[:, CD:2 * CD], 128)
    place(C_V, aqkv[:, 2 * CD:], 128)
    place(C_O, ao[...], 128)
    place(C_UP, aup[...], 512)
    cg = jnp.concatenate(
        [jnp.sum(ag1[...], axis=1, keepdims=True), jnp.sum(ag2[...], axis=1, keepdims=True)], axis=1
    )
    cg = jnp.concatenate([cg, jnp.zeros((CD, 126), F32)], axis=1).T
    wg = wgains_ref[...]
    for d in range(SHARES):
        rows = [
            jnp.concatenate([cg[0:1, d * 16:d * 16 + 16], jnp.zeros((1, 112), F32)], axis=1),
            jnp.concatenate([cg[1:2, d * 16:d * 16 + 16], jnp.zeros((1, 112), F32)], axis=1),
            jnp.concatenate([wg[0:1, d * 32:d * 32 + 32], jnp.zeros((1, 96), F32)], axis=1),
            jnp.concatenate([wg[1:2, d * 32:d * 32 + 32], jnp.zeros((1, 96), F32)], axis=1),
            jnp.zeros((12, 128), F32),
        ]
        tile = jnp.concatenate(rows, axis=0).astype(LOW)
        bundle[0, share_order(d), C_GAIN:C_GAIN + 16, :] = tile
        bundle[1, share_order(d), C_GAIN:C_GAIN + 16, :] = tile
    stores = [
        pltpu.make_async_copy(bundle.at[0], keep_hbm, osem.at[0]),
        pltpu.make_async_copy(bundle.at[1], send_hbm, osem.at[1]),
    ]
    for s in stores:
        s.start()
    for s in stores:
        s.wait()


ANYWHERE = pl.BlockSpec(memory_space=pl.ANY)
INSIDE = pl.BlockSpec(memory_space=pltpu.VMEM)


def call_a(char_counts, char_ids, segment_ids, out_cotangent, weights):
    shape = jax.ShapeDtypeStruct
    v = pltpu.VMEM
    return pl.pallas_call(
        kernel_a,
        out_shape=(
            shape((BLOCKS, KEPT_LOW, SPAN), LOW),
            shape((BLOCKS, KEPT_F32, SPAN), F32),
            shape((CD, WORDS), LOW),
            shape((SHARES, W_ROWS, 256), LOW),
            shape((SHARES, W_ROWS, 256), LOW),
            shape((WORDS, WD), LOW),
            shape((8, WD), F32),
        ),
        in_specs=[INSIDE] * 3 + [ANYWHERE] + [INSIDE] * 10 + [INSIDE] + [ANYWHERE] * 4 + [INSIDE] + [ANYWHERE] * 2,
        out_specs=(ANYWHERE, ANYWHERE, INSIDE, ANYWHERE, ANYWHERE, INSIDE, INSIDE),
        scratch_shapes=[
            v((WORDS, WD), LOW),
            v((WD, WD), LOW), v((WD, WD), LOW), v((WD, WD), LOW), v((WD, WD), LOW),
            v((WD, WFF), LOW), v((WFF, WD), LOW),
            v((CD, CVOC), LOW), v((3 * CD, CD), LOW), v((CD, CD), LOW), v((CFF, CD), LOW), v((128, 32), LOW),
            v((2, KEPT_LOW, SPAN), LOW), v((2, KEPT_F32, SPAN), F32),
            v((WORDS, CFF), F32), v((WORDS, CD), F32), v((16, WORDS), LOW),
            v((2, SHARES, W_ROWS, 256), LOW),
            v((WORDS, WD), F32), v((WORDS, WD), F32),
            v((WORD_HEADS, WORDS, WORDS), LOW), v((WORDS, WFF), LOW), v((WORDS, WFF), LOW),
            pltpu.SemaphoreType.DMA((7,)),
            pltpu.SemaphoreType.DMA((2, 2)),
            pltpu.SemaphoreType.DMA((2,)),
        ],
        compiler_params=pltpu.CompilerParams(vmem_limit_bytes=60 * 2**20),
        cost_estimate=pl.CostEstimate(flops=20 * 10**9, bytes_accessed=60 * 10**6, transcendentals=10**6),
        name="forward_and_words",
    )(char_counts, char_ids, segment_ids, out_cotangent, *weights)


def call_b(char_counts, gw, wgains, weights, keptl, keptf):
    shape = jax.ShapeDtypeStruct
    v = pltpu.VMEM
    return pl.pallas_call(
        kernel_b,
        out_shape=(shape((SHARES, C_ROWS, 128), LOW), shape((SHARES, C_ROWS, 128), LOW)),
        in_specs=[INSIDE] * 11 + [ANYWHERE] * 2,
        out_specs=(ANYWHERE, ANYWHERE),
        scratch_shapes=[
            v((2, KEPT_LOW, SPAN), LOW), v((2, KEPT_F32, SPAN), F32),
            v((CD, 3 * CD), LOW),
            v((CD, CFF), F32), v((CD, 3 * CD), F32), v((CD, CD), F32), v((CVOC, CD), F32),
            v((CD, SPAN), F32), v((CD, SPAN), F32),
            v((2, SHARES, C_ROWS, 128), LOW),
            pltpu.SemaphoreType.DMA((2, 2)),
            pltpu.SemaphoreType.DMA((2,)),
        ],
        compiler_params=pltpu.CompilerParams(vmem_limit_bytes=60 * 2**20),
        cost_estimate=pl.CostEstimate(flops=20 * 10**9, bytes_accessed=60 * 10**6, transcendentals=10**6),
        name="character_backward",
    )(char_counts, gw, wgains, *weights, keptl, keptf)


def flip(value, axis, bits):
    count = lax.axis_size(axis)
    return lax.ppermute(value, axis, [(i, i ^ bits) for i in range(count)])


def pick(value, index):
    return lax.dynamic_index_in_dim(value, index, 0, keepdims=False)


def scatter_sum(keep, send):
    rows, width = keep.shape[1:]
    got = flip(send, "phase", 1)
    total = (keep.astype(F32) + got.astype(F32)).astype(LOW).reshape(4, 4, rows, width)
    dp = lax.axis_index("dp")
    plane, line = lax.rem(dp, 4), lax.div(dp, 4)
    got = [flip(pick(total, lax.bitwise_xor(plane, k)), "dp", k) for k in range(1, 4)]
    total = pick(total, plane).astype(F32)
    for g in got:
        total = total + g.astype(F32)
    total = total.astype(LOW)
    got = [flip(pick(total, lax.bitwise_xor(line, k)), "dp", 4 * k) for k in range(1, 4)]
    total = pick(total, line).astype(F32)
    for g in got:
        total = total + g.astype(F32)
    return total


def body(
    char_ids, char_counts, segment_ids, out_cotangent,
    char_table, char_gain_one, char_query, char_key, char_value, char_output, char_gain_two, char_up, char_down,
    char_project,
    word_gain_one, word_query, word_key, word_value, word_output, word_gain_two, word_up, word_down,
):
    phase = lax.axis_index("phase")
    g1, g2 = char_gain_one.reshape(1, CD), char_gain_two.reshape(1, CD)
    wg1, wg2 = word_gain_one.reshape(1, WD), word_gain_two.reshape(1, WD)
    keptl, keptf, gw, wkeep, wsend, word_out, wgains = call_a(
        char_counts, char_ids, segment_ids, out_cotangent,
        (char_table, g1, char_query, char_key, char_value, char_output, g2, char_up, char_down, char_project,
         wg1, word_query, word_key, word_value, word_output, wg2, word_up, word_down),
    )
    ckeep, csend = call_b(
        char_counts, gw, wgains,
        (g1, char_query, char_key, char_value, char_output, g2, char_up, char_down), keptl, keptf,
    )
    halves = word_out.reshape(WORDS, 2, WD // 2).transpose(1, 0, 2)
    got = flip(pick(halves, 1 - phase), "phase", 1)
    own = pick(halves, phase)
    first = phase == 0
    outs = jnp.stack([jnp.where(first, own, got), jnp.where(first, got, own)])[:, None]
    if lax.axis_size("dp") == SHARES:
        w = scatter_sum(wkeep, wsend)
        c = scatter_sum(ckeep, csend)
        cdown = w[W_CDOWN:W_CDOWN + 32]
        cdown = jnp.concatenate([cdown[:, :128], cdown[:, 128:]], axis=0)

        def wide(rows, pieces, n):
            return jnp.concatenate([rows[i * n:(i + 1) * n] for i in range(pieces)], axis=1)

        return (
            outs,
            c[C_TABLE:C_TABLE + 16], c[C_GAIN, :16],
            c[C_Q:C_Q + 16], c[C_K:C_K + 16], c[C_V:C_V + 16], c[C_O:C_O + 16], c[C_GAIN + 1, :16],
            wide(c[C_UP:C_UP + 64], 4, 16), cdown, w[W_PROJ:W_PROJ + 16],
            c[C_GAIN + 2, :32],
            w[W_Q:W_Q + 32], w[W_K:W_K + 32], w[W_V:W_V + 32], w[W_O:W_O + 32], c[C_GAIN + 3, :32],
            wide(w[W_UP:W_UP + 128], 4, 32), w[W_DOWN:W_DOWN + 128],
        )
    return general_sums(outs, wkeep, wsend, ckeep, csend)


def general_sums(outs, wkeep, wsend, ckeep, csend):
    order = jnp.asarray([share_order(d) for d in range(SHARES)])

    def natural(keep, send):
        total = keep.astype(F32) + flip(send, "phase", 1).astype(F32)
        return jnp.take(total, order, axis=0)

    w, c = natural(wkeep, wsend), natural(ckeep, csend)

    def whole(rows):
        return rows.reshape(-1, rows.shape[-1])

    def wide(rows, pieces):
        n = rows.shape[1] // pieces
        return whole(rows.reshape(SHARES, pieces, n, rows.shape[-1]).transpose(0, 2, 1, 3).reshape(SHARES, n, -1))

    cdown = w[:, W_CDOWN:W_CDOWN + 32]
    cdown = jnp.concatenate([cdown[..., :128], cdown[..., 128:]], axis=1)
    parts = (
        whole(c[:, C_TABLE:C_TABLE + 16]), c[:, C_GAIN, :16].reshape(-1),
        whole(c[:, C_Q:C_Q + 16]), whole(c[:, C_K:C_K + 16]), whole(c[:, C_V:C_V + 16]), whole(c[:, C_O:C_O + 16]),
        c[:, C_GAIN + 1, :16].reshape(-1),
        wide(c[:, C_UP:C_UP + 64], 4), whole(cdown), whole(w[:, W_PROJ:W_PROJ + 16]),
        c[:, C_GAIN + 2, :32].reshape(-1),
        whole(w[:, W_Q:W_Q + 32]), whole(w[:, W_K:W_K + 32]), whole(w[:, W_V:W_V + 32]), whole(w[:, W_O:W_O + 32]),
        c[:, C_GAIN + 3, :32].reshape(-1),
        wide(w[:, W_UP:W_UP + 128], 4), whole(w[:, W_DOWN:W_DOWN + 128]),
    )
    return (outs,) + tuple(lax.psum_scatter(p, "dp", scatter_dimension=0, tiled=True) for p in parts)


def solution(mesh):
    rows = P(None, "dp", None)
    both = P("dp", "phase")
    one = P("dp")
    return jax.shard_map(
        body,
        mesh=mesh,
        in_specs=(rows, rows, rows, P(None, "dp", None, None)) + (P(),) * 18,
        out_specs=(
            P(None, "dp", None, "phase"),
            both, one, both, both, both, both, one, both, both, both,
            one, both, both, both, both, one, both, both,
        ),
        check_vma=False,
    )
```

time: 2030 us -> 193 us (0.10)
  waiting for transfers between devices: 1130 us -> 58.4 us
  local copies, waits for them, and re-layouts: 395 us -> 13.6 us
  matrix products: 288 us -> 0 us
  other arithmetic: 127 us -> 8.74 us
  Pallas kernels: 0 us -> 93.6 us
  blocking collectives: 43.5 us -> 0 us
    reduce_scatter x22 -> x0, waiting for transfers between devices: 1120 us -> none  [the longest x14 1040 us: body(): lax.psum_scatter(local_total, 'dp', scatter_dimension=0, tiled=True)]
    dot_general x70 -> x0, matrix products: 288 us -> none  [the longest x24 89.6 us: product(): return jnp.dot(left, right, preferred_element_type=jnp.float32)]
    convert_element_type x28 -> x0, local copies, waits for them, and re-layouts: 158 us -> none  [the longest x8 44.6 us: layer_forward(): heads_forward(query_low, key_low, value_low, setup).astype(jnp.bfloat16)]
    pallas_call x0 -> x2, Pallas kernels: none -> 93.6 us  [the longest x1 53.4 us: call_a(): pl.pallas_call(kernel_a, out_shape=(shape((BLOCKS, KEPT_LOW, SPAN), LOW),...]
    reshape x14 -> x5, local copies, waits for them, and re-layouts: 100 us -> 6.82 us  [the longest x2 2.52 us: body(): wg1, wg2 = (word_gain_one.reshape(1, WD), word_gain_two.reshape(1, WD))]
    gather x4 -> x0, local copies, waits for them, and re-layouts: 58.4 us -> none  [char_forward(): embedded = jnp.take(char_table, identifiers, axis=0).astype(jnp.float32)]
    ppermute x6 -> x15, waiting for transfers between devices: 0.02 us -> 58.4 us  [flip(): return lax.ppermute(value, axis, [(i, i ^ bits) for i in range(count)])]
    convert_element_type x52 -> x4, other arithmetic: 55.5 us -> 4.94 us  [the longest x2 4.36 us: scatter_sum(): (keep.astype(F32) + got.astype(F32)).astype(LOW).reshape(4, 4, rows, width)]
  transfers between devices with their start and end apart: 34 -> 15, of which waited for: 23 -> 8; matrix products, arithmetic and copies ran while one was open for 22% -> 7% of each run, Pallas kernels for 0% -> 21%
where the time goes in v1:
time: 193 us
  Pallas kernels  93.6 us (48%)
  waiting for transfers between devices  58.4 us (30%)
  starting transfers between devices  17.6 us (9%)
  local copies, waits for them, and re-layouts  13.6 us (7%)
  other arithmetic  8.74 us (5%)
    ppermute x15, waiting for transfers between devices, flip(): return lax.ppermute(value, axis, [(i, i ^ bits) for i in range(count)])  58.4 us
    pallas_call x1, Pallas kernels, call_a(): pl.pallas_call(kernel_a, out_shape=(shape((BLOCKS, KEPT_LOW, SPAN), LOW),...  53.4 us
    pallas_call x1, Pallas kernels, call_b(): pl.pallas_call(kernel_b, out_shape=(shape((SHARES, C_ROWS, 128), LOW), sh...  40.2 us
    ppermute x15, starting transfers between devices, flip(): return lax.ppermute(value, axis, [(i, i ^ bits) for i in range(count)])  17.6 us
    convert_element_type x2, other arithmetic, scatter_sum(): (keep.astype(F32) + got.astype(F32)).astype(LOW).reshape(4, 4, rows, width)  4.36 us
  transfers between devices with their start and end apart: 15, of which 8 were waited for; matrix products, arithmetic and copies ran while one was open for 7% of the time, Pallas kernels for 21%

profile of v1, /device:TPU:0, one launch (start us, length us, event | category | flops | bytes accessed | tf_op | source)
XLA Modules:
  0.0 192.8 jit_solution(15830233838441303225)
XLA Ops:
  0.7 1.2 reshape.71.g1_ref
  1.9 1.2 reshape.72.g2_ref
  3.1 1.3 reshape.73.wg1_ref
  4.4 1.3 reshape.74.wg2_ref
  5.6 53.4 %forward_and_words.1 = (bf16[18,3328,256]{2,1,0:T(8,128)(2,1)}, f32[18,264,256]{2,1,0:T(8,128)}, bf16[256,256]{1,0:T(8,128)(2,1)}, bf16[16,432,256]{2,1,0:T(8,12...) custom-call(s32[2,1,256]{2,1,0:T(1,128)} %counts_ref.3, ...), custom_call_target="tpu_custom_call" | custom-call | flops 20000000000 | bytes 60000000 | tf_op jit(solution)/shard_map/forward_and_words/pallas_call | solution.py:470
  59.5 40.2 %character_backward.1 = (bf16[16,160,128]{2,1,0:T(8,128)(2,1)}, bf16[16,160,128]{2,1,0:T(8,128)(2,1)}) custom-call(s32[2,1,256]{2,1,0:T(1,128)} %counts_ref.3, bf16[256,256]{1,0:T(8,128)(2,1)} %get-tuple-element.29.gw_ref, f32[8,512]{1,0:T(8,128)} %get-tuple-element.30.wgains_ref, bf16[1,256]{1,0:T(2,128)(2,1)} %reshape.71.g1_ref, bf16[256,256]{1,0:T(8,128)(2,1)} %wq_ref.3, ...), custom_call_target="tpu_custom_call" | custom-call | flops 20000000000 | bytes 60000000 | tf_op jit(solution)/shard_map/character_backward/pallas_call | solution.py:506
  99.9 1.9 reshape.75
  101.7 2.3 %constant_dynamic-slice_fusion.1 = (bf16[256,1,256]{2,1,0:T(2,128)(2,1)}, bf16[256,1,256]{2,1,0:T(2,128)(2,1)S(1)}) fusion(bf16[256,2,256]{2,1,0:T(2,128)(2,1)} %reshape.75, s32[]{:T(128)S(6)} %select_n.56, s32[]{:T(128)S(6)} %select_n.57), kind=kLoop, calls=%fused_computation.37 | loop fusion | bytes 524296 | tf_op jit(solution)/shard_map/dynamic-slice
  104.0 0.7 copy.52
  105.3 1.5 add_convert_fusion.1
  106.8 3.3 %collective-permute-start.4 = (bf16[4,160,128]{2,1,0:T(8,128)(2,1)S(1)}, bf16[4,160,128]{2,1,0:T(8,128)(2,1)S(1)}, u32[]{:S(2)}, u32[]{:S(2)}) collective-permute-start(bf16[4,160,128]{2,1,0:T(8,128)(2,1)S(1)} %get-tuple-element.63), channel_id=1, source_target_pairs={{0,3},{1,2},{2,1},{3,0},{4,7},{5,6},{6,5},{7,4},{8,11},{9,10},{10,... | collective-permute-start | bytes 491528 | tf_op jit(solution)/shard_map/ppermute | solution.py:528
  110.0 0.6 collective-permute-start.2
  110.7 1.0 select_bitcast_fusion.1
  111.7 3.3 %collective-permute-done.4 = bf16[4,160,128]{2,1,0:T(8,128)(2,1)S(1)} collective-permute-done((bf16[4,160,128]{2,1,0:T(8,128)(2,1)S(1)}, bf16[4,160,128]{2,1,0:T(8,128)(2,1)S(1)}, u32[]{:S(2)}, u32[]{:S(2)}) %collective-permute-start.4) | collective-permute-done | bytes 163872 | tf_op jit(solution)/shard_map/ppermute | solution.py:528
  115.0 3.1 %collective-permute-done.3 = bf16[4,160,128]{2,1,0:T(8,128)(2,1)S(1)} collective-permute-done((bf16[4,160,128]{2,1,0:T(8,128)(2,1)S(1)}, bf16[4,160,128]{2,1,0:T(8,128)(2,1)S(1)}, u32[]{:S(2)}, u32[]{:S(2)}) %collective-permute-start.3) | collective-permute-done | bytes 163872 | tf_op jit(solution)/shard_map/ppermute | solution.py:528
  118.5 3.3 %collective-permute-start.7 = (bf16[160,128]{1,0:T(8,128)(2,1)S(1)}, bf16[160,128]{1,0:T(8,128)(2,1)S(1)}, u32[]{:S(2)}, u32[]{:S(2)}) collective-permute-start(bf16[160,128]{1,0:T(8,128)(2,1)S(1)} %get-tuple-element.80), channel_id=1, source_target_pairs={{0,12},{1,13},{2,14},{3,15},{4,8},{5,9},{6,10},{7,11},{8,4},{9,5},... | collective-permute-start | bytes 122888 | tf_op jit(solution)/shard_map/ppermute | solution.py:528
  121.8 1.1 collective-permute-start.5
  123.0 2.9 %add_convert_fusion = bf16[16,432,256]{2,1,0:T(8,128)(2,1)S(1)} fusion(bf16[16,432,256]{2,1,0:T(8,128)(2,1)} %collective-permute-done.8, bf16[16,432,256]{2,1,0:T(8,128)(2,1)S(1)} %copy-done), kind=kLoop, calls=%fused_computation | loop fusion | flops 7077888 | bytes 10616832 | tf_op jit(solution)/shard_map/convert_element_type | solution.py:538
  126.1 1.6 collective-permute-start.11
  127.7 1.4 collective-permute-start.10
  129.6 0.7 maximum_bitcast_fusion
  130.4 0.6 fusion.12
  131.0 0.6 pad_maximum_fusion.1
  132.1 17.5 %collective-permute-done.11 = bf16[4,432,256]{2,1,0:T(8,128)(2,1)S(1)} collective-permute-done((bf16[4,432,256]{2,1,0:T(8,128)(2,1)S(1)}, bf16[4,432,256]{2,1,0:T(8,128)(2,1)S(1)}, u32[]{:S(2)}, u32[]{:S(2)}) %collective-permute-start.11) | collective-permute-done | bytes 884768 | tf_op jit(solution)/shard_map/ppermute | solution.py:528
  149.6 16.8 %collective-permute-done.10 = bf16[4,432,256]{2,1,0:T(8,128)(2,1)S(1)} collective-permute-done((bf16[4,432,256]{2,1,0:T(8,128)(2,1)S(1)}, bf16[4,432,256]{2,1,0:T(8,128)(2,1)S(1)}, u32[]{:S(2)}, u32[]{:S(2)}) %collective-permute-start.10) | collective-permute-done | bytes 884768 | tf_op jit(solution)/shard_map/ppermute | solution.py:528
  167.3 3.3 %collective-permute-start.14 = (bf16[432,256]{1,0:T(8,128)(2,1)S(1)}, bf16[432,256]{1,0:T(8,128)(2,1)S(1)}, u32[]{:S(2)}, u32[]{:S(2)}) collective-permute-start(bf16[432,256]{1,0:T(8,128)(2,1)S(1)} %get-tuple-element.60), channel_id=1, source_target_pairs={{0,12},{1,13},{2,14},{3,15},{4,8},{5,9},{6,10},{7,11},{8,4},{9,5},... | collective-permute-start | bytes 663560 | tf_op jit(solution)/shard_map/ppermute | solution.py:528
  170.6 1.1 collective-permute-start.12
  172.3 5.3 %collective-permute-done.14 = bf16[432,256]{1,0:T(8,128)(2,1)S(1)} collective-permute-done((bf16[432,256]{1,0:T(8,128)(2,1)S(1)}, bf16[432,256]{1,0:T(8,128)(2,1)S(1)}, u32[]{:S(2)}, u32[]{:S(2)}) %collective-permute-start.14) | collective-permute-done | bytes 221216 | tf_op jit(solution)/shard_map/ppermute | solution.py:528
  177.6 11.8 %collective-permute-done.13 = bf16[432,256]{1,0:T(8,128)(2,1)S(1)} collective-permute-done((bf16[432,256]{1,0:T(8,128)(2,1)S(1)}, bf16[432,256]{1,0:T(8,128)(2,1)S(1)}, u32[]{:S(2)}, u32[]{:S(2)}) %collective-permute-start.13) | collective-permute-done | bytes 221216 | tf_op jit(solution)/shard_map/ppermute | solution.py:528
  190.2 0.7 fusion.10
  190.8 0.7 slice.137
  192.1 0.7 pad_maximum_fusion
  (31 shorter events, 5.7 us)
Async XLA Ops:
  59.0 63.9 %collective-permute-start.8 = (bf16[16,432,256]{2,1,0:T(8,128)(2,1)}, bf16[16,432,256]{2,1,0:T(8,128)(2,1)}, u32[]{:S(2)}, u32[]{:S(2)}) collective-permute-start(bf16[16,432,256]{2,1,0:T(8,128)(2,1)} %get-tuple-element.36), channel_id=1, source_target_pairs={{0,16},{16,0},{1,17},{17,1},{2,18},{18,2},{3,19},{19,3},{4,20},{20... | collective-permute-start | bytes 10616840 | tf_op jit(solution)/shard_map/ppermute | solution.py:528
  99.8 23.2 %copy-start = (bf16[16,432,256]{2,1,0:T(8,128)(2,1)S(1)}, bf16[16,432,256]{2,1,0:T(8,128)(2,1)}, u32[]{:S(2)}) copy-start(bf16[16,432,256]{2,1,0:T(8,128)(2,1)} %get-tuple-element.35) | copy-start | bytes 10616836
  99.8 5.5 %collective-permute-start.1 = (bf16[16,160,128]{2,1,0:T(8,128)(2,1)}, bf16[16,160,128]{2,1,0:T(8,128)(2,1)}, u32[]{:S(2)}, u32[]{:S(2)}) collective-permute-start(bf16[16,160,128]{2,1,0:T(8,128)(2,1)} %get-tuple-element.34), channel_id=1, source_target_pairs={{0,16},{16,0},{1,17},{17,1},{2,18},{18,2},{3,19},{19,3},{4,20},{20... | collective-permute-start | bytes 1966088 | tf_op jit(solution)/shard_map/ppermute | solution.py:528
  104.7 6.0 %collective-permute-start = (bf16[256,256]{1,0:T(8,128)(2,1)}, bf16[256,256]{1,0:T(8,128)(2,1)}, u32[]{:S(2)}, u32[]{:S(2)}) collective-permute-start(bf16[256,256]{1,0:T(8,128)(2,1)} %bitcast.62), channel_id=1, source_target_pairs={{0,16},{16,0},{1,17},{17,1},{2,18},{18,2},{3,19},{19,3},{4,20},{20... | collective-permute-start | bytes 393224 | tf_op jit(solution)/shard_map/ppermute | solution.py:528
  106.8 8.3 %collective-permute-start.4 = (bf16[4,160,128]{2,1,0:T(8,128)(2,1)S(1)}, bf16[4,160,128]{2,1,0:T(8,128)(2,1)S(1)}, u32[]{:S(2)}, u32[]{:S(2)}) collective-permute-start(bf16[4,160,128]{2,1,0:T(8,128)(2,1)S(1)} %get-tuple-element.63), channel_id=1, source_target_pairs={{0,3},{1,2},{2,1},{3,0},{4,7},{5,6},{6,5},{7,4},{8,11},{9,10},{10,... | collective-permute-start | bytes 491528 | tf_op jit(solution)/shard_map/ppermute | solution.py:528
  110.0 8.0 %collective-permute-start.3 = (bf16[4,160,128]{2,1,0:T(8,128)(2,1)S(1)}, bf16[4,160,128]{2,1,0:T(8,128)(2,1)S(1)}, u32[]{:S(2)}, u32[]{:S(2)}) collective-permute-start(bf16[4,160,128]{2,1,0:T(8,128)(2,1)S(1)} %get-tuple-element.64), channel_id=1, source_target_pairs={{0,2},{1,3},{2,0},{3,1},{4,6},{5,7},{6,4},{7,5},{8,10},{9,11},{10,... | collective-permute-start | bytes 491528 | tf_op jit(solution)/shard_map/ppermute | solution.py:528
  110.0 8.3 %collective-permute-start.2 = (bf16[4,160,128]{2,1,0:T(8,128)(2,1)S(1)}, bf16[4,160,128]{2,1,0:T(8,128)(2,1)S(1)}, u32[]{:S(2)}, u32[]{:S(2)}) collective-permute-start(bf16[4,160,128]{2,1,0:T(8,128)(2,1)S(1)} %get-tuple-element.62), channel_id=1, source_target_pairs={{0,1},{1,0},{2,3},{3,2},{4,5},{5,4},{6,7},{7,6},{8,9},{9,8},{10,11... | collective-permute-start | bytes 491528 | tf_op jit(solution)/shard_map/ppermute | solution.py:528
  118.5 10.6 %collective-permute-start.7 = (bf16[160,128]{1,0:T(8,128)(2,1)S(1)}, bf16[160,128]{1,0:T(8,128)(2,1)S(1)}, u32[]{:S(2)}, u32[]{:S(2)}) collective-permute-start(bf16[160,128]{1,0:T(8,128)(2,1)S(1)} %get-tuple-element.80), channel_id=1, source_target_pairs={{0,12},{1,13},{2,14},{3,15},{4,8},{5,9},{6,10},{7,11},{8,4},{9,5},... | collective-permute-start | bytes 122888 | tf_op jit(solution)/shard_map/ppermute | solution.py:528
  121.8 8.5 %collective-permute-start.6 = (bf16[160,128]{1,0:T(8,128)(2,1)S(1)}, bf16[160,128]{1,0:T(8,128)(2,1)S(1)}, u32[]{:S(2)}, u32[]{:S(2)}) collective-permute-start(bf16[160,128]{1,0:T(8,128)(2,1)S(1)} %get-tuple-element.81), channel_id=1, source_target_pairs={{0,8},{1,9},{2,10},{3,11},{4,12},{5,13},{6,14},{7,15},{8,0},{9,1},... | collective-permute-start | bytes 122888 | tf_op jit(solution)/shard_map/ppermute | solution.py:528
  121.8 8.5 %collective-permute-start.5 = (bf16[160,128]{1,0:T(8,128)(2,1)S(1)}, bf16[160,128]{1,0:T(8,128)(2,1)S(1)}, u32[]{:S(2)}, u32[]{:S(2)}) collective-permute-start(bf16[160,128]{1,0:T(8,128)(2,1)S(1)} %get-tuple-element.79), channel_id=1, source_target_pairs={{0,4},{1,5},{2,6},{3,7},{4,0},{5,1},{6,2},{7,3},{8,12},{9,13},{10,... | collective-permute-start | bytes 122888 | tf_op jit(solution)/shard_map/ppermute | solution.py:528
  126.1 23.6 %collective-permute-start.11 = (bf16[4,432,256]{2,1,0:T(8,128)(2,1)S(1)}, bf16[4,432,256]{2,1,0:T(8,128)(2,1)S(1)}, u32[]{:S(2)}, u32[]{:S(2)}) collective-permute-start(bf16[4,432,256]{2,1,0:T(8,128)(2,1)S(1)} %get-tuple-element.57), channel_id=1, source_target_pairs={{0,3},{1,2},{2,1},{3,0},{4,7},{5,6},{6,5},{7,4},{8,11},{9,10},{10,... | collective-permute-start | bytes 2654216 | tf_op jit(solution)/shard_map/ppermute | solution.py:528
  127.7 38.8 %collective-permute-start.10 = (bf16[4,432,256]{2,1,0:T(8,128)(2,1)S(1)}, bf16[4,432,256]{2,1,0:T(8,128)(2,1)S(1)}, u32[]{:S(2)}, u32[]{:S(2)}) collective-permute-start(bf16[4,432,256]{2,1,0:T(8,128)(2,1)S(1)} %get-tuple-element.58), channel_id=1, source_target_pairs={{0,2},{1,3},{2,0},{3,1},{4,6},{5,7},{6,4},{7,5},{8,10},{9,11},{10,... | collective-permute-start | bytes 2654216 | tf_op jit(solution)/shard_map/ppermute | solution.py:528
  129.1 37.7 %collective-permute-start.9 = (bf16[4,432,256]{2,1,0:T(8,128)(2,1)S(1)}, bf16[4,432,256]{2,1,0:T(8,128)(2,1)S(1)}, u32[]{:S(2)}, u32[]{:S(2)}) collective-permute-start(bf16[4,432,256]{2,1,0:T(8,128)(2,1)S(1)} %get-tuple-element.56), channel_id=1, source_target_pairs={{0,1},{1,0},{2,3},{3,2},{4,5},{5,4},{6,7},{7,6},{8,9},{9,8},{10,11... | collective-permute-start | bytes 2654216 | tf_op jit(solution)/shard_map/ppermute | solution.py:528
  167.3 10.3 %collective-permute-start.14 = (bf16[432,256]{1,0:T(8,128)(2,1)S(1)}, bf16[432,256]{1,0:T(8,128)(2,1)S(1)}, u32[]{:S(2)}, u32[]{:S(2)}) collective-permute-start(bf16[432,256]{1,0:T(8,128)(2,1)S(1)} %get-tuple-element.60), channel_id=1, source_target_pairs={{0,12},{1,13},{2,14},{3,15},{4,8},{5,9},{6,10},{7,11},{8,4},{9,5},... | collective-permute-start | bytes 663560 | tf_op jit(solution)/shard_map/ppermute | solution.py:528
  170.6 18.8 %collective-permute-start.13 = (bf16[432,256]{1,0:T(8,128)(2,1)S(1)}, bf16[432,256]{1,0:T(8,128)(2,1)S(1)}, u32[]{:S(2)}, u32[]{:S(2)}) collective-permute-start(bf16[432,256]{1,0:T(8,128)(2,1)S(1)} %get-tuple-element.61), channel_id=1, source_target_pairs={{0,8},{1,9},{2,10},{3,11},{4,12},{5,13},{6,14},{7,15},{8,0},{9,1},... | collective-permute-start | bytes 663560 | tf_op jit(solution)/shard_map/ppermute | solution.py:528
  170.6 18.8 %collective-permute-start.12 = (bf16[432,256]{1,0:T(8,128)(2,1)S(1)}, bf16[432,256]{1,0:T(8,128)(2,1)S(1)}, u32[]{:S(2)}, u32[]{:S(2)}) collective-permute-start(bf16[432,256]{1,0:T(8,128)(2,1)S(1)} %get-tuple-element.59), channel_id=1, source_target_pairs={{0,4},{1,5},{2,6},{3,7},{4,0},{5,1},{6,2},{7,3},{8,12},{9,13},{10,... | collective-permute-start | bytes 663560 | tf_op jit(solution)/shard_map/ppermute | solution.py:528

commit v2 on v1

v2 whole, which is shorter than its diff:
```python
from functools import partial

import jax
import jax.numpy as jnp
from jax import lax
from jax.experimental import pallas as pl
from jax.experimental.pallas import tpu as pltpu
from jax.sharding import PartitionSpec as P

F32 = jnp.float32
LOW = jnp.bfloat16

CD = 256
CFF = 1024
CPW = 16
CVOC = 256
CHAR_HEADS = 4
HEAD = 64
WD = 512
WFF = 2048
WORD_HEADS = 8
WORDS = 256

SPAN = 256
STEP = 240
WIDE = 2 * SPAN
TURNS = ((WORDS * CPW - 1) // STEP + 2) // 2

epsilon = 1e-06
half_root = 0.7071067811865476
density = 0.3989422804014327
floor_score = -1e30

R_EMB, R_Q, R_K, R_V, R_P, R_MIX = 0, 256, 512, 768, 1024, 2048
KEPT_LOW = 2304
KEPT_ALL = KEPT_LOW + CFF
I_INV1, I_INV2, I_IDENT, I_WORD = 0, 1, 2, 3
BAND = 144
WINDOW = 96

X_Q, X_K, X_V, X_O, X_UP, X_CDOWN = 0, 32, 64, 96, 128, 256
X_ROWS = 288
Z_DOWN, Z_PROJ = 0, 128
Z_ROWS = 144
C_TABLE, C_Q, C_K, C_V, C_O, C_UP, C_GAIN = 0, 16, 32, 48, 64, 80, 144
C_ROWS = 160
SHARES = 16


def nn(left, right):
    return lax.dot_general(left, right, (((1,), (0,)), ((), ())), preferred_element_type=F32)


def nt(left, right):
    return lax.dot_general(left, right, (((1,), (1,)), ((), ())), preferred_element_type=F32)


def iota(shape, axis):
    return lax.broadcasted_iota(jnp.int32, shape, axis)


def eye(n):
    return iota((n, n), 0) == iota((n, n), 1)


def row_to_column(row):
    n = row.shape[1]
    return jnp.sum(jnp.where(eye(n), row, 0.0), axis=1, keepdims=True)


def gelu_pair(v):
    full = 0.5 + 0.5 * lax.erf(v * half_root)
    return v * full, full + v * (density * jnp.exp(-0.5 * v * v))


def plane_first(d):
    return (d % 4) * 4 + d // 4


def line_first(d):
    return d


def lane_places(turn):
    lane = iota((1, WIDE), 1)
    second = lane >= SPAN
    base = (turn * (2 * STEP)).astype(F32) + jnp.where(second, float(STEP), 0.0)
    return (lane - jnp.where(second, SPAN, 0)).astype(F32) + base, base


def members(word, first, count):
    return jnp.where((iota((count, WIDE), 0) + first).astype(F32) == word, 1.0, 0.0).astype(LOW)


def word_starts(counts_row):
    earlier = iota((WORDS, WORDS), 1) < iota((WORDS, WORDS), 0)
    starts = jnp.sum(jnp.where(earlier, counts_row, 0.0), axis=1, keepdims=True)
    counts = row_to_column(counts_row)
    return starts, counts


def put(bundle, phase, order, row, value, width, share_rows):
    low = value.astype(LOW)
    lanes = bundle.shape[-1]
    for half in range(2):
        side = jnp.bitwise_xor(phase, half)
        for piece in range(max(1, width // lanes)):
            take = min(width, lanes)
            cols = low[:, half * width + piece * lanes:half * width + piece * lanes + take]
            for i in range(value.shape[0] // share_rows):
                part = cols[i * share_rows:(i + 1) * share_rows]
                if take < lanes:
                    part = jnp.concatenate([part[:share_rows // 2], part[share_rows // 2:]], axis=1)
                m = part.shape[0]
                bundle[side, order(i), row + piece * share_rows:row + piece * share_rows + m, :] = part


def band(t):
    keys = slice(0, BAND) if t % 2 == 0 else slice(SPAN - BAND, SPAN)
    return t // 2, keys, slice(t * 128, (t + 1) * 128)


def two_heads(pair):
    zero = jnp.zeros((HEAD, pair.shape[1]), LOW)
    first = jnp.concatenate([pair[:HEAD], zero], axis=0)
    second = jnp.concatenate([zero, pair[HEAD:]], axis=0)
    return jnp.concatenate([first, second], axis=1)


def two_heads_rows(pair):
    left = iota(pair.shape, 1) < HEAD
    zero = jnp.zeros(pair.shape, LOW)
    return jnp.concatenate([jnp.where(left, pair, zero), jnp.where(left, zero, pair)], axis=0)


def softmax_keys(s):
    e = jnp.exp(s - jnp.max(s, axis=0, keepdims=True))
    return (e * (1.0 / jnp.sum(e, axis=0, keepdims=True))).astype(LOW)


def kernel_a(
    counts_ref, ids_ref, segs_ref, cot_hbm,
    table_ref, g1_ref, wq_ref, wk_ref, wv_ref, wo_ref, g2_ref, up_ref, down_ref, proj_ref,
    wg1_ref, wwq_hbm, wwk_hbm, wwv_hbm, wwo_hbm, wg2_ref, wup_hbm, wdown_hbm,
    keptl_hbm, kepts_hbm, keptm_hbm, kepti_hbm, turns_ref, gw_ref,
    xkeep_hbm, xsend_hbm, zkeep_hbm, zsend_hbm, outk_ref, outs_ref, gains_ref,
    cot, wwq, wwk, wwv, wwo, wup, wdown,
    tab_t, wqkv_t, wo_t, up_t, ids_t, slow, smid, sinfo, pa, pm, rowinfo, firsts_v, firsts, before_s, act_s, prob_s, found_s,
    xbundle, zbundle, xs, midw, pw, actw, slopew,
    wsem, ksem, osem,
):
    phase = lax.axis_index("phase")
    loads = [
        pltpu.make_async_copy(src, dst, wsem.at[i])
        for i, (src, dst) in enumerate(
            ((wwq_hbm, wwq), (wwk_hbm, wwk), (wwv_hbm, wwv), (wwo_hbm, wwo),
             (wup_hbm, wup), (wdown_hbm, wdown), (cot_hbm.at[phase, 0], cot))
        )
    ]
    for load in loads:
        load.start()

    counts_row = counts_ref[phase].astype(F32)
    starts, counts = word_starts(counts_row)
    last = jnp.max(starts)
    n_turns = last.astype(jnp.int32) // (2 * STEP) + 1
    turns_ref[0] = n_turns
    bases = (iota((1, 128), 1) * (2 * STEP)).astype(F32)
    first = jnp.sum(jnp.where(starts < bases, 1.0, 0.0), axis=0, keepdims=True)
    firsts_v[...] = jnp.broadcast_to(first, (8, 128)).astype(jnp.int32)
    first_copy = pltpu.make_async_copy(firsts_v, firsts, wsem.at[7])
    first_copy.start()
    tab_t[...] = table_ref[...].T
    wqkv_t[0:CD] = (wq_ref[...] * 0.125).T
    wqkv_t[CD:2 * CD] = wk_ref[...].T
    wqkv_t[2 * CD:] = wv_ref[...].T
    wo_t[...] = wo_ref[...].T
    up_t[...] = up_ref[...].T
    g1 = row_to_column(g1_ref[...].astype(F32)[None, :])
    g2 = row_to_column(g2_ref[...].astype(F32)[None, :])
    ids = ids_ref[phase]
    ids_t[...] = jnp.concatenate(
        [ids[:, 128 * a:128 * a + 128] for a in range(32)], axis=0
    ).astype(F32).T.astype(LOW)
    starts_row = jnp.sum(
        jnp.where(iota((WORDS, WORDS), 0) < iota((WORDS, WORDS), 1), counts, 0.0), axis=0, keepdims=True
    )
    high = jnp.floor(starts_row * 0.0625)
    number = iota((1, WORDS), 1).astype(F32)
    rowinfo[...] = jnp.concatenate(
        [high, starts_row - 16.0 * high, number, jnp.ones((1, WORDS), F32), jnp.zeros((12, WORDS), F32)], axis=0
    ).astype(LOW)
    pa[...] = jnp.zeros_like(pa)
    pm[...] = jnp.zeros_like(pm)
    prob_s[...] = jnp.zeros_like(prob_s)
    for slot in range(2):
        slow[slot, R_P:R_P + CHAR_HEADS * SPAN] = jnp.zeros((CHAR_HEADS * SPAN, WIDE), LOW)
    first_copy.wait()

    def find(turn):
        place, base = lane_places(turn)
        own = (starts >= base) & (starts < base + STEP) & (starts <= place) & (place < starts + counts)
        info = nn(rowinfo[...], jnp.where(own, 1.0, 0.0).astype(LOW))
        word = info[2:3]
        flat = (word * 16.0 + place - (info[0:1] * 16.0 + info[1:2])).astype(jnp.int32)
        chosen = jnp.where(iota((32, WIDE), 0) == (flat >> 7), 1.0, 0.0).astype(LOW)
        lanes = nn(ids_t[...], chosen)
        ident = jnp.sum(jnp.where(iota((128, WIDE), 0) == (flat & 127), lanes, 0.0), axis=0, keepdims=True)
        valid = info[3:4] > 0.5
        none = jnp.full((6, WIDE), -1.0, F32)
        return jnp.concatenate([jnp.where(valid, ident, -1.0), jnp.where(valid, word, -1.0), none], axis=0)

    found_s[...] = find(jnp.int32(0))

    def kept_copies(b, slot):
        return (
            pltpu.make_async_copy(slow.at[slot, pl.ds(0, KEPT_LOW)], keptl_hbm.at[b], ksem.at[0, slot]),
            pltpu.make_async_copy(slow.at[slot, pl.ds(KEPT_LOW, CFF)], kepts_hbm.at[b], ksem.at[1, slot]),
            pltpu.make_async_copy(smid.at[slot], keptm_hbm.at[b], ksem.at[2, slot]),
            pltpu.make_async_copy(sinfo.at[slot], kepti_hbm.at[b], ksem.at[3, slot]),
        )

    def turn(b, carry):
        slot = lax.rem(b, 2)

        @pl.when(b >= 2)
        def _():
            for c in kept_copies(b - 2, slot):
                c.wait()

        ident = found_s[0:1]
        word = found_s[1:2]
        hot = jnp.where(iota((CVOC, WIDE), 0).astype(F32) == ident, 1.0, 0.0).astype(LOW)
        emb = nn(tab_t[...], hot)
        inv1 = lax.rsqrt(jnp.mean(emb * emb, axis=0, keepdims=True) + epsilon)
        normed = (emb * inv1 * g1).astype(LOW)
        qkv = nn(wqkv_t[...], normed).astype(LOW)
        key_rows = [qkv[CD:2 * CD, u * SPAN:(u + 1) * SPAN].T for u in range(2)]
        value_t = qkv[2 * CD:]
        word_col = jnp.broadcast_to(jnp.where(word < 0.0, -2.0, word), (8, WIDE)).T[:, 0:1]
        for t in range(4):
            u, ks, ql = band(t)
            bias = jnp.where(word_col[u * SPAN + ks.start:u * SPAN + ks.stop] == word[:, ql], 0.0, floor_score)
            for pair in range(CHAR_HEADS // 2):
                fs = slice(pair * 128, pair * 128 + 128)
                s = nn(key_rows[u][ks, fs], two_heads(qkv[fs, ql]))
                for i in range(2):
                    p = softmax_keys(s[:, i * 128:i * 128 + 128] + bias)
                    row = (pair * 2 + i) * SPAN
                    prob_s[row + ks.start:row + ks.stop, ql] = p
                    slow[slot, R_P + row + ks.start:R_P + row + ks.stop, ql] = p
        slow[slot, R_EMB:R_EMB + CD] = emb.astype(LOW)
        slow[slot, R_Q:R_Q + 2 * CD] = qkv[:2 * CD]
        for u in range(2):
            us = slice(u * SPAN, (u + 1) * SPAN)
            slow[slot, R_V:R_V + SPAN, us] = value_t[:, us].T
        mixed = []
        for h in range(CHAR_HEADS):
            hs = slice(h * HEAD, (h + 1) * HEAD)
            both = []
            for u in range(2):
                us = slice(u * SPAN, (u + 1) * SPAN)
                both.append(nn(value_t[hs, us], prob_s[h * SPAN:(h + 1) * SPAN, us]).astype(LOW))
            mixed.append(jnp.concatenate(both, axis=1))
        mixed = jnp.concatenate(mixed, axis=0)
        slow[slot, R_MIX:R_MIX + CD] = mixed
        middle = emb + nn(wo_t[...], mixed)
        inv2 = lax.rsqrt(jnp.mean(middle * middle, axis=0, keepdims=True) + epsilon)
        smid[slot] = middle
        sinfo[slot] = jnp.concatenate([inv1, inv2, ident, word, jnp.zeros((4, WIDE), F32)], axis=0)
        normed_two = (middle * inv2 * g2).astype(LOW)
        before_s[...] = nn(up_t[...], normed_two)
        found_s[...] = find(b + 1)
        for c in range(CFF // 32):
            cs = slice(c * 32, (c + 1) * 32)
            act, slope = gelu_pair(before_s[cs])
            slow[slot, KEPT_LOW + c * 32:KEPT_LOW + (c + 1) * 32] = slope.astype(LOW)
            act_s[cs] = act.astype(LOW)
        middle_hi = middle.astype(LOW)
        middle_lo = (middle - middle_hi.astype(F32)).astype(LOW)
        w0 = (firsts[0, b] // 16) * 16
        windows = (firsts[0, b + 1] - w0 + WINDOW - 1) // WINDOW

        def pool(i, carry):
            first = w0 + i * WINDOW
            w = pl.ds(pl.multiple_of(first, 16), WINDOW)
            near = members(word, first, WINDOW)
            pa[w, :] += nt(near, act_s[...])
            pm[w, :] += nt(near, middle_hi) + nt(near, middle_lo)
            return carry

        pool(0, 0)
        lax.fori_loop(1, windows, pool, 0)
        for c in kept_copies(b, slot):
            c.start()
        return carry

    lax.fori_loop(0, n_turns, turn, 0)

    pa_hi = pa[0:WORDS].astype(LOW)
    pa_lo = (pa[0:WORDS] - pa_hi.astype(F32)).astype(LOW)
    per_count = 1.0 / counts
    pooled = (pm[0:WORDS] + nn(pa_hi, down_ref[...]) + nn(pa_lo, down_ref[...])) * per_count
    pooled_low = pooled.astype(LOW)
    x = nn(pooled_low, proj_ref[...]).astype(LOW).astype(F32)
    xs[...] = x
    for load in loads:
        load.wait()
    wg1 = wg1_ref[...].astype(F32)[None, :]
    wg2 = wg2_ref[...].astype(F32)[None, :]
    winv1 = lax.rsqrt(jnp.mean(x * x, axis=1, keepdims=True) + epsilon)
    normed = (x * winv1 * wg1).astype(LOW)
    q = (nn(normed, wwq[...]) * 0.125).astype(LOW)
    k = nn(normed, wwk[...]).astype(LOW)
    v = nn(normed, wwv[...]).astype(LOW)
    seg_row = segs_ref[phase].astype(F32)
    seg_col = row_to_column(seg_row)
    allowed = (seg_row == seg_col) & (iota((WORDS, WORDS), 0) <= iota((WORDS, WORDS), 1))
    bias = jnp.where(allowed, 0.0, floor_score)
    k_t = k.T
    v_t = v.T
    for h in range(WORD_HEADS):
        pw[h, 128:, 0:128] = jnp.zeros((128, 128), LOW)
    for t in range(2):
        ks, ql = slice(0, 128 * (t + 1)), slice(128 * t, 128 * (t + 1))
        for pair in range(WORD_HEADS // 2):
            fs = slice(pair * 128, pair * 128 + 128)
            s = nt(k[ks, fs], two_heads_rows(q[ql, fs]))
            for i in range(2):
                pw[pair * 2 + i, ks, ql] = softmax_keys(s[:, i * 128:i * 128 + 128] + bias[ks, ql])
    mixed_t = jnp.concatenate(
        [nn(v_t[h * HEAD:(h + 1) * HEAD], pw[h]).astype(LOW) for h in range(WORD_HEADS)], axis=0
    )
    middle = x + nn(mixed_t.T, wwo[...])
    midw[...] = middle
    winv2 = lax.rsqrt(jnp.mean(middle * middle, axis=1, keepdims=True) + epsilon)
    normed_two = (middle * winv2 * wg2).astype(LOW)
    result = middle
    for c in range(WFF // 512):
        cs = slice(c * 512, (c + 1) * 512)
        act, slope = gelu_pair(nn(normed_two, wup[:, cs]))
        act = act.astype(LOW)
        actw[:, cs] = act
        slopew[:, cs] = slope.astype(LOW)
        result = result + nn(act, wdown[cs, :])
    result = result.astype(LOW)
    front = phase == 0
    outk_ref[...] = jnp.where(front, result[:, :256], result[:, 256:])
    outs_ref[...] = jnp.where(front, result[:, 256:], result[:, :256])

    cot_low = cot[...]
    n2d = jnp.zeros((WORDS, WD), F32)
    n2_t = normed_two.T
    for c in range(WFF // 512):
        cs = slice(c * 512, (c + 1) * 512)
        gd = nn(actw[:, cs].T, cot_low)
        put(zbundle, phase, lambda i: line_first(c * 4 + i), Z_DOWN, gd, 256, 128)
        bd = (nt(cot_low, wdown[cs, :]) * slopew[:, cs].astype(F32)).astype(LOW)
        gu = nn(n2_t, bd).astype(LOW)
        side = jnp.bitwise_xor(phase, c // 2)
        for piece in range(2):
            row = X_UP + ((c % 2) * 2 + piece) * 32
            for d in range(SHARES):
                xbundle[side, plane_first(d), row:row + 32, :] = gu[d * 32:(d + 1) * 32, piece * 256:piece * 256 + 256]
        n2d = n2d + nt(bd, wup[:, cs])
    middle = midw[...]
    vhat = middle * winv2
    gain2 = jnp.sum(n2d * vhat, axis=0, keepdims=True)
    lifted = n2d * wg2
    md = cot_low.astype(F32) + winv2 * (lifted - vhat * jnp.mean(lifted * vhat, axis=1, keepdims=True))
    md_low = md.astype(LOW)
    put(xbundle, phase, plane_first, X_O, nn(mixed_t, md_low), 256, 32)
    do = nt(md_low, wwo[...]).astype(LOW)
    dq_t, dk, dv = [], [], []
    left = iota((WORDS, 128), 1) < HEAD
    for pair in range(WORD_HEADS // 2):
        fs = slice(pair * 128, pair * 128 + 128)
        ds = []
        for t in range(2):
            ks, ql = slice(0, 128 * (t + 1)), slice(128 * t, 128 * (t + 1))
            dp = nt(v[ks, fs], two_heads_rows(do[ql, fs]))
            for i in range(2):
                pf = pw[pair * 2 + i, ks, ql].astype(F32)
                dph = dp[:, i * 128:i * 128 + 128]
                d = (pf * (dph - jnp.sum(pf * dph, axis=0, keepdims=True))).astype(LOW)
                ds.append(d if t else jnp.concatenate([d, jnp.zeros((128, 128), LOW)], axis=0))
        both = [jnp.concatenate([ds[i], ds[i + 2]], axis=1) for i in range(2)]
        for i in range(2):
            h = pair * 2 + i
            dq_t.append(nn(k_t[h * HEAD:(h + 1) * HEAD], both[i]))
        dk.append(jnp.where(left, nn(both[0], q[:, fs]), nn(both[1], q[:, fs])).astype(LOW))
        dv.append(jnp.where(left, nn(pw[pair * 2], do[:, fs]), nn(pw[pair * 2 + 1], do[:, fs])).astype(LOW))
    dq = (jnp.concatenate(dq_t, axis=0) * 0.125).astype(LOW).T
    dk = jnp.concatenate(dk, axis=1)
    dv = jnp.concatenate(dv, axis=1)
    normed_t = normed.T
    put(xbundle, phase, plane_first, X_Q, nn(normed_t, dq), 256, 32)
    put(xbundle, phase, plane_first, X_K, nn(normed_t, dk), 256, 32)
    put(xbundle, phase, plane_first, X_V, nn(normed_t, dv), 256, 32)
    nd = nt(dq, wwq[...]) + nt(dk, wwk[...]) + nt(dv, wwv[...])
    vhat = xs[...] * winv1
    gain1 = jnp.sum(nd * vhat, axis=0, keepdims=True)
    lifted = nd * wg1
    xd = md + winv1 * (lifted - vhat * jnp.mean(lifted * vhat, axis=1, keepdims=True))
    vd = xd.astype(LOW)
    put(zbundle, phase, line_first, Z_PROJ, nn(pooled_low.T, vd), 256, 16)
    gw = (nt(vd, proj_ref[...]) * per_count).astype(LOW)
    gw_ref[...] = gw.T
    put(xbundle, phase, plane_first, X_CDOWN, nn(pa_hi.T, gw), 128, 64)
    gains_ref[...] = jnp.concatenate([gain1, gain2, jnp.zeros((6, WD), F32)], axis=0)
    stores = [
        pltpu.make_async_copy(xbundle.at[0], xkeep_hbm, osem.at[0]),
        pltpu.make_async_copy(xbundle.at[1], xsend_hbm, osem.at[1]),
        pltpu.make_async_copy(zbundle.at[0], zkeep_hbm, osem.at[2]),
        pltpu.make_async_copy(zbundle.at[1], zsend_hbm, osem.at[3]),
    ]
    for s in stores:
        s.start()

    def drain(b, carry):
        for c in kept_copies(b, lax.rem(b, 2)):
            c.wait()
        return carry

    lax.fori_loop(jnp.maximum(n_turns - 2, 0), n_turns, drain, 0)
    for s in stores:
        s.wait()


def kernel_b1(
    turns_ref, gw_ref, g2_ref, up_ref, down_ref, kepts_hbm, keptm_hbm, kepti_hbm,
    keptd_hbm, aup_ref, gain_ref,
    sslope, smid, sinfo, sdelta, aup, ag2, ksem, dsem,
):
    n_turns = turns_ref[0]

    def kept_copies(b, slot):
        return (
            pltpu.make_async_copy(kepts_hbm.at[b], sslope.at[slot], ksem.at[0, slot]),
            pltpu.make_async_copy(keptm_hbm.at[b], smid.at[slot], ksem.at[1, slot]),
            pltpu.make_async_copy(kepti_hbm.at[b], sinfo.at[slot], ksem.at[2, slot]),
        )

    def delta_copy(b, slot):
        return pltpu.make_async_copy(sdelta.at[slot], keptd_hbm.at[b], dsem.at[slot])

    for c in kept_copies(0, 0):
        c.start()
    g2 = row_to_column(g2_ref[...].astype(F32)[None, :])
    aup[...] = jnp.zeros_like(aup)
    ag2[...] = jnp.zeros_like(ag2)

    def turn(b, carry):
        slot = lax.rem(b, 2)

        @pl.when(b + 1 < n_turns)
        def _():
            for c in kept_copies(b + 1, 1 - slot):
                c.start()

        @pl.when(b >= 2)
        def _():
            delta_copy(b - 2, slot).wait()

        for c in kept_copies(b, slot):
            c.wait()
        inv2 = sinfo[slot, I_INV2:I_INV2 + 1]
        g_low = nn(gw_ref[...], members(sinfo[slot, I_WORD:I_WORD + 1], 0, WORDS)).astype(LOW)
        vhat = smid[slot] * inv2
        normed_two = (vhat * g2).astype(LOW)
        n2d = jnp.zeros((CD, WIDE), F32)
        for c in range(CFF // 256):
            cs = slice(c * 256, (c + 1) * 256)
            bd = (nn(down_ref[cs, :], g_low) * sslope[slot, cs].astype(F32)).astype(LOW)
            aup[:, cs] += nt(normed_two, bd)
            n2d = n2d + nn(up_ref[:, cs], bd)
        ag2[...] += n2d * vhat
        lifted = n2d * g2
        md = g_low.astype(F32) + inv2 * (lifted - vhat * jnp.mean(lifted * vhat, axis=0, keepdims=True))
        sdelta[slot] = md.astype(LOW)
        delta_copy(b, slot).start()
        return carry

    lax.fori_loop(0, n_turns, turn, 0)
    aup_ref[...] = aup[...].astype(LOW)
    gain_ref[...] = jnp.broadcast_to(jnp.sum(ag2[...], axis=1, keepdims=True), (CD, 8)).T

    def drain(b, carry):
        delta_copy(b, lax.rem(b, 2)).wait()
        return carry

    lax.fori_loop(jnp.maximum(n_turns - 2, 0), n_turns, drain, 0)


def kernel_b2(
    turns_ref, wgains_ref, gain2_ref, aup_ref, g1_ref, wq_ref, wk_ref, wv_ref, wo_ref,
    keptl_hbm, keptd_hbm, kepti_hbm,
    keep_hbm, send_hbm,
    slow, sinfo, sdelta, dscore, wqkv, aqkv, ao, atab, ag1, bundle, ksem, osem,
):
    phase = lax.axis_index("phase")
    n_turns = turns_ref[0]

    def kept_copies(b, slot):
        return (
            pltpu.make_async_copy(keptl_hbm.at[b], slow.at[slot], ksem.at[0, slot]),
            pltpu.make_async_copy(keptd_hbm.at[b], sdelta.at[slot], ksem.at[1, slot]),
            pltpu.make_async_copy(kepti_hbm.at[b], sinfo.at[slot], ksem.at[2, slot]),
        )

    for c in kept_copies(0, 0):
        c.start()
    g1 = row_to_column(g1_ref[...].astype(F32)[None, :])
    for i, w in enumerate((wq_ref, wk_ref, wv_ref)):
        wqkv[:, i * CD:(i + 1) * CD] = w[...]
    for acc in (aqkv, ao, atab, ag1, dscore):
        acc[...] = jnp.zeros_like(acc)

    def turn(b, carry):
        slot = lax.rem(b, 2)

        @pl.when(b + 1 < n_turns)
        def _():
            for c in kept_copies(b + 1, 1 - slot):
                c.start()

        for c in kept_copies(b, slot):
            c.wait()
        inv1 = sinfo[slot, I_INV1:I_INV1 + 1]
        ident = sinfo[slot, I_IDENT:I_IDENT + 1]
        md_low = sdelta[slot]
        ao[...] += nt(slow[slot, R_MIX:R_MIX + CD], md_low)
        do = nn(wo_ref[...], md_low).astype(LOW)
        for t in range(4):
            u, ks, ql = band(t)
            for pair in range(CHAR_HEADS // 2):
                fs = slice(u * SPAN + pair * 128, u * SPAN + pair * 128 + 128)
                dp = nn(
                    slow[slot, R_V + ks.start:R_V + ks.stop, fs], two_heads(do[pair * 128:pair * 128 + 128, ql])
                )
                for i in range(2):
                    row = (pair * 2 + i) * SPAN
                    pf = slow[slot, R_P + row + ks.start:R_P + row + ks.stop, ql].astype(F32)
                    dph = dp[:, i * 128:i * 128 + 128]
                    d = pf * (dph - jnp.sum(pf * dph, axis=0, keepdims=True))
                    dscore[row + ks.start:row + ks.stop, ql] = d.astype(LOW)
        dq, dk, dv = [], [], []
        for h in range(CHAR_HEADS):
            hs = slice(h * HEAD, (h + 1) * HEAD)
            one, two, three = [], [], []
            for u in range(2):
                us = slice(u * SPAN, (u + 1) * SPAN)
                p = slow[slot, R_P + h * SPAN:R_P + (h + 1) * SPAN, us]
                ds = dscore[h * SPAN:(h + 1) * SPAN, us]
                one.append((nn(slow[slot, R_K + h * HEAD:R_K + (h + 1) * HEAD, us], ds) * 0.125).astype(LOW))
                two.append(nt(slow[slot, R_Q + h * HEAD:R_Q + (h + 1) * HEAD, us], ds).astype(LOW))
                three.append(nt(do[hs, us], p).astype(LOW))
            for part, pair in ((dq, one), (dk, two), (dv, three)):
                part.append(jnp.concatenate(pair, axis=1))
        dqkv = jnp.concatenate(dq + dk + dv, axis=0)
        emb = slow[slot, R_EMB:R_EMB + CD].astype(F32)
        ehat = emb * inv1
        normed = (ehat * g1).astype(LOW)
        aqkv[...] += nt(normed, dqkv)
        nd = nn(wqkv[...], dqkv)
        ag1[...] += nd * ehat
        lifted = nd * g1
        ed = md_low.astype(F32) + inv1 * (lifted - ehat * jnp.mean(lifted * ehat, axis=0, keepdims=True))
        hot = jnp.where(iota((CVOC, WIDE), 0).astype(F32) == ident, 1.0, 0.0).astype(LOW)
        atab[...] += nt(hot, ed.astype(LOW))
        return carry

    lax.fori_loop(0, n_turns, turn, 0)

    put(bundle, phase, plane_first, C_TABLE, atab[...], 128, 16)
    put(bundle, phase, plane_first, C_Q, aqkv[:, 0:CD], 128, 16)
    put(bundle, phase, plane_first, C_K, aqkv[:, CD:2 * CD], 128, 16)
    put(bundle, phase, plane_first, C_V, aqkv[:, 2 * CD:], 128, 16)
    put(bundle, phase, plane_first, C_O, ao[...], 128, 16)
    put(bundle, phase, plane_first, C_UP, aup_ref[...], 512, 16)
    cg1 = jnp.broadcast_to(jnp.sum(ag1[...], axis=1, keepdims=True), (CD, 8)).T[0:1]
    cg2 = gain2_ref[0:1]
    wg = wgains_ref[...]
    for d in range(SHARES):
        rows = [
            jnp.concatenate([cg1[:, d * 16:d * 16 + 16], jnp.zeros((1, 112), F32)], axis=1),
            jnp.concatenate([cg2[:, d * 16:d * 16 + 16], jnp.zeros((1, 112), F32)], axis=1),
            jnp.concatenate([wg[0:1, d * 32:d * 32 + 32], jnp.zeros((1, 96), F32)], axis=1),
            jnp.concatenate([wg[1:2, d * 32:d * 32 + 32], jnp.zeros((1, 96), F32)], axis=1),
            jnp.zeros((12, 128), F32),
        ]
        tile = jnp.concatenate(rows, axis=0).astype(LOW)
        bundle[0, plane_first(d), C_GAIN:C_GAIN + 16, :] = tile
        bundle[1, plane_first(d), C_GAIN:C_GAIN + 16, :] = tile
    stores = [
        pltpu.make_async_copy(bundle.at[0], keep_hbm, osem.at[0]),
        pltpu.make_async_copy(bundle.at[1], send_hbm, osem.at[1]),
    ]
    for s in stores:
        s.start()
    for s in stores:
        s.wait()


def kernel_f(
    xown_hbm, xg1, xg2, xg3, zown_hbm, zg1, zg2, zg3, cown_hbm, cg1, cg2, cg3, outk, outg,
    word_out, d_table, d_g1, d_q, d_k, d_v, d_o, d_g2, d_up, d_down, d_proj,
    e_g1, e_q, e_k, e_v, e_o, e_g2, e_up, e_down,
    xown, zown, cown, sem,
):
    phase = lax.axis_index("phase")
    dp = lax.axis_index("dp")
    plane, line = lax.rem(dp, 4), lax.div(dp, 4)
    loads = [
        pltpu.make_async_copy(xown_hbm.at[line], xown, sem.at[0]),
        pltpu.make_async_copy(zown_hbm.at[plane], zown, sem.at[1]),
        pltpu.make_async_copy(cown_hbm.at[line], cown, sem.at[2]),
    ]
    for load in loads:
        load.start()
    word_out[phase, 0] = outk[...]
    word_out[1 - phase, 0] = outg[...]
    for load in loads:
        load.wait()

    def total(own, parts, rows):
        t = own[rows].astype(F32)
        for p in parts:
            t = t + p[rows].astype(F32)
        return t

    def x(row, n):
        return total(xown, (xg1, xg2, xg3), slice(row, row + n))

    def z(row, n):
        return total(zown, (zg1, zg2, zg3), slice(row, row + n))

    def c(row, n):
        return total(cown, (cg1, cg2, cg3), slice(row, row + n))

    d_table[...] = c(C_TABLE, 16)
    d_q[...] = c(C_Q, 16)
    d_k[...] = c(C_K, 16)
    d_v[...] = c(C_V, 16)
    d_o[...] = c(C_O, 16)
    for i in range(4):
        d_up[:, i * 128:(i + 1) * 128] = c(C_UP + i * 16, 16)
        e_up[:, i * 256:(i + 1) * 256] = x(X_UP + i * 32, 32)
    gains = c(C_GAIN, 16)
    d_g1[...] = gains[0, :16]
    d_g2[...] = gains[1, :16]
    e_g1[...] = gains[2, :32]
    e_g2[...] = gains[3, :32]
    cd = x(X_CDOWN, 32)
    d_down[0:32] = cd[:, :128]
    d_down[32:64] = cd[:, 128:]
    d_proj[...] = z(Z_PROJ, 16)
    e_q[...] = x(X_Q, 32)
    e_k[...] = x(X_K, 32)
    e_v[...] = x(X_V, 32)
    e_o[...] = x(X_O, 32)
    e_down[...] = z(Z_DOWN, 128)


ANYWHERE = pl.BlockSpec(memory_space=pl.ANY)
INSIDE = pl.BlockSpec(memory_space=pltpu.VMEM)
SCALARS = pl.BlockSpec(memory_space=pltpu.SMEM)
shape = jax.ShapeDtypeStruct


def params():
    return pltpu.CompilerParams(vmem_limit_bytes=60 * 2**20)


def call_a(char_counts, char_ids, segment_ids, out_cotangent, weights):
    v = pltpu.VMEM
    return pl.pallas_call(
        kernel_a,
        out_shape=(
            shape((TURNS, KEPT_LOW, WIDE), LOW),
            shape((TURNS, CFF, WIDE), LOW),
            shape((TURNS, CD, WIDE), F32),
            shape((TURNS, 8, WIDE), F32),
            shape((1,), jnp.int32),
            shape((CD, WORDS), LOW),
            shape((SHARES, X_ROWS, 256), LOW),
            shape((SHARES, X_ROWS, 256), LOW),
            shape((SHARES, Z_ROWS, 256), LOW),
            shape((SHARES, Z_ROWS, 256), LOW),
            shape((WORDS, WD // 2), LOW),
            shape((WORDS, WD // 2), LOW),
            shape((8, WD), F32),
        ),
        in_specs=[INSIDE] * 3 + [ANYWHERE] + [INSIDE] * 10 + [INSIDE] + [ANYWHERE] * 4 + [INSIDE] + [ANYWHERE] * 2,
        out_specs=(ANYWHERE,) * 4 + (SCALARS, INSIDE) + (ANYWHERE,) * 4 + (INSIDE,) * 3,
        scratch_shapes=[
            v((WORDS, WD), LOW),
            v((WD, WD), LOW), v((WD, WD), LOW), v((WD, WD), LOW), v((WD, WD), LOW),
            v((WD, WFF), LOW), v((WFF, WD), LOW),
            v((CD, CVOC), LOW), v((3 * CD, CD), LOW), v((CD, CD), LOW), v((CFF, CD), LOW), v((128, 32), LOW),
            v((2, KEPT_ALL, WIDE), LOW), v((2, CD, WIDE), F32), v((2, 8, WIDE), F32),
            v((WORDS + WINDOW, CFF), F32), v((WORDS + WINDOW, CD), F32), v((16, WORDS), LOW),
            v((8, 128), jnp.int32), pltpu.SMEM((8, 128), jnp.int32),
            v((CFF, WIDE), F32), v((CFF, WIDE), LOW), v((CHAR_HEADS * SPAN, WIDE), LOW), v((8, WIDE), F32),
            v((2, SHARES, X_ROWS, 256), LOW), v((2, SHARES, Z_ROWS, 256), LOW),
            v((WORDS, WD), F32), v((WORDS, WD), F32),
            v((WORD_HEADS, WORDS, WORDS), LOW), v((WORDS, WFF), LOW), v((WORDS, WFF), LOW),
            pltpu.SemaphoreType.DMA((8,)),
            pltpu.SemaphoreType.DMA((4, 2)),
            pltpu.SemaphoreType.DMA((4,)),
        ],
        compiler_params=params(),
        cost_estimate=pl.CostEstimate(flops=200 * 10**9, bytes_accessed=60 * 10**6, transcendentals=10**6),
        name="forward_and_words",
    )(char_counts, char_ids, segment_ids, out_cotangent, *weights)


def call_b1(turns, gw, gain, up, down, kepts, keptm, kepti):
    v = pltpu.VMEM
    return pl.pallas_call(
        kernel_b1,
        out_shape=(shape((TURNS, CD, WIDE), LOW), shape((CD, CFF), LOW), shape((8, CD), F32)),
        in_specs=[SCALARS] + [INSIDE] * 4 + [ANYWHERE] * 3,
        out_specs=(ANYWHERE, INSIDE, INSIDE),
        scratch_shapes=[
            v((2, CFF, WIDE), LOW), v((2, CD, WIDE), F32), v((2, 8, WIDE), F32), v((2, CD, WIDE), LOW),
            v((CD, CFF), F32), v((CD, WIDE), F32),
            pltpu.SemaphoreType.DMA((3, 2)),
            pltpu.SemaphoreType.DMA((2,)),
        ],
        compiler_params=params(),
        cost_estimate=pl.CostEstimate(flops=200 * 10**9, bytes_accessed=20 * 10**6, transcendentals=10**6),
        name="character_backward_one",
    )(turns, gw, gain, up, down, kepts, keptm, kepti)


def call_b2(turns, wgains, gain2, aup, weights, keptl, keptd, kepti):
    v = pltpu.VMEM
    return pl.pallas_call(
        kernel_b2,
        out_shape=(shape((SHARES, C_ROWS, 128), LOW), shape((SHARES, C_ROWS, 128), LOW)),
        in_specs=[SCALARS] + [INSIDE] * 8 + [ANYWHERE] * 3,
        out_specs=(ANYWHERE, ANYWHERE),
        scratch_shapes=[
            v((2, KEPT_LOW, WIDE), LOW), v((2, 8, WIDE), F32), v((2, CD, WIDE), LOW),
            v((CHAR_HEADS * SPAN, WIDE), LOW),
            v((CD, 3 * CD), LOW),
            v((CD, 3 * CD), F32), v((CD, CD), F32), v((CVOC, CD), F32), v((CD, WIDE), F32),
            v((2, SHARES, C_ROWS, 128), LOW),
            pltpu.SemaphoreType.DMA((3, 2)),
            pltpu.SemaphoreType.DMA((2,)),
        ],
        compiler_params=params(),
        cost_estimate=pl.CostEstimate(flops=200 * 10**9, bytes_accessed=40 * 10**6, transcendentals=10**6),
        name="character_backward_two",
    )(turns, wgains, gain2, aup, *weights, keptl, keptd, kepti)


def call_f(x, z, c, outk, outg):
    v = pltpu.VMEM
    outs = ((CVOC, CD), (CD,), (CD, CD), (CD, CD), (CD, CD), (CD, CD), (CD,), (CD, CFF), (CFF, CD), (CD, WD),
            (WD,), (WD, WD), (WD, WD), (WD, WD), (WD, WD), (WD,), (WD, WFF), (WFF, WD))
    outs = [(s[0] // SHARES,) + tuple(n // 2 for n in s[1:]) for s in outs]
    return pl.pallas_call(
        kernel_f,
        out_shape=(shape((2, 1, WORDS, WD // 2), LOW),) + tuple(shape(s, F32) for s in outs),
        in_specs=([ANYWHERE] + [INSIDE] * 3) * 3 + [INSIDE] * 2,
        out_specs=(INSIDE,) * 19,
        scratch_shapes=[
            v((X_ROWS, 256), LOW), v((Z_ROWS, 256), LOW), v((C_ROWS, 128), LOW), pltpu.SemaphoreType.DMA((3,)),
        ],
        compiler_params=params(),
        name="finish",
    )(x[0], *x[1], z[0], *z[1], c[0], *c[1], outk, outg)


def flip(value, axis, bits):
    count = lax.axis_size(axis)
    return lax.ppermute(value, axis, [(i, i ^ bits) for i in range(count)])


def pick(value, index):
    return lax.dynamic_index_in_dim(value, index, 0, keepdims=False)


def plus(first, *others):
    total = first.astype(F32)
    for other in others:
        total = total + other.astype(F32)
    return total.astype(LOW)


def quarters(total, place):
    return [pick(total, lax.bitwise_xor(place, k)) for k in range(1, 4)]


def over_plane(parts):
    return [flip(part, "dp", k) for k, part in enumerate(parts, 1)]


def over_line(parts):
    return [flip(part, "dp", 4 * k) for k, part in enumerate(parts, 1)]


def after(value, *others):
    return lax.optimization_barrier((value,) + others)[0]


def body(
    char_ids, char_counts, segment_ids, out_cotangent,
    char_table, char_gain_one, char_query, char_key, char_value, char_output, char_gain_two, char_up, char_down,
    char_project,
    word_gain_one, word_query, word_key, word_value, word_output, word_gain_two, word_up, word_down,
):
    keptl, kepts, keptm, kepti, turns, gw, xkeep, xsend, zkeep, zsend, outk, outs, wgains = call_a(
        char_counts, char_ids, segment_ids, out_cotangent,
        (char_table, char_gain_one, char_query, char_key, char_value, char_output, char_gain_two, char_up, char_down,
         char_project,
         word_gain_one, word_query, word_key, word_value, word_output, word_gain_two, word_up, word_down),
    )
    fast = lax.axis_size("dp") == SHARES
    dp = lax.axis_index("dp")
    plane, line = lax.rem(dp, 4), lax.div(dp, 4)
    zgot, xgot, outg = flip(zsend, "phase", 1), flip(xsend, "phase", 1), flip(outs, "phase", 1)
    keptd, aup, gain2 = call_b1(turns, gw, char_gain_two, char_up, char_down, kepts, keptm, kepti)
    attention = (char_gain_one, char_query, char_key, char_value, char_output)
    if not fast:
        ckeep, csend = call_b2(turns, wgains, gain2, aup, attention, keptl, keptd, kepti)
        return general_sums(outk, outg, (xkeep, xgot), (zkeep, zgot), (ckeep, flip(csend, "phase", 1)))
    xgot, zgot = after(xgot, keptd), after(zgot, keptd)
    xsum = plus(xkeep, xgot).reshape(4, 4, X_ROWS, 256)
    zsum = plus(zkeep, zgot).reshape(4, 4, Z_ROWS, 256)
    xparts, zparts = quarters(xsum, plane), quarters(zsum, line)
    keptd = after(keptd, *xparts, *zparts)
    xparts, zparts = over_plane(xparts), over_line(zparts)
    ckeep, csend = call_b2(turns, wgains, gain2, aup, attention, keptl, keptd, kepti)
    ckeep, csend, xparts, zparts, xsum, zsum = lax.optimization_barrier((ckeep, csend, xparts, zparts, xsum, zsum))
    cgot = flip(csend, "phase", 1)
    xsum = plus(pick(xsum, plane), *xparts)
    zsum = plus(pick(zsum, line), *zparts)
    xparts = over_line(quarters(xsum, line))
    zparts = over_plane(quarters(zsum, plane))
    csum = plus(ckeep, cgot).reshape(4, 4, C_ROWS, 128)
    csum = plus(pick(csum, plane), *over_plane(quarters(csum, plane)))
    cparts = over_line(quarters(csum, line))
    return call_f((xsum, xparts), (zsum, zparts), (csum, cparts), outk, outg)


def general_sums(outk, outg, xs, zs, cs):
    first = lax.axis_index("phase") == 0
    outs = jnp.stack([jnp.where(first, outk, outg), jnp.where(first, outg, outk)])[:, None]
    order = jnp.asarray([plane_first(d) for d in range(SHARES)])

    def natural(pair):
        return pair[0].astype(F32) + pair[1].astype(F32)

    x, c = (jnp.take(natural(pair), order, axis=0) for pair in (xs, cs))
    z = natural(zs)

    def whole(rows):
        return rows.reshape(-1, rows.shape[-1])

    def wide(rows, pieces):
        n = rows.shape[1] // pieces
        return whole(rows.reshape(SHARES, pieces, n, rows.shape[-1]).transpose(0, 2, 1, 3).reshape(SHARES, n, -1))

    cdown = x[:, X_CDOWN:X_CDOWN + 32]
    cdown = jnp.concatenate([cdown[..., :128], cdown[..., 128:]], axis=1)
    parts = (
        whole(c[:, C_TABLE:C_TABLE + 16]), c[:, C_GAIN, :16].reshape(-1),
        whole(c[:, C_Q:C_Q + 16]), whole(c[:, C_K:C_K + 16]), whole(c[:, C_V:C_V + 16]), whole(c[:, C_O:C_O + 16]),
        c[:, C_GAIN + 1, :16].reshape(-1),
        wide(c[:, C_UP:C_UP + 64], 4), whole(cdown), whole(z[:, Z_PROJ:Z_PROJ + 16]),
        c[:, C_GAIN + 2, :32].reshape(-1),
        whole(x[:, X_Q:X_Q + 32]), whole(x[:, X_K:X_K + 32]), whole(x[:, X_V:X_V + 32]), whole(x[:, X_O:X_O + 32]),
        c[:, C_GAIN + 3, :32].reshape(-1),
        wide(x[:, X_UP:X_UP + 128], 4), whole(z[:, Z_DOWN:Z_DOWN + 128]),
    )
    return (outs,) + tuple(lax.psum_scatter(p, "dp", scatter_dimension=0, tiled=True) for p in parts)


def solution(mesh):
    rows = P(None, "dp", None)
    both = P("dp", "phase")
    one = P("dp")
    return jax.shard_map(
        body,
        mesh=mesh,
        in_specs=(rows, rows, rows, P(None, "dp", None, None)) + (P(),) * 18,
        out_specs=(
            P(None, "dp", None, "phase"),
            both, one, both, both, both, both, one, both, both, both,
            one, both, both, both, both, one, both, both,
        ),
        check_vma=False,
    )
```

time: 193 us -> 130 us (0.67)
  waiting for transfers between devices: 58.4 us -> 17.6 us
  Pallas kernels: 93.6 us -> 67.9 us
  starting transfers between devices: 17.6 us -> 29.9 us
  local copies, waits for them, and re-layouts: 13.6 us -> 5.15 us
    ppermute x15 -> x22, waiting for transfers between devices: 58.4 us -> 17.6 us  [flip(): return lax.ppermute(value, axis, [(i, i ^ bits) for i in range(count)])]
    pallas_call x2 -> x4, Pallas kernels: 93.6 us -> 67.9 us  [the longest x1 35.2 us: call_a(): pl.pallas_call(kernel_a, out_shape=(shape((TURNS, KEPT_LOW, WIDE), LOW),...]
    ppermute x15 -> x22, starting transfers between devices: 17.6 us -> 29.9 us  [flip(): return lax.ppermute(value, axis, [(i, i ^ bits) for i in range(count)])]
    reshape x5 -> x0, local copies, waits for them, and re-layouts: 6.82 us -> none  [the longest x2 2.52 us: body(): wg1, wg2 = (word_gain_one.reshape(1, WD), word_gain_two.reshape(1, WD))]
    convert_element_type x4 -> x6, other arithmetic: 4.94 us -> 7.53 us  [plus(): return total.astype(LOW)]
    slice x5 -> x0, local copies, waits for them, and re-layouts: 2.55 us -> none  [the longest x2 1.27 us: wide(): rows[i * n:(i + 1) * n]]
    another operation x1 -> x0, local copies, waits for them, and re-layouts: 2.27 us -> none
    squeeze x4 -> x6, local copies, waits for them, and re-layouts: 0.3 us -> 2.39 us  [pick(): return lax.dynamic_index_in_dim(value, index, 0, keepdims=False)]
  transfers between devices with their start and end apart: 15 -> 22, of which waited for: 8 -> 7; matrix products, arithmetic and copies ran while one was open for 7% -> 8% of each run, Pallas kernels for 21% -> 23%
where the time goes in v2:
time: 130 us; the launch traced here: 129 us
  Pallas kernels  67.9 us (52%)
  starting transfers between devices  29.9 us (23%)
  waiting for transfers between devices  17.6 us (14%)
  other arithmetic  7.53 us (6%)
  local copies, waits for them, and re-layouts  5.15 us (4%)
    pallas_call x1, Pallas kernels, call_a(): pl.pallas_call(kernel_a, out_shape=(shape((TURNS, KEPT_LOW, WIDE), LOW),...  35.2 us
    ppermute x22, starting transfers between devices, flip(): return lax.ppermute(value, axis, [(i, i ^ bits) for i in range(count)])  29.9 us
    ppermute x22, waiting for transfers between devices, flip(): return lax.ppermute(value, axis, [(i, i ^ bits) for i in range(count)])  17.6 us
    pallas_call x1, Pallas kernels, call_b2(): pl.pallas_call(kernel_b2, out_shape=(shape((SHARES, C_ROWS, 128), LOW), s...  15.9 us
    pallas_call x1, Pallas kernels, call_b1(): pl.pallas_call(kernel_b1, out_shape=(shape((TURNS, CD, WIDE), LOW), shape...  13.6 us
    convert_element_type x6, other arithmetic, plus(): return total.astype(LOW)  7.53 us
    pallas_call x1, Pallas kernels, call_f(): pl.pallas_call(kernel_f, out_shape=(shape((2, 1, WORDS, WD // 2), LOW),)...  3.22 us
    unnamed x42, local copies, waits for them, and re-layouts  2.76 us
  transfers between devices with their start and end apart: 22, of which 7 were waited for; matrix products, arithmetic and copies ran while one was open for 8% of the time, Pallas kernels for 23%

profile of v2, /device:TPU:0, one launch (start us, length us, event | category | flops | bytes accessed | tf_op | source)
XLA Modules:
  0.0 129.4 jit_solution(18401319032306365451)
XLA Ops:
  0.7 35.2 %forward_and_words.1 = (bf16[9,2304,512]{2,1,0:T(8,128)(2,1)}, bf16[9,1024,512]{2,1,0:T(8,128)(2,1)}, f32[9,256,512]{2,1,0:T(8,128)}, f32[9,8,512]{2,1,0:T(8,128...) custom-call(s32[2,1,256]{2,1,0:T(1,128)} %counts_ref.1, ...), custom_call_target="tpu_custom_call" | custom-call | flops 199999995904 | bytes 60000000 | tf_op jit(solution)/shard_map/forward_and_words/pallas_call | solution.py:677
  36.5 13.6 %character_backward_one.1 = (bf16[9,256,512]{2,1,0:T(8,128)(2,1)}, bf16[256,1024]{1,0:T(8,128)(2,1)}, f32[8,256]{1,0:T(8,128)}) custom-call(s32[1]{0:T(128)} %get-tuple-element.50.turns_ref, bf16[256,256]{1,0:T(8,128)(2,1)} %get-tuple-element.52.gw_ref, bf16[256]{0:T(256)(128)(2,1)} %g2_ref.3, bf16[256,1024]{1,0:T(8,128)(2,1)} %up_ref.3, ...), custom_call_target="tpu_custom_call" | custom-call | flops 199999995904 | bytes 20000000 | tf_op jit(solution)/shard_map/character_backward_one/pallas_call | solution.py:720
  50.1 1.7 %add_convert_fusion.1 = bf16[16,144,256]{2,1,0:T(8,128)(2,1)S(1)} fusion(bf16[16,144,256]{2,1,0:T(8,128)(2,1)} %collective-permute-done.1, bf16[16,144,256]{2,1,0:T(8,128)(2,1)S(1)} %copy-done.6), kind=kLoop, calls=%fused_computation.1 | loop fusion | flops 2359296 | bytes 3538944 | tf_op jit(solution)/shard_map/convert_element_type | solution.py:790
  51.8 1.0 dynamic-slice_bitcast_fusion.3
  52.8 3.0 %collective-permute-start.5 = (bf16[4,144,256]{2,1,0:T(8,128)(2,1)S(1)}, bf16[4,144,256]{2,1,0:T(8,128)(2,1)S(1)}, u32[]{:S(2)}, u32[]{:S(2)}) collective-permute-start(bf16[4,144,256]{2,1,0:T(8,128)(2,1)S(1)} %get-tuple-element.86), channel_id=1, source_target_pairs={{0,4},{1,5},{2,6},{3,7},{4,0},{5,1},{6,2},{7,3},{8,12},{9,13},{10,... | collective-permute-start | bytes 884744 | tf_op jit(solution)/shard_map/ppermute | solution.py:779
  55.9 2.6 %collective-permute-start.6 = (bf16[4,144,256]{2,1,0:T(8,128)(2,1)}, bf16[4,144,256]{2,1,0:T(8,128)(2,1)}, u32[]{:S(2)}, u32[]{:S(2)}) collective-permute-start(bf16[4,144,256]{2,1,0:T(8,128)(2,1)} %get-tuple-element.85), channel_id=1, source_target_pairs={{0,8},{1,9},{2,10},{3,11},{4,12},{5,13},{6,14},{7,15},{8,0},{9,1},... | collective-permute-start | bytes 884744 | tf_op jit(solution)/shard_map/ppermute | solution.py:779
  58.5 2.4 %add_convert_fusion = bf16[16,288,256]{2,1,0:T(8,128)(2,1)S(1)} fusion(bf16[16,288,256]{2,1,0:T(8,128)(2,1)} %collective-permute-done, bf16[16,288,256]{2,1,0:T(8,128)(2,1)S(1)} %copy-done.3), kind=kLoop, calls=%fused_computation | loop fusion | flops 4718592 | bytes 7077888 | tf_op jit(solution)/shard_map/convert_element_type | solution.py:790
  60.9 1.4 %copy-done = bf16[16,288,256]{2,1,0:T(8,128)(2,1)} copy-done((bf16[16,288,256]{2,1,0:T(8,128)(2,1)}, bf16[16,288,256]{2,1,0:T(8,128)(2,1)S(1)}, u32[]{:S(2)}) %copy-start) | copy-done | bytes 2359320
  62.3 1.3 dynamic-slice_bitcast_fusion
  63.6 1.7 %collective-permute-start.2 = (bf16[4,288,256]{2,1,0:T(8,128)(2,1)}, bf16[4,288,256]{2,1,0:T(8,128)(2,1)}, u32[]{:S(2)}, u32[]{:S(2)}) collective-permute-start(bf16[4,288,256]{2,1,0:T(8,128)(2,1)} %get-tuple-element.83), channel_id=1, source_target_pairs={{0,1},{1,0},{2,3},{3,2},{4,5},{5,4},{6,7},{7,6},{8,9},{9,8},{10,11... | collective-permute-start | bytes 1769480 | tf_op jit(solution)/shard_map/ppermute | solution.py:779
  65.3 1.5 %collective-permute-start.3 = (bf16[4,288,256]{2,1,0:T(8,128)(2,1)}, bf16[4,288,256]{2,1,0:T(8,128)(2,1)}, u32[]{:S(2)}, u32[]{:S(2)}) collective-permute-start(bf16[4,288,256]{2,1,0:T(8,128)(2,1)} %get-tuple-element.82), channel_id=1, source_target_pairs={{0,2},{1,3},{2,0},{3,1},{4,6},{5,7},{6,4},{7,5},{8,10},{9,11},{10,... | collective-permute-start | bytes 1769480 | tf_op jit(solution)/shard_map/ppermute | solution.py:779
  66.8 1.9 %collective-permute-done.5 = bf16[4,144,256]{2,1,0:T(8,128)(2,1)S(1)} collective-permute-done((bf16[4,144,256]{2,1,0:T(8,128)(2,1)S(1)}, bf16[4,144,256]{2,1,0:T(8,128)(2,1)S(1)}, u32[]{:S(2)}, u32[]{:S(2)}) %collective-permute-start.5) | collective-permute-done | bytes 294944 | tf_op jit(solution)/shard_map/ppermute | solution.py:779
  69.4 2.6 %collective-permute-start.4 = (bf16[4,288,256]{2,1,0:T(8,128)(2,1)}, bf16[4,288,256]{2,1,0:T(8,128)(2,1)}, u32[]{:S(2)}, u32[]{:S(2)}) collective-permute-start(bf16[4,288,256]{2,1,0:T(8,128)(2,1)} %get-tuple-element.81), channel_id=1, source_target_pairs={{0,3},{1,2},{2,1},{3,0},{4,7},{5,6},{6,5},{7,4},{8,11},{9,10},{10,... | collective-permute-start | bytes 1769480 | tf_op jit(solution)/shard_map/ppermute | solution.py:779
  72.0 15.9 %character_backward_two.1 = (bf16[16,160,128]{2,1,0:T(8,128)(2,1)}, bf16[16,160,128]{2,1,0:T(8,128)(2,1)}) custom-call(s32[1]{0:T(128)} %get-tuple-element.50.turns_ref, f32[8,512]{1,0:T(8,128)} %get-tuple-element.51.wgains_ref, f32[8,256]{1,0:T(8,128)} %get-tuple-element.56.gain2_ref, bf16[256,1024]{1,0:T(8,128)(2,1)} %get-tuple-element.57.aup_ref, ...), custom_call_target="tpu_custom_call" | custom-call | flops 199999995904 | bytes 40000000 | tf_op jit(solution)/shard_map/character_backward_two/pallas_call | solution.py:739
  88.0 4.5 %collective-permute-done.3 = bf16[4,288,256]{2,1,0:T(8,128)(2,1)} collective-permute-done((bf16[4,288,256]{2,1,0:T(8,128)(2,1)}, bf16[4,288,256]{2,1,0:T(8,128)(2,1)}, u32[]{:S(2)}, u32[]{:S(2)}) %collective-permute-start.3) | collective-permute-done | bytes 589856 | tf_op jit(solution)/shard_map/ppermute | solution.py:779
  93.0 1.9 %fusion.2.xown_hbm = bf16[4,288,256]{2,1,0:T(8,128)(2,1)S(1)} fusion(bf16[4,288,256]{2,1,0:T(8,128)(2,1)} %collective-permute-done.4, bf16[4,288,256]{2,1,0:T(8,128)(2,1)} %collective-permute-done.3, bf16[4,288,256]{2,1,0:T(8,128)(2,1)} %collective-permute-done.2, bf16[4,4,288,256]{3,2,1,0:T(8,128)(2,1)} %bitcast.49, s32[]{:T(128)S(6)} %select_n.49), kind=kLoop, calls=%fused_computation.6 | loop fusion | flops 2359296 | bytes 2949124 | tf_op jit(solution)/shard_map/convert_element_type | solution.py:790
  95.9 1.6 %collective-permute-start.17 = (bf16[4,160,128]{2,1,0:T(8,128)(2,1)S(1)}, bf16[4,160,128]{2,1,0:T(8,128)(2,1)S(1)}, u32[]{:S(2)}, u32[]{:S(2)}) collective-permute-start(bf16[4,160,128]{2,1,0:T(8,128)(2,1)S(1)} %get-tuple-element.88), channel_id=1, source_target_pairs={{0,3},{1,2},{2,1},{3,0},{4,7},{5,6},{6,5},{7,4},{8,11},{9,10},{10,... | collective-permute-start | bytes 491528 | tf_op jit(solution)/shard_map/ppermute | solution.py:779
  97.4 1.2 collective-permute-start.16
  99.4 1.3 fusion.5.zown_hbm
  100.8 3.2 %collective-permute-done.17 = bf16[4,160,128]{2,1,0:T(8,128)(2,1)S(1)} collective-permute-done((bf16[4,160,128]{2,1,0:T(8,128)(2,1)S(1)}, bf16[4,160,128]{2,1,0:T(8,128)(2,1)S(1)}, u32[]{:S(2)}, u32[]{:S(2)}) %collective-permute-start.17) | collective-permute-done | bytes 163872 | tf_op jit(solution)/shard_map/ppermute | solution.py:779
  104.0 3.5 %collective-permute-start.9 = (bf16[288,256]{1,0:T(8,128)(2,1)S(1)}, bf16[288,256]{1,0:T(8,128)(2,1)S(1)}, u32[]{:S(2)}, u32[]{:S(2)}) collective-permute-start(bf16[288,256]{1,0:T(8,128)(2,1)S(1)} %get-tuple-element.91), channel_id=1, source_target_pairs={{0,8},{1,9},{2,10},{3,11},{4,12},{5,13},{6,14},{7,15},{8,0},{9,1},... | collective-permute-start | bytes 442376 | tf_op jit(solution)/shard_map/ppermute | solution.py:779
  107.5 2.0 %collective-permute-start.10 = (bf16[288,256]{1,0:T(8,128)(2,1)S(1)}, bf16[288,256]{1,0:T(8,128)(2,1)S(1)}, u32[]{:S(2)}, u32[]{:S(2)}) collective-permute-start(bf16[288,256]{1,0:T(8,128)(2,1)S(1)} %get-tuple-element.90), channel_id=1, source_target_pairs={{0,12},{1,13},{2,14},{3,15},{4,8},{5,9},{6,10},{7,11},{8,4},{9,5},... | collective-permute-start | bytes 442376 | tf_op jit(solution)/shard_map/ppermute | solution.py:779
  109.5 1.2 collective-permute-start.11
  110.8 0.9 collective-permute-start.12
  111.7 2.1 %collective-permute-done.11.zg1 = bf16[144,256]{1,0:T(8,128)(2,1)S(1)} collective-permute-done((bf16[144,256]{1,0:T(8,128)(2,1)S(1)}, bf16[144,256]{1,0:T(8,128)(2,1)S(1)}, u32[]{:S(2)}, u32[]{:S(2)}) %collective-permute-start.11) | collective-permute-done | bytes 73760 | tf_op jit(solution)/shard_map/ppermute | solution.py:779
  113.8 1.5 %collective-permute-start.13 = (bf16[144,256]{1,0:T(8,128)(2,1)S(1)}, bf16[144,256]{1,0:T(8,128)(2,1)S(1)}, u32[]{:S(2)}, u32[]{:S(2)}) collective-permute-start(bf16[144,256]{1,0:T(8,128)(2,1)S(1)} %get-tuple-element.93), channel_id=1, source_target_pairs={{0,3},{1,2},{2,1},{3,0},{4,7},{5,6},{6,5},{7,4},{8,11},{9,10},{10,... | collective-permute-start | bytes 221192 | tf_op jit(solution)/shard_map/ppermute | solution.py:779
  115.3 0.9 collective-permute-start.18
  116.2 2.9 %collective-permute-done.13.zg3 = bf16[144,256]{1,0:T(8,128)(2,1)S(1)} collective-permute-done((bf16[144,256]{1,0:T(8,128)(2,1)S(1)}, bf16[144,256]{1,0:T(8,128)(2,1)S(1)}, u32[]{:S(2)}, u32[]{:S(2)}) %collective-permute-start.13) | collective-permute-done | bytes 73760 | tf_op jit(solution)/shard_map/ppermute | solution.py:779
  119.4 2.8 %collective-permute-start.20 = (bf16[160,128]{1,0:T(8,128)(2,1)S(1)}, bf16[160,128]{1,0:T(8,128)(2,1)S(1)}, u32[]{:S(2)}, u32[]{:S(2)}) collective-permute-start(bf16[160,128]{1,0:T(8,128)(2,1)S(1)} %get-tuple-element.96), channel_id=1, source_target_pairs={{0,12},{1,13},{2,14},{3,15},{4,8},{5,9},{6,10},{7,11},{8,4},{9,5},... | collective-permute-start | bytes 122888 | tf_op jit(solution)/shard_map/ppermute | solution.py:779
  122.3 2.1 %collective-permute-done.19.cg2 = bf16[160,128]{1,0:T(8,128)(2,1)S(1)} collective-permute-done((bf16[160,128]{1,0:T(8,128)(2,1)S(1)}, bf16[160,128]{1,0:T(8,128)(2,1)S(1)}, u32[]{:S(2)}, u32[]{:S(2)}) %collective-permute-start.19) | collective-permute-done | bytes 40992 | tf_op jit(solution)/shard_map/ppermute | solution.py:779
  124.4 0.9 collective-permute-done.20.cg3
  126.0 3.2 %finish.1 = (bf16[2,1,256,256]{3,2,1,0:T(8,128)(2,1)}, f32[16,128]{1,0:T(8,128)}, f32[16]{0:T(128)}, f32[16,128]{1,0:T(8,128)}, f32[16,128]{1,0:T(8,128)}, /*ind...) custom-call(bf16[4,288,256]{2,1,0:T(8,128)(2,1)} %copy-done.2, ...), custom_call_target="tpu_custom_call" | custom-call | tf_op jit(solution)/shard_map/finish/pallas_call | solution.py:764
  (70 shorter events, 4.6 us)
Async XLA Ops:
  35.9 22.6 %collective-permute-start = (bf16[16,288,256]{2,1,0:T(8,128)(2,1)}, bf16[16,288,256]{2,1,0:T(8,128)(2,1)}, u32[]{:S(2)}, u32[]{:S(2)}) collective-permute-start(bf16[16,288,256]{2,1,0:T(8,128)(2,1)} %get-tuple-element.61), channel_id=1, source_target_pairs={{0,16},{16,0},{1,17},{17,1},{2,18},{18,2},{3,19},{19,3},{4,20},{20... | collective-permute-start | bytes 7077896 | tf_op jit(solution)/shard_map/ppermute | solution.py:779
  36.4 13.7 %collective-permute-start.1 = (bf16[16,144,256]{2,1,0:T(8,128)(2,1)}, bf16[16,144,256]{2,1,0:T(8,128)(2,1)}, u32[]{:S(2)}, u32[]{:S(2)}) collective-permute-start(bf16[16,144,256]{2,1,0:T(8,128)(2,1)} %get-tuple-element.64), channel_id=1, source_target_pairs={{0,16},{16,0},{1,17},{17,1},{2,18},{18,2},{3,19},{19,3},{4,20},{20... | collective-permute-start | bytes 3538952 | tf_op jit(solution)/shard_map/ppermute | solution.py:779
  36.4 13.6 %copy-start.6 = (bf16[16,144,256]{2,1,0:T(8,128)(2,1)S(1)}, bf16[16,144,256]{2,1,0:T(8,128)(2,1)}, u32[]{:S(2)}) copy-start(bf16[16,144,256]{2,1,0:T(8,128)(2,1)} %get-tuple-element.63) | copy-start | bytes 3538948
  50.1 8.4 %copy-start.3 = (bf16[16,288,256]{2,1,0:T(8,128)(2,1)S(1)}, bf16[16,288,256]{2,1,0:T(8,128)(2,1)}, u32[]{:S(2)}) copy-start(bf16[16,288,256]{2,1,0:T(8,128)(2,1)} %get-tuple-element.60) | copy-start | bytes 7077892
  51.8 6.6 %copy-start.1 = (bf16[16,144,256]{2,1,0:T(8,128)(2,1)}, bf16[16,144,256]{2,1,0:T(8,128)(2,1)S(1)}, u32[]{:S(2)}) copy-start(bf16[16,144,256]{2,1,0:T(8,128)(2,1)S(1)} %add_convert_fusion.1) | copy-start | bytes 3538948
  52.8 15.8 %collective-permute-start.5 = (bf16[4,144,256]{2,1,0:T(8,128)(2,1)S(1)}, bf16[4,144,256]{2,1,0:T(8,128)(2,1)S(1)}, u32[]{:S(2)}, u32[]{:S(2)}) collective-permute-start(bf16[4,144,256]{2,1,0:T(8,128)(2,1)S(1)} %get-tuple-element.86), channel_id=1, source_target_pairs={{0,4},{1,5},{2,6},{3,7},{4,0},{5,1},{6,2},{7,3},{8,12},{9,13},{10,... | collective-permute-start | bytes 884744 | tf_op jit(solution)/shard_map/ppermute | solution.py:779
  55.9 32.1 %collective-permute-start.6 = (bf16[4,144,256]{2,1,0:T(8,128)(2,1)}, bf16[4,144,256]{2,1,0:T(8,128)(2,1)}, u32[]{:S(2)}, u32[]{:S(2)}) collective-permute-start(bf16[4,144,256]{2,1,0:T(8,128)(2,1)} %get-tuple-element.85), channel_id=1, source_target_pairs={{0,8},{1,9},{2,10},{3,11},{4,12},{5,13},{6,14},{7,15},{8,0},{9,1},... | collective-permute-start | bytes 884744 | tf_op jit(solution)/shard_map/ppermute | solution.py:779
  58.4 29.6 %collective-permute-start.7 = (bf16[4,144,256]{2,1,0:T(8,128)(2,1)}, bf16[4,144,256]{2,1,0:T(8,128)(2,1)}, u32[]{:S(2)}, u32[]{:S(2)}) collective-permute-start(bf16[4,144,256]{2,1,0:T(8,128)(2,1)} %get-tuple-element.84), channel_id=1, source_target_pairs={{0,12},{1,13},{2,14},{3,15},{4,8},{5,9},{6,10},{7,11},{8,4},{9,5},... | collective-permute-start | bytes 884744 | tf_op jit(solution)/shard_map/ppermute | solution.py:779
  63.6 24.5 %collective-permute-start.2 = (bf16[4,288,256]{2,1,0:T(8,128)(2,1)}, bf16[4,288,256]{2,1,0:T(8,128)(2,1)}, u32[]{:S(2)}, u32[]{:S(2)}) collective-permute-start(bf16[4,288,256]{2,1,0:T(8,128)(2,1)} %get-tuple-element.83), channel_id=1, source_target_pairs={{0,1},{1,0},{2,3},{3,2},{4,5},{5,4},{6,7},{7,6},{8,9},{9,8},{10,11... | collective-permute-start | bytes 1769480 | tf_op jit(solution)/shard_map/ppermute | solution.py:779
  65.3 27.2 %collective-permute-start.3 = (bf16[4,288,256]{2,1,0:T(8,128)(2,1)}, bf16[4,288,256]{2,1,0:T(8,128)(2,1)}, u32[]{:S(2)}, u32[]{:S(2)}) collective-permute-start(bf16[4,288,256]{2,1,0:T(8,128)(2,1)} %get-tuple-element.82), channel_id=1, source_target_pairs={{0,2},{1,3},{2,0},{3,1},{4,6},{5,7},{6,4},{7,5},{8,10},{9,11},{10,... | collective-permute-start | bytes 1769480 | tf_op jit(solution)/shard_map/ppermute | solution.py:779
  69.4 23.1 %collective-permute-start.4 = (bf16[4,288,256]{2,1,0:T(8,128)(2,1)}, bf16[4,288,256]{2,1,0:T(8,128)(2,1)}, u32[]{:S(2)}, u32[]{:S(2)}) collective-permute-start(bf16[4,288,256]{2,1,0:T(8,128)(2,1)} %get-tuple-element.81), channel_id=1, source_target_pairs={{0,3},{1,2},{2,1},{3,0},{4,7},{5,6},{6,5},{7,4},{8,11},{9,10},{10,... | collective-permute-start | bytes 1769480 | tf_op jit(solution)/shard_map/ppermute | solution.py:779
  72.0 20.5 %copy-start.20 = (bf16[256,256]{1,0:T(8,128)(2,1)S(1)}, bf16[256,256]{1,0:T(8,128)(2,1)}, u32[]{:S(2)}) copy-start(bf16[256,256]{1,0:T(8,128)(2,1)} %get-tuple-element.80) | copy-start | bytes 393220
  88.0 7.6 %copy-start.7 = (bf16[16,160,128]{2,1,0:T(8,128)(2,1)S(1)}, bf16[16,160,128]{2,1,0:T(8,128)(2,1)}, u32[]{:S(2)}) copy-start(bf16[16,160,128]{2,1,0:T(8,128)(2,1)} %get-tuple-element.77) | copy-start | bytes 1966084
  92.5 3.1 %collective-permute-start.14 = (bf16[16,160,128]{2,1,0:T(8,128)(2,1)}, bf16[16,160,128]{2,1,0:T(8,128)(2,1)S(1)}, u32[]{:S(2)}, u32[]{:S(2)}) collective-permute-start(bf16[16,160,128]{2,1,0:T(8,128)(2,1)} %get-tuple-element.78), channel_id=1, source_target_pairs={{0,16},{16,0},{1,17},{17,1},{2,18},{18,2},{3,19},{19,3},{4,20},{20... | collective-permute-start | bytes 1966088 | tf_op jit(solution)/shard_map/ppermute | solution.py:779
  92.5 18.3 %collective-permute-start.21 = (bf16[256,256]{1,0:T(8,128)(2,1)S(1)}, bf16[256,256]{1,0:T(8,128)(2,1)S(1)}, u32[]{:S(2)}, u32[]{:S(2)}) collective-permute-start(bf16[256,256]{1,0:T(8,128)(2,1)S(1)} %copy-done.20), channel_id=1, source_target_pairs={{0,16},{16,0},{1,17},{17,1},{2,18},{18,2},{3,19},{19,3},{4,20},{20... | collective-permute-start | bytes 393224 | tf_op jit(solution)/shard_map/ppermute | solution.py:779
  95.0 24.5 %collective-permute-start.8 = (bf16[288,256]{1,0:T(8,128)(2,1)S(1)}, bf16[288,256]{1,0:T(8,128)(2,1)S(1)}, u32[]{:S(2)}, u32[]{:S(2)}) collective-permute-start(bf16[288,256]{1,0:T(8,128)(2,1)S(1)} %get-tuple-element.92), channel_id=1, source_target_pairs={{0,4},{1,5},{2,6},{3,7},{4,0},{5,1},{6,2},{7,3},{8,12},{9,13},{10,... | collective-permute-start | bytes 442376 | tf_op jit(solution)/shard_map/ppermute | solution.py:779
  95.9 8.1 %collective-permute-start.17 = (bf16[4,160,128]{2,1,0:T(8,128)(2,1)S(1)}, bf16[4,160,128]{2,1,0:T(8,128)(2,1)S(1)}, u32[]{:S(2)}, u32[]{:S(2)}) collective-permute-start(bf16[4,160,128]{2,1,0:T(8,128)(2,1)S(1)} %get-tuple-element.88), channel_id=1, source_target_pairs={{0,3},{1,2},{2,1},{3,0},{4,7},{5,6},{6,5},{7,4},{8,11},{9,10},{10,... | collective-permute-start | bytes 491528 | tf_op jit(solution)/shard_map/ppermute | solution.py:779
  97.4 10.0 %collective-permute-start.16 = (bf16[4,160,128]{2,1,0:T(8,128)(2,1)S(1)}, bf16[4,160,128]{2,1,0:T(8,128)(2,1)S(1)}, u32[]{:S(2)}, u32[]{:S(2)}) collective-permute-start(bf16[4,160,128]{2,1,0:T(8,128)(2,1)S(1)} %get-tuple-element.89), channel_id=1, source_target_pairs={{0,2},{1,3},{2,0},{3,1},{4,6},{5,7},{6,4},{7,5},{8,10},{9,11},{10,... | collective-permute-start | bytes 491528 | tf_op jit(solution)/shard_map/ppermute | solution.py:779
  98.6 10.9 %collective-permute-start.15 = (bf16[4,160,128]{2,1,0:T(8,128)(2,1)S(1)}, bf16[4,160,128]{2,1,0:T(8,128)(2,1)S(1)}, u32[]{:S(2)}, u32[]{:S(2)}) collective-permute-start(bf16[4,160,128]{2,1,0:T(8,128)(2,1)S(1)} %get-tuple-element.87), channel_id=1, source_target_pairs={{0,1},{1,0},{2,3},{3,2},{4,5},{5,4},{6,7},{7,6},{8,9},{9,8},{10,11... | collective-permute-start | bytes 491528 | tf_op jit(solution)/shard_map/ppermute | solution.py:779
  100.7 24.6 %copy-start.4 = (bf16[4,144,256]{2,1,0:T(8,128)(2,1)}, bf16[4,144,256]{2,1,0:T(8,128)(2,1)S(1)}, u32[]{:S(2)}) copy-start(bf16[4,144,256]{2,1,0:T(8,128)(2,1)S(1)} %fusion.5.zown_hbm) | copy-start | bytes 884740
  104.0 18.3 %collective-permute-start.9 = (bf16[288,256]{1,0:T(8,128)(2,1)S(1)}, bf16[288,256]{1,0:T(8,128)(2,1)S(1)}, u32[]{:S(2)}, u32[]{:S(2)}) collective-permute-start(bf16[288,256]{1,0:T(8,128)(2,1)S(1)} %get-tuple-element.91), channel_id=1, source_target_pairs={{0,8},{1,9},{2,10},{3,11},{4,12},{5,13},{6,14},{7,15},{8,0},{9,1},... | collective-permute-start | bytes 442376 | tf_op jit(solution)/shard_map/ppermute | solution.py:779
  107.5 14.8 %collective-permute-start.10 = (bf16[288,256]{1,0:T(8,128)(2,1)S(1)}, bf16[288,256]{1,0:T(8,128)(2,1)S(1)}, u32[]{:S(2)}, u32[]{:S(2)}) collective-permute-start(bf16[288,256]{1,0:T(8,128)(2,1)S(1)} %get-tuple-element.90), channel_id=1, source_target_pairs={{0,12},{1,13},{2,14},{3,15},{4,8},{5,9},{6,10},{7,11},{8,4},{9,5},... | collective-permute-start | bytes 442376 | tf_op jit(solution)/shard_map/ppermute | solution.py:779
  109.5 4.4 %collective-permute-start.11 = (bf16[144,256]{1,0:T(8,128)(2,1)S(1)}, bf16[144,256]{1,0:T(8,128)(2,1)S(1)}, u32[]{:S(2)}, u32[]{:S(2)}) collective-permute-start(bf16[144,256]{1,0:T(8,128)(2,1)S(1)} %get-tuple-element.95), channel_id=1, source_target_pairs={{0,1},{1,0},{2,3},{3,2},{4,5},{5,4},{6,7},{7,6},{8,9},{9,8},{10,11... | collective-permute-start | bytes 221192 | tf_op jit(solution)/shard_map/ppermute | solution.py:779
  110.8 14.6 %copy-start.5 = (bf16[4,160,128]{2,1,0:T(8,128)(2,1)}, bf16[4,160,128]{2,1,0:T(8,128)(2,1)S(1)}, u32[]{:S(2)}) copy-start(bf16[4,160,128]{2,1,0:T(8,128)(2,1)S(1)} %fusion.8.cown_hbm) | copy-start | bytes 491524
  110.8 14.5 %copy-start.13 = (bf16[256,256]{1,0:T(8,128)(2,1)}, bf16[256,256]{1,0:T(8,128)(2,1)S(1)}, u32[]{:S(2)}) copy-start(bf16[256,256]{1,0:T(8,128)(2,1)S(1)} %collective-permute-done.21.outg) | copy-start | bytes 393220
  110.8 4.5 %collective-permute-start.12 = (bf16[144,256]{1,0:T(8,128)(2,1)S(1)}, bf16[144,256]{1,0:T(8,128)(2,1)S(1)}, u32[]{:S(2)}, u32[]{:S(2)}) collective-permute-start(bf16[144,256]{1,0:T(8,128)(2,1)S(1)} %get-tuple-element.94), channel_id=1, source_target_pairs={{0,2},{1,3},{2,0},{3,1},{4,6},{5,7},{6,4},{7,5},{8,10},{9,11},{10,... | collective-permute-start | bytes 221192 | tf_op jit(solution)/shard_map/ppermute | solution.py:779
  113.8 11.5 %copy-start.14 = (bf16[144,256]{1,0:T(8,128)(2,1)}, bf16[144,256]{1,0:T(8,128)(2,1)S(1)}, u32[]{:S(2)}) copy-start(bf16[144,256]{1,0:T(8,128)(2,1)S(1)} %collective-permute-done.11.zg1) | copy-start | bytes 221188
  113.8 5.3 %collective-permute-start.13 = (bf16[144,256]{1,0:T(8,128)(2,1)S(1)}, bf16[144,256]{1,0:T(8,128)(2,1)S(1)}, u32[]{:S(2)}, u32[]{:S(2)}) collective-permute-start(bf16[144,256]{1,0:T(8,128)(2,1)S(1)} %get-tuple-element.93), channel_id=1, source_target_pairs={{0,3},{1,2},{2,1},{3,0},{4,7},{5,6},{6,5},{7,4},{8,11},{9,10},{10,... | collective-permute-start | bytes 221192 | tf_op jit(solution)/shard_map/ppermute | solution.py:779
  115.3 10.0 %copy-start.15 = (bf16[144,256]{1,0:T(8,128)(2,1)}, bf16[144,256]{1,0:T(8,128)(2,1)S(1)}, u32[]{:S(2)}) copy-start(bf16[144,256]{1,0:T(8,128)(2,1)S(1)} %collective-permute-done.12.zg2) | copy-start | bytes 221188
  115.3 7.0 %collective-permute-start.18 = (bf16[160,128]{1,0:T(8,128)(2,1)S(1)}, bf16[160,128]{1,0:T(8,128)(2,1)S(1)}, u32[]{:S(2)}, u32[]{:S(2)}) collective-permute-start(bf16[160,128]{1,0:T(8,128)(2,1)S(1)} %get-tuple-element.98), channel_id=1, source_target_pairs={{0,4},{1,5},{2,6},{3,7},{4,0},{5,1},{6,2},{7,3},{8,12},{9,13},{10,... | collective-permute-start | bytes 122888 | tf_op jit(solution)/shard_map/ppermute | solution.py:779
  119.1 5.3 %collective-permute-start.19 = (bf16[160,128]{1,0:T(8,128)(2,1)S(1)}, bf16[160,128]{1,0:T(8,128)(2,1)S(1)}, u32[]{:S(2)}, u32[]{:S(2)}) collective-permute-start(bf16[160,128]{1,0:T(8,128)(2,1)S(1)} %get-tuple-element.97), channel_id=1, source_target_pairs={{0,8},{1,9},{2,10},{3,11},{4,12},{5,13},{6,14},{7,15},{8,0},{9,1},... | collective-permute-start | bytes 122888 | tf_op jit(solution)/shard_map/ppermute | solution.py:779
  119.4 5.9 %collective-permute-start.20 = (bf16[160,128]{1,0:T(8,128)(2,1)S(1)}, bf16[160,128]{1,0:T(8,128)(2,1)S(1)}, u32[]{:S(2)}, u32[]{:S(2)}) collective-permute-start(bf16[160,128]{1,0:T(8,128)(2,1)S(1)} %get-tuple-element.96), channel_id=1, source_target_pairs={{0,12},{1,13},{2,14},{3,15},{4,8},{5,9},{6,10},{7,11},{8,4},{9,5},... | collective-permute-start | bytes 122888 | tf_op jit(solution)/shard_map/ppermute | solution.py:779
  (11 other events, 35.7 us)

commit v3 on v2

v3 whole, which is shorter than its diff:
```python
from functools import partial

import jax
import jax.numpy as jnp
from jax import lax
from jax.experimental import pallas as pl
from jax.experimental.pallas import tpu as pltpu
from jax.sharding import PartitionSpec as P

F32 = jnp.float32
LOW = jnp.bfloat16

CD = 256
CFF = 1024
CPW = 16
CVOC = 256
CHAR_HEADS = 4
HEAD = 64
WD = 512
WFF = 2048
WORD_HEADS = 8
WORDS = 256

SPAN = 256
STEP = 240
WIDE = 2 * SPAN
TURNS = ((WORDS * CPW - 1) // STEP + 2) // 2

epsilon = 1e-06
half_root = 0.7071067811865476
density = 0.3989422804014327
floor_score = -1e30
log2_e = 1.4426950408889634

R_EMB, R_Q, R_K, R_V, R_P, R_MIX = 0, 256, 512, 768, 1024, 2048
KEPT_LOW = 2304
I_INV1, I_INV2, I_IDENT, I_WORD = 0, 1, 2, 3
BAND = 144
WINDOW = 96

F_UP, F_DOWN = 0, 128
F_ROWS = 256
T_Q, T_K, T_V, T_O, T_CDOWN, T_PROJ = 0, 32, 64, 96, 128, 160
T_ROWS = 176
C_TABLE, C_Q, C_K, C_V, C_O, C_UP, C_GAIN = 0, 16, 32, 48, 64, 80, 144
C_ROWS = 160
SHARES = 16


def nn(left, right):
    return lax.dot_general(left, right, (((1,), (0,)), ((), ())), preferred_element_type=F32)


def nt(left, right):
    return lax.dot_general(left, right, (((1,), (1,)), ((), ())), preferred_element_type=F32)


def iota(shape, axis):
    return lax.broadcasted_iota(jnp.int32, shape, axis)


def eye(n):
    return iota((n, n), 0) == iota((n, n), 1)


def row_to_column(row):
    n = row.shape[1]
    return jnp.sum(jnp.where(eye(n), row, 0.0), axis=1, keepdims=True)


def gelu_pair(v):
    e = lax.erf(v * half_root)
    half = 0.5 * v
    bell = jnp.exp2(v * v * (-0.5 * log2_e))
    return half + half * e, 0.5 + 0.5 * e + (density * v) * bell


def gelu_twice(v):
    u = v * half_root
    whole = 1.0 + lax.erf(u)
    bell = jnp.exp2(u * u * (-log2_e))
    return v * whole, whole + (2.0 * density * v) * bell


def bits(d):
    return d % 2, d // 2 % 2, d // 4 % 2, d // 8


def plane_first(d, core=0):
    return (d % 4) * 4 + d // 4


def by_core(d, core):
    x, y, low, high = bits(d)
    return (y * 8 + x * 4 if core else x * 8 + y * 4) + low * 2 + high


def members(word, first, count, weight=1.0):
    return jnp.where((iota((count, WIDE), 0) + first).astype(F32) == word, weight, 0.0).astype(LOW)


def word_starts(counts_row):
    earlier = iota((WORDS, WORDS), 1) < iota((WORDS, WORDS), 0)
    return jnp.sum(jnp.where(earlier, counts_row, 0.0), axis=1, keepdims=True)


def column_to_row(column):
    return jnp.sum(jnp.where(eye(column.shape[0]), column, 0.0), axis=0, keepdims=True)


def put(bundle, phase, order, row, value, width, share_rows):
    low = value.astype(LOW)
    lanes = bundle.shape[-1]
    for half in range(2):
        side = jnp.bitwise_xor(phase, half)
        for piece in range(max(1, width // lanes)):
            take = min(width, lanes)
            cols = low[:, half * width + piece * lanes:half * width + piece * lanes + take]
            for i in range(value.shape[0] // share_rows):
                part = cols[i * share_rows:(i + 1) * share_rows]
                if take < lanes:
                    part = jnp.concatenate([part[:share_rows // 2], part[share_rows // 2:]], axis=1)
                m = part.shape[0]
                bundle[side, order(i, half), row + piece * share_rows:row + piece * share_rows + m, :] = part


def band(t):
    keys = slice(0, BAND) if t % 2 == 0 else slice(SPAN - BAND, SPAN)
    return t // 2, keys, slice(t * 128, (t + 1) * 128)


def two_heads(pair):
    zero = jnp.zeros((HEAD, pair.shape[1]), LOW)
    first = jnp.concatenate([pair[:HEAD], zero], axis=0)
    second = jnp.concatenate([zero, pair[HEAD:]], axis=0)
    return jnp.concatenate([first, second], axis=1)


def two_heads_rows(pair):
    left = iota(pair.shape, 1) < HEAD
    zero = jnp.zeros(pair.shape, LOW)
    return jnp.concatenate([jnp.where(left, pair, zero), jnp.where(left, zero, pair)], axis=0)


def softmax_keys(s):
    e = jnp.exp(s - jnp.max(s, axis=0, keepdims=True))
    return (e * (1.0 / jnp.sum(e, axis=0, keepdims=True))).astype(LOW)


def kernel_a(
    counts_hbm, ids_hbm, segs_hbm, cot_hbm,
    table_hbm, g1_hbm, wq_hbm, wk_hbm, wv_hbm, wo_hbm, g2_hbm, up_hbm, down_hbm, proj_hbm,
    wg1_hbm, wwq_hbm, wwk_hbm, wwv_hbm, wwo_hbm, wg2_hbm, wup_hbm, wdown_hbm,
    keptl_hbm, kepts_hbm, keptm_hbm, kepti_hbm, turns_ref,
    keep_hbm, send_hbm, outk_ref, outs_ref, gain_ref,
    q_ref, k_ref, v_ref, probs_ref, mixt_ref, normed_ref, xhat_ref, winv_ref, md_ref, pooled_ref, pa_ref,
    counts_ref, ids_ref, segs_ref,
    table_ref, g1_ref, wq_ref, wk_ref, wv_ref, wo_ref, g2_ref, up_ref, down_ref, proj_ref, wg1_ref, wg2_ref,
    cot, wwq, wwk, wwv, wwo, wup, wdown,
    tab_t, wqkv_t, wo_t, up_t, ids_t, slow, sslope, smid, sinfo, pa, pm, rowinfo, firsts_v, firsts, before_s, act_s, prob_s, found_s,
    next_s, mid_s, word_s,
    bundle, actw, slopew,
    csem, wsem, ksem, osem,
):
    phase = lax.axis_index("phase")
    tiny = [
        pltpu.make_async_copy(src.at[phase], dst, csem.at[12 + i])
        for i, (src, dst) in enumerate(((counts_hbm, counts_ref), (ids_hbm, ids_ref), (segs_hbm, segs_ref)))
    ]
    for load in tiny:
        load.start()
    early = [
        pltpu.make_async_copy(src, dst, csem.at[i])
        for i, (src, dst) in enumerate(
            ((g1_hbm, g1_ref), (g2_hbm, g2_ref), (table_hbm, table_ref), (wq_hbm, wq_ref), (wk_hbm, wk_ref),
             (wv_hbm, wv_ref), (wo_hbm, wo_ref), (up_hbm, up_ref), (down_hbm, down_ref), (proj_hbm, proj_ref),
             (wg1_hbm, wg1_ref), (wg2_hbm, wg2_ref))
        )
    ]
    for load in early:
        load.start()
    loads = [
        pltpu.make_async_copy(src, dst, wsem.at[i])
        for i, (src, dst) in enumerate(
            ((wwq_hbm, wwq), (wwk_hbm, wwk), (wwv_hbm, wwv), (wwo_hbm, wwo),
             (wup_hbm, wup), (wdown_hbm, wdown), (cot_hbm.at[phase, 0], cot))
        )
    ]
    for load in tiny:
        load.wait()
    counts_row = counts_ref[...].astype(F32)
    starts = word_starts(counts_row)
    counts = row_to_column(counts_row)
    blocks = jnp.floor((starts + 0.5) * (1.0 / STEP))
    places = starts + (SPAN - STEP) * blocks
    n_turns = jnp.max(places).astype(jnp.int32) // WIDE + 1
    turns_ref[0] = n_turns
    bases = (iota((1, 128), 1) * WIDE).astype(F32)
    first = jnp.sum(jnp.where(places < bases, 1.0, 0.0), axis=0, keepdims=True)
    firsts_v[...] = jnp.broadcast_to(first, (8, 128)).astype(jnp.int32)
    first_copy = pltpu.make_async_copy(firsts_v, firsts, wsem.at[7])
    first_copy.start()
    ids = ids_ref[...]
    ids_t[...] = jnp.concatenate(
        [ids[:, 128 * a:128 * a + 128] for a in range(32)], axis=0
    ).astype(F32).T.astype(LOW)
    places_row = column_to_row(places)
    none = jnp.zeros((1, 1), F32)
    rowinfo[...] = jnp.concatenate(
        [places_row - jnp.concatenate([none, places_row[:, :-1]], axis=1),
         counts_row - jnp.concatenate([none, counts_row[:, :-1]], axis=1),
         jnp.ones((1, WORDS), F32), jnp.zeros((13, WORDS), F32)], axis=0
    ).astype(LOW)
    pa[...] = jnp.zeros_like(pa)
    pm[...] = jnp.zeros_like(pm)
    for load in early:
        load.wait()
    for load in loads:
        load.start()
    tab_t[...] = table_ref[...].T
    wqkv_t[0:CD] = (wq_ref[...] * 0.125).T
    wqkv_t[CD:2 * CD] = wk_ref[...].T
    wqkv_t[2 * CD:] = wv_ref[...].T
    wo_t[...] = wo_ref[...].T
    up_t[...] = up_ref[...].T
    g1 = row_to_column(g1_ref[...].astype(F32)[None, :])
    g2 = row_to_column(g2_ref[...].astype(F32)[None, :])
    prob_s[...] = jnp.zeros_like(prob_s)
    for slot in range(2):
        slow[slot, R_P:R_P + CHAR_HEADS * SPAN] = jnp.zeros((CHAR_HEADS * SPAN, WIDE), LOW)
    first_copy.wait()

    def find(turn):
        place = (iota((1, WIDE), 1) + turn * WIDE).astype(F32)
        begun = jnp.where(places <= place, 1.0, 0.0).astype(LOW)
        info = nn(rowinfo[...], begun)
        word = info[2:3] - 1.0
        slot = place - info[0:1]
        flat = (word * 16.0 + slot).astype(jnp.int32)
        chosen = jnp.where(iota((32, WIDE), 0) == (flat >> 7), 1.0, 0.0).astype(LOW)
        lanes = nn(ids_t[...], chosen)
        ident = jnp.sum(jnp.where(iota((128, WIDE), 0) == (flat & 127), lanes, 0.0), axis=0, keepdims=True)
        valid = slot < info[1:2]
        none = jnp.full((6, WIDE), -1.0, F32)
        return jnp.concatenate([jnp.where(valid, ident, -1.0), jnp.where(valid, word, -1.0), none], axis=0)

    found_s[...] = find(jnp.int32(0))

    def copies(b):
        slot = lax.rem(b, 2)
        return (
            pltpu.make_async_copy(slow.at[slot], keptl_hbm.at[b], ksem.at[0, slot]),
            pltpu.make_async_copy(sslope.at[slot], kepts_hbm.at[b], ksem.at[1, slot]),
            pltpu.make_async_copy(smid.at[slot], keptm_hbm.at[b], ksem.at[2, slot]),
            pltpu.make_async_copy(sinfo.at[slot], kepti_hbm.at[b], ksem.at[3, slot]),
        )

    def start(copies):
        for c in copies:
            c.start()

    def wait(copies):
        for c in copies:
            c.wait()

    def near_words(b):
        first = (firsts[0, b] // 16) * 16
        return first, (firsts[0, b + 1] - first + WINDOW - 1) // WINDOW

    def window(first):
        return pl.ds(pl.multiple_of(first, 16), WINDOW)

    def attend(b):
        slot = lax.rem(b, 2)
        ident = found_s[0:1]
        word = found_s[1:2]
        hot = jnp.where(iota((CVOC, WIDE), 0).astype(F32) == ident, 1.0, 0.0).astype(LOW)
        emb = nn(tab_t[...], hot)
        inv1 = lax.rsqrt(jnp.mean(emb * emb, axis=0, keepdims=True) + epsilon)
        normed = (emb * inv1 * g1).astype(LOW)
        yield
        qkv = nn(wqkv_t[...], normed).astype(LOW)
        key_rows = [qkv[CD:2 * CD, u * SPAN:(u + 1) * SPAN].T for u in range(2)]
        value_t = qkv[2 * CD:]
        word_col = jnp.broadcast_to(jnp.where(word < 0.0, -2.0, word), (8, WIDE)).T[:, 0:1]
        yield
        for t in range(4):
            u, ks, ql = band(t)
            bias = jnp.where(word_col[u * SPAN + ks.start:u * SPAN + ks.stop] == word[:, ql], 0.0, floor_score)
            for pair in range(CHAR_HEADS // 2):
                fs = slice(pair * 128, pair * 128 + 128)
                s = nn(key_rows[u][ks, fs], two_heads(qkv[fs, ql]))
                for i in range(2):
                    p = softmax_keys(s[:, i * 128:i * 128 + 128] + bias)
                    row = (pair * 2 + i) * SPAN
                    prob_s[row + ks.start:row + ks.stop, ql] = p
                    slow[slot, R_P + row + ks.start:R_P + row + ks.stop, ql] = p
                yield
        slow[slot, R_EMB:R_EMB + CD] = emb.astype(LOW)
        slow[slot, R_Q:R_Q + 2 * CD] = qkv[:2 * CD]
        for u in range(2):
            us = slice(u * SPAN, (u + 1) * SPAN)
            slow[slot, R_V:R_V + SPAN, us] = value_t[:, us].T
        mixed = []
        for h in range(CHAR_HEADS):
            hs = slice(h * HEAD, (h + 1) * HEAD)
            both = []
            for u in range(2):
                us = slice(u * SPAN, (u + 1) * SPAN)
                both.append(nn(value_t[hs, us], prob_s[h * SPAN:(h + 1) * SPAN, us]).astype(LOW))
            mixed.append(jnp.concatenate(both, axis=1))
        mixed = jnp.concatenate(mixed, axis=0)
        slow[slot, R_MIX:R_MIX + CD] = mixed
        yield
        middle = emb + nn(wo_t[...], mixed)
        inv2 = lax.rsqrt(jnp.mean(middle * middle, axis=0, keepdims=True) + epsilon)
        smid[slot] = middle
        sinfo[slot] = jnp.concatenate([inv1, inv2, ident, word, jnp.zeros((4, WIDE), F32)], axis=0)
        normed_two = (middle * inv2 * g2).astype(LOW)
        yield
        first, _ = near_words(b)
        near = members(word, first, WINDOW)
        middle_low = middle.astype(LOW)
        pm[window(first), :] += nt(near, middle_low)
        mid_s[...] = middle_low
        next_s[...] = normed_two
        word_s[0:1] = word
        found_s[...] = find(b + 1)
        yield

    def feed(b):
        slot = lax.rem(b, 2)
        word = word_s[0:1]
        before_s[...] = nn(up_t[...], next_s[...])
        yield
        for c in range(CFF // 32):
            cs = slice(c * 32, (c + 1) * 32)
            act, slope = gelu_twice(before_s[cs])
            sslope[slot, cs] = slope.astype(LOW)
            act_s[cs] = act.astype(LOW)
            if c % 4 == 3:
                yield
        first, _ = near_words(b)
        pa[window(first), :] += nt(members(word, first, WINDOW, 0.5), act_s[...])
        yield

    def run(*parts):
        parts = list(parts)
        while parts:
            for part in tuple(parts):
                if next(part, parts) is parts:
                    parts.remove(part)

    def turn(b, carry):
        @pl.when(b >= 2)
        def _():
            wait(copies(b - 2))

        run(attend(b))
        run(feed(b))
        first, windows = near_words(b)

        def more(i, carry):
            at = first + i * WINDOW
            pm[window(at), :] += nt(members(word_s[0:1], at, WINDOW), mid_s[...])
            pa[window(at), :] += nt(members(word_s[0:1], at, WINDOW, 0.5), act_s[...])
            return carry

        lax.fori_loop(1, windows, more, 0)
        start(copies(b))
        return carry

    lax.fori_loop(0, n_turns, turn, 0)

    pa_hi = pa[0:WORDS].astype(LOW)
    pa_lo = (pa[0:WORDS] - pa_hi.astype(F32)).astype(LOW)
    per_count = 1.0 / counts
    pooled = (pm[0:WORDS] + nn(pa_hi, down_ref[...]) + nn(pa_lo, down_ref[...])) * per_count
    pooled_low = pooled.astype(LOW)
    pooled_ref[...] = pooled_low
    pa_ref[...] = pa_hi
    x = nn(pooled_low, proj_ref[...]).astype(LOW).astype(F32)
    for load in loads:
        load.wait()
    wg1 = wg1_ref[...].astype(F32)[None, :]
    wg2 = wg2_ref[...].astype(F32)[None, :]
    winv1 = lax.rsqrt(jnp.mean(x * x, axis=1, keepdims=True) + epsilon)
    xhat = x * winv1
    normed = (xhat * wg1).astype(LOW)
    xhat_ref[...] = xhat
    winv_ref[...] = jnp.broadcast_to(winv1, (WORDS, 128))
    normed_ref[...] = normed
    q = (nn(normed, wwq[...]) * 0.125).astype(LOW)
    k = nn(normed, wwk[...]).astype(LOW)
    v = nn(normed, wwv[...]).astype(LOW)
    seg_row = segs_ref[...].astype(F32)
    seg_col = row_to_column(seg_row)
    allowed = (seg_row == seg_col) & (iota((WORDS, WORDS), 0) <= iota((WORDS, WORDS), 1))
    bias = jnp.where(allowed, 0.0, floor_score)
    q_ref[...] = q
    k_ref[...] = k
    v_ref[...] = v
    v_t = v.T
    for h in range(WORD_HEADS):
        probs_ref[h, 128:, 0:128] = jnp.zeros((128, 128), LOW)
    for t in range(2):
        ks, ql = slice(0, 128 * (t + 1)), slice(128 * t, 128 * (t + 1))
        for pair in range(WORD_HEADS // 2):
            fs = slice(pair * 128, pair * 128 + 128)
            s = nt(k[ks, fs], two_heads_rows(q[ql, fs]))
            for i in range(2):
                probs_ref[pair * 2 + i, ks, ql] = softmax_keys(s[:, i * 128:i * 128 + 128] + bias[ks, ql])
    mixed_t = jnp.concatenate(
        [nn(v_t[h * HEAD:(h + 1) * HEAD], probs_ref[h]).astype(LOW) for h in range(WORD_HEADS)], axis=0
    )
    mixt_ref[...] = mixed_t
    middle = x + nn(mixed_t.T, wwo[...])
    winv2 = lax.rsqrt(jnp.mean(middle * middle, axis=1, keepdims=True) + epsilon)
    normed_two = (middle * winv2 * wg2).astype(LOW)
    result = middle
    for c in range(WFF // 512):
        cs = slice(c * 512, (c + 1) * 512)
        act, slope = gelu_pair(nn(normed_two, wup[:, cs]))
        act = act.astype(LOW)
        actw[:, cs] = act
        slopew[:, cs] = slope.astype(LOW)
        result = result + nn(act, wdown[cs, :])
    result = result.astype(LOW)
    front = phase == 0
    outk_ref[...] = jnp.where(front, result[:, :256], result[:, 256:])
    outs_ref[...] = jnp.where(front, result[:, 256:], result[:, :256])

    cot_low = cot[...]
    n2d = jnp.zeros((WORDS, WD), F32)
    n2_t = normed_two.T
    for c in range(WFF // 512):
        cs = slice(c * 512, (c + 1) * 512)
        gd = nn(actw[:, cs].T, cot_low)
        put(bundle, phase, lambda i, p: by_core(c * 4 + i, p), F_DOWN, gd, 256, 128)
        bd = (nt(cot_low, wdown[cs, :]) * slopew[:, cs].astype(F32)).astype(LOW)
        gu = nn(n2_t, bd).astype(LOW)
        side = jnp.bitwise_xor(phase, c // 2)
        for piece in range(2):
            row = F_UP + ((c % 2) * 2 + piece) * 32
            for d in range(SHARES):
                bundle[side, by_core(d, c // 2), row:row + 32, :] = gu[d * 32:(d + 1) * 32, piece * 256:piece * 256 + 256]
        n2d = n2d + nt(bd, wup[:, cs])
    stores = [
        pltpu.make_async_copy(bundle.at[0], keep_hbm, osem.at[0]),
        pltpu.make_async_copy(bundle.at[1], send_hbm, osem.at[1]),
    ]
    for s in stores:
        s.start()
    vhat = middle * winv2
    gain_ref[...] = jnp.broadcast_to(jnp.sum(n2d * vhat, axis=0, keepdims=True), (8, WD))
    lifted = n2d * wg2
    md_ref[...] = cot[...].astype(F32) + winv2 * (lifted - vhat * jnp.mean(lifted * vhat, axis=1, keepdims=True))

    def drain(b, carry):
        wait(copies(b))
        return carry

    lax.fori_loop(jnp.maximum(n_turns - 2, 0), n_turns, drain, 0)
    for s in stores:
        s.wait()


def kernel_a2(
    counts_ref, q_ref, k_ref, v_ref, pw, mixt_ref, normed_ref, xhat_ref, winv_ref, md_ref, pooled_ref, pa_ref,
    wg1_ref, proj_ref, wwq_hbm, wwk_hbm, wwv_hbm, wwo_hbm,
    gw_ref, keep_hbm, send_hbm, gain_ref,
    wwq, wwk, wwv, wwo, bundle, wsem, osem,
):
    phase = lax.axis_index("phase")
    loads = [
        pltpu.make_async_copy(src, dst, wsem.at[i])
        for i, (src, dst) in enumerate(((wwo_hbm, wwo), (wwq_hbm, wwq), (wwk_hbm, wwk), (wwv_hbm, wwv)))
    ]
    for load in loads:
        load.start()
    wg1 = wg1_ref[...].astype(F32)[None, :]
    q, k, v, normed, pooled_low = q_ref[...], k_ref[...], v_ref[...], normed_ref[...], pooled_ref[...]
    per_count = 1.0 / row_to_column(counts_ref[phase].astype(F32))
    md = md_ref[...]
    md_low = md.astype(LOW)
    put(bundle, phase, by_core, T_O, nn(mixt_ref[...], md_low), 256, 32)
    k_t = k.T
    loads[0].wait()
    do = nt(md_low, wwo[...]).astype(LOW)
    dq_t, dk, dv = [], [], []
    left = iota((WORDS, 128), 1) < HEAD
    for pair in range(WORD_HEADS // 2):
        fs = slice(pair * 128, pair * 128 + 128)
        ds = []
        for t in range(2):
            ks, ql = slice(0, 128 * (t + 1)), slice(128 * t, 128 * (t + 1))
            dp = nt(v[ks, fs], two_heads_rows(do[ql, fs]))
            for i in range(2):
                pf = pw[pair * 2 + i, ks, ql].astype(F32)
                dph = dp[:, i * 128:i * 128 + 128]
                d = (pf * (dph - jnp.sum(pf * dph, axis=0, keepdims=True))).astype(LOW)
                ds.append(d if t else jnp.concatenate([d, jnp.zeros((128, 128), LOW)], axis=0))
        both = [jnp.concatenate([ds[i], ds[i + 2]], axis=1) for i in range(2)]
        for i in range(2):
            h = pair * 2 + i
            dq_t.append(nn(k_t[h * HEAD:(h + 1) * HEAD], both[i]))
        dk.append(jnp.where(left, nn(both[0], q[:, fs]), nn(both[1], q[:, fs])).astype(LOW))
        dv.append(jnp.where(left, nn(pw[pair * 2], do[:, fs]), nn(pw[pair * 2 + 1], do[:, fs])).astype(LOW))
    dq = (jnp.concatenate(dq_t, axis=0) * 0.125).astype(LOW).T
    dk = jnp.concatenate(dk, axis=1)
    dv = jnp.concatenate(dv, axis=1)
    normed_t = normed.T
    for load in loads[1:]:
        load.wait()
    nd = nt(dq, wwq[...]) + nt(dk, wwk[...]) + nt(dv, wwv[...])
    put(bundle, phase, by_core, T_Q, nn(normed_t, dq), 256, 32)
    put(bundle, phase, by_core, T_K, nn(normed_t, dk), 256, 32)
    put(bundle, phase, by_core, T_V, nn(normed_t, dv), 256, 32)
    vhat = xhat_ref[...]
    gain_ref[...] = jnp.broadcast_to(jnp.sum(nd * vhat, axis=0, keepdims=True), (8, WD))
    lifted = nd * wg1
    xd = md + winv_ref[:, 0:1] * (lifted - vhat * jnp.mean(lifted * vhat, axis=1, keepdims=True))
    vd = xd.astype(LOW)
    put(bundle, phase, by_core, T_PROJ, nn(pooled_low.T, vd), 256, 16)
    gw = (nt(vd, proj_ref[...]) * per_count).astype(LOW)
    gw_ref[...] = gw.T
    put(bundle, phase, by_core, T_CDOWN, nn(pa_ref[...].T, gw), 128, 64)
    stores = [
        pltpu.make_async_copy(bundle.at[0], keep_hbm, osem.at[0]),
        pltpu.make_async_copy(bundle.at[1], send_hbm, osem.at[1]),
    ]
    for s in stores:
        s.start()
    for s in stores:
        s.wait()


def kernel_b1(
    turns_ref, gw_ref, g2_ref, up_ref, down_ref, kepts_hbm, keptm_hbm, kepti_hbm,
    keptd_hbm, aup_ref, gain_ref,
    sslope, smid, sinfo, sdelta, aup, ag2, down, ksem, dsem,
):
    n_turns = turns_ref[0]

    def kept_copies(b, slot):
        return (
            pltpu.make_async_copy(kepts_hbm.at[b], sslope.at[slot], ksem.at[0, slot]),
            pltpu.make_async_copy(keptm_hbm.at[b], smid.at[slot], ksem.at[1, slot]),
            pltpu.make_async_copy(kepti_hbm.at[b], sinfo.at[slot], ksem.at[2, slot]),
        )

    def delta_copy(b, slot):
        return pltpu.make_async_copy(sdelta.at[slot], keptd_hbm.at[b], dsem.at[slot])

    for c in kept_copies(0, 0):
        c.start()
    g2 = row_to_column(g2_ref[...].astype(F32)[None, :])
    down[...] = down_ref[...] * 0.5
    aup[...] = jnp.zeros_like(aup)
    ag2[...] = jnp.zeros_like(ag2)

    def turn(b, carry):
        slot = lax.rem(b, 2)

        @pl.when(b + 1 < n_turns)
        def _():
            for c in kept_copies(b + 1, 1 - slot):
                c.start()

        @pl.when(b >= 2)
        def _():
            delta_copy(b - 2, slot).wait()

        for c in kept_copies(b, slot):
            c.wait()
        inv2 = sinfo[slot, I_INV2:I_INV2 + 1]
        g_low = nn(gw_ref[...], members(sinfo[slot, I_WORD:I_WORD + 1], 0, WORDS)).astype(LOW)
        vhat = smid[slot] * inv2
        normed_two = (vhat * g2).astype(LOW)
        n2d = jnp.zeros((CD, WIDE), F32)
        for c in range(CFF // 256):
            cs = slice(c * 256, (c + 1) * 256)
            bd = (nn(down[cs, :], g_low) * sslope[slot, cs].astype(F32)).astype(LOW)
            aup[:, cs] += nt(normed_two, bd)
            n2d = n2d + nn(up_ref[:, cs], bd)
        ag2[...] += n2d * vhat
        lifted = n2d * g2
        md = g_low.astype(F32) + inv2 * (lifted - vhat * jnp.mean(lifted * vhat, axis=0, keepdims=True))
        sdelta[slot] = md.astype(LOW)
        delta_copy(b, slot).start()
        return carry

    lax.fori_loop(0, n_turns, turn, 0)
    aup_ref[...] = aup[...].astype(LOW)
    gain_ref[...] = jnp.broadcast_to(jnp.sum(ag2[...], axis=1, keepdims=True), (CD, 8)).T

    def drain(b, carry):
        delta_copy(b, lax.rem(b, 2)).wait()
        return carry

    lax.fori_loop(jnp.maximum(n_turns - 2, 0), n_turns, drain, 0)


def kernel_b2(
    turns_ref, wgain1_ref, wgain2_ref, gain2_ref, aup_ref, g1_ref, wq_ref, wk_ref, wv_ref, wo_ref,
    keptl_hbm, keptd_hbm, kepti_hbm,
    keep_hbm, send_hbm,
    slow, sinfo, sdelta, dscore, wqkv, aqkv, ao, atab, ag1, bundle, ksem, osem,
):
    phase = lax.axis_index("phase")
    n_turns = turns_ref[0]

    def kept_copies(b, slot):
        return (
            pltpu.make_async_copy(keptl_hbm.at[b], slow.at[slot], ksem.at[0, slot]),
            pltpu.make_async_copy(keptd_hbm.at[b], sdelta.at[slot], ksem.at[1, slot]),
            pltpu.make_async_copy(kepti_hbm.at[b], sinfo.at[slot], ksem.at[2, slot]),
        )

    for c in kept_copies(0, 0):
        c.start()
    g1 = row_to_column(g1_ref[...].astype(F32)[None, :])
    for i, w in enumerate((wq_ref, wk_ref, wv_ref)):
        wqkv[:, i * CD:(i + 1) * CD] = w[...]
    for acc in (aqkv, ao, atab, ag1, dscore):
        acc[...] = jnp.zeros_like(acc)

    def turn(b, carry):
        slot = lax.rem(b, 2)

        @pl.when(b + 1 < n_turns)
        def _():
            for c in kept_copies(b + 1, 1 - slot):
                c.start()

        for c in kept_copies(b, slot):
            c.wait()
        inv1 = sinfo[slot, I_INV1:I_INV1 + 1]
        ident = sinfo[slot, I_IDENT:I_IDENT + 1]
        md_low = sdelta[slot]
        ao[...] += nt(slow[slot, R_MIX:R_MIX + CD], md_low)
        do = nn(wo_ref[...], md_low).astype(LOW)
        for t in range(4):
            u, ks, ql = band(t)
            for pair in range(CHAR_HEADS // 2):
                fs = slice(u * SPAN + pair * 128, u * SPAN + pair * 128 + 128)
                dp = nn(
                    slow[slot, R_V + ks.start:R_V + ks.stop, fs], two_heads(do[pair * 128:pair * 128 + 128, ql])
                )
                for i in range(2):
                    row = (pair * 2 + i) * SPAN
                    pf = slow[slot, R_P + row + ks.start:R_P + row + ks.stop, ql].astype(F32)
                    dph = dp[:, i * 128:i * 128 + 128]
                    d = pf * (dph - jnp.sum(pf * dph, axis=0, keepdims=True))
                    dscore[row + ks.start:row + ks.stop, ql] = d.astype(LOW)
        dq, dk, dv = [], [], []
        for h in range(CHAR_HEADS):
            hs = slice(h * HEAD, (h + 1) * HEAD)
            one, two, three = [], [], []
            for u in range(2):
                us = slice(u * SPAN, (u + 1) * SPAN)
                p = slow[slot, R_P + h * SPAN:R_P + (h + 1) * SPAN, us]
                ds = dscore[h * SPAN:(h + 1) * SPAN, us]
                one.append((nn(slow[slot, R_K + h * HEAD:R_K + (h + 1) * HEAD, us], ds) * 0.125).astype(LOW))
                two.append(nt(slow[slot, R_Q + h * HEAD:R_Q + (h + 1) * HEAD, us], ds).astype(LOW))
                three.append(nt(do[hs, us], p).astype(LOW))
            for part, pair in ((dq, one), (dk, two), (dv, three)):
                part.append(jnp.concatenate(pair, axis=1))
        dqkv = jnp.concatenate(dq + dk + dv, axis=0)
        emb = slow[slot, R_EMB:R_EMB + CD].astype(F32)
        ehat = emb * inv1
        normed = (ehat * g1).astype(LOW)
        aqkv[...] += nt(normed, dqkv)
        nd = nn(wqkv[...], dqkv)
        ag1[...] += nd * ehat
        lifted = nd * g1
        ed = md_low.astype(F32) + inv1 * (lifted - ehat * jnp.mean(lifted * ehat, axis=0, keepdims=True))
        hot = jnp.where(iota((CVOC, WIDE), 0).astype(F32) == ident, 1.0, 0.0).astype(LOW)
        atab[...] += nt(hot, ed.astype(LOW))
        return carry

    lax.fori_loop(0, n_turns, turn, 0)

    put(bundle, phase, plane_first, C_TABLE, atab[...], 128, 16)
    put(bundle, phase, plane_first, C_Q, aqkv[:, 0:CD], 128, 16)
    put(bundle, phase, plane_first, C_K, aqkv[:, CD:2 * CD], 128, 16)
    put(bundle, phase, plane_first, C_V, aqkv[:, 2 * CD:], 128, 16)
    put(bundle, phase, plane_first, C_O, ao[...], 128, 16)
    put(bundle, phase, plane_first, C_UP, aup_ref[...], 512, 16)
    cg1 = jnp.broadcast_to(jnp.sum(ag1[...], axis=1, keepdims=True), (CD, 8)).T[0:1]
    cg2 = gain2_ref[0:1]
    for d in range(SHARES):
        rows = [
            jnp.concatenate([cg1[:, d * 16:d * 16 + 16], jnp.zeros((1, 112), F32)], axis=1),
            jnp.concatenate([cg2[:, d * 16:d * 16 + 16], jnp.zeros((1, 112), F32)], axis=1),
            jnp.concatenate([wgain1_ref[0:1, d * 32:d * 32 + 32], jnp.zeros((1, 96), F32)], axis=1),
            jnp.concatenate([wgain2_ref[0:1, d * 32:d * 32 + 32], jnp.zeros((1, 96), F32)], axis=1),
            jnp.zeros((12, 128), F32),
        ]
        tile = jnp.concatenate(rows, axis=0).astype(LOW)
        bundle[0, plane_first(d), C_GAIN:C_GAIN + 16, :] = tile
        bundle[1, plane_first(d), C_GAIN:C_GAIN + 16, :] = tile
    stores = [
        pltpu.make_async_copy(bundle.at[0], keep_hbm, osem.at[0]),
        pltpu.make_async_copy(bundle.at[1], send_hbm, osem.at[1]),
    ]
    for s in stores:
        s.start()
    for s in stores:
        s.wait()


def kernel_f(
    f0, f1, f2, f3, f4, f5, t0, t1, t2, t3, t4, t5, c0, c1, c2, c3, c4, c5, c6, c7, outk, outg,
    word_out, d_table, d_g1, d_q, d_k, d_v, d_o, d_g2, d_up, d_down, d_proj,
    e_g1, e_q, e_k, e_v, e_o, e_g2, e_up, e_down,
    fs, ts, cs, sem,
):
    phase = lax.axis_index("phase")
    dp = lax.axis_index("dp")
    x, y, low, high = (lax.rem(lax.div(dp, n), 2) for n in (1, 2, 4, 8))
    a, b = jnp.where(phase == 0, x, y), jnp.where(phase == 0, y, x)
    loads = []
    at = a * 8 + b * 4 + low * 2 + high
    line = lax.div(dp, 4)
    both = (at, at, lax.rem(at, 8), lax.rem(at, 4), lax.rem(at, 2), 0)
    place = lax.rem(dp, 4) * 4 + line
    for i, (parts, places, here) in enumerate((
        ((f0, f1, f2, f3, f4, f5), both, fs),
        ((t0, t1, t2, t3, t4, t5), both, ts),
        ((c0, c1, c2, c3, c4), (place, place, line, line, line), cs),
    )):
        for j, (part, n) in enumerate(zip(parts, places)):
            loads.append(pltpu.make_async_copy(part.at[n], here.at[j], sem.at[i]))
    for j, part in enumerate((c5, c6, c7)):
        loads.append(pltpu.make_async_copy(part, cs.at[5 + j], sem.at[2]))
    for load in loads:
        load.start()
    word_out[phase, 0] = outk[...]
    word_out[1 - phase, 0] = outg[...]
    for load in loads:
        load.wait()

    def total(parts, row, n):
        t = parts[0, row:row + n].astype(F32) + parts[1, row:row + n].astype(F32)
        for j in range(2, parts.shape[0]):
            t = t + parts[j, row:row + n].astype(F32)
        return t

    f, t, c = partial(total, fs), partial(total, ts), partial(total, cs)
    d_table[...] = c(C_TABLE, 16)
    d_q[...] = c(C_Q, 16)
    d_k[...] = c(C_K, 16)
    d_v[...] = c(C_V, 16)
    d_o[...] = c(C_O, 16)
    for i in range(4):
        d_up[:, i * 128:(i + 1) * 128] = c(C_UP + i * 16, 16)
        e_up[:, i * 256:(i + 1) * 256] = f(F_UP + i * 32, 32)
    gains = c(C_GAIN, 16)
    d_g1[...] = gains[0, :16]
    d_g2[...] = gains[1, :16]
    e_g1[...] = gains[2, :32]
    e_g2[...] = gains[3, :32]
    cd = t(T_CDOWN, 32)
    d_down[0:32] = cd[:, :128]
    d_down[32:64] = cd[:, 128:]
    d_proj[...] = t(T_PROJ, 16)
    e_q[...] = t(T_Q, 32)
    e_k[...] = t(T_K, 32)
    e_v[...] = t(T_V, 32)
    e_o[...] = t(T_O, 32)
    e_down[...] = f(F_DOWN, 128)


ANYWHERE = pl.BlockSpec(memory_space=pltpu.HBM)
INSIDE = pl.BlockSpec(memory_space=pltpu.VMEM)
SCALARS = pl.BlockSpec(memory_space=pltpu.SMEM)
shape = jax.ShapeDtypeStruct


def params(mib):
    return pltpu.CompilerParams(vmem_limit_bytes=mib * 2**20)


def outside(dims, dtype):
    return pltpu.HBM(dims, dtype)


def kept_outside(*values):
    return tuple(pltpu.with_memory_space_constraint(v, pltpu.HBM) for v in values)


def call_a(char_counts, char_ids, segment_ids, out_cotangent, weights):
    v = pltpu.VMEM
    return pl.pallas_call(
        kernel_a,
        out_shape=(
            outside((TURNS, KEPT_LOW, WIDE), LOW),
            outside((TURNS, CFF, WIDE), LOW),
            outside((TURNS, CD, WIDE), F32),
            outside((TURNS, 8, WIDE), F32),
            shape((1,), jnp.int32),
            outside((SHARES, F_ROWS, 256), LOW),
            outside((SHARES, F_ROWS, 256), LOW),
            shape((WORDS, WD // 2), LOW),
            shape((WORDS, WD // 2), LOW),
            shape((8, WD), F32),
            shape((WORDS, WD), LOW), shape((WORDS, WD), LOW), shape((WORDS, WD), LOW),
            shape((WORD_HEADS, WORDS, WORDS), LOW), shape((WD, WORDS), LOW), shape((WORDS, WD), LOW),
            shape((WORDS, WD), F32), shape((WORDS, 128), F32), shape((WORDS, WD), F32),
            shape((WORDS, CD), LOW), shape((WORDS, CFF), LOW),
        ),
        in_specs=[ANYWHERE] * 22,
        out_specs=(ANYWHERE,) * 4 + (SCALARS,) + (ANYWHERE,) * 2 + (INSIDE,) * 14,
        scratch_shapes=[
            v((1, WORDS), jnp.int32), v((1, WORDS * CPW), jnp.int32), v((1, WORDS), jnp.int32),
            v((CVOC, CD), LOW), v((CD,), LOW), v((CD, CD), LOW), v((CD, CD), LOW), v((CD, CD), LOW), v((CD, CD), LOW),
            v((CD,), LOW), v((CD, CFF), LOW), v((CFF, CD), LOW), v((CD, WD), LOW), v((WD,), LOW), v((WD,), LOW),
            v((WORDS, WD), LOW),
            v((WD, WD), LOW), v((WD, WD), LOW), v((WD, WD), LOW), v((WD, WD), LOW),
            v((WD, WFF), LOW), v((WFF, WD), LOW),
            v((CD, CVOC), LOW), v((3 * CD, CD), LOW), v((CD, CD), LOW), v((CFF, CD), LOW), v((128, 32), LOW),
            v((2, KEPT_LOW, WIDE), LOW), v((2, CFF, WIDE), LOW), v((2, CD, WIDE), F32), v((2, 8, WIDE), F32),
            v((WORDS + WINDOW, CFF), F32), v((WORDS + WINDOW, CD), F32), v((16, WORDS), LOW),
            v((8, 128), jnp.int32), pltpu.SMEM((8, 128), jnp.int32),
            v((CFF, WIDE), F32), v((CFF, WIDE), LOW), v((CHAR_HEADS * SPAN, WIDE), LOW), v((8, WIDE), F32),
            v((CD, WIDE), LOW), v((CD, WIDE), LOW), v((8, WIDE), F32),
            v((2, SHARES, F_ROWS, 256), LOW),
            v((WORDS, WFF), LOW), v((WORDS, WFF), LOW),
            pltpu.SemaphoreType.DMA((15,)),
            pltpu.SemaphoreType.DMA((8,)),
            pltpu.SemaphoreType.DMA((4, 2)),
            pltpu.SemaphoreType.DMA((2,)),
        ],
        compiler_params=params(44),
        cost_estimate=pl.CostEstimate(flops=200 * 10**9, bytes_accessed=60 * 10**6, transcendentals=10**6),
        name="forward_and_words",
    )(*kept_outside(char_counts, char_ids, segment_ids, out_cotangent, *weights))


def call_a2(char_counts, kept, gain, project, weights):
    v = pltpu.VMEM
    return pl.pallas_call(
        kernel_a2,
        out_shape=(
            shape((CD, WORDS), LOW),
            outside((SHARES, T_ROWS, 256), LOW),
            outside((SHARES, T_ROWS, 256), LOW),
            shape((8, WD), F32),
        ),
        in_specs=[INSIDE] * 14 + [ANYWHERE] * 4,
        out_specs=(INSIDE, ANYWHERE, ANYWHERE, INSIDE),
        scratch_shapes=[
            v((WD, WD), LOW), v((WD, WD), LOW), v((WD, WD), LOW), v((WD, WD), LOW),
            v((2, SHARES, T_ROWS, 256), LOW),
            pltpu.SemaphoreType.DMA((4,)),
            pltpu.SemaphoreType.DMA((2,)),
        ],
        compiler_params=params(20),
        cost_estimate=pl.CostEstimate(flops=200 * 10**9, bytes_accessed=10 * 10**6, transcendentals=10**6),
        name="word_attention_backward",
    )(char_counts, *kept, gain, project, *kept_outside(*weights))


def call_b1(turns, gw, gain, up, down, kepts, keptm, kepti):
    v = pltpu.VMEM
    return pl.pallas_call(
        kernel_b1,
        out_shape=(outside((TURNS, CD, WIDE), LOW), shape((CD, CFF), LOW), shape((8, CD), F32)),
        in_specs=[SCALARS] + [INSIDE] * 4 + [ANYWHERE] * 3,
        out_specs=(ANYWHERE, INSIDE, INSIDE),
        scratch_shapes=[
            v((2, CFF, WIDE), LOW), v((2, CD, WIDE), F32), v((2, 8, WIDE), F32), v((2, CD, WIDE), LOW),
            v((CD, CFF), F32), v((CD, WIDE), F32), v((CFF, CD), LOW),
            pltpu.SemaphoreType.DMA((3, 2)),
            pltpu.SemaphoreType.DMA((2,)),
        ],
        compiler_params=params(16),
        cost_estimate=pl.CostEstimate(flops=200 * 10**9, bytes_accessed=20 * 10**6, transcendentals=10**6),
        name="character_backward_one",
    )(turns, gw, gain, up, down, *kept_outside(kepts, keptm, kepti))


def call_b2(turns, wgain1, wgain2, gain2, aup, weights, keptl, keptd, kepti):
    v = pltpu.VMEM
    return pl.pallas_call(
        kernel_b2,
        out_shape=(outside((SHARES, C_ROWS, 128), LOW), outside((SHARES, C_ROWS, 128), LOW)),
        in_specs=[SCALARS] + [INSIDE] * 9 + [ANYWHERE] * 3,
        out_specs=(ANYWHERE, ANYWHERE),
        scratch_shapes=[
            v((2, KEPT_LOW, WIDE), LOW), v((2, 8, WIDE), F32), v((2, CD, WIDE), LOW),
            v((CHAR_HEADS * SPAN, WIDE), LOW),
            v((CD, 3 * CD), LOW),
            v((CD, 3 * CD), F32), v((CD, CD), F32), v((CVOC, CD), F32), v((CD, WIDE), F32),
            v((2, SHARES, C_ROWS, 128), LOW),
            pltpu.SemaphoreType.DMA((3, 2)),
            pltpu.SemaphoreType.DMA((2,)),
        ],
        compiler_params=params(20),
        cost_estimate=pl.CostEstimate(flops=200 * 10**9, bytes_accessed=40 * 10**6, transcendentals=10**6),
        name="character_backward_two",
    )(turns, wgain1, wgain2, gain2, aup, *weights, *kept_outside(keptl, keptd, kepti))


def call_f(f, t, c, outk, outg):
    v = pltpu.VMEM
    outs = ((CVOC, CD), (CD,), (CD, CD), (CD, CD), (CD, CD), (CD, CD), (CD,), (CD, CFF), (CFF, CD), (CD, WD),
            (WD,), (WD, WD), (WD, WD), (WD, WD), (WD, WD), (WD,), (WD, WFF), (WFF, WD))
    outs = [(s[0] // SHARES,) + tuple(n // 2 for n in s[1:]) for s in outs]
    return pl.pallas_call(
        kernel_f,
        out_shape=(shape((2, 1, WORDS, WD // 2), LOW),) + tuple(shape(s, F32) for s in outs),
        in_specs=[ANYWHERE] * 20 + [INSIDE] * 2,
        out_specs=(INSIDE,) * 19,
        scratch_shapes=[
            v((6, F_ROWS, 256), LOW), v((6, T_ROWS, 256), LOW), v((8, C_ROWS, 128), LOW), pltpu.SemaphoreType.DMA((3,)),
        ],
        compiler_params=params(8),
        name="finish",
    )(*kept_outside(*f, *t, *c), outk, outg)


def flip(value, axis, bits):
    count = lax.axis_size(axis)
    return lax.ppermute(value, axis, [(i, i ^ bits) for i in range(count)])


def flip_both(value, first, second):
    pairs = [(i, i ^ first) for i in range(SHARES)] + [(SHARES + i, SHARES + (i ^ second)) for i in range(SHARES)]
    return lax.ppermute(value, ("phase", "dp"), pairs)


def pick(value, index):
    return lax.dynamic_index_in_dim(value, index, 0, keepdims=False)


def plus(*parts):
    total = parts[0].astype(F32)
    for part in parts[1:]:
        total = total + part.astype(F32)
    return total.astype(LOW)


class Sum:
    def __init__(self, keep):
        phase, dp = lax.axis_index("phase"), lax.axis_index("dp")
        x, y, low, high = (lax.rem(lax.div(dp, n), 2) for n in (1, 2, 4, 8))
        self.bits = [jnp.where(phase == 0, x, y), jnp.where(phase == 0, y, x), low, high]
        self.flips = [(1, 2), (2, 1), (4, 4), (8, 8)]
        self.parts = [keep]

    def send(self):
        step = len(self.parts) - 2
        half = SHARES >> (step + 1)
        total = None
        for part in self.parts:
            at, size = 0, part.shape[0]
            for bit, n in zip(self.bits[:step], (8, 4, 2, 1)):
                if n < size:
                    at = at + bit * n
            at = at + (1 - self.bits[step]) * half
            piece = lax.dynamic_slice_in_dim(part, at, half, 0).astype(F32)
            total = piece if total is None else total + piece
        return total.astype(LOW)

    def across(self, value):
        return flip_both(value, *self.flips[len(self.parts) - 2])


def together(*values):
    return lax.optimization_barrier(values)


def body(
    char_ids, char_counts, segment_ids, out_cotangent,
    char_table, char_gain_one, char_query, char_key, char_value, char_output, char_gain_two, char_up, char_down,
    char_project,
    word_gain_one, word_query, word_key, word_value, word_output, word_gain_two, word_up, word_down,
):
    keptl, kepts, keptm, kepti, turns, fkeep, fsend, outk, outs, wgain2, *words = call_a(
        char_counts, char_ids, segment_ids, out_cotangent,
        (char_table, char_gain_one, char_query, char_key, char_value, char_output, char_gain_two, char_up, char_down,
         char_project,
         word_gain_one, word_query, word_key, word_value, word_output, word_gain_two, word_up, word_down),
    )
    fgot = flip(fsend, "phase", 1)
    outg = flip(outs, "phase", 1)
    gw, tkeep, tsend, wgain1 = call_a2(
        char_counts, words, word_gain_one, char_project, (word_query, word_key, word_value, word_output)
    )
    one = (char_gain_two, char_up, char_down, kepts, keptm, kepti)
    two = (char_gain_one, char_query, char_key, char_value, char_output)
    if lax.axis_size("dp") != SHARES:
        keptd, aup, gain2 = call_b1(turns, gw, *one)
        ckeep, csend = call_b2(turns, wgain1, wgain2, gain2, aup, two, keptl, keptd, kepti)
        got = [flip(v, "phase", 1) for v in (tsend, csend)]
        return general_sums(outk, outg, (fkeep, fgot), (tkeep, got[0]), (ckeep, got[1]))
    f, t = Sum(fkeep), Sum(tkeep)
    gw, tsend, fgot, outg = together(gw, tsend, fgot, outg)
    f.parts.append(fgot)
    send = f.send()
    gw, send = together(gw, send)
    fgot, tgot = f.across(send), flip(tsend, "phase", 1)
    keptd, aup, gain2 = call_b1(turns, gw, *one)
    keptd, fgot, tgot = together(keptd, fgot, tgot)
    f.parts.append(fgot)
    t.parts.append(tgot)
    fsend, tsend = f.send(), t.send()
    keptd, fsend, tsend = together(keptd, fsend, tsend)
    fgot, tgot = f.across(fsend), t.across(tsend)
    ckeep, csend = call_b2(turns, wgain1, wgain2, gain2, aup, two, keptl, keptd, kepti)
    ckeep, csend, fgot, tgot = together(ckeep, csend, fgot, tgot)
    f.parts.append(fgot)
    t.parts.append(tgot)
    cphase, fgot, tgot = flip(csend, "phase", 1), f.across(f.send()), t.across(t.send())
    f.parts.append(fgot)
    t.parts.append(tgot)
    dp = lax.axis_index("dp")
    plane, line = lax.rem(dp, 4), lax.div(dp, 4)
    c = [ckeep.reshape(4, 4, C_ROWS, 128), cphase.reshape(4, 4, C_ROWS, 128)]
    sends = [plus(*(pick(part, lax.bitwise_xor(plane, k)) for part in c)) for k in range(1, 4)]
    cgot, fgot, tgot = (
        [flip(send, "dp", k) for k, send in enumerate(sends, 1)], f.across(f.send()), t.across(t.send())
    )
    f.parts.append(fgot)
    t.parts.append(tgot)
    c = [pick(part, plane) for part in c] + cgot
    sends = [plus(*(pick(part, lax.bitwise_xor(line, k)) for part in c)) for k in range(1, 4)]
    cline, tgot = [flip(send, "dp", 4 * k) for k, send in enumerate(sends, 1)], t.across(t.send())
    t.parts.append(tgot)
    return call_f(f.parts, t.parts, (ckeep, cphase, *cgot, *cline), outk, outg)


def general_sums(outk, outg, fs, ts, cs):
    phase = lax.axis_index("phase")
    first = phase == 0
    outs = jnp.stack([jnp.where(first, outk, outg), jnp.where(first, outg, outk)])[:, None]
    plain, swapped = (jnp.asarray([by_core(d, core) for d in range(SHARES)]) for core in range(2))

    def natural(pair, order):
        return jnp.take(pair[0].astype(F32) + pair[1].astype(F32), order, axis=0)

    order = jnp.where(first, plain, swapped)
    f, t, c = natural(fs, order), natural(ts, order), natural(cs, jnp.asarray([plane_first(d) for d in range(SHARES)]))

    def whole(rows):
        return rows.reshape(-1, rows.shape[-1])

    def wide(rows, pieces):
        n = rows.shape[1] // pieces
        return whole(rows.reshape(SHARES, pieces, n, rows.shape[-1]).transpose(0, 2, 1, 3).reshape(SHARES, n, -1))

    cdown = t[:, T_CDOWN:T_CDOWN + 32]
    cdown = jnp.concatenate([cdown[..., :128], cdown[..., 128:]], axis=1)
    parts = (
        whole(c[:, C_TABLE:C_TABLE + 16]), c[:, C_GAIN, :16].reshape(-1),
        whole(c[:, C_Q:C_Q + 16]), whole(c[:, C_K:C_K + 16]), whole(c[:, C_V:C_V + 16]), whole(c[:, C_O:C_O + 16]),
        c[:, C_GAIN + 1, :16].reshape(-1),
        wide(c[:, C_UP:C_UP + 64], 4), whole(cdown), whole(t[:, T_PROJ:T_PROJ + 16]),
        c[:, C_GAIN + 2, :32].reshape(-1),
        whole(t[:, T_Q:T_Q + 32]), whole(t[:, T_K:T_K + 32]), whole(t[:, T_V:T_V + 32]), whole(t[:, T_O:T_O + 32]),
        c[:, C_GAIN + 3, :32].reshape(-1),
        wide(f[:, F_UP:F_UP + 128], 4), whole(f[:, F_DOWN:F_DOWN + 128]),
    )
    return (outs,) + tuple(lax.psum_scatter(p, "dp", scatter_dimension=0, tiled=True) for p in parts)


def solution(mesh):
    rows = P(None, "dp", None)
    both = P("dp", "phase")
    one = P("dp")
    return jax.shard_map(
        body,
        mesh=mesh,
        in_specs=(rows, rows, rows, P(None, "dp", None, None)) + (P(),) * 18,
        out_specs=(
            P(None, "dp", None, "phase"),
            both, one, both, both, both, both, one, both, both, both,
            one, both, both, both, both, one, both, both,
        ),
        check_vma=False,
    )
```

time: 130 us -> 113 us (0.87)
  starting transfers between devices: 29.9 us -> 22 us
  waiting for transfers between devices: 17.6 us -> 11.3 us
  other arithmetic: 7.53 us -> 13.8 us
  Pallas kernels: 67.9 us -> 63.4 us
  local copies, waits for them, and re-layouts: 5.15 us -> 0.67 us
    ppermute x22 -> x10, starting transfers between devices: 29.9 us -> 8.67 us  [flip(): return lax.ppermute(value, axis, [(i, i ^ bits) for i in range(count)])]
    ppermute x22 -> x10, waiting for transfers between devices: 17.6 us -> 0.67 us  [flip(): return lax.ppermute(value, axis, [(i, i ^ bits) for i in range(count)])]
    convert_element_type x0 -> x8, other arithmetic: none -> 13.6 us  [send(): return total.astype(LOW)]
    ppermute x0 -> x8, starting transfers between devices: none -> 13.4 us  [flip_both(): return lax.ppermute(value, ('phase', 'dp'), pairs)]
    ppermute x0 -> x8, waiting for transfers between devices: none -> 10.6 us  [flip_both(): return lax.ppermute(value, ('phase', 'dp'), pairs)]
    convert_element_type x6 -> x2, other arithmetic: 7.53 us -> 0.24 us  [plus(): return total.astype(LOW)]
    pallas_call x3 -> x4, Pallas kernels: 64.7 us -> 60.1 us  [the longest x1 27.3 us: call_a(): pl.pallas_call(kernel_a, out_shape=(outside((TURNS, KEPT_LOW, WIDE), LOW)...]
    squeeze x6 -> x0, local copies, waits for them, and re-layouts: 2.39 us -> none  [pick(): return lax.dynamic_index_in_dim(value, index, 0, keepdims=False)]
  transfers between devices with their start and end apart: 22 -> 18, of which waited for: 7 -> 6; matrix products, arithmetic and copies ran while one was open for 8% -> 6% of each run, Pallas kernels for 23% -> 29%
where the time goes in v3:
time: 113 us; the launch traced here: 112 us
  Pallas kernels  63.4 us (56%)
  starting transfers between devices  22 us (19%)
  other arithmetic  13.8 us (12%)
  waiting for transfers between devices  11.3 us (10%)
  between operations  1.17 us (1%)
    pallas_call x1, Pallas kernels, call_a(): pl.pallas_call(kernel_a, out_shape=(outside((TURNS, KEPT_LOW, WIDE), LOW)...  27.3 us
    pallas_call x1, Pallas kernels, call_b2(): pl.pallas_call(kernel_b2, out_shape=(outside((SHARES, C_ROWS, 128), LOW),...  14.6 us
    convert_element_type x8, other arithmetic, send(): return total.astype(LOW)  13.6 us
    ppermute x8, starting transfers between devices, flip_both(): return lax.ppermute(value, ('phase', 'dp'), pairs)  13.4 us
    pallas_call x1, Pallas kernels, call_b1(): pl.pallas_call(kernel_b1, out_shape=(outside((TURNS, CD, WIDE), LOW), sha...  11.5 us
    ppermute x8, waiting for transfers between devices, flip_both(): return lax.ppermute(value, ('phase', 'dp'), pairs)  10.6 us
    ppermute x10, starting transfers between devices, flip(): return lax.ppermute(value, axis, [(i, i ^ bits) for i in range(count)])  8.67 us
    pallas_call x1, Pallas kernels, call_a2(): pl.pallas_call(kernel_a2, out_shape=(shape((CD, WORDS), LOW), outside((SH...  6.75 us
  transfers between devices with their start and end apart: 18, of which 6 were waited for; matrix products, arithmetic and copies ran while one was open for 6% of the time, Pallas kernels for 29%

profile of v3, /device:TPU:0, one launch (start us, length us, event | category | flops | bytes accessed | tf_op | source)
XLA Modules:
  0.0 112.3 jit_solution(16850314016909222639)
XLA Ops:
  0.7 27.3 %forward_and_words.1 = (bf16[9,2304,512]{2,1,0:T(8,128)(2,1)}, bf16[9,1024,512]{2,1,0:T(8,128)(2,1)}, f32[9,256,512]{2,1,0:T(8,128)}, f32[9,8,512]{2,1,0:T(8,128...) custom-call(s32[2,1,256]{2,1,0:T(1,128)} %counts_ref.1, ...), custom_call_target="tpu_custom_call" | custom-call | flops 199999995904 | bytes 60000000 | tf_op jit(solution)/shard_map/forward_and_words/pallas_call | solution.py:795
  28.0 0.5 collective-permute-start
  28.6 6.8 %word_attention_backward.1 = (bf16[256,256]{1,0:T(8,128)(2,1)S(1)}, bf16[16,176,256]{2,1,0:T(8,128)(2,1)}, bf16[16,176,256]{2,1,0:T(8,128)(2,1)}, f32[8,512]{1,0:T(8,128)S(1)}) custom-call(s32[2,1,256]{2,1,0:T(1,128)S(1)} %copy-done.7, bf16[256,512]{1,0:T(8,128)(2,1)S(1)} %get-tuple-element.66.q_ref, bf16[256,512]{1,0:T(8,128)(2,1)S(1)} %get-tuple-element.67.k_ref, ...), custom_call_target="tpu_custom_call" | custom-call | flops 199999995904 | bytes 10000000 | tf_op jit(solution)/shard_map/word_attention_backward/pallas_call | solution.py:843
  35.5 2.6 %add_convert_fusion = bf16[8,256,256]{2,1,0:T(8,128)(2,1)} fusion(bf16[16,256,256]{2,1,0:T(8,128)(2,1)} %collective-permute-done.f1, s32[]{:T(128)S(6)} %select_n.105, bf16[16,256,256]{2,1,0:T(8,128)(2,1)S(1)} %copy-done.11), kind=kLoop, calls=%fused_computation | loop fusion | flops 2097152 | bytes 3145732 | tf_op jit(solution)/shard_map/convert_element_type | solution.py:965
  38.0 2.9 %collective-permute-start.2 = (bf16[8,256,256]{2,1,0:T(8,128)(2,1)}, bf16[8,256,256]{2,1,0:T(8,128)(2,1)}, u32[]{:S(2)}, u32[]{:S(2)}) collective-permute-start(bf16[8,256,256]{2,1,0:T(8,128)(2,1)} %add_convert_fusion), channel_id=1, source_target_pairs={{0,1},{1,0},{2,3},{3,2},{4,5},{5,4},{6,7},{7,6},{8,9},{9,8},{10,11... | collective-permute-start | bytes 3145736 | tf_op jit(solution)/shard_map/ppermute | solution.py:931
  41.0 11.5 %character_backward_one.1 = (bf16[9,256,512]{2,1,0:T(8,128)(2,1)}, bf16[256,1024]{1,0:T(8,128)(2,1)S(1)}, f32[8,256]{1,0:T(8,128)S(1)}) custom-call(s32[1]{0:T(128)} %get-tuple-element.82.turns_ref, bf16[256,256]{1,0:T(8,128)(2,1)S(1)} %get-tuple-element.84.gw_ref, bf16[256]{0:T(256)(128)(2,1)S(1)} %copy-done.9, bf16[256,1024]{1,0:T(8,128)(2,1)S(1)} %copy-done, ...), custom_call_target="tpu_custom_call" | custom-call | flops 199999995904 | bytes 20000000 | tf_op jit(solution)/shard_map/character_backward_one/pallas_call | solution.py:867
  52.4 1.6 %collective-permute-done.2.f2 = bf16[8,256,256]{2,1,0:T(8,128)(2,1)} collective-permute-done((bf16[8,256,256]{2,1,0:T(8,128)(2,1)}, bf16[8,256,256]{2,1,0:T(8,128)(2,1)}, u32[]{:S(2)}, u32[]{:S(2)}) %collective-permute-start.2) | collective-permute-done | bytes 1048608 | tf_op jit(solution)/shard_map/ppermute | solution.py:931
  54.1 2.2 %add_convert_fusion.1 = bf16[8,176,256]{2,1,0:T(8,128)(2,1)} fusion(bf16[16,176,256]{2,1,0:T(8,128)(2,1)} %collective-permute-done.3.t1, s32[]{:T(128)S(6)} %select_n.105, bf16[16,176,256]{2,1,0:T(8,128)(2,1)S(1)} %copy-done.12), kind=kLoop, calls=%fused_computation.1 | loop fusion | flops 1441792 | bytes 2162692 | tf_op jit(solution)/shard_map/convert_element_type | solution.py:965
  56.3 2.3 %add_convert_fusion.2 = bf16[4,256,256]{2,1,0:T(8,128)(2,1)} fusion(bf16[8,256,256]{2,1,0:T(8,128)(2,1)} %collective-permute-done.2.f2, s32[]{:T(128)S(6)} %select_n.108, bf16[16,256,256]{2,1,0:T(8,128)(2,1)} %collective-permute-done.f1, s32[]{:T(128)S(6)} %select_n.107, bf16[16,256,256]{2,1,0:T(8,128)(2,1)} %get-tuple-element.65.f0), kind=kLoop, calls=%fused_computation.2 | loop fusion | flops 1572864 | bytes 2097160 | tf_op jit(solution)/shard_map/convert_element_type | solution.py:965
  58.7 2.0 %collective-permute-start.5 = (bf16[8,176,256]{2,1,0:T(8,128)(2,1)}, bf16[8,176,256]{2,1,0:T(8,128)(2,1)}, u32[]{:S(2)}, u32[]{:S(2)}) collective-permute-start(bf16[8,176,256]{2,1,0:T(8,128)(2,1)} %add_convert_fusion.1), channel_id=1, source_target_pairs={{0,1},{1,0},{2,3},{3,2},{4,5},{5,4},{6,7},{7,6},{8,9},{9,8},{10,11... | collective-permute-start | bytes 2162696 | tf_op jit(solution)/shard_map/ppermute | solution.py:931
  60.7 1.5 %collective-permute-start.4 = (bf16[4,256,256]{2,1,0:T(8,128)(2,1)}, bf16[4,256,256]{2,1,0:T(8,128)(2,1)}, u32[]{:S(2)}, u32[]{:S(2)}) collective-permute-start(bf16[4,256,256]{2,1,0:T(8,128)(2,1)} %add_convert_fusion.2), channel_id=1, source_target_pairs={{0,2},{1,3},{2,0},{3,1},{4,6},{5,7},{6,4},{7,5},{8,10},{9,11},{10,... | collective-permute-start | bytes 1572872 | tf_op jit(solution)/shard_map/ppermute | solution.py:931
  62.2 14.6 %character_backward_two.1 = (bf16[16,160,128]{2,1,0:T(8,128)(2,1)}, bf16[16,160,128]{2,1,0:T(8,128)(2,1)}) custom-call(s32[1]{0:T(128)} %get-tuple-element.82.turns_ref, f32[8,512]{1,0:T(8,128)S(1)} %get-tuple-element.92.wgain1_ref, f32[8,512]{1,0:T(8,128)S(1)} %get-tuple-element.93.wgain2_ref, f32[8,256]{1,0:T(8,128)S(1)} %get-tuple-element.94.gain2_ref, ...), custom_call_target="tpu_custom_call" | custom-call | flops 199999995904 | bytes 40000000 | tf_op jit(solution)/shard_map/character_backward_two/pallas_call | solution.py:886
  77.0 1.4 %add_convert_fusion.3 = bf16[4,176,256]{2,1,0:T(8,128)(2,1)S(1)} fusion(bf16[8,176,256]{2,1,0:T(8,128)(2,1)} %collective-permute-done.5.t2, s32[]{:T(128)S(6)} %select_n.108, bf16[16,176,256]{2,1,0:T(8,128)(2,1)} %collective-permute-done.3.t1, s32[]{:T(128)S(6)} %select_n.107, bf16[16,176,256]{2,1,0:T(8,128)(2,1)} %get-tuple-element.98.t0), kind=kLoop, calls=%fused_computation.3 | loop fusion | flops 1081344 | bytes 1441800 | tf_op jit(solution)/shard_map/convert_element_type | solution.py:965
  78.4 0.6 collective-permute-start.8
  79.0 1.3 %add_convert_fusion.4 = bf16[2,256,256]{2,1,0:T(8,128)(2,1)S(1)} fusion(bf16[4,256,256]{2,1,0:T(8,128)(2,1)} %collective-permute-done.4.f3, s32[]{:T(128)S(6)} %select_n.111, bf16[8,256,256]{2,1,0:T(8,128)(2,1)} %collective-permute-done.2.f2, s32[]{:T(128)S(6)} %select_n.110, bf16[16,256,256]{2,1,0:T(8,128)(2,1)} %collective-permute-done.f1, ...), kind=kLoop, calls=%fused_computation.4 | loop fusion | flops 1048576 | bytes 1310732 | tf_op jit(solution)/shard_map/convert_element_type | solution.py:965
  80.3 1.6 %collective-permute-start.6 = (bf16[2,256,256]{2,1,0:T(8,128)(2,1)S(1)}, bf16[2,256,256]{2,1,0:T(8,128)(2,1)S(1)}, u32[]{:S(2)}, u32[]{:S(2)}) collective-permute-start(bf16[2,256,256]{2,1,0:T(8,128)(2,1)S(1)} %add_convert_fusion.4), channel_id=1, source_target_pairs={{0,4},{1,5},{2,6},{3,7},{4,0},{5,1},{6,2},{7,3},{8,12},{9,13},{10,... | collective-permute-start | bytes 786440 | tf_op jit(solution)/shard_map/ppermute | solution.py:931
  81.9 4.0 %collective-permute-done.8.t3 = bf16[4,176,256]{2,1,0:T(8,128)(2,1)S(1)} collective-permute-done((bf16[4,176,256]{2,1,0:T(8,128)(2,1)S(1)}, bf16[4,176,256]{2,1,0:T(8,128)(2,1)S(1)}, u32[]{:S(2)}, u32[]{:S(2)}) %collective-permute-start.8) | collective-permute-done | bytes 360480 | tf_op jit(solution)/shard_map/ppermute | solution.py:931
  85.9 1.3 %add_convert_fusion.5 = bf16[2,176,256]{2,1,0:T(8,128)(2,1)S(1)} fusion(bf16[4,176,256]{2,1,0:T(8,128)(2,1)S(1)} %collective-permute-done.8.t3, s32[]{:T(128)S(6)} %select_n.111, bf16[8,176,256]{2,1,0:T(8,128)(2,1)} %collective-permute-done.5.t2, s32[]{:T(128)S(6)} %select_n.110, bf16[16,176,256]{2,1,0:T(8,128)(2,1)} %collective-permute-done.3.t1, ...), kind=kLoop, calls=%fused_computation.5 | loop fusion | flops 720896 | bytes 901132 | tf_op jit(solution)/shard_map/convert_element_type | solution.py:965
  87.2 1.6 %collective-permute-start.9 = (bf16[2,176,256]{2,1,0:T(8,128)(2,1)S(1)}, bf16[2,176,256]{2,1,0:T(8,128)(2,1)S(1)}, u32[]{:S(2)}, u32[]{:S(2)}) collective-permute-start(bf16[2,176,256]{2,1,0:T(8,128)(2,1)S(1)} %add_convert_fusion.5), channel_id=1, source_target_pairs={{0,4},{1,5},{2,6},{3,7},{4,0},{5,1},{6,2},{7,3},{8,12},{9,13},{10,... | collective-permute-start | bytes 540680 | tf_op jit(solution)/shard_map/ppermute | solution.py:931
  89.0 0.6 collective-permute-start.12
  89.6 0.5 collective-permute-start.13
  90.1 2.4 %collective-permute-start.14 = (bf16[4,160,128]{2,1,0:T(8,128)(2,1)S(1)}, bf16[4,160,128]{2,1,0:T(8,128)(2,1)S(1)}, u32[]{:S(2)}, u32[]{:S(2)}) collective-permute-start(bf16[4,160,128]{2,1,0:T(8,128)(2,1)S(1)} %get-tuple-element.114), channel_id=1, source_target_pairs={{0,3},{1,2},{2,1},{3,0},{4,7},{5,6},{6,5},{7,4},{8,11},{9,10},{10,... | collective-permute-start | bytes 491528 | tf_op jit(solution)/shard_map/ppermute | solution.py:926
  92.6 1.3 %add_convert_fusion.9 = bf16[1,256,256]{2,1,0:T(8,128)(2,1)S(1)} fusion(bf16[2,256,256]{2,1,0:T(8,128)(2,1)S(1)} %collective-permute-done.6.f4, s32[]{:T(128)S(6)} %select_n.115, bf16[4,256,256]{2,1,0:T(8,128)(2,1)} %collective-permute-done.4.f3, s32[]{:T(128)S(6)} %select_n.114, bf16[8,256,256]{2,1,0:T(8,128)(2,1)} %collective-permute-done.2.f2, ...), kind=kLoop, calls=%fused_computation.9 | loop fusion | flops 655360 | bytes 786448 | tf_op jit(solution)/shard_map/convert_element_type | solution.py:965
  93.8 2.7 %collective-permute-start.7 = (bf16[1,256,256]{2,1,0:T(8,128)(2,1)S(1)}, bf16[1,256,256]{2,1,0:T(8,128)(2,1)S(1)}, u32[]{:S(2)}, u32[]{:S(2)}) collective-permute-start(bf16[1,256,256]{2,1,0:T(8,128)(2,1)S(1)} %add_convert_fusion.9), channel_id=1, source_target_pairs={{0,8},{1,9},{2,10},{3,11},{4,12},{5,13},{6,14},{7,15},{8,0},{9,1},... | collective-permute-start | bytes 393224 | tf_op jit(solution)/shard_map/ppermute | solution.py:931
  96.5 1.1 add_convert_fusion.10
  98.3 0.5 collective-permute-start.15
  98.9 2.6 %collective-permute-start.16 = (bf16[160,128]{1,0:T(8,128)(2,1)S(1)}, bf16[160,128]{1,0:T(8,128)(2,1)S(1)}, u32[]{:S(2)}, u32[]{:S(2)}) collective-permute-start(bf16[160,128]{1,0:T(8,128)(2,1)S(1)} %get-tuple-element.112), channel_id=1, source_target_pairs={{0,8},{1,9},{2,10},{3,11},{4,12},{5,13},{6,14},{7,15},{8,0},{9,1},... | collective-permute-start | bytes 122888 | tf_op jit(solution)/shard_map/ppermute | solution.py:926
  101.5 1.3 %collective-permute-start.17 = (bf16[160,128]{1,0:T(8,128)(2,1)S(1)}, bf16[160,128]{1,0:T(8,128)(2,1)S(1)}, u32[]{:S(2)}, u32[]{:S(2)}) collective-permute-start(bf16[160,128]{1,0:T(8,128)(2,1)S(1)} %get-tuple-element.111), channel_id=1, source_target_pairs={{0,12},{1,13},{2,14},{3,15},{4,8},{5,9},{6,10},{7,11},{8,4},{9,5},... | collective-permute-start | bytes 122888 | tf_op jit(solution)/shard_map/ppermute | solution.py:926
  102.8 3.1 %collective-permute-done.7.f5 = bf16[1,256,256]{2,1,0:T(8,128)(2,1)S(1)} collective-permute-done((bf16[1,256,256]{2,1,0:T(8,128)(2,1)S(1)}, bf16[1,256,256]{2,1,0:T(8,128)(2,1)S(1)}, u32[]{:S(2)}, u32[]{:S(2)}) %collective-permute-start.7) | collective-permute-done | bytes 131104 | tf_op jit(solution)/shard_map/ppermute | solution.py:931
  105.9 2.0 %collective-permute-done.10.t5 = bf16[1,176,256]{2,1,0:T(8,128)(2,1)S(1)} collective-permute-done((bf16[1,176,256]{2,1,0:T(8,128)(2,1)S(1)}, bf16[1,176,256]{2,1,0:T(8,128)(2,1)S(1)}, u32[]{:S(2)}, u32[]{:S(2)}) %collective-permute-start.10) | collective-permute-done | bytes 90144 | tf_op jit(solution)/shard_map/ppermute | solution.py:931
  107.8 0.4 collective-permute-done.16.c6
  108.9 3.2 %finish.1 = (bf16[2,1,256,256]{3,2,1,0:T(8,128)(2,1)}, f32[16,128]{1,0:T(8,128)}, f32[16]{0:T(128)}, f32[16,128]{1,0:T(8,128)}, f32[16,128]{1,0:T(8,128)}, /*ind...) custom-call(bf16[16,256,256]{2,1,0:T(8,128)(2,1)} %get-tuple-element, ...), custom_call_target="tpu_custom_call" | custom-call | tf_op jit(solution)/shard_map/finish/pallas_call | solution.py:911
  (71 shorter events, 1.7 us)
Async XLA Ops:
  0.7 27.9 %copy-start.2 = (bf16[256,512]{1,0:T(8,128)(2,1)S(1)}, bf16[256,512]{1,0:T(8,128)(2,1)}, u32[]{:S(2)}) copy-start(bf16[256,512]{1,0:T(8,128)(2,1)} %proj_ref.1) | copy-start | bytes 786436
  0.7 27.9 %copy-start.7 = (s32[2,1,256]{2,1,0:T(1,128)S(1)}, s32[2,1,256]{2,1,0:T(1,128)}, u32[]{:S(2)}) copy-start(s32[2,1,256]{2,1,0:T(1,128)} %counts_ref.1) | copy-start | bytes 6148
  0.7 27.9 %copy-start.8 = (bf16[512]{0:T(512)(128)(2,1)S(1)}, bf16[512]{0:T(512)(128)(2,1)}, u32[]{:S(2)}) copy-start(bf16[512]{0:T(512)(128)(2,1)} %wg1_ref.1) | copy-start | bytes 3076
  28.0 7.5 %collective-permute-start = (bf16[16,256,256]{2,1,0:T(8,128)(2,1)}, bf16[16,256,256]{2,1,0:T(8,128)(2,1)}, u32[]{:S(2)}, u32[]{:S(2)}) collective-permute-start(bf16[16,256,256]{2,1,0:T(8,128)(2,1)} %get-tuple-element.79), channel_id=1, source_target_pairs={{0,16},{16,0},{1,17},{17,1},{2,18},{18,2},{3,19},{19,3},{4,20},{20... | collective-permute-start | bytes 6291464 | tf_op jit(solution)/shard_map/ppermute | solution.py:926
  28.5 6.9 %collective-permute-start.1 = (bf16[256,256]{1,0:T(8,128)(2,1)}, bf16[256,256]{1,0:T(8,128)(2,1)}, u32[]{:S(2)}, u32[]{:S(2)}) collective-permute-start(bf16[256,256]{1,0:T(8,128)(2,1)} %get-tuple-element.80), channel_id=1, source_target_pairs={{0,16},{16,0},{1,17},{17,1},{2,18},{18,2},{3,19},{19,3},{4,20},{20... | collective-permute-start | bytes 393224 | tf_op jit(solution)/shard_map/ppermute | solution.py:926
  38.0 16.0 %collective-permute-start.2 = (bf16[8,256,256]{2,1,0:T(8,128)(2,1)}, bf16[8,256,256]{2,1,0:T(8,128)(2,1)}, u32[]{:S(2)}, u32[]{:S(2)}) collective-permute-start(bf16[8,256,256]{2,1,0:T(8,128)(2,1)} %add_convert_fusion), channel_id=1, source_target_pairs={{0,1},{1,0},{2,3},{3,2},{4,5},{5,4},{6,7},{7,6},{8,9},{9,8},{10,11... | collective-permute-start | bytes 3145736 | tf_op jit(solution)/shard_map/ppermute | solution.py:931
  40.9 13.1 %collective-permute-start.3 = (bf16[16,176,256]{2,1,0:T(8,128)(2,1)}, bf16[16,176,256]{2,1,0:T(8,128)(2,1)}, u32[]{:S(2)}, u32[]{:S(2)}) collective-permute-start(bf16[16,176,256]{2,1,0:T(8,128)(2,1)} %get-tuple-element.90), channel_id=1, source_target_pairs={{0,16},{16,0},{1,17},{17,1},{2,18},{18,2},{3,19},{19,3},{4,20},{20... | collective-permute-start | bytes 4325384 | tf_op jit(solution)/shard_map/ppermute | solution.py:926
  41.0 13.1 %copy-start.12 = (bf16[16,176,256]{2,1,0:T(8,128)(2,1)S(1)}, bf16[16,176,256]{2,1,0:T(8,128)(2,1)}, u32[]{:S(2)}) copy-start(bf16[16,176,256]{2,1,0:T(8,128)(2,1)} %get-tuple-element.98.t0) | copy-start | bytes 4325380
  54.0 8.2 %copy-start.3 = (bf16[256,256]{1,0:T(8,128)(2,1)S(1)}, bf16[256,256]{1,0:T(8,128)(2,1)}, u32[]{:S(2)}) copy-start(bf16[256,256]{1,0:T(8,128)(2,1)} %wq_ref.1) | copy-start | bytes 393220
  54.0 8.2 %copy-start.4 = (bf16[256,256]{1,0:T(8,128)(2,1)S(1)}, bf16[256,256]{1,0:T(8,128)(2,1)}, u32[]{:S(2)}) copy-start(bf16[256,256]{1,0:T(8,128)(2,1)} %wk_ref.1) | copy-start | bytes 393220
  58.7 18.2 %collective-permute-start.5 = (bf16[8,176,256]{2,1,0:T(8,128)(2,1)}, bf16[8,176,256]{2,1,0:T(8,128)(2,1)}, u32[]{:S(2)}, u32[]{:S(2)}) collective-permute-start(bf16[8,176,256]{2,1,0:T(8,128)(2,1)} %add_convert_fusion.1), channel_id=1, source_target_pairs={{0,1},{1,0},{2,3},{3,2},{4,5},{5,4},{6,7},{7,6},{8,9},{9,8},{10,11... | collective-permute-start | bytes 2162696 | tf_op jit(solution)/shard_map/ppermute | solution.py:931
  60.7 16.2 %collective-permute-start.4 = (bf16[4,256,256]{2,1,0:T(8,128)(2,1)}, bf16[4,256,256]{2,1,0:T(8,128)(2,1)}, u32[]{:S(2)}, u32[]{:S(2)}) collective-permute-start(bf16[4,256,256]{2,1,0:T(8,128)(2,1)} %add_convert_fusion.2), channel_id=1, source_target_pairs={{0,2},{1,3},{2,0},{3,1},{4,6},{5,7},{6,4},{7,5},{8,10},{9,11},{10,... | collective-permute-start | bytes 1572872 | tf_op jit(solution)/shard_map/ppermute | solution.py:931
  76.9 12.0 %copy-start.13 = (bf16[16,160,128]{2,1,0:T(8,128)(2,1)S(1)}, bf16[16,160,128]{2,1,0:T(8,128)(2,1)}, u32[]{:S(2)}) copy-start(bf16[16,160,128]{2,1,0:T(8,128)(2,1)} %get-tuple-element.107.c0) | copy-start | bytes 1966084
  76.9 11.9 %collective-permute-start.11 = (bf16[16,160,128]{2,1,0:T(8,128)(2,1)}, bf16[16,160,128]{2,1,0:T(8,128)(2,1)S(1)}, u32[]{:S(2)}, u32[]{:S(2)}) collective-permute-start(bf16[16,160,128]{2,1,0:T(8,128)(2,1)} %get-tuple-element.108), channel_id=1, source_target_pairs={{0,16},{16,0},{1,17},{17,1},{2,18},{18,2},{3,19},{19,3},{4,20},{20... | collective-permute-start | bytes 1966088 | tf_op jit(solution)/shard_map/ppermute | solution.py:926
  78.4 7.5 %collective-permute-start.8 = (bf16[4,176,256]{2,1,0:T(8,128)(2,1)S(1)}, bf16[4,176,256]{2,1,0:T(8,128)(2,1)S(1)}, u32[]{:S(2)}, u32[]{:S(2)}) collective-permute-start(bf16[4,176,256]{2,1,0:T(8,128)(2,1)S(1)} %add_convert_fusion.3), channel_id=1, source_target_pairs={{0,2},{1,3},{2,0},{3,1},{4,6},{5,7},{6,4},{7,5},{8,10},{9,11},{10,... | collective-permute-start | bytes 1081352 | tf_op jit(solution)/shard_map/ppermute | solution.py:931
  80.3 12.3 %collective-permute-start.6 = (bf16[2,256,256]{2,1,0:T(8,128)(2,1)S(1)}, bf16[2,256,256]{2,1,0:T(8,128)(2,1)S(1)}, u32[]{:S(2)}, u32[]{:S(2)}) collective-permute-start(bf16[2,256,256]{2,1,0:T(8,128)(2,1)S(1)} %add_convert_fusion.4), channel_id=1, source_target_pairs={{0,4},{1,5},{2,6},{3,7},{4,0},{5,1},{6,2},{7,3},{8,12},{9,13},{10,... | collective-permute-start | bytes 786440 | tf_op jit(solution)/shard_map/ppermute | solution.py:931
  85.9 12.5 %copy-start.15 = (bf16[4,176,256]{2,1,0:T(8,128)(2,1)}, bf16[4,176,256]{2,1,0:T(8,128)(2,1)S(1)}, u32[]{:S(2)}) copy-start(bf16[4,176,256]{2,1,0:T(8,128)(2,1)S(1)} %collective-permute-done.8.t3) | copy-start | bytes 1081348
  87.2 9.3 %collective-permute-start.9 = (bf16[2,176,256]{2,1,0:T(8,128)(2,1)S(1)}, bf16[2,176,256]{2,1,0:T(8,128)(2,1)S(1)}, u32[]{:S(2)}, u32[]{:S(2)}) collective-permute-start(bf16[2,176,256]{2,1,0:T(8,128)(2,1)S(1)} %add_convert_fusion.5), channel_id=1, source_target_pairs={{0,4},{1,5},{2,6},{3,7},{4,0},{5,1},{6,2},{7,3},{8,12},{9,13},{10,... | collective-permute-start | bytes 540680 | tf_op jit(solution)/shard_map/ppermute | solution.py:931
  88.8 19.4 %copy-start.14 = (bf16[16,160,128]{2,1,0:T(8,128)(2,1)}, bf16[16,160,128]{2,1,0:T(8,128)(2,1)S(1)}, u32[]{:S(2)}) copy-start(bf16[16,160,128]{2,1,0:T(8,128)(2,1)S(1)} %collective-permute-done.11.c1) | copy-start | bytes 1966084
  89.0 9.0 %collective-permute-start.12 = (bf16[4,160,128]{2,1,0:T(8,128)(2,1)S(1)}, bf16[4,160,128]{2,1,0:T(8,128)(2,1)S(1)}, u32[]{:S(2)}, u32[]{:S(2)}) collective-permute-start(bf16[4,160,128]{2,1,0:T(8,128)(2,1)S(1)} %get-tuple-element.116), channel_id=1, source_target_pairs={{0,1},{1,0},{2,3},{3,2},{4,5},{5,4},{6,7},{7,6},{8,9},{9,8},{10,11... | collective-permute-start | bytes 491528 | tf_op jit(solution)/shard_map/ppermute | solution.py:926
  89.6 8.6 %collective-permute-start.13 = (bf16[4,160,128]{2,1,0:T(8,128)(2,1)S(1)}, bf16[4,160,128]{2,1,0:T(8,128)(2,1)S(1)}, u32[]{:S(2)}, u32[]{:S(2)}) collective-permute-start(bf16[4,160,128]{2,1,0:T(8,128)(2,1)S(1)} %get-tuple-element.115), channel_id=1, source_target_pairs={{0,2},{1,3},{2,0},{3,1},{4,6},{5,7},{6,4},{7,5},{8,10},{9,11},{10,... | collective-permute-start | bytes 491528 | tf_op jit(solution)/shard_map/ppermute | solution.py:926
  90.1 8.1 %collective-permute-start.14 = (bf16[4,160,128]{2,1,0:T(8,128)(2,1)S(1)}, bf16[4,160,128]{2,1,0:T(8,128)(2,1)S(1)}, u32[]{:S(2)}, u32[]{:S(2)}) collective-permute-start(bf16[4,160,128]{2,1,0:T(8,128)(2,1)S(1)} %get-tuple-element.114), channel_id=1, source_target_pairs={{0,3},{1,2},{2,1},{3,0},{4,7},{5,6},{6,5},{7,4},{8,11},{9,10},{10,... | collective-permute-start | bytes 491528 | tf_op jit(solution)/shard_map/ppermute | solution.py:926
  92.6 15.7 %copy-start.16 = (bf16[2,256,256]{2,1,0:T(8,128)(2,1)}, bf16[2,256,256]{2,1,0:T(8,128)(2,1)S(1)}, u32[]{:S(2)}) copy-start(bf16[2,256,256]{2,1,0:T(8,128)(2,1)S(1)} %collective-permute-done.6.f4) | copy-start | bytes 786436
  93.8 12.0 %collective-permute-start.7 = (bf16[1,256,256]{2,1,0:T(8,128)(2,1)S(1)}, bf16[1,256,256]{2,1,0:T(8,128)(2,1)S(1)}, u32[]{:S(2)}, u32[]{:S(2)}) collective-permute-start(bf16[1,256,256]{2,1,0:T(8,128)(2,1)S(1)} %add_convert_fusion.9), channel_id=1, source_target_pairs={{0,8},{1,9},{2,10},{3,11},{4,12},{5,13},{6,14},{7,15},{8,0},{9,1},... | collective-permute-start | bytes 393224 | tf_op jit(solution)/shard_map/ppermute | solution.py:931
  96.5 11.8 %copy-start.20 = (bf16[2,176,256]{2,1,0:T(8,128)(2,1)}, bf16[2,176,256]{2,1,0:T(8,128)(2,1)S(1)}, u32[]{:S(2)}) copy-start(bf16[2,176,256]{2,1,0:T(8,128)(2,1)S(1)} %collective-permute-done.9.t4) | copy-start | bytes 540676
  97.6 10.2 %collective-permute-start.10 = (bf16[1,176,256]{2,1,0:T(8,128)(2,1)S(1)}, bf16[1,176,256]{2,1,0:T(8,128)(2,1)S(1)}, u32[]{:S(2)}, u32[]{:S(2)}) collective-permute-start(bf16[1,176,256]{2,1,0:T(8,128)(2,1)S(1)} %add_convert_fusion.10), channel_id=1, source_target_pairs={{0,8},{1,9},{2,10},{3,11},{4,12},{5,13},{6,14},{7,15},{8,0},{9,1},... | collective-permute-start | bytes 270344 | tf_op jit(solution)/shard_map/ppermute | solution.py:931
  98.0 10.3 %copy-start.17 = (bf16[4,160,128]{2,1,0:T(8,128)(2,1)}, bf16[4,160,128]{2,1,0:T(8,128)(2,1)S(1)}, u32[]{:S(2)}) copy-start(bf16[4,160,128]{2,1,0:T(8,128)(2,1)S(1)} %collective-permute-done.12.c2) | copy-start | bytes 491524
  98.2 10.1 %copy-start.18 = (bf16[4,160,128]{2,1,0:T(8,128)(2,1)}, bf16[4,160,128]{2,1,0:T(8,128)(2,1)S(1)}, u32[]{:S(2)}) copy-start(bf16[4,160,128]{2,1,0:T(8,128)(2,1)S(1)} %collective-permute-done.13.c3) | copy-start | bytes 491524
  98.2 10.1 %copy-start.19 = (bf16[4,160,128]{2,1,0:T(8,128)(2,1)}, bf16[4,160,128]{2,1,0:T(8,128)(2,1)S(1)}, u32[]{:S(2)}) copy-start(bf16[4,160,128]{2,1,0:T(8,128)(2,1)S(1)} %collective-permute-done.14.c4) | copy-start | bytes 491524
  98.3 9.5 %collective-permute-start.15 = (bf16[160,128]{1,0:T(8,128)(2,1)S(1)}, bf16[160,128]{1,0:T(8,128)(2,1)S(1)}, u32[]{:S(2)}, u32[]{:S(2)}) collective-permute-start(bf16[160,128]{1,0:T(8,128)(2,1)S(1)} %get-tuple-element.113), channel_id=1, source_target_pairs={{0,4},{1,5},{2,6},{3,7},{4,0},{5,1},{6,2},{7,3},{8,12},{9,13},{10,... | collective-permute-start | bytes 122888 | tf_op jit(solution)/shard_map/ppermute | solution.py:926
  98.9 9.4 %collective-permute-start.16 = (bf16[160,128]{1,0:T(8,128)(2,1)S(1)}, bf16[160,128]{1,0:T(8,128)(2,1)S(1)}, u32[]{:S(2)}, u32[]{:S(2)}) collective-permute-start(bf16[160,128]{1,0:T(8,128)(2,1)S(1)} %get-tuple-element.112), channel_id=1, source_target_pairs={{0,8},{1,9},{2,10},{3,11},{4,12},{5,13},{6,14},{7,15},{8,0},{9,1},... | collective-permute-start | bytes 122888 | tf_op jit(solution)/shard_map/ppermute | solution.py:926
  101.5 6.8 %collective-permute-start.17 = (bf16[160,128]{1,0:T(8,128)(2,1)S(1)}, bf16[160,128]{1,0:T(8,128)(2,1)S(1)}, u32[]{:S(2)}, u32[]{:S(2)}) collective-permute-start(bf16[160,128]{1,0:T(8,128)(2,1)S(1)} %get-tuple-element.111), channel_id=1, source_target_pairs={{0,12},{1,13},{2,14},{3,15},{4,8},{5,9},{6,10},{7,11},{8,4},{9,5},... | collective-permute-start | bytes 122888 | tf_op jit(solution)/shard_map/ppermute | solution.py:926
  (12 other events, 53.1 us)

commit v4 on v3

--- a/solution.py
+++ b/solution.py
@@ -22,7 +22,7 @@
 WORDS = 256
 
 SPAN = 256
-STEP = 240
+STEP = 241
 WIDE = 2 * SPAN
 TURNS = ((WORDS * CPW - 1) // STEP + 2) // 2
 
@@ -90,9 +90,32 @@
     return (d % 4) * 4 + d // 4
 
 
-def by_core(d, core):
+def feed_order(d, core):
     x, y, low, high = bits(d)
-    return (y * 8 + x * 4 if core else x * 8 + y * 4) + low * 2 + high
+    return (y * 8 + x * 2 if core else x * 8 + y * 2) + low * 4 + high
+
+
+def word_order(d, core=0):
+    _, _, low, high = bits(d)
+    return (d % 4) * 4 + low * 2 + high
+
+
+def own_bits():
+    phase, dp = lax.axis_index("phase"), lax.axis_index("dp")
+    x, y, low, high = (lax.rem(lax.div(dp, n), 2) for n in (1, 2, 4, 8))
+    return jnp.where(phase == 0, x, y), jnp.where(phase == 0, y, x), low, high
+
+
+def own_plane():
+    return lax.rem(lax.axis_index("dp"), 4)
+
+
+def add_up(out, *parts):
+    for i in range(out.shape[0]):
+        total = parts[0][i].astype(F32)
+        for part in parts[1:]:
+            total = total + part[i].astype(F32)
+        out[i] = total.astype(LOW)
 
 
 def members(word, first, count, weight=1.0):
@@ -186,6 +209,11 @@
              (wup_hbm, wup), (wdown_hbm, wdown), (cot_hbm.at[phase, 0], cot))
         )
     ]
+    pa[...] = jnp.zeros_like(pa)
+    pm[...] = jnp.zeros_like(pm)
+    prob_s[...] = jnp.zeros_like(prob_s)
+    for slot in range(2):
+        slow[slot, R_P:R_P + CHAR_HEADS * SPAN] = jnp.zeros((CHAR_HEADS * SPAN, WIDE), LOW)
     for load in tiny:
         load.wait()
     counts_row = counts_ref[...].astype(F32)
@@ -211,8 +239,6 @@
          counts_row - jnp.concatenate([none, counts_row[:, :-1]], axis=1),
          jnp.ones((1, WORDS), F32), jnp.zeros((13, WORDS), F32)], axis=0
     ).astype(LOW)
-    pa[...] = jnp.zeros_like(pa)
-    pm[...] = jnp.zeros_like(pm)
     for load in early:
         load.wait()
     for load in loads:
@@ -225,9 +251,6 @@
     up_t[...] = up_ref[...].T
     g1 = row_to_column(g1_ref[...].astype(F32)[None, :])
     g2 = row_to_column(g2_ref[...].astype(F32)[None, :])
-    prob_s[...] = jnp.zeros_like(prob_s)
-    for slot in range(2):
-        slow[slot, R_P:R_P + CHAR_HEADS * SPAN] = jnp.zeros((CHAR_HEADS * SPAN, WIDE), LOW)
     first_copy.wait()
 
     def find(turn):
@@ -436,14 +459,14 @@
     for c in range(WFF // 512):
         cs = slice(c * 512, (c + 1) * 512)
         gd = nn(actw[:, cs].T, cot_low)
-        put(bundle, phase, lambda i, p: by_core(c * 4 + i, p), F_DOWN, gd, 256, 128)
+        put(bundle, phase, lambda i, p: feed_order(c * 4 + i, p), F_DOWN, gd, 256, 128)
         bd = (nt(cot_low, wdown[cs, :]) * slopew[:, cs].astype(F32)).astype(LOW)
         gu = nn(n2_t, bd).astype(LOW)
         side = jnp.bitwise_xor(phase, c // 2)
         for piece in range(2):
             row = F_UP + ((c % 2) * 2 + piece) * 32
             for d in range(SHARES):
-                bundle[side, by_core(d, c // 2), row:row + 32, :] = gu[d * 32:(d + 1) * 32, piece * 256:piece * 256 + 256]
+                bundle[side, feed_order(d, c // 2), row:row + 32, :] = gu[d * 32:(d + 1) * 32, piece * 256:piece * 256 + 256]
         n2d = n2d + nt(bd, wup[:, cs])
     stores = [
         pltpu.make_async_copy(bundle.at[0], keep_hbm, osem.at[0]),
@@ -467,25 +490,18 @@
 
 def kernel_a2(
     counts_ref, q_ref, k_ref, v_ref, pw, mixt_ref, normed_ref, xhat_ref, winv_ref, md_ref, pooled_ref, pa_ref,
-    wg1_ref, proj_ref, wwq_hbm, wwk_hbm, wwv_hbm, wwo_hbm,
+    wg1_ref, proj_ref, wwq, wwk, wwv, wwo,
     gw_ref, keep_hbm, send_hbm, gain_ref,
-    wwq, wwk, wwv, wwo, bundle, wsem, osem,
+    bundle, osem,
 ):
     phase = lax.axis_index("phase")
-    loads = [
-        pltpu.make_async_copy(src, dst, wsem.at[i])
-        for i, (src, dst) in enumerate(((wwo_hbm, wwo), (wwq_hbm, wwq), (wwk_hbm, wwk), (wwv_hbm, wwv)))
-    ]
-    for load in loads:
-        load.start()
     wg1 = wg1_ref[...].astype(F32)[None, :]
     q, k, v, normed, pooled_low = q_ref[...], k_ref[...], v_ref[...], normed_ref[...], pooled_ref[...]
     per_count = 1.0 / row_to_column(counts_ref[phase].astype(F32))
     md = md_ref[...]
     md_low = md.astype(LOW)
-    put(bundle, phase, by_core, T_O, nn(mixt_ref[...], md_low), 256, 32)
+    put(bundle, phase, word_order, T_O, nn(mixt_ref[...], md_low), 256, 32)
     k_t = k.T
-    loads[0].wait()
     do = nt(md_low, wwo[...]).astype(LOW)
     dq_t, dk, dv = [], [], []
     left = iota((WORDS, 128), 1) < HEAD
@@ -510,35 +526,36 @@
     dk = jnp.concatenate(dk, axis=1)
     dv = jnp.concatenate(dv, axis=1)
     normed_t = normed.T
-    for load in loads[1:]:
-        load.wait()
     nd = nt(dq, wwq[...]) + nt(dk, wwk[...]) + nt(dv, wwv[...])
-    put(bundle, phase, by_core, T_Q, nn(normed_t, dq), 256, 32)
-    put(bundle, phase, by_core, T_K, nn(normed_t, dk), 256, 32)
-    put(bundle, phase, by_core, T_V, nn(normed_t, dv), 256, 32)
+    put(bundle, phase, word_order, T_Q, nn(normed_t, dq), 256, 32)
+    put(bundle, phase, word_order, T_K, nn(normed_t, dk), 256, 32)
+    put(bundle, phase, word_order, T_V, nn(normed_t, dv), 256, 32)
+    stores = [
+        pltpu.make_async_copy(bundle.at[side, :, rows], out.at[:, rows], osem.at[i, side])
+        for i, rows in enumerate((pl.ds(0, T_CDOWN), pl.ds(T_CDOWN, T_ROWS - T_CDOWN)))
+        for side, out in enumerate((keep_hbm, send_hbm))
+    ]
+    for store in stores[:2]:
+        store.start()
     vhat = xhat_ref[...]
     gain_ref[...] = jnp.broadcast_to(jnp.sum(nd * vhat, axis=0, keepdims=True), (8, WD))
     lifted = nd * wg1
     xd = md + winv_ref[:, 0:1] * (lifted - vhat * jnp.mean(lifted * vhat, axis=1, keepdims=True))
     vd = xd.astype(LOW)
-    put(bundle, phase, by_core, T_PROJ, nn(pooled_low.T, vd), 256, 16)
+    put(bundle, phase, word_order, T_PROJ, nn(pooled_low.T, vd), 256, 16)
     gw = (nt(vd, proj_ref[...]) * per_count).astype(LOW)
     gw_ref[...] = gw.T
-    put(bundle, phase, by_core, T_CDOWN, nn(pa_ref[...].T, gw), 128, 64)
-    stores = [
-        pltpu.make_async_copy(bundle.at[0], keep_hbm, osem.at[0]),
-        pltpu.make_async_copy(bundle.at[1], send_hbm, osem.at[1]),
-    ]
-    for s in stores:
-        s.start()
-    for s in stores:
-        s.wait()
+    put(bundle, phase, word_order, T_CDOWN, nn(pa_ref[...].T, gw), 128, 64)
+    for store in stores[2:]:
+        store.start()
+    for store in stores:
+        store.wait()
 
 
 def kernel_b1(
-    turns_ref, gw_ref, g2_ref, up_ref, down_ref, kepts_hbm, keptm_hbm, kepti_hbm,
-    keptd_hbm, aup_ref, gain_ref,
-    sslope, smid, sinfo, sdelta, aup, ag2, down, ksem, dsem,
+    turns_ref, gw_ref, g2_ref, up_ref, down_ref, kepts_hbm, keptm_hbm, kepti_hbm, f0_hbm, f1_hbm,
+    keptd_hbm, aup_ref, gain_ref, facc_ref,
+    sslope, smid, sinfo, sdelta, aup, ag2, down, f0, f1, ksem, dsem, fsem,
 ):
     n_turns = turns_ref[0]
 
@@ -554,6 +571,13 @@
 
     for c in kept_copies(0, 0):
         c.start()
+    a, _, _, _ = own_bits()
+    loads = [
+        pltpu.make_async_copy(src.at[pl.ds(a * 8, 8)], dst, fsem.at[i])
+        for i, (src, dst) in enumerate(((f0_hbm, f0), (f1_hbm, f1)))
+    ]
+    for load in loads:
+        load.start()
     g2 = row_to_column(g2_ref[...].astype(F32)[None, :])
     down[...] = down_ref[...] * 0.5
     aup[...] = jnp.zeros_like(aup)
@@ -592,6 +616,9 @@
 
     lax.fori_loop(0, n_turns, turn, 0)
     aup_ref[...] = aup[...].astype(LOW)
+    for load in loads:
+        load.wait()
+    add_up(facc_ref, f0, f1)
     gain_ref[...] = jnp.broadcast_to(jnp.sum(ag2[...], axis=1, keepdims=True), (CD, 8)).T
 
     def drain(b, carry):
@@ -603,9 +630,9 @@
 
 def kernel_b2(
     turns_ref, wgain1_ref, wgain2_ref, gain2_ref, aup_ref, g1_ref, wq_ref, wk_ref, wv_ref, wo_ref,
-    keptl_hbm, keptd_hbm, kepti_hbm,
-    keep_hbm, send_hbm,
-    slow, sinfo, sdelta, dscore, wqkv, aqkv, ao, atab, ag1, bundle, ksem, osem,
+    keptl_hbm, keptd_hbm, kepti_hbm, facc_ref, f2_hbm, t0_hbm, t1_hbm,
+    keep_ref, send_ref, fnext_ref, tacc_ref,
+    slow, sinfo, sdelta, dscore, wqkv, aqkv, ao, atab, ag1, bundle, f2, t0, t1, ksem, fsem,
 ):
     phase = lax.axis_index("phase")
     n_turns = turns_ref[0]
@@ -619,6 +646,14 @@
 
     for c in kept_copies(0, 0):
         c.start()
+    _, _, low, _ = own_bits()
+    quarter = pl.ds(own_plane() * 4, 4)
+    loads = [
+        pltpu.make_async_copy(src.at[at], dst, fsem.at[i])
+        for i, (src, at, dst) in enumerate(((f2_hbm, pl.ds(low * 4, 4), f2), (t0_hbm, quarter, t0), (t1_hbm, quarter, t1)))
+    ]
+    for load in loads:
+        load.start()
     g1 = row_to_column(g1_ref[...].astype(F32)[None, :])
     for i, w in enumerate((wq_ref, wk_ref, wv_ref)):
         wqkv[:, i * CD:(i + 1) * CD] = w[...]
@@ -681,6 +716,10 @@
 
     lax.fori_loop(0, n_turns, turn, 0)
 
+    for load in loads:
+        load.wait()
+    add_up(fnext_ref, facc_ref.at[pl.ds(low * 4, 4)], f2)
+    add_up(tacc_ref, t0, t1)
     put(bundle, phase, plane_first, C_TABLE, atab[...], 128, 16)
     put(bundle, phase, plane_first, C_Q, aqkv[:, 0:CD], 128, 16)
     put(bundle, phase, plane_first, C_K, aqkv[:, CD:2 * CD], 128, 16)
@@ -700,34 +739,72 @@
         tile = jnp.concatenate(rows, axis=0).astype(LOW)
         bundle[0, plane_first(d), C_GAIN:C_GAIN + 16, :] = tile
         bundle[1, plane_first(d), C_GAIN:C_GAIN + 16, :] = tile
-    stores = [
-        pltpu.make_async_copy(bundle.at[0], keep_hbm, osem.at[0]),
-        pltpu.make_async_copy(bundle.at[1], send_hbm, osem.at[1]),
-    ]
-    for s in stores:
-        s.start()
-    for s in stores:
-        s.wait()
+    keep_ref[...] = bundle[0]
+    send_ref[...] = bundle[1]
+
+
+def kernel_add_one(f0_hbm, f1_hbm, send_ref, one, two, sem):
+    a, _, _, _ = own_bits()
+    other = pl.ds((1 - a) * 8, 8)
+    loads = [pltpu.make_async_copy(src.at[other], dst, sem.at[i]) for i, (src, dst) in enumerate(((f0_hbm, one), (f1_hbm, two)))]
+    for load in loads:
+        load.start()
+    for load in loads:
+        load.wait()
+    add_up(send_ref, one, two)
+
+
+def kernel_add_two(facc_ref, f2_hbm, t0_hbm, t1_hbm, fsend_ref, ts1_ref, ts2_ref, ts3_ref, f2, t0, t1, sem):
+    _, _, low, _ = own_bits()
+    half = pl.ds((1 - low) * 4, 4)
+    loads = [pltpu.make_async_copy(f2_hbm.at[half], f2, sem.at[0])]
+    for k in range(1, 4):
+        at = pl.ds(lax.bitwise_xor(own_plane(), k) * 4, 4)
+        for i, (src, dst) in enumerate(((t0_hbm, t0), (t1_hbm, t1))):
+            loads.append(pltpu.make_async_copy(src.at[at], dst.at[k - 1], sem.at[1 + i]))
+    for load in loads:
+        load.start()
+    loads[0].wait()
+    add_up(fsend_ref, facc_ref.at[half], f2)
+    for load in loads[1:]:
+        load.wait()
+    for k, out in enumerate((ts1_ref, ts2_ref, ts3_ref)):
+        add_up(out, t0.at[k], t1.at[k])
+
+
+def kernel_add_three(
+    facc_ref, f3_hbm, tacc_ref, tg1_hbm, tg2_hbm, tg3_hbm, fsend_ref, fkeep_ref, tsend_ref, tkeep_ref, f3, tg, sem
+):
+    _, b, low, _ = own_bits()
+    loads = [pltpu.make_async_copy(src, tg.at[i], sem.at[0]) for i, src in enumerate((tg1_hbm, tg2_hbm, tg3_hbm))]
+    loads.append(pltpu.make_async_copy(f3_hbm, f3, sem.at[1]))
+    for load in loads:
+        load.start()
+    for load in loads[:3]:
+        load.wait()
+    for out, bit in ((tsend_ref, 1 - low), (tkeep_ref, low)):
+        at = pl.ds(bit * 2, 2)
+        add_up(out, tacc_ref.at[at], *(tg.at[k, at] for k in range(3)))
+    loads[3].wait()
+    for out, bit in ((fsend_ref, 1 - b), (fkeep_ref, b)):
+        add_up(out, facc_ref.at[pl.ds(bit * 2, 2)], f3.at[pl.ds(bit * 2, 2)])
 
 
 def kernel_f(
-    f0, f1, f2, f3, f4, f5, t0, t1, t2, t3, t4, t5, c0, c1, c2, c3, c4, c5, c6, c7, outk, outg,
+    f3, f4, t2, t3, last, c0, c1, c2, c3, c4, c5, c6, c7, outk, outg,
     word_out, d_table, d_g1, d_q, d_k, d_v, d_o, d_g2, d_up, d_down, d_proj,
     e_g1, e_q, e_k, e_v, e_o, e_g2, e_up, e_down,
     fs, ts, cs, sem,
 ):
     phase = lax.axis_index("phase")
     dp = lax.axis_index("dp")
-    x, y, low, high = (lax.rem(lax.div(dp, n), 2) for n in (1, 2, 4, 8))
-    a, b = jnp.where(phase == 0, x, y), jnp.where(phase == 0, y, x)
+    _, _, low, high = own_bits()
     loads = []
-    at = a * 8 + b * 4 + low * 2 + high
     line = lax.div(dp, 4)
-    both = (at, at, lax.rem(at, 8), lax.rem(at, 4), lax.rem(at, 2), 0)
     place = lax.rem(dp, 4) * 4 + line
     for i, (parts, places, here) in enumerate((
-        ((f0, f1, f2, f3, f4, f5), both, fs),
-        ((t0, t1, t2, t3, t4, t5), both, ts),
+        ((f3, f4, last), (high, high, pl.ds(0, F_ROWS)), fs),
+        ((t2, t3, last), (high, high, pl.ds(F_ROWS, T_ROWS)), ts),
         ((c0, c1, c2, c3, c4), (place, place, line, line, line), cs),
     )):
         for j, (part, n) in enumerate(zip(parts, places)):
@@ -848,62 +925,99 @@
             outside((SHARES, T_ROWS, 256), LOW),
             shape((8, WD), F32),
         ),
-        in_specs=[INSIDE] * 14 + [ANYWHERE] * 4,
+        in_specs=[INSIDE] * 18,
         out_specs=(INSIDE, ANYWHERE, ANYWHERE, INSIDE),
         scratch_shapes=[
-            v((WD, WD), LOW), v((WD, WD), LOW), v((WD, WD), LOW), v((WD, WD), LOW),
             v((2, SHARES, T_ROWS, 256), LOW),
-            pltpu.SemaphoreType.DMA((4,)),
-            pltpu.SemaphoreType.DMA((2,)),
+            pltpu.SemaphoreType.DMA((2, 2)),
         ],
         compiler_params=params(20),
         cost_estimate=pl.CostEstimate(flops=200 * 10**9, bytes_accessed=10 * 10**6, transcendentals=10**6),
         name="word_attention_backward",
-    )(char_counts, *kept, gain, project, *kept_outside(*weights))
-
-
-def call_b1(turns, gw, gain, up, down, kepts, keptm, kepti):
+    )(char_counts, *kept, gain, project, *weights)
+
+
+def call_b1(turns, gw, gain, up, down, kepts, keptm, kepti, f0, f1):
     v = pltpu.VMEM
     return pl.pallas_call(
         kernel_b1,
-        out_shape=(outside((TURNS, CD, WIDE), LOW), shape((CD, CFF), LOW), shape((8, CD), F32)),
-        in_specs=[SCALARS] + [INSIDE] * 4 + [ANYWHERE] * 3,
-        out_specs=(ANYWHERE, INSIDE, INSIDE),
+        out_shape=(outside((TURNS, CD, WIDE), LOW), shape((CD, CFF), LOW), shape((8, CD), F32), v((8, F_ROWS, 256), LOW)),
+        in_specs=[SCALARS] + [INSIDE] * 4 + [ANYWHERE] * 5,
+        out_specs=(ANYWHERE, INSIDE, INSIDE, INSIDE),
         scratch_shapes=[
             v((2, CFF, WIDE), LOW), v((2, CD, WIDE), F32), v((2, 8, WIDE), F32), v((2, CD, WIDE), LOW),
             v((CD, CFF), F32), v((CD, WIDE), F32), v((CFF, CD), LOW),
+            v((8, F_ROWS, 256), LOW), v((8, F_ROWS, 256), LOW),
             pltpu.SemaphoreType.DMA((3, 2)),
             pltpu.SemaphoreType.DMA((2,)),
+            pltpu.SemaphoreType.DMA((2,)),
         ],
-        compiler_params=params(16),
+        compiler_params=params(18),
         cost_estimate=pl.CostEstimate(flops=200 * 10**9, bytes_accessed=20 * 10**6, transcendentals=10**6),
         name="character_backward_one",
-    )(turns, gw, gain, up, down, *kept_outside(kepts, keptm, kepti))
-
-
-def call_b2(turns, wgain1, wgain2, gain2, aup, weights, keptl, keptd, kepti):
+    )(turns, gw, gain, up, down, *kept_outside(kepts, keptm, kepti, f0, f1))
+
+
+def call_b2(turns, wgain1, wgain2, gain2, aup, weights, keptl, keptd, kepti, facc, f2, t0, t1):
     v = pltpu.VMEM
     return pl.pallas_call(
         kernel_b2,
-        out_shape=(outside((SHARES, C_ROWS, 128), LOW), outside((SHARES, C_ROWS, 128), LOW)),
-        in_specs=[SCALARS] + [INSIDE] * 9 + [ANYWHERE] * 3,
-        out_specs=(ANYWHERE, ANYWHERE),
+        out_shape=(
+            v((SHARES, C_ROWS, 128), LOW), v((SHARES, C_ROWS, 128), LOW), v((4, F_ROWS, 256), LOW), v((4, T_ROWS, 256), LOW)
+        ),
+        in_specs=[SCALARS] + [INSIDE] * 9 + [ANYWHERE] * 3 + [INSIDE] + [ANYWHERE] * 3,
+        out_specs=(INSIDE,) * 4,
         scratch_shapes=[
             v((2, KEPT_LOW, WIDE), LOW), v((2, 8, WIDE), F32), v((2, CD, WIDE), LOW),
             v((CHAR_HEADS * SPAN, WIDE), LOW),
             v((CD, 3 * CD), LOW),
             v((CD, 3 * CD), F32), v((CD, CD), F32), v((CVOC, CD), F32), v((CD, WIDE), F32),
             v((2, SHARES, C_ROWS, 128), LOW),
+            v((4, F_ROWS, 256), LOW), v((4, T_ROWS, 256), LOW), v((4, T_ROWS, 256), LOW),
             pltpu.SemaphoreType.DMA((3, 2)),
-            pltpu.SemaphoreType.DMA((2,)),
+            pltpu.SemaphoreType.DMA((3,)),
         ],
-        compiler_params=params(20),
+        compiler_params=params(24),
         cost_estimate=pl.CostEstimate(flops=200 * 10**9, bytes_accessed=40 * 10**6, transcendentals=10**6),
         name="character_backward_two",
-    )(turns, wgain1, wgain2, gain2, aup, *weights, *kept_outside(keptl, keptd, kepti))
-
-
-def call_f(f, t, c, outk, outg):
+    )(turns, wgain1, wgain2, gain2, aup, *weights, *kept_outside(keptl, keptd, kepti), facc, *kept_outside(f2, t0, t1))
+
+
+def call_add(kernel, name, outs, parts, specs, scratch):
+    v = pltpu.VMEM
+    return pl.pallas_call(
+        kernel,
+        out_shape=tuple(v(s, LOW) for s in outs),
+        in_specs=specs,
+        out_specs=(INSIDE,) * len(outs),
+        scratch_shapes=[v(s, LOW) for s in scratch] + [pltpu.SemaphoreType.DMA((len(scratch),))],
+        compiler_params=params(12),
+        name=name,
+    )(*parts)
+
+
+def add_one(f0, f1):
+    half = (8, F_ROWS, 256)
+    return call_add(kernel_add_one, "add_one", (half,), kept_outside(f0, f1), [ANYWHERE] * 2, (half, half))[0]
+
+
+def add_two(facc, f2, t0, t1):
+    fs, ts = (4, F_ROWS, 256), (4, T_ROWS, 256)
+    return call_add(
+        kernel_add_two, "add_two", (fs, ts, ts, ts), (facc, *kept_outside(f2, t0, t1)), [INSIDE] + [ANYWHERE] * 3,
+        (fs, (3,) + ts, (3,) + ts),
+    )
+
+
+def add_three(facc, f3, tacc, tgot):
+    fs, ts = (2, F_ROWS, 256), (2, T_ROWS, 256)
+    return call_add(
+        kernel_add_three, "add_three", (fs, fs, ts, ts), (facc, *kept_outside(f3), tacc, *kept_outside(*tgot)),
+        [INSIDE, ANYWHERE] * 2 + [ANYWHERE] * 2, ((4, F_ROWS, 256), (3, 4, T_ROWS, 256)),
+    )
+
+
+def call_f(words, c, outk, outg):
     v = pltpu.VMEM
     outs = ((CVOC, CD), (CD,), (CD, CD), (CD, CD), (CD, CD), (CD, CD), (CD,), (CD, CFF), (CFF, CD), (CD, WD),
             (WD,), (WD, WD), (WD, WD), (WD, WD), (WD, WD), (WD,), (WD, WFF), (WFF, WD))
@@ -911,14 +1025,14 @@
     return pl.pallas_call(
         kernel_f,
         out_shape=(shape((2, 1, WORDS, WD // 2), LOW),) + tuple(shape(s, F32) for s in outs),
-        in_specs=[ANYWHERE] * 20 + [INSIDE] * 2,
+        in_specs=[pl.BlockSpec(memory_space=pl.ANY)] * 13 + [INSIDE] * 2,
         out_specs=(INSIDE,) * 19,
         scratch_shapes=[
-            v((6, F_ROWS, 256), LOW), v((6, T_ROWS, 256), LOW), v((8, C_ROWS, 128), LOW), pltpu.SemaphoreType.DMA((3,)),
+            v((3, F_ROWS, 256), LOW), v((3, T_ROWS, 256), LOW), v((8, C_ROWS, 128), LOW), pltpu.SemaphoreType.DMA((3,)),
         ],
         compiler_params=params(8),
         name="finish",
-    )(*kept_outside(*f, *t, *c), outk, outg)
+    )(*words, *c, outk, outg)
 
 
 def flip(value, axis, bits):
@@ -942,30 +1056,16 @@
     return total.astype(LOW)
 
 
-class Sum:
-    def __init__(self, keep):
-        phase, dp = lax.axis_index("phase"), lax.axis_index("dp")
-        x, y, low, high = (lax.rem(lax.div(dp, n), 2) for n in (1, 2, 4, 8))
-        self.bits = [jnp.where(phase == 0, x, y), jnp.where(phase == 0, y, x), low, high]
-        self.flips = [(1, 2), (2, 1), (4, 4), (8, 8)]
-        self.parts = [keep]
-
-    def send(self):
-        step = len(self.parts) - 2
-        half = SHARES >> (step + 1)
-        total = None
-        for part in self.parts:
-            at, size = 0, part.shape[0]
-            for bit, n in zip(self.bits[:step], (8, 4, 2, 1)):
-                if n < size:
-                    at = at + bit * n
-            at = at + (1 - self.bits[step]) * half
-            piece = lax.dynamic_slice_in_dim(part, at, half, 0).astype(F32)
-            total = piece if total is None else total + piece
-        return total.astype(LOW)
-
-    def across(self, value):
-        return flip_both(value, *self.flips[len(self.parts) - 2])
+def across(value, side):
+    return flip_both(value, *((1, 2), (2, 1), (4, 4), (8, 8))[side])
+
+
+def half(bit, *parts):
+    return plus(*(lax.dynamic_slice_in_dim(part, bit * (part.shape[0] // 2), part.shape[0] // 2, 0) for part in parts))
+
+
+def after(value, *others):
+    return lax.optimization_barrier((value,) + others)[0]
 
 
 def together(*values):
@@ -992,57 +1092,52 @@
     one = (char_gain_two, char_up, char_down, kepts, keptm, kepti)
     two = (char_gain_one, char_query, char_key, char_value, char_output)
     if lax.axis_size("dp") != SHARES:
-        keptd, aup, gain2 = call_b1(turns, gw, *one)
-        ckeep, csend = call_b2(turns, wgain1, wgain2, gain2, aup, two, keptl, keptd, kepti)
-        got = [flip(v, "phase", 1) for v in (tsend, csend)]
-        return general_sums(outk, outg, (fkeep, fgot), (tkeep, got[0]), (ckeep, got[1]))
-    f, t = Sum(fkeep), Sum(tkeep)
+        keptd, aup, gain2, facc = call_b1(turns, gw, *one, fkeep, fgot)
+        tgot = flip(tsend, "phase", 1)
+        ckeep, csend, _, _ = call_b2(turns, wgain1, wgain2, gain2, aup, two, keptl, keptd, kepti, facc, facc, tkeep, tgot)
+        return general_sums(outk, outg, (fkeep, fgot), (tkeep, tgot), (ckeep, flip(csend, "phase", 1)))
     gw, tsend, fgot, outg = together(gw, tsend, fgot, outg)
-    f.parts.append(fgot)
-    send = f.send()
-    gw, send = together(gw, send)
-    fgot, tgot = f.across(send), flip(tsend, "phase", 1)
-    keptd, aup, gain2 = call_b1(turns, gw, *one)
-    keptd, fgot, tgot = together(keptd, fgot, tgot)
-    f.parts.append(fgot)
-    t.parts.append(tgot)
-    fsend, tsend = f.send(), t.send()
-    keptd, fsend, tsend = together(keptd, fsend, tsend)
-    fgot, tgot = f.across(fsend), t.across(tsend)
-    ckeep, csend = call_b2(turns, wgain1, wgain2, gain2, aup, two, keptl, keptd, kepti)
-    ckeep, csend, fgot, tgot = together(ckeep, csend, fgot, tgot)
-    f.parts.append(fgot)
-    t.parts.append(tgot)
-    cphase, fgot, tgot = flip(csend, "phase", 1), f.across(f.send()), t.across(t.send())
-    f.parts.append(fgot)
-    t.parts.append(tgot)
+    gw, fsend = together(gw, add_one(fkeep, fgot))
+    f2, tgot = across(fsend, 0), flip(tsend, "phase", 1)
+    keptd, aup, gain2, facc = call_b1(turns, gw, *one, fkeep, fgot)
+    keptd, f2, tgot = together(keptd, f2, tgot)
+    sends = add_two(facc, f2, tkeep, tgot)
+    keptd, fsend, *tsends = together(keptd, *sends)
+    f3, *tparts = across(fsend, 2), *(flip(send, "dp", k) for k, send in enumerate(tsends, 1))
+    ckeep, csend, facc, tacc = call_b2(
+        turns, wgain1, wgain2, gain2, aup, two, keptl, keptd, kepti, facc, f2, tkeep, tgot
+    )
+    ckeep, csend, facc, f3, *tparts = together(ckeep, csend, facc, f3, *tparts)
+    _, _, low, high = own_bits()
+    cphase = flip(csend, "phase", 1)
+    fsend, facc, tsend, tacc = add_three(facc, f3, tacc, tparts)
+    f4, t3 = across(fsend, 1), across(tsend, 2)
     dp = lax.axis_index("dp")
     plane, line = lax.rem(dp, 4), lax.div(dp, 4)
     c = [ckeep.reshape(4, 4, C_ROWS, 128), cphase.reshape(4, 4, C_ROWS, 128)]
     sends = [plus(*(pick(part, lax.bitwise_xor(plane, k)) for part in c)) for k in range(1, 4)]
-    cgot, fgot, tgot = (
-        [flip(send, "dp", k) for k, send in enumerate(sends, 1)], f.across(f.send()), t.across(t.send())
-    )
-    f.parts.append(fgot)
-    t.parts.append(tgot)
+    cgot = [flip(send, "dp", k) for k, send in enumerate(sends, 1)]
+    f4, t3 = after(f4, *sends), after(t3, *sends)
+    last = jnp.concatenate([pick(half(1 - high, facc, f4), 0), pick(half(1 - high, tacc, t3), 0)], axis=0)
+    last = across(last, 3)
     c = [pick(part, plane) for part in c] + cgot
     sends = [plus(*(pick(part, lax.bitwise_xor(line, k)) for part in c)) for k in range(1, 4)]
-    cline, tgot = [flip(send, "dp", 4 * k) for k, send in enumerate(sends, 1)], t.across(t.send())
-    t.parts.append(tgot)
-    return call_f(f.parts, t.parts, (ckeep, cphase, *cgot, *cline), outk, outg)
+    cline = [flip(send, "dp", 4 * k) for k, send in enumerate(sends, 1)]
+    return call_f((facc, f4, tacc, t3, last), (ckeep, cphase, *cgot, *cline), outk, outg)
 
 
 def general_sums(outk, outg, fs, ts, cs):
     phase = lax.axis_index("phase")
     first = phase == 0
     outs = jnp.stack([jnp.where(first, outk, outg), jnp.where(first, outg, outk)])[:, None]
-    plain, swapped = (jnp.asarray([by_core(d, core) for d in range(SHARES)]) for core in range(2))
+    def order(places):
+        plain, swapped = (jnp.asarray([places(d, core) for d in range(SHARES)]) for core in range(2))
+        return jnp.where(first, plain, swapped)
 
     def natural(pair, order):
         return jnp.take(pair[0].astype(F32) + pair[1].astype(F32), order, axis=0)
 
-    order = jnp.where(first, plain, swapped)
-    f, t, c = natural(fs, order), natural(ts, order), natural(cs, jnp.asarray([plane_first(d) for d in range(SHARES)]))
+    f, t, c = natural(fs, order(feed_order)), natural(ts, order(word_order)), natural(cs, jnp.asarray([plane_first(d) for d in range(SHARES)]))
 
     def whole(rows):
         return rows.reshape(-1, rows.shape[-1])

time: 113 us -> 105 us (0.929)
  other arithmetic: 13.8 us -> 1.01 us
  Pallas kernels: 63.4 us -> 68.8 us
    convert_element_type x8 -> x0, other arithmetic: 13.6 us -> none  [send(): return total.astype(LOW)]
    ppermute x10 -> x13, waiting for transfers between devices: 0.67 us -> 8.35 us  [flip(): return lax.ppermute(value, axis, [(i, i ^ bits) for i in range(count)])]
    pallas_call x1 -> x4, Pallas kernels: 14.6 us -> 22.2 us  [the longest x1 14.9 us: call_b2(): pl.pallas_call(kernel_b2, out_shape=(v((SHARES, C_ROWS, 128), LOW), v((SH...]
    ppermute x8 -> x5, waiting for transfers between devices: 10.6 us -> 3.56 us  [flip_both(): return lax.ppermute(value, ('phase', 'dp'), pairs)]
    ppermute x8 -> x5, starting transfers between devices: 13.4 us -> 9.84 us  [flip_both(): return lax.ppermute(value, ('phase', 'dp'), pairs)]
    ppermute x10 -> x13, starting transfers between devices: 8.67 us -> 12.1 us  [flip(): return lax.ppermute(value, axis, [(i, i ^ bits) for i in range(count)])]
    pallas_call x1, Pallas kernels: 6.75 us -> 4.96 us  [call_a2(): pl.pallas_call(kernel_a2, out_shape=(shape((CD, WORDS), LOW), outside((SH...]
  transfers between devices with their start and end apart: 18 -> 18, of which waited for: 6 -> 9; matrix products, arithmetic and copies ran while one was open for 6% -> 1% of each run, Pallas kernels for 29% -> 31%
where the time goes in v4:
time: 105 us
  Pallas kernels  68.8 us (66%)
  starting transfers between devices  21.9 us (21%)
  waiting for transfers between devices  11.9 us (11%)
  between operations  1.1 us (1%)
    pallas_call x1, Pallas kernels, call_a(): pl.pallas_call(kernel_a, out_shape=(outside((TURNS, KEPT_LOW, WIDE), LOW)...  27.2 us
    pallas_call x1, Pallas kernels, call_b2(): pl.pallas_call(kernel_b2, out_shape=(v((SHARES, C_ROWS, 128), LOW), v((SH...  14.9 us
    ppermute x13, starting transfers between devices, flip(): return lax.ppermute(value, axis, [(i, i ^ bits) for i in range(count)])  12.1 us
    pallas_call x1, Pallas kernels, call_b1(): pl.pallas_call(kernel_b1, out_shape=(outside((TURNS, CD, WIDE), LOW), sha...  11.3 us
    ppermute x5, starting transfers between devices, flip_both(): return lax.ppermute(value, ('phase', 'dp'), pairs)  9.84 us
    ppermute x13, waiting for transfers between devices, flip(): return lax.ppermute(value, axis, [(i, i ^ bits) for i in range(count)])  8.35 us
    pallas_call x3, Pallas kernels, call_add(): pl.pallas_call(kernel, out_shape=tuple((v(s, LOW) for s in outs)), in_spe...  7.33 us
    pallas_call x1, Pallas kernels, call_a2(): pl.pallas_call(kernel_a2, out_shape=(shape((CD, WORDS), LOW), outside((SH...  4.96 us
  transfers between devices with their start and end apart: 18, of which 9 were waited for; matrix products, arithmetic and copies ran while one was open for 1% of the time, Pallas kernels for 31%

profile of v4, /device:TPU:0, one launch (start us, length us, event | category | flops | bytes accessed | tf_op | source)
XLA Modules:
  0.0 104.8 jit_solution(13838737922517651705)
XLA Ops:
  0.7 27.2 %forward_and_words.1 = (bf16[9,2304,512]{2,1,0:T(8,128)(2,1)}, bf16[9,1024,512]{2,1,0:T(8,128)(2,1)}, f32[9,256,512]{2,1,0:T(8,128)}, f32[9,8,512]{2,1,0:T(8,128...) custom-call(s32[2,1,256]{2,1,0:T(1,128)} %counts_ref.1, ...), custom_call_target="tpu_custom_call" | custom-call | flops 199999995904 | bytes 60000000 | tf_op jit(solution)/shard_map/forward_and_words/pallas_call | solution.py:872
  27.9 0.5 collective-permute-start
  28.6 5.0 %word_attention_backward.1 = (bf16[256,256]{1,0:T(8,128)(2,1)S(1)}, bf16[16,176,256]{2,1,0:T(8,128)(2,1)}, bf16[16,176,256]{2,1,0:T(8,128)(2,1)}, f32[8,512]{1,0:T(8,128)S(1)}) custom-call(s32[2,1,256]{2,1,0:T(1,128)S(1)} %copy-done.11, bf16[256,512]{1,0:T(8,128)(2,1)S(1)} %get-tuple-element.84.q_ref, bf16[256,512]{1,0:T(8,128)(2,1)S(1)} %get-tuple-element.85.k_ref, ...), custom_call_target="tpu_custom_call" | custom-call | flops 199999995904 | bytes 10000000 | tf_op jit(solution)/shard_map/word_attention_backward/pallas_call | solution.py:920
  33.6 2.9 %add_one.1 = bf16[8,256,256]{2,1,0:T(8,128)(2,1)} custom-call(bf16[16,256,256]{2,1,0:T(8,128)(2,1)} %get-tuple-element.102.f0_hbm, bf16[16,256,256]{2,1,0:T(8,128)(2,1)} %collective-permute-done.f1_hbm), custom_call_target="tpu_custom_call" | custom-call | tf_op jit(solution)/shard_map/add_one/pallas_call | solution.py:988
  36.5 3.0 %collective-permute-start.2 = (bf16[8,256,256]{2,1,0:T(8,128)(2,1)}, bf16[8,256,256]{2,1,0:T(8,128)(2,1)}, u32[]{:S(2)}, u32[]{:S(2)}) collective-permute-start(bf16[8,256,256]{2,1,0:T(8,128)(2,1)} %add_one.1), channel_id=1, source_target_pairs={{0,1},{1,0},{2,3},{3,2},{4,5},{5,4},{6,7},{7,6},{8,9},{9,8},{10,11... | collective-permute-start | bytes 3145736 | tf_op jit(solution)/shard_map/ppermute | solution.py:1045
  39.5 11.3 %character_backward_one.1 = (bf16[9,256,512]{2,1,0:T(8,128)(2,1)}, bf16[256,1024]{1,0:T(8,128)(2,1)S(1)}, f32[8,256]{1,0:T(8,128)S(1)}, bf16[8,256,256]{2,1,0:T(8,128)(2,1)S(1)}) custom-call(s32[1]{0:T(128)} %get-tuple-element.83.turns_ref, bf16[256,256]{1,0:T(8,128)(2,1)S(1)} %get-tuple-element.104.gw_ref, bf16[256]{0:T(256)(128)(2,1)S(1)} %copy-done.13, ...), custom_call_target="tpu_custom_call" | custom-call | flops 199999995904 | bytes 20000000 | tf_op jit(solution)/shard_map/character_backward_one/pallas_call | solution.py:942
  50.8 1.7 %collective-permute-done.2.f2_hbm = bf16[8,256,256]{2,1,0:T(8,128)(2,1)} collective-permute-done((bf16[8,256,256]{2,1,0:T(8,128)(2,1)}, bf16[8,256,256]{2,1,0:T(8,128)(2,1)}, u32[]{:S(2)}, u32[]{:S(2)}) %collective-permute-start.2) | collective-permute-done | bytes 1048608 | tf_op jit(solution)/shard_map/ppermute | solution.py:1045
  52.6 3.0 %add_two.1 = (bf16[4,256,256]{2,1,0:T(8,128)(2,1)}, bf16[4,176,256]{2,1,0:T(8,128)(2,1)}, bf16[4,176,256]{2,1,0:T(8,128)(2,1)}, bf16[4,176,256]{2,1,0:T(8,128)(2,1)}) custom-call(bf16[8,256,256]{2,1,0:T(8,128)(2,1)S(1)} %get-tuple-element.115.facc_ref, bf16[8,256,256]{2,1,0:T(8,128)(2,1)} %collective-permute-done.2.f2_hbm, ...), custom_call_target="tpu_custom_call" | custom-call | tf_op jit(solution)/shard_map/add_two/pallas_call | solution.py:988
  55.5 2.2 %collective-permute-start.4 = (bf16[4,256,256]{2,1,0:T(8,128)(2,1)}, bf16[4,256,256]{2,1,0:T(8,128)(2,1)}, u32[]{:S(2)}, u32[]{:S(2)}) collective-permute-start(bf16[4,256,256]{2,1,0:T(8,128)(2,1)} %get-tuple-element.127), channel_id=1, source_target_pairs={{0,4},{1,5},{2,6},{3,7},{4,0},{5,1},{6,2},{7,3},{8,12},{9,13},{10,... | collective-permute-start | bytes 1572872 | tf_op jit(solution)/shard_map/ppermute | solution.py:1045
  57.7 1.5 %collective-permute-start.5 = (bf16[4,176,256]{2,1,0:T(8,128)(2,1)}, bf16[4,176,256]{2,1,0:T(8,128)(2,1)}, u32[]{:S(2)}, u32[]{:S(2)}) collective-permute-start(bf16[4,176,256]{2,1,0:T(8,128)(2,1)} %get-tuple-element.128), channel_id=1, source_target_pairs={{0,1},{1,0},{2,3},{3,2},{4,5},{5,4},{6,7},{7,6},{8,9},{9,8},{10,11... | collective-permute-start | bytes 1081352 | tf_op jit(solution)/shard_map/ppermute | solution.py:1040
  59.2 1.5 %collective-permute-start.6 = (bf16[4,176,256]{2,1,0:T(8,128)(2,1)}, bf16[4,176,256]{2,1,0:T(8,128)(2,1)}, u32[]{:S(2)}, u32[]{:S(2)}) collective-permute-start(bf16[4,176,256]{2,1,0:T(8,128)(2,1)} %get-tuple-element.129), channel_id=1, source_target_pairs={{0,2},{1,3},{2,0},{3,1},{4,6},{5,7},{6,4},{7,5},{8,10},{9,11},{10,... | collective-permute-start | bytes 1081352 | tf_op jit(solution)/shard_map/ppermute | solution.py:1040
  60.7 0.5 collective-permute-start.7
  61.2 14.9 %character_backward_two.1 = (bf16[16,160,128]{2,1,0:T(8,128)(2,1)S(1)}, bf16[16,160,128]{2,1,0:T(8,128)(2,1)}, bf16[4,256,256]{2,1,0:T(8,128)(2,1)S(1)}, bf16[4,176,256]{2,1,0:T(8,128)(2,1)S(1)}) custom-call(s32[1]{0:T(128)} %get-tuple-element.83.turns_ref, f32[8,512]{1,0:T(8,128)S(1)} %get-tuple-element.95.wgain1_ref, ...), custom_call_target="tpu_custom_call" | custom-call | flops 199999995904 | bytes 40000000 | tf_op jit(solution)/shard_map/character_backward_two/pallas_call | solution.py:963
  76.3 1.5 %add_three.1 = (bf16[2,256,256]{2,1,0:T(8,128)(2,1)S(1)}, bf16[2,256,256]{2,1,0:T(8,128)(2,1)S(1)}, bf16[2,176,256]{2,1,0:T(8,128)(2,1)S(1)}, bf16[2,176,256]{2,1,0:T(8,128)(2,1)S(1)}) custom-call(bf16[4,256,256]{2,1,0:T(8,128)(2,1)S(1)} %get-tuple-element.131.facc_ref, bf16[4,256,256]{2,1,0:T(8,128)(2,1)} %collective-permute-done.4.f3_hbm, ...), custom_call_target="tpu_custom_call" | custom-call | tf_op jit(solution)/shard_map/add_three/pallas_call | solution.py:988
  77.8 1.6 %collective-permute-start.8 = (bf16[2,256,256]{2,1,0:T(8,128)(2,1)S(1)}, bf16[2,256,256]{2,1,0:T(8,128)(2,1)S(1)}, u32[]{:S(2)}, u32[]{:S(2)}) collective-permute-start(bf16[2,256,256]{2,1,0:T(8,128)(2,1)S(1)} %get-tuple-element.138), channel_id=1, source_target_pairs={{0,2},{1,3},{2,0},{3,1},{4,6},{5,7},{6,4},{7,5},{8,10},{9,11},{10,... | collective-permute-start | bytes 786440 | tf_op jit(solution)/shard_map/ppermute | solution.py:1045
  79.4 0.4 collective-permute-start.10
  79.8 0.8 fusion.2
  80.7 1.5 %collective-permute-start.12 = (bf16[4,160,128]{2,1,0:T(8,128)(2,1)}, bf16[4,160,128]{2,1,0:T(8,128)(2,1)S(1)}, u32[]{:S(2)}, u32[]{:S(2)}) collective-permute-start(bf16[4,160,128]{2,1,0:T(8,128)(2,1)} %get-tuple-element.152), channel_id=1, source_target_pairs={{0,1},{1,0},{2,3},{3,2},{4,5},{5,4},{6,7},{7,6},{8,9},{9,8},{10,11... | collective-permute-start | bytes 491528 | tf_op jit(solution)/shard_map/ppermute | solution.py:1040
  82.2 0.5 collective-permute-start.13
  82.7 1.5 %collective-permute-start.14 = (bf16[4,160,128]{2,1,0:T(8,128)(2,1)S(1)}, bf16[4,160,128]{2,1,0:T(8,128)(2,1)S(1)}, u32[]{:S(2)}, u32[]{:S(2)}) collective-permute-start(bf16[4,160,128]{2,1,0:T(8,128)(2,1)S(1)} %get-tuple-element.150), channel_id=1, source_target_pairs={{0,3},{1,2},{2,1},{3,0},{4,7},{5,6},{6,5},{7,4},{8,11},{9,10},{10,... | collective-permute-start | bytes 491528 | tf_op jit(solution)/shard_map/ppermute | solution.py:1040
  84.2 0.6 collective-permute-done.8.f4
  84.8 1.2 %collective-permute-done.10.t3 = bf16[2,176,256]{2,1,0:T(8,128)(2,1)S(1)} collective-permute-done((bf16[2,176,256]{2,1,0:T(8,128)(2,1)S(1)}, bf16[2,176,256]{2,1,0:T(8,128)(2,1)S(1)}, u32[]{:S(2)}, u32[]{:S(2)}) %collective-permute-start.10) | collective-permute-done | bytes 180256 | tf_op jit(solution)/shard_map/ppermute | solution.py:1045
  86.1 2.7 %collective-permute-start.11 = (bf16[432,256]{1,0:T(8,128)(2,1)S(1)}, bf16[432,256]{1,0:T(8,128)(2,1)S(1)}, u32[]{:S(2)}, u32[]{:S(2)}) collective-permute-start(bf16[432,256]{1,0:T(8,128)(2,1)S(1)} %pad_maximum_fusion), channel_id=1, source_target_pairs={{0,8},{1,9},{2,10},{3,11},{4,12},{5,13},{6,14},{7,15},{8,0},{9,1},... | collective-permute-start | bytes 663560 | tf_op jit(solution)/shard_map/ppermute | solution.py:1045
  88.8 1.7 %collective-permute-done.13.c3 = bf16[4,160,128]{2,1,0:T(8,128)(2,1)S(1)} collective-permute-done((bf16[4,160,128]{2,1,0:T(8,128)(2,1)}, bf16[4,160,128]{2,1,0:T(8,128)(2,1)S(1)}, u32[]{:S(2)}, u32[]{:S(2)}) %collective-permute-start.13) | collective-permute-done | bytes 163872 | tf_op jit(solution)/shard_map/ppermute | solution.py:1040
  90.4 1.0 collective-permute-done.14.c4
  91.5 1.5 %collective-permute-start.15 = (bf16[160,128]{1,0:T(8,128)(2,1)S(1)}, bf16[160,128]{1,0:T(8,128)(2,1)S(1)}, u32[]{:S(2)}, u32[]{:S(2)}) collective-permute-start(bf16[160,128]{1,0:T(8,128)(2,1)S(1)} %get-tuple-element.149), channel_id=1, source_target_pairs={{0,4},{1,5},{2,6},{3,7},{4,0},{5,1},{6,2},{7,3},{8,12},{9,13},{10,... | collective-permute-start | bytes 122888 | tf_op jit(solution)/shard_map/ppermute | solution.py:1040
  93.1 2.6 %collective-permute-start.16 = (bf16[160,128]{1,0:T(8,128)(2,1)S(1)}, bf16[160,128]{1,0:T(8,128)(2,1)S(1)}, u32[]{:S(2)}, u32[]{:S(2)}) collective-permute-start(bf16[160,128]{1,0:T(8,128)(2,1)S(1)} %get-tuple-element.148), channel_id=1, source_target_pairs={{0,8},{1,9},{2,10},{3,11},{4,12},{5,13},{6,14},{7,15},{8,0},{9,1},... | collective-permute-start | bytes 122888 | tf_op jit(solution)/shard_map/ppermute | solution.py:1040
  95.7 0.3 collective-permute-start.17
  96.0 2.4 %collective-permute-done.15.c5 = bf16[160,128]{1,0:T(8,128)(2,1)S(1)} collective-permute-done((bf16[160,128]{1,0:T(8,128)(2,1)S(1)}, bf16[160,128]{1,0:T(8,128)(2,1)S(1)}, u32[]{:S(2)}, u32[]{:S(2)}) %collective-permute-start.15) | collective-permute-done | bytes 40992 | tf_op jit(solution)/shard_map/ppermute | solution.py:1040
  98.3 2.3 %collective-permute-done.16.c6 = bf16[160,128]{1,0:T(8,128)(2,1)S(1)} collective-permute-done((bf16[160,128]{1,0:T(8,128)(2,1)S(1)}, bf16[160,128]{1,0:T(8,128)(2,1)S(1)}, u32[]{:S(2)}, u32[]{:S(2)}) %collective-permute-start.16) | collective-permute-done | bytes 40992 | tf_op jit(solution)/shard_map/ppermute | solution.py:1040
  100.7 0.9 collective-permute-done.17.c7
  101.6 3.1 %finish.1 = (bf16[2,1,256,256]{3,2,1,0:T(8,128)(2,1)}, f32[16,128]{1,0:T(8,128)}, f32[16]{0:T(128)}, f32[16,128]{1,0:T(8,128)}, f32[16,128]{1,0:T(8,128)}, /*ind...) custom-call(bf16[2,256,256]{2,1,0:T(8,128)(2,1)S(1)} %get-tuple-elem, ...), custom_call_target="tpu_custom_call" | custom-call | tf_op jit(solution)/shard_map/finish/pallas_call | solution.py:1025
  (47 shorter events, 0.5 us)
Async XLA Ops:
  0.7 27.9 %copy-start = (bf16[512,512]{1,0:T(8,128)(2,1)S(1)}, bf16[512,512]{1,0:T(8,128)(2,1)}, u32[]{:S(2)}) copy-start(bf16[512,512]{1,0:T(8,128)(2,1)} %wwq.1) | copy-start | bytes 1572868
  0.7 27.9 %copy-start.1 = (bf16[512,512]{1,0:T(8,128)(2,1)S(1)}, bf16[512,512]{1,0:T(8,128)(2,1)}, u32[]{:S(2)}) copy-start(bf16[512,512]{1,0:T(8,128)(2,1)} %wwk.1) | copy-start | bytes 1572868
  0.7 27.8 %copy-start.2 = (bf16[512,512]{1,0:T(8,128)(2,1)S(1)}, bf16[512,512]{1,0:T(8,128)(2,1)}, u32[]{:S(2)}) copy-start(bf16[512,512]{1,0:T(8,128)(2,1)} %wwv.1) | copy-start | bytes 1572868
  0.7 27.8 %copy-start.3 = (bf16[512,512]{1,0:T(8,128)(2,1)S(1)}, bf16[512,512]{1,0:T(8,128)(2,1)}, u32[]{:S(2)}) copy-start(bf16[512,512]{1,0:T(8,128)(2,1)} %wwo.1) | copy-start | bytes 1572868
  0.7 27.8 %copy-start.6 = (bf16[256,512]{1,0:T(8,128)(2,1)S(1)}, bf16[256,512]{1,0:T(8,128)(2,1)}, u32[]{:S(2)}) copy-start(bf16[256,512]{1,0:T(8,128)(2,1)} %proj_ref.1) | copy-start | bytes 786436
  0.7 27.8 %copy-start.11 = (s32[2,1,256]{2,1,0:T(1,128)S(1)}, s32[2,1,256]{2,1,0:T(1,128)}, u32[]{:S(2)}) copy-start(s32[2,1,256]{2,1,0:T(1,128)} %counts_ref.1) | copy-start | bytes 6148
  0.7 27.8 %copy-start.12 = (bf16[512]{0:T(512)(128)(2,1)S(1)}, bf16[512]{0:T(512)(128)(2,1)}, u32[]{:S(2)}) copy-start(bf16[512]{0:T(512)(128)(2,1)} %wg1_ref.1) | copy-start | bytes 3076
  27.9 5.6 %collective-permute-start = (bf16[16,256,256]{2,1,0:T(8,128)(2,1)}, bf16[16,256,256]{2,1,0:T(8,128)(2,1)}, u32[]{:S(2)}, u32[]{:S(2)}) collective-permute-start(bf16[16,256,256]{2,1,0:T(8,128)(2,1)} %get-tuple-element.99), channel_id=1, source_target_pairs={{0,16},{16,0},{1,17},{17,1},{2,18},{18,2},{3,19},{19,3},{4,20},{20... | collective-permute-start | bytes 6291464 | tf_op jit(solution)/shard_map/ppermute | solution.py:1040
  28.4 5.1 %collective-permute-start.1 = (bf16[256,256]{1,0:T(8,128)(2,1)}, bf16[256,256]{1,0:T(8,128)(2,1)}, u32[]{:S(2)}, u32[]{:S(2)}) collective-permute-start(bf16[256,256]{1,0:T(8,128)(2,1)} %get-tuple-element.100), channel_id=1, source_target_pairs={{0,16},{16,0},{1,17},{17,1},{2,18},{18,2},{3,19},{19,3},{4,20},{20... | collective-permute-start | bytes 393224 | tf_op jit(solution)/shard_map/ppermute | solution.py:1040
  33.6 5.9 %copy-start.4 = (bf16[256,1024]{1,0:T(8,128)(2,1)S(1)}, bf16[256,1024]{1,0:T(8,128)(2,1)}, u32[]{:S(2)}) copy-start(bf16[256,1024]{1,0:T(8,128)(2,1)} %up_ref.1) | copy-start | bytes 1572868
  33.6 5.9 %copy-start.5 = (bf16[1024,256]{1,0:T(8,128)(2,1)S(1)}, bf16[1024,256]{1,0:T(8,128)(2,1)}, u32[]{:S(2)}) copy-start(bf16[1024,256]{1,0:T(8,128)(2,1)} %down_ref.1) | copy-start | bytes 1572868
  36.5 16.1 %collective-permute-start.2 = (bf16[8,256,256]{2,1,0:T(8,128)(2,1)}, bf16[8,256,256]{2,1,0:T(8,128)(2,1)}, u32[]{:S(2)}, u32[]{:S(2)}) collective-permute-start(bf16[8,256,256]{2,1,0:T(8,128)(2,1)} %add_one.1), channel_id=1, source_target_pairs={{0,1},{1,0},{2,3},{3,2},{4,5},{5,4},{6,7},{7,6},{8,9},{9,8},{10,11... | collective-permute-start | bytes 3145736 | tf_op jit(solution)/shard_map/ppermute | solution.py:1045
  39.4 13.1 %collective-permute-start.3 = (bf16[16,176,256]{2,1,0:T(8,128)(2,1)}, bf16[16,176,256]{2,1,0:T(8,128)(2,1)}, u32[]{:S(2)}, u32[]{:S(2)}) collective-permute-start(bf16[16,176,256]{2,1,0:T(8,128)(2,1)} %get-tuple-element.113), channel_id=1, source_target_pairs={{0,16},{16,0},{1,17},{17,1},{2,18},{18,2},{3,19},{19,3},{4,20},{20... | collective-permute-start | bytes 4325384 | tf_op jit(solution)/shard_map/ppermute | solution.py:1040
  52.5 8.7 %copy-start.7 = (bf16[256,256]{1,0:T(8,128)(2,1)S(1)}, bf16[256,256]{1,0:T(8,128)(2,1)}, u32[]{:S(2)}) copy-start(bf16[256,256]{1,0:T(8,128)(2,1)} %wq_ref.1) | copy-start | bytes 393220
  52.5 8.7 %copy-start.8 = (bf16[256,256]{1,0:T(8,128)(2,1)S(1)}, bf16[256,256]{1,0:T(8,128)(2,1)}, u32[]{:S(2)}) copy-start(bf16[256,256]{1,0:T(8,128)(2,1)} %wk_ref.1) | copy-start | bytes 393220
  52.5 8.7 %copy-start.9 = (bf16[256,256]{1,0:T(8,128)(2,1)S(1)}, bf16[256,256]{1,0:T(8,128)(2,1)}, u32[]{:S(2)}) copy-start(bf16[256,256]{1,0:T(8,128)(2,1)} %wv_ref.1) | copy-start | bytes 393220
  52.5 8.7 %copy-start.10 = (bf16[256,256]{1,0:T(8,128)(2,1)S(1)}, bf16[256,256]{1,0:T(8,128)(2,1)}, u32[]{:S(2)}) copy-start(bf16[256,256]{1,0:T(8,128)(2,1)} %wo_ref.1) | copy-start | bytes 393220
  52.6 8.6 %copy-start.14 = (bf16[256]{0:T(256)(128)(2,1)S(1)}, bf16[256]{0:T(256)(128)(2,1)}, u32[]{:S(2)}) copy-start(bf16[256]{0:T(256)(128)(2,1)} %g1_ref.1) | copy-start | bytes 1540
  55.5 20.7 %collective-permute-start.4 = (bf16[4,256,256]{2,1,0:T(8,128)(2,1)}, bf16[4,256,256]{2,1,0:T(8,128)(2,1)}, u32[]{:S(2)}, u32[]{:S(2)}) collective-permute-start(bf16[4,256,256]{2,1,0:T(8,128)(2,1)} %get-tuple-element.127), channel_id=1, source_target_pairs={{0,4},{1,5},{2,6},{3,7},{4,0},{5,1},{6,2},{7,3},{8,12},{9,13},{10,... | collective-permute-start | bytes 1572872 | tf_op jit(solution)/shard_map/ppermute | solution.py:1045
  57.7 18.4 %collective-permute-start.5 = (bf16[4,176,256]{2,1,0:T(8,128)(2,1)}, bf16[4,176,256]{2,1,0:T(8,128)(2,1)}, u32[]{:S(2)}, u32[]{:S(2)}) collective-permute-start(bf16[4,176,256]{2,1,0:T(8,128)(2,1)} %get-tuple-element.128), channel_id=1, source_target_pairs={{0,1},{1,0},{2,3},{3,2},{4,5},{5,4},{6,7},{7,6},{8,9},{9,8},{10,11... | collective-permute-start | bytes 1081352 | tf_op jit(solution)/shard_map/ppermute | solution.py:1040
  59.2 17.0 %collective-permute-start.6 = (bf16[4,176,256]{2,1,0:T(8,128)(2,1)}, bf16[4,176,256]{2,1,0:T(8,128)(2,1)}, u32[]{:S(2)}, u32[]{:S(2)}) collective-permute-start(bf16[4,176,256]{2,1,0:T(8,128)(2,1)} %get-tuple-element.129), channel_id=1, source_target_pairs={{0,2},{1,3},{2,0},{3,1},{4,6},{5,7},{6,4},{7,5},{8,10},{9,11},{10,... | collective-permute-start | bytes 1081352 | tf_op jit(solution)/shard_map/ppermute | solution.py:1040
  60.7 15.5 %collective-permute-start.7 = (bf16[4,176,256]{2,1,0:T(8,128)(2,1)}, bf16[4,176,256]{2,1,0:T(8,128)(2,1)}, u32[]{:S(2)}, u32[]{:S(2)}) collective-permute-start(bf16[4,176,256]{2,1,0:T(8,128)(2,1)} %get-tuple-element.130), channel_id=1, source_target_pairs={{0,3},{1,2},{2,1},{3,0},{4,7},{5,6},{6,5},{7,4},{8,11},{9,10},{10,... | collective-permute-start | bytes 1081352 | tf_op jit(solution)/shard_map/ppermute | solution.py:1040
  76.2 3.6 %collective-permute-start.9 = (bf16[16,160,128]{2,1,0:T(8,128)(2,1)}, bf16[16,160,128]{2,1,0:T(8,128)(2,1)S(1)}, u32[]{:S(2)}, u32[]{:S(2)}) collective-permute-start(bf16[16,160,128]{2,1,0:T(8,128)(2,1)} %get-tuple-element.140), channel_id=1, source_target_pairs={{0,16},{16,0},{1,17},{17,1},{2,18},{18,2},{3,19},{19,3},{4,20},{20... | collective-permute-start | bytes 1966088 | tf_op jit(solution)/shard_map/ppermute | solution.py:1040
  77.8 7.0 %collective-permute-start.8 = (bf16[2,256,256]{2,1,0:T(8,128)(2,1)S(1)}, bf16[2,256,256]{2,1,0:T(8,128)(2,1)S(1)}, u32[]{:S(2)}, u32[]{:S(2)}) collective-permute-start(bf16[2,256,256]{2,1,0:T(8,128)(2,1)S(1)} %get-tuple-element.138), channel_id=1, source_target_pairs={{0,2},{1,3},{2,0},{3,1},{4,6},{5,7},{6,4},{7,5},{8,10},{9,11},{10,... | collective-permute-start | bytes 786440 | tf_op jit(solution)/shard_map/ppermute | solution.py:1045
  79.4 6.6 %collective-permute-start.10 = (bf16[2,176,256]{2,1,0:T(8,128)(2,1)S(1)}, bf16[2,176,256]{2,1,0:T(8,128)(2,1)S(1)}, u32[]{:S(2)}, u32[]{:S(2)}) collective-permute-start(bf16[2,176,256]{2,1,0:T(8,128)(2,1)S(1)} %get-tuple-element.143), channel_id=1, source_target_pairs={{0,4},{1,5},{2,6},{3,7},{4,0},{5,1},{6,2},{7,3},{8,12},{9,13},{10,... | collective-permute-start | bytes 540680 | tf_op jit(solution)/shard_map/ppermute | solution.py:1045
  80.7 8.1 %collective-permute-start.12 = (bf16[4,160,128]{2,1,0:T(8,128)(2,1)}, bf16[4,160,128]{2,1,0:T(8,128)(2,1)S(1)}, u32[]{:S(2)}, u32[]{:S(2)}) collective-permute-start(bf16[4,160,128]{2,1,0:T(8,128)(2,1)} %get-tuple-element.152), channel_id=1, source_target_pairs={{0,1},{1,0},{2,3},{3,2},{4,5},{5,4},{6,7},{7,6},{8,9},{9,8},{10,11... | collective-permute-start | bytes 491528 | tf_op jit(solution)/shard_map/ppermute | solution.py:1040
  82.2 8.3 %collective-permute-start.13 = (bf16[4,160,128]{2,1,0:T(8,128)(2,1)}, bf16[4,160,128]{2,1,0:T(8,128)(2,1)S(1)}, u32[]{:S(2)}, u32[]{:S(2)}) collective-permute-start(bf16[4,160,128]{2,1,0:T(8,128)(2,1)} %get-tuple-element.151), channel_id=1, source_target_pairs={{0,2},{1,3},{2,0},{3,1},{4,6},{5,7},{6,4},{7,5},{8,10},{9,11},{10,... | collective-permute-start | bytes 491528 | tf_op jit(solution)/shard_map/ppermute | solution.py:1040
  82.7 8.8 %collective-permute-start.14 = (bf16[4,160,128]{2,1,0:T(8,128)(2,1)S(1)}, bf16[4,160,128]{2,1,0:T(8,128)(2,1)S(1)}, u32[]{:S(2)}, u32[]{:S(2)}) collective-permute-start(bf16[4,160,128]{2,1,0:T(8,128)(2,1)S(1)} %get-tuple-element.150), channel_id=1, source_target_pairs={{0,3},{1,2},{2,1},{3,0},{4,7},{5,6},{6,5},{7,4},{8,11},{9,10},{10,... | collective-permute-start | bytes 491528 | tf_op jit(solution)/shard_map/ppermute | solution.py:1040
  86.1 15.5 %collective-permute-start.11 = (bf16[432,256]{1,0:T(8,128)(2,1)S(1)}, bf16[432,256]{1,0:T(8,128)(2,1)S(1)}, u32[]{:S(2)}, u32[]{:S(2)}) collective-permute-start(bf16[432,256]{1,0:T(8,128)(2,1)S(1)} %pad_maximum_fusion), channel_id=1, source_target_pairs={{0,8},{1,9},{2,10},{3,11},{4,12},{5,13},{6,14},{7,15},{8,0},{9,1},... | collective-permute-start | bytes 663560 | tf_op jit(solution)/shard_map/ppermute | solution.py:1045
  91.5 6.8 %collective-permute-start.15 = (bf16[160,128]{1,0:T(8,128)(2,1)S(1)}, bf16[160,128]{1,0:T(8,128)(2,1)S(1)}, u32[]{:S(2)}, u32[]{:S(2)}) collective-permute-start(bf16[160,128]{1,0:T(8,128)(2,1)S(1)} %get-tuple-element.149), channel_id=1, source_target_pairs={{0,4},{1,5},{2,6},{3,7},{4,0},{5,1},{6,2},{7,3},{8,12},{9,13},{10,... | collective-permute-start | bytes 122888 | tf_op jit(solution)/shard_map/ppermute | solution.py:1040
  93.1 7.6 %collective-permute-start.16 = (bf16[160,128]{1,0:T(8,128)(2,1)S(1)}, bf16[160,128]{1,0:T(8,128)(2,1)S(1)}, u32[]{:S(2)}, u32[]{:S(2)}) collective-permute-start(bf16[160,128]{1,0:T(8,128)(2,1)S(1)} %get-tuple-element.148), channel_id=1, source_target_pairs={{0,8},{1,9},{2,10},{3,11},{4,12},{5,13},{6,14},{7,15},{8,0},{9,1},... | collective-permute-start | bytes 122888 | tf_op jit(solution)/shard_map/ppermute | solution.py:1040
  95.7 5.9 %collective-permute-start.17 = (bf16[160,128]{1,0:T(8,128)(2,1)S(1)}, bf16[160,128]{1,0:T(8,128)(2,1)S(1)}, u32[]{:S(2)}, u32[]{:S(2)}) collective-permute-start(bf16[160,128]{1,0:T(8,128)(2,1)S(1)} %get-tuple-element.147), channel_id=1, source_target_pairs={{0,12},{1,13},{2,14},{3,15},{4,8},{5,9},{6,10},{7,11},{8,4},{9,5},... | collective-permute-start | bytes 122888 | tf_op jit(solution)/shard_map/ppermute | solution.py:1040
  (1 other events, 5.9 us)

commit v5 on v4

--- a/solution.py
+++ b/solution.py
@@ -21,6 +21,7 @@
 WORD_HEADS = 8
 WORDS = 256
 
+SCHEDULE = "aaaafaaaaaaaaafaaaaaaaaafaaaaafa"
 SPAN = 256
 STEP = 241
 WIDE = 2 * SPAN
@@ -112,6 +113,9 @@
 
 def add_up(out, *parts):
     for i in range(out.shape[0]):
+        if len(parts) == 2:
+            out[i] = parts[0][i] + parts[1][i]
+            continue
         total = parts[0][i].astype(F32)
         for part in parts[1:]:
             total = total + part[i].astype(F32)
@@ -131,20 +135,28 @@
     return jnp.sum(jnp.where(eye(column.shape[0]), column, 0.0), axis=0, keepdims=True)
 
 
-def put(bundle, phase, order, row, value, width, share_rows):
-    low = value.astype(LOW)
-    lanes = bundle.shape[-1]
-    for half in range(2):
-        side = jnp.bitwise_xor(phase, half)
-        for piece in range(max(1, width // lanes)):
-            take = min(width, lanes)
-            cols = low[:, half * width + piece * lanes:half * width + piece * lanes + take]
-            for i in range(value.shape[0] // share_rows):
-                part = cols[i * share_rows:(i + 1) * share_rows]
-                if take < lanes:
+def put(keep, send, phase, order, row, halves, share_rows):
+    width, lanes = halves[0].shape[1], keep.shape[-1]
+    first = phase == 0
+    mine, other = jnp.where(first, halves[0], halves[1]), jnp.where(first, halves[1], halves[0])
+    for out, low, core in ((keep, mine, phase), (send, other, 1 - phase)):
+        for i in range(low.shape[0] // share_rows):
+            at, swapped = order(i, 0), order(i, 1)
+            if at != swapped:
+                at = at + core * (swapped - at)
+            rows = low[i * share_rows:(i + 1) * share_rows]
+            for piece in range(max(1, width // lanes)):
+                part = rows[:, piece * lanes:piece * lanes + min(width, lanes)]
+                if width < lanes:
                     part = jnp.concatenate([part[:share_rows // 2], part[share_rows // 2:]], axis=1)
                 m = part.shape[0]
-                bundle[side, order(i, half), row + piece * share_rows:row + piece * share_rows + m, :] = part
+                out[at, row + piece * share_rows:row + piece * share_rows + m, :] = part
+
+
+def column_halves(value):
+    width = value.shape[1] // 2
+    low = value.astype(LOW)
+    return low[:, :width], low[:, width:]
 
 
 def band(t):
@@ -175,15 +187,15 @@
     table_hbm, g1_hbm, wq_hbm, wk_hbm, wv_hbm, wo_hbm, g2_hbm, up_hbm, down_hbm, proj_hbm,
     wg1_hbm, wwq_hbm, wwk_hbm, wwv_hbm, wwo_hbm, wg2_hbm, wup_hbm, wdown_hbm,
     keptl_hbm, kepts_hbm, keptm_hbm, kepti_hbm, turns_ref,
-    keep_hbm, send_hbm, outk_ref, outs_ref, gain_ref,
+    keep_ref, send_ref, outk_ref, outs_ref, gain_ref,
     q_ref, k_ref, v_ref, probs_ref, mixt_ref, normed_ref, xhat_ref, winv_ref, md_ref, pooled_ref, pa_ref,
     counts_ref, ids_ref, segs_ref,
     table_ref, g1_ref, wq_ref, wk_ref, wv_ref, wo_ref, g2_ref, up_ref, down_ref, proj_ref, wg1_ref, wg2_ref,
     cot, wwq, wwk, wwv, wwo, wup, wdown,
     tab_t, wqkv_t, wo_t, up_t, ids_t, slow, sslope, smid, sinfo, pa, pm, rowinfo, firsts_v, firsts, before_s, act_s, prob_s, found_s,
-    next_s, mid_s, word_s,
-    bundle, actw, slopew,
-    csem, wsem, ksem, osem,
+    mid_s, word_s, old_s,
+    actw, slopew,
+    csem, wsem, ksem,
 ):
     phase = lax.axis_index("phase")
     tiny = [
@@ -269,14 +281,17 @@
 
     found_s[...] = find(jnp.int32(0))
 
-    def copies(b):
+    def copies_one(b):
         slot = lax.rem(b, 2)
         return (
             pltpu.make_async_copy(slow.at[slot], keptl_hbm.at[b], ksem.at[0, slot]),
-            pltpu.make_async_copy(sslope.at[slot], kepts_hbm.at[b], ksem.at[1, slot]),
             pltpu.make_async_copy(smid.at[slot], keptm_hbm.at[b], ksem.at[2, slot]),
             pltpu.make_async_copy(sinfo.at[slot], kepti_hbm.at[b], ksem.at[3, slot]),
         )
+
+    def copies_two(b):
+        slot = lax.rem(b, 2)
+        return (pltpu.make_async_copy(sslope.at[slot], kepts_hbm.at[b], ksem.at[1, slot]),)
 
     def start(copies):
         for c in copies:
@@ -302,103 +317,141 @@
         inv1 = lax.rsqrt(jnp.mean(emb * emb, axis=0, keepdims=True) + epsilon)
         normed = (emb * inv1 * g1).astype(LOW)
         yield
-        qkv = nn(wqkv_t[...], normed).astype(LOW)
-        key_rows = [qkv[CD:2 * CD, u * SPAN:(u + 1) * SPAN].T for u in range(2)]
-        value_t = qkv[2 * CD:]
+        qkv = []
+        for i in range(3):
+            qkv.append(nn(wqkv_t[i * CD:(i + 1) * CD], normed).astype(LOW))
+            yield
+        query_t, key_t, value_t = qkv
+        slow[slot, R_EMB:R_EMB + CD] = emb.astype(LOW)
+        slow[slot, R_Q:R_Q + CD] = query_t
+        slow[slot, R_K:R_K + CD] = key_t
+        key_rows = [key_t[:, u * SPAN:(u + 1) * SPAN].T for u in range(2)]
         word_col = jnp.broadcast_to(jnp.where(word < 0.0, -2.0, word), (8, WIDE)).T[:, 0:1]
         yield
+        scores = []
+        for t in range(4):
+            u, ks, ql = band(t)
+            for pair in range(CHAR_HEADS // 2):
+                fs = slice(pair * 128, pair * 128 + 128)
+                scores.append(nn(key_rows[u][ks, fs], two_heads(query_t[fs, ql])))
+                yield
+        for u in range(2):
+            us = slice(u * SPAN, (u + 1) * SPAN)
+            slow[slot, R_V:R_V + SPAN, us] = value_t[:, us].T
         for t in range(4):
             u, ks, ql = band(t)
             bias = jnp.where(word_col[u * SPAN + ks.start:u * SPAN + ks.stop] == word[:, ql], 0.0, floor_score)
             for pair in range(CHAR_HEADS // 2):
-                fs = slice(pair * 128, pair * 128 + 128)
-                s = nn(key_rows[u][ks, fs], two_heads(qkv[fs, ql]))
+                s = scores[t * 2 + pair]
                 for i in range(2):
                     p = softmax_keys(s[:, i * 128:i * 128 + 128] + bias)
                     row = (pair * 2 + i) * SPAN
                     prob_s[row + ks.start:row + ks.stop, ql] = p
                     slow[slot, R_P + row + ks.start:R_P + row + ks.stop, ql] = p
-                yield
-        slow[slot, R_EMB:R_EMB + CD] = emb.astype(LOW)
-        slow[slot, R_Q:R_Q + 2 * CD] = qkv[:2 * CD]
+        yield
+        mixed = [[], []]
         for u in range(2):
             us = slice(u * SPAN, (u + 1) * SPAN)
-            slow[slot, R_V:R_V + SPAN, us] = value_t[:, us].T
-        mixed = []
-        for h in range(CHAR_HEADS):
-            hs = slice(h * HEAD, (h + 1) * HEAD)
-            both = []
-            for u in range(2):
-                us = slice(u * SPAN, (u + 1) * SPAN)
-                both.append(nn(value_t[hs, us], prob_s[h * SPAN:(h + 1) * SPAN, us]).astype(LOW))
-            mixed.append(jnp.concatenate(both, axis=1))
-        mixed = jnp.concatenate(mixed, axis=0)
+            for h in range(CHAR_HEADS):
+                hs = slice(h * HEAD, (h + 1) * HEAD)
+                mixed[u].append(nn(value_t[hs, us], prob_s[h * SPAN:(h + 1) * SPAN, us]).astype(LOW))
+                yield
+        mixed = jnp.concatenate([jnp.concatenate(part, axis=0) for part in mixed], axis=1)
         slow[slot, R_MIX:R_MIX + CD] = mixed
+        middle = emb + nn(wo_t[...], mixed)
         yield
-        middle = emb + nn(wo_t[...], mixed)
         inv2 = lax.rsqrt(jnp.mean(middle * middle, axis=0, keepdims=True) + epsilon)
         smid[slot] = middle
         sinfo[slot] = jnp.concatenate([inv1, inv2, ident, word, jnp.zeros((4, WIDE), F32)], axis=0)
         normed_two = (middle * inv2 * g2).astype(LOW)
+        middle_low = middle.astype(LOW)
         yield
-        first, _ = near_words(b)
-        near = members(word, first, WINDOW)
-        middle_low = middle.astype(LOW)
-        pm[window(first), :] += nt(near, middle_low)
-        mid_s[...] = middle_low
-        next_s[...] = normed_two
-        word_s[0:1] = word
-        found_s[...] = find(b + 1)
-        yield
+        for c in range(CFF // 256):
+            cs = slice(c * 256, (c + 1) * 256)
+            before_s[cs] = nn(up_t[cs], normed_two)
+            if c == 0:
+                found_s[...] = find(b + 1)
+            if c == 1:
+                first, _ = near_words(b)
+                pm[window(first), :] += nt(members(word, first, WINDOW), middle_low)
+                mid_s[...] = middle_low
+            if c == 3:
+                old_s[0:1] = word_s[0:1]
+                word_s[0:1] = word
+            yield
 
     def feed(b):
         slot = lax.rem(b, 2)
-        word = word_s[0:1]
-        before_s[...] = nn(up_t[...], next_s[...])
-        yield
-        for c in range(CFF // 32):
-            cs = slice(c * 32, (c + 1) * 32)
-            act, slope = gelu_twice(before_s[cs])
-            sslope[slot, cs] = slope.astype(LOW)
-            act_s[cs] = act.astype(LOW)
-            if c % 4 == 3:
-                yield
         first, _ = near_words(b)
-        pa[window(first), :] += nt(members(word, first, WINDOW, 0.5), act_s[...])
-        yield
-
-    def run(*parts):
-        parts = list(parts)
-        while parts:
-            for part in tuple(parts):
-                if next(part, parts) is parts:
-                    parts.remove(part)
+        near = members(word_s[0:1], first, WINDOW, 0.5)
+        for c in range(CFF // 256):
+            for d in range(8):
+                cs = slice(c * 256 + d * 32, c * 256 + (d + 1) * 32)
+                act, slope = gelu_twice(before_s[cs])
+                sslope[slot, cs] = slope.astype(LOW)
+                act_s[cs] = act.astype(LOW)
+            cs = slice(c * 256, (c + 1) * 256)
+            pa[window(first), cs] += nt(near, act_s[cs])
+            yield
+
+    def run(order, one, two):
+        parts = {"a": one, "f": two}
+        for step in order:
+            next(parts[step])
+
+    def more_one(b):
+        first, windows = near_words(b)
+
+        def more(i, carry):
+            at = first + i * WINDOW
+            pm[window(at), :] += nt(members(word_s[0:1], at, WINDOW), mid_s[...])
+            return carry
+
+        lax.fori_loop(1, windows, more, 0)
+
+    def more_two(b, word):
+        first, windows = near_words(b)
+
+        def more(i, carry):
+            at = first + i * WINDOW
+            pa[window(at), :] += nt(members(word[0:1], at, WINDOW, 0.5), act_s[...])
+            return carry
+
+        lax.fori_loop(1, windows, more, 0)
+
+    run("a" * 28, attend(jnp.int32(0)), None)
+    more_one(jnp.int32(0))
+    start(copies_one(jnp.int32(0)))
 
     def turn(b, carry):
         @pl.when(b >= 2)
         def _():
-            wait(copies(b - 2))
-
-        run(attend(b))
-        run(feed(b))
-        first, windows = near_words(b)
-
-        def more(i, carry):
-            at = first + i * WINDOW
-            pm[window(at), :] += nt(members(word_s[0:1], at, WINDOW), mid_s[...])
-            pa[window(at), :] += nt(members(word_s[0:1], at, WINDOW, 0.5), act_s[...])
-            return carry
-
-        lax.fori_loop(1, windows, more, 0)
-        start(copies(b))
+            wait(copies_one(b - 2))
+
+        @pl.when(b >= 3)
+        def _():
+            wait(copies_two(b - 3))
+
+        run(SCHEDULE, attend(b), feed(b - 1))
+        more_one(b)
+        more_two(b - 1, old_s)
+        start(copies_one(b))
+        start(copies_two(b - 1))
         return carry
 
-    lax.fori_loop(0, n_turns, turn, 0)
+    lax.fori_loop(1, n_turns, turn, 0)
+
+    @pl.when(n_turns >= 3)
+    def _():
+        wait(copies_two(n_turns - 3))
+
+    run("f" * 4, None, feed(n_turns - 1))
+    more_two(n_turns - 1, word_s)
+    start(copies_two(n_turns - 1))
 
     pa_hi = pa[0:WORDS].astype(LOW)
-    pa_lo = (pa[0:WORDS] - pa_hi.astype(F32)).astype(LOW)
     per_count = 1.0 / counts
-    pooled = (pm[0:WORDS] + nn(pa_hi, down_ref[...]) + nn(pa_lo, down_ref[...])) * per_count
+    pooled = (pm[0:WORDS] + nn(pa_hi, down_ref[...])) * per_count
     pooled_low = pooled.astype(LOW)
     pooled_ref[...] = pooled_low
     pa_ref[...] = pa_hi
@@ -426,16 +479,17 @@
     v_t = v.T
     for h in range(WORD_HEADS):
         probs_ref[h, 128:, 0:128] = jnp.zeros((128, 128), LOW)
-    for t in range(2):
-        ks, ql = slice(0, 128 * (t + 1)), slice(128 * t, 128 * (t + 1))
-        for pair in range(WORD_HEADS // 2):
-            fs = slice(pair * 128, pair * 128 + 128)
-            s = nt(k[ks, fs], two_heads_rows(q[ql, fs]))
+    halves = [(slice(0, 128 * (t + 1)), slice(128 * t, 128 * (t + 1))) for t in range(2)]
+    pairs = [slice(pair * 128, pair * 128 + 128) for pair in range(WORD_HEADS // 2)]
+    scores = [[nt(k[ks, fs], two_heads_rows(q[ql, fs])) for ks, ql in halves] for fs in pairs]
+    mixed_t = []
+    for pair in range(WORD_HEADS // 2):
+        for (ks, ql), s in zip(halves, scores[pair]):
             for i in range(2):
                 probs_ref[pair * 2 + i, ks, ql] = softmax_keys(s[:, i * 128:i * 128 + 128] + bias[ks, ql])
-    mixed_t = jnp.concatenate(
-        [nn(v_t[h * HEAD:(h + 1) * HEAD], probs_ref[h]).astype(LOW) for h in range(WORD_HEADS)], axis=0
-    )
+        for h in (pair * 2, pair * 2 + 1):
+            mixed_t.append(nn(v_t[h * HEAD:(h + 1) * HEAD], probs_ref[h]).astype(LOW))
+    mixed_t = jnp.concatenate(mixed_t, axis=0)
     mixt_ref[...] = mixed_t
     middle = x + nn(mixed_t.T, wwo[...])
     winv2 = lax.rsqrt(jnp.mean(middle * middle, axis=1, keepdims=True) + epsilon)
@@ -456,43 +510,35 @@
     cot_low = cot[...]
     n2d = jnp.zeros((WORDS, WD), F32)
     n2_t = normed_two.T
-    for c in range(WFF // 512):
+    held = {}
+    for c in (0, 2, 1, 3):
         cs = slice(c * 512, (c + 1) * 512)
         gd = nn(actw[:, cs].T, cot_low)
-        put(bundle, phase, lambda i, p: feed_order(c * 4 + i, p), F_DOWN, gd, 256, 128)
+        put(keep_ref, send_ref, phase, lambda i, p: feed_order(c * 4 + i, p), F_DOWN, column_halves(gd), 128)
         bd = (nt(cot_low, wdown[cs, :]) * slopew[:, cs].astype(F32)).astype(LOW)
         gu = nn(n2_t, bd).astype(LOW)
-        side = jnp.bitwise_xor(phase, c // 2)
-        for piece in range(2):
-            row = F_UP + ((c % 2) * 2 + piece) * 32
-            for d in range(SHARES):
-                bundle[side, feed_order(d, c // 2), row:row + 32, :] = gu[d * 32:(d + 1) * 32, piece * 256:piece * 256 + 256]
+        if c < 2:
+            held[c] = gu
+        else:
+            put(keep_ref, send_ref, phase, feed_order, F_UP + (c - 2) * 64, (held[c - 2], gu), 32)
         n2d = n2d + nt(bd, wup[:, cs])
-    stores = [
-        pltpu.make_async_copy(bundle.at[0], keep_hbm, osem.at[0]),
-        pltpu.make_async_copy(bundle.at[1], send_hbm, osem.at[1]),
-    ]
-    for s in stores:
-        s.start()
     vhat = middle * winv2
     gain_ref[...] = jnp.broadcast_to(jnp.sum(n2d * vhat, axis=0, keepdims=True), (8, WD))
     lifted = n2d * wg2
     md_ref[...] = cot[...].astype(F32) + winv2 * (lifted - vhat * jnp.mean(lifted * vhat, axis=1, keepdims=True))
 
     def drain(b, carry):
-        wait(copies(b))
+        wait(copies_one(b))
+        wait(copies_two(b))
         return carry
 
     lax.fori_loop(jnp.maximum(n_turns - 2, 0), n_turns, drain, 0)
-    for s in stores:
-        s.wait()
 
 
 def kernel_a2(
     counts_ref, q_ref, k_ref, v_ref, pw, mixt_ref, normed_ref, xhat_ref, winv_ref, md_ref, pooled_ref, pa_ref,
     wg1_ref, proj_ref, wwq, wwk, wwv, wwo,
-    gw_ref, keep_hbm, send_hbm, gain_ref,
-    bundle, osem,
+    gw_ref, keep_ref, send_ref, gain_ref,
 ):
     phase = lax.axis_index("phase")
     wg1 = wg1_ref[...].astype(F32)[None, :]
@@ -500,62 +546,61 @@
     per_count = 1.0 / row_to_column(counts_ref[phase].astype(F32))
     md = md_ref[...]
     md_low = md.astype(LOW)
-    put(bundle, phase, word_order, T_O, nn(mixt_ref[...], md_low), 256, 32)
+    put(keep_ref, send_ref, phase, word_order, T_O, column_halves(nn(mixt_ref[...], md_low)), 32)
     k_t = k.T
     do = nt(md_low, wwo[...]).astype(LOW)
     dq_t, dk, dv = [], [], []
     left = iota((WORDS, 128), 1) < HEAD
-    for pair in range(WORD_HEADS // 2):
-        fs = slice(pair * 128, pair * 128 + 128)
+    pairs = [slice(pair * 128, pair * 128 + 128) for pair in range(WORD_HEADS // 2)]
+    halves = [(slice(0, 128 * (t + 1)), slice(128 * t, 128 * (t + 1))) for t in range(2)]
+    deltas = [[nt(v[ks, fs], two_heads_rows(do[ql, fs])) for ks, ql in halves] for fs in pairs]
+
+    def scores(pair):
         ds = []
-        for t in range(2):
-            ks, ql = slice(0, 128 * (t + 1)), slice(128 * t, 128 * (t + 1))
-            dp = nt(v[ks, fs], two_heads_rows(do[ql, fs]))
+        for (ks, ql), dp in zip(halves, deltas[pair]):
             for i in range(2):
                 pf = pw[pair * 2 + i, ks, ql].astype(F32)
                 dph = dp[:, i * 128:i * 128 + 128]
                 d = (pf * (dph - jnp.sum(pf * dph, axis=0, keepdims=True))).astype(LOW)
-                ds.append(d if t else jnp.concatenate([d, jnp.zeros((128, 128), LOW)], axis=0))
-        both = [jnp.concatenate([ds[i], ds[i + 2]], axis=1) for i in range(2)]
-        for i in range(2):
-            h = pair * 2 + i
-            dq_t.append(nn(k_t[h * HEAD:(h + 1) * HEAD], both[i]))
-        dk.append(jnp.where(left, nn(both[0], q[:, fs]), nn(both[1], q[:, fs])).astype(LOW))
-        dv.append(jnp.where(left, nn(pw[pair * 2], do[:, fs]), nn(pw[pair * 2 + 1], do[:, fs])).astype(LOW))
+                ds.append(d if ks.stop == WORDS else jnp.concatenate([d, jnp.zeros((128, 128), LOW)], axis=0))
+        return [jnp.concatenate([ds[i], ds[i + 2]], axis=1) for i in range(2)]
+
+    both = None
+    for pair in range(WORD_HEADS // 2 + 1):
+        ahead = scores(pair) if pair < WORD_HEADS // 2 else None
+        if ahead is not None:
+            fs = pairs[pair]
+            dv.append(jnp.where(left, nn(pw[pair * 2], do[:, fs]), nn(pw[pair * 2 + 1], do[:, fs])).astype(LOW))
+        if both is not None:
+            fs = pairs[pair - 1]
+            for i in range(2):
+                h = (pair - 1) * 2 + i
+                dq_t.append(nn(k_t[h * HEAD:(h + 1) * HEAD], both[i]))
+            dk.append(jnp.where(left, nn(both[0], q[:, fs]), nn(both[1], q[:, fs])).astype(LOW))
+        both = ahead
     dq = (jnp.concatenate(dq_t, axis=0) * 0.125).astype(LOW).T
     dk = jnp.concatenate(dk, axis=1)
     dv = jnp.concatenate(dv, axis=1)
     normed_t = normed.T
     nd = nt(dq, wwq[...]) + nt(dk, wwk[...]) + nt(dv, wwv[...])
-    put(bundle, phase, word_order, T_Q, nn(normed_t, dq), 256, 32)
-    put(bundle, phase, word_order, T_K, nn(normed_t, dk), 256, 32)
-    put(bundle, phase, word_order, T_V, nn(normed_t, dv), 256, 32)
-    stores = [
-        pltpu.make_async_copy(bundle.at[side, :, rows], out.at[:, rows], osem.at[i, side])
-        for i, rows in enumerate((pl.ds(0, T_CDOWN), pl.ds(T_CDOWN, T_ROWS - T_CDOWN)))
-        for side, out in enumerate((keep_hbm, send_hbm))
-    ]
-    for store in stores[:2]:
-        store.start()
+    put(keep_ref, send_ref, phase, word_order, T_Q, column_halves(nn(normed_t, dq)), 32)
+    put(keep_ref, send_ref, phase, word_order, T_K, column_halves(nn(normed_t, dk)), 32)
+    put(keep_ref, send_ref, phase, word_order, T_V, column_halves(nn(normed_t, dv)), 32)
     vhat = xhat_ref[...]
     gain_ref[...] = jnp.broadcast_to(jnp.sum(nd * vhat, axis=0, keepdims=True), (8, WD))
     lifted = nd * wg1
     xd = md + winv_ref[:, 0:1] * (lifted - vhat * jnp.mean(lifted * vhat, axis=1, keepdims=True))
     vd = xd.astype(LOW)
-    put(bundle, phase, word_order, T_PROJ, nn(pooled_low.T, vd), 256, 16)
+    put(keep_ref, send_ref, phase, word_order, T_PROJ, column_halves(nn(pooled_low.T, vd)), 16)
     gw = (nt(vd, proj_ref[...]) * per_count).astype(LOW)
     gw_ref[...] = gw.T
-    put(bundle, phase, word_order, T_CDOWN, nn(pa_ref[...].T, gw), 128, 64)
-    for store in stores[2:]:
-        store.start()
-    for store in stores:
-        store.wait()
+    put(keep_ref, send_ref, phase, word_order, T_CDOWN, column_halves(nn(pa_ref[...].T, gw)), 64)
 
 
 def kernel_b1(
-    turns_ref, gw_ref, g2_ref, up_ref, down_ref, kepts_hbm, keptm_hbm, kepti_hbm, f0_hbm, f1_hbm,
+    turns_ref, gw_ref, g2_ref, up_ref, down_ref, kepts_hbm, keptm_hbm, kepti_hbm, f0_ref, f1_hbm,
     keptd_hbm, aup_ref, gain_ref, facc_ref,
-    sslope, smid, sinfo, sdelta, aup, ag2, down, f0, f1, ksem, dsem, fsem,
+    sslope, smid, sinfo, sdelta, aup, ag2, down, f1, ksem, dsem, fsem,
 ):
     n_turns = turns_ref[0]
 
@@ -572,12 +617,8 @@
     for c in kept_copies(0, 0):
         c.start()
     a, _, _, _ = own_bits()
-    loads = [
-        pltpu.make_async_copy(src.at[pl.ds(a * 8, 8)], dst, fsem.at[i])
-        for i, (src, dst) in enumerate(((f0_hbm, f0), (f1_hbm, f1)))
-    ]
-    for load in loads:
-        load.start()
+    load = pltpu.make_async_copy(f1_hbm.at[pl.ds(a * 8, 8)], f1, fsem.at[0])
+    load.start()
     g2 = row_to_column(g2_ref[...].astype(F32)[None, :])
     down[...] = down_ref[...] * 0.5
     aup[...] = jnp.zeros_like(aup)
@@ -616,9 +657,8 @@
 
     lax.fori_loop(0, n_turns, turn, 0)
     aup_ref[...] = aup[...].astype(LOW)
-    for load in loads:
-        load.wait()
-    add_up(facc_ref, f0, f1)
+    load.wait()
+    add_up(facc_ref, f0_ref.at[pl.ds(a * 8, 8)], f1)
     gain_ref[...] = jnp.broadcast_to(jnp.sum(ag2[...], axis=1, keepdims=True), (CD, 8)).T
 
     def drain(b, carry):
@@ -630,9 +670,9 @@
 
 def kernel_b2(
     turns_ref, wgain1_ref, wgain2_ref, gain2_ref, aup_ref, g1_ref, wq_ref, wk_ref, wv_ref, wo_ref,
-    keptl_hbm, keptd_hbm, kepti_hbm, facc_ref, f2_hbm, t0_hbm, t1_hbm,
+    keptl_hbm, keptd_hbm, kepti_hbm, facc_ref, f2_hbm, t0_ref, t1_hbm,
     keep_ref, send_ref, fnext_ref, tacc_ref,
-    slow, sinfo, sdelta, dscore, wqkv, aqkv, ao, atab, ag1, bundle, f2, t0, t1, ksem, fsem,
+    slow, sinfo, sdelta, dscore, wqkv, aqkv, ao, atab, ag1, f2, t1, ksem, fsem,
 ):
     phase = lax.axis_index("phase")
     n_turns = turns_ref[0]
@@ -650,7 +690,7 @@
     quarter = pl.ds(own_plane() * 4, 4)
     loads = [
         pltpu.make_async_copy(src.at[at], dst, fsem.at[i])
-        for i, (src, at, dst) in enumerate(((f2_hbm, pl.ds(low * 4, 4), f2), (t0_hbm, quarter, t0), (t1_hbm, quarter, t1)))
+        for i, (src, at, dst) in enumerate(((f2_hbm, pl.ds(low * 4, 4), f2), (t1_hbm, quarter, t1)))
     ]
     for load in loads:
         load.start()
@@ -673,44 +713,49 @@
         inv1 = sinfo[slot, I_INV1:I_INV1 + 1]
         ident = sinfo[slot, I_IDENT:I_IDENT + 1]
         md_low = sdelta[slot]
-        ao[...] += nt(slow[slot, R_MIX:R_MIX + CD], md_low)
         do = nn(wo_ref[...], md_low).astype(LOW)
+        emb = slow[slot, R_EMB:R_EMB + CD].astype(F32)
+        ehat = emb * inv1
+        normed = (ehat * g1).astype(LOW)
+        hot = jnp.where(iota((CVOC, WIDE), 0).astype(F32) == ident, 1.0, 0.0).astype(LOW)
+        deltas = []
         for t in range(4):
             u, ks, ql = band(t)
             for pair in range(CHAR_HEADS // 2):
                 fs = slice(u * SPAN + pair * 128, u * SPAN + pair * 128 + 128)
-                dp = nn(
+                deltas.append(nn(
                     slow[slot, R_V + ks.start:R_V + ks.stop, fs], two_heads(do[pair * 128:pair * 128 + 128, ql])
-                )
+                ))
+        dq, dk, dv = ([[None, None] for _ in range(CHAR_HEADS)] for _ in range(3))
+        for t in range(4):
+            u, ks, ql = band(t)
+            for pair in range(CHAR_HEADS // 2):
+                dp = deltas[t * 2 + pair]
                 for i in range(2):
                     row = (pair * 2 + i) * SPAN
                     pf = slow[slot, R_P + row + ks.start:R_P + row + ks.stop, ql].astype(F32)
                     dph = dp[:, i * 128:i * 128 + 128]
                     d = pf * (dph - jnp.sum(pf * dph, axis=0, keepdims=True))
                     dscore[row + ks.start:row + ks.stop, ql] = d.astype(LOW)
-        dq, dk, dv = [], [], []
+                h, v = (t % 2) * 2 + pair, t // 2
+                vs = slice(v * SPAN, (v + 1) * SPAN)
+                dv[h][v] = nt(do[h * HEAD:(h + 1) * HEAD, vs], slow[slot, R_P + h * SPAN:R_P + (h + 1) * SPAN, vs]).astype(LOW)
         for h in range(CHAR_HEADS):
-            hs = slice(h * HEAD, (h + 1) * HEAD)
-            one, two, three = [], [], []
             for u in range(2):
                 us = slice(u * SPAN, (u + 1) * SPAN)
-                p = slow[slot, R_P + h * SPAN:R_P + (h + 1) * SPAN, us]
                 ds = dscore[h * SPAN:(h + 1) * SPAN, us]
-                one.append((nn(slow[slot, R_K + h * HEAD:R_K + (h + 1) * HEAD, us], ds) * 0.125).astype(LOW))
-                two.append(nt(slow[slot, R_Q + h * HEAD:R_Q + (h + 1) * HEAD, us], ds).astype(LOW))
-                three.append(nt(do[hs, us], p).astype(LOW))
-            for part, pair in ((dq, one), (dk, two), (dv, three)):
-                part.append(jnp.concatenate(pair, axis=1))
-        dqkv = jnp.concatenate(dq + dk + dv, axis=0)
-        emb = slow[slot, R_EMB:R_EMB + CD].astype(F32)
-        ehat = emb * inv1
-        normed = (ehat * g1).astype(LOW)
-        aqkv[...] += nt(normed, dqkv)
+                dq[h][u] = (nn(slow[slot, R_K + h * HEAD:R_K + (h + 1) * HEAD, us], ds) * 0.125).astype(LOW)
+                dk[h][u] = nt(slow[slot, R_Q + h * HEAD:R_Q + (h + 1) * HEAD, us], ds).astype(LOW)
+        dqkv = jnp.concatenate([jnp.concatenate(pair, axis=1) for part in (dq, dk, dv) for pair in part], axis=0)
         nd = nn(wqkv[...], dqkv)
+        aqkv[:, 0:CD] += nt(normed, dqkv[0:CD])
         ag1[...] += nd * ehat
         lifted = nd * g1
-        ed = md_low.astype(F32) + inv1 * (lifted - ehat * jnp.mean(lifted * ehat, axis=0, keepdims=True))
-        hot = jnp.where(iota((CVOC, WIDE), 0).astype(F32) == ident, 1.0, 0.0).astype(LOW)
+        aqkv[:, CD:2 * CD] += nt(normed, dqkv[CD:2 * CD])
+        mean = jnp.mean(lifted * ehat, axis=0, keepdims=True)
+        aqkv[:, 2 * CD:] += nt(normed, dqkv[2 * CD:])
+        ed = md_low.astype(F32) + inv1 * (lifted - ehat * mean)
+        ao[...] += nt(slow[slot, R_MIX:R_MIX + CD], md_low)
         atab[...] += nt(hot, ed.astype(LOW))
         return carry
 
@@ -719,13 +764,13 @@
     for load in loads:
         load.wait()
     add_up(fnext_ref, facc_ref.at[pl.ds(low * 4, 4)], f2)
-    add_up(tacc_ref, t0, t1)
-    put(bundle, phase, plane_first, C_TABLE, atab[...], 128, 16)
-    put(bundle, phase, plane_first, C_Q, aqkv[:, 0:CD], 128, 16)
-    put(bundle, phase, plane_first, C_K, aqkv[:, CD:2 * CD], 128, 16)
-    put(bundle, phase, plane_first, C_V, aqkv[:, 2 * CD:], 128, 16)
-    put(bundle, phase, plane_first, C_O, ao[...], 128, 16)
-    put(bundle, phase, plane_first, C_UP, aup_ref[...], 512, 16)
+    add_up(tacc_ref, t0_ref.at[quarter], t1)
+    put(keep_ref, send_ref, phase, plane_first, C_TABLE, column_halves(atab[...]), 16)
+    put(keep_ref, send_ref, phase, plane_first, C_Q, column_halves(aqkv[:, 0:CD]), 16)
+    put(keep_ref, send_ref, phase, plane_first, C_K, column_halves(aqkv[:, CD:2 * CD]), 16)
+    put(keep_ref, send_ref, phase, plane_first, C_V, column_halves(aqkv[:, 2 * CD:]), 16)
+    put(keep_ref, send_ref, phase, plane_first, C_O, column_halves(ao[...]), 16)
+    put(keep_ref, send_ref, phase, plane_first, C_UP, column_halves(aup_ref[...]), 16)
     cg1 = jnp.broadcast_to(jnp.sum(ag1[...], axis=1, keepdims=True), (CD, 8)).T[0:1]
     cg2 = gain2_ref[0:1]
     for d in range(SHARES):
@@ -737,39 +782,37 @@
             jnp.zeros((12, 128), F32),
         ]
         tile = jnp.concatenate(rows, axis=0).astype(LOW)
-        bundle[0, plane_first(d), C_GAIN:C_GAIN + 16, :] = tile
-        bundle[1, plane_first(d), C_GAIN:C_GAIN + 16, :] = tile
-    keep_ref[...] = bundle[0]
-    send_ref[...] = bundle[1]
-
-
-def kernel_add_one(f0_hbm, f1_hbm, send_ref, one, two, sem):
+        keep_ref[plane_first(d), C_GAIN:C_GAIN + 16, :] = tile
+        send_ref[plane_first(d), C_GAIN:C_GAIN + 16, :] = tile
+
+
+def kernel_add_one(f0_ref, f1_hbm, send_ref, f1, sem):
     a, _, _, _ = own_bits()
-    other = pl.ds((1 - a) * 8, 8)
-    loads = [pltpu.make_async_copy(src.at[other], dst, sem.at[i]) for i, (src, dst) in enumerate(((f0_hbm, one), (f1_hbm, two)))]
+    loads = [
+        pltpu.make_async_copy(f1_hbm.at[pl.ds((1 - a) * 8 + i, 2)], f1.at[pl.ds(i, 2)], sem.at[i // 2]) for i in range(0, 8, 2)
+    ]
     for load in loads:
         load.start()
-    for load in loads:
+    for i, load in enumerate(loads):
         load.wait()
-    add_up(send_ref, one, two)
-
-
-def kernel_add_two(facc_ref, f2_hbm, t0_hbm, t1_hbm, fsend_ref, ts1_ref, ts2_ref, ts3_ref, f2, t0, t1, sem):
+        at = pl.ds(i * 2, 2)
+        add_up(send_ref.at[at], f0_ref.at[pl.ds((1 - a) * 8 + i * 2, 2)], f1.at[at])
+
+
+def kernel_add_two(facc_ref, f2_hbm, t0_ref, t1_hbm, fsend_ref, ts1_ref, ts2_ref, ts3_ref, f2, t1, sem):
     _, _, low, _ = own_bits()
     half = pl.ds((1 - low) * 4, 4)
     loads = [pltpu.make_async_copy(f2_hbm.at[half], f2, sem.at[0])]
-    for k in range(1, 4):
-        at = pl.ds(lax.bitwise_xor(own_plane(), k) * 4, 4)
-        for i, (src, dst) in enumerate(((t0_hbm, t0), (t1_hbm, t1))):
-            loads.append(pltpu.make_async_copy(src.at[at], dst.at[k - 1], sem.at[1 + i]))
+    places = [pl.ds(lax.bitwise_xor(own_plane(), k) * 4, 4) for k in range(1, 4)]
+    for k, at in enumerate(places):
+        loads.append(pltpu.make_async_copy(t1_hbm.at[at], t1.at[k], sem.at[1 + k]))
     for load in loads:
         load.start()
     loads[0].wait()
     add_up(fsend_ref, facc_ref.at[half], f2)
-    for load in loads[1:]:
-        load.wait()
     for k, out in enumerate((ts1_ref, ts2_ref, ts3_ref)):
-        add_up(out, t0.at[k], t1.at[k])
+        loads[1 + k].wait()
+        add_up(out, t0_ref.at[places[k]], t1.at[k])
 
 
 def kernel_add_three(
@@ -794,34 +837,26 @@
     f3, f4, t2, t3, last, c0, c1, c2, c3, c4, c5, c6, c7, outk, outg,
     word_out, d_table, d_g1, d_q, d_k, d_v, d_o, d_g2, d_up, d_down, d_proj,
     e_g1, e_q, e_k, e_v, e_o, e_g2, e_up, e_down,
-    fs, ts, cs, sem,
 ):
     phase = lax.axis_index("phase")
     dp = lax.axis_index("dp")
     _, _, low, high = own_bits()
-    loads = []
     line = lax.div(dp, 4)
     place = lax.rem(dp, 4) * 4 + line
-    for i, (parts, places, here) in enumerate((
-        ((f3, f4, last), (high, high, pl.ds(0, F_ROWS)), fs),
-        ((t2, t3, last), (high, high, pl.ds(F_ROWS, T_ROWS)), ts),
-        ((c0, c1, c2, c3, c4), (place, place, line, line, line), cs),
-    )):
-        for j, (part, n) in enumerate(zip(parts, places)):
-            loads.append(pltpu.make_async_copy(part.at[n], here.at[j], sem.at[i]))
-    for j, part in enumerate((c5, c6, c7)):
-        loads.append(pltpu.make_async_copy(part, cs.at[5 + j], sem.at[2]))
-    for load in loads:
-        load.start()
+    fs = ((f3, high), (f4, high), (last, 0))
+    ts = ((t2, high), (t3, high), (last, F_ROWS))
+    cs = ((c0, place), (c1, place), (c2, line), (c3, line), (c4, line), (c5, None), (c6, None), (c7, None))
     word_out[phase, 0] = outk[...]
     word_out[1 - phase, 0] = outg[...]
-    for load in loads:
-        load.wait()
 
     def total(parts, row, n):
-        t = parts[0, row:row + n].astype(F32) + parts[1, row:row + n].astype(F32)
-        for j in range(2, parts.shape[0]):
-            t = t + parts[j, row:row + n].astype(F32)
+        t = None
+        for part, at in parts:
+            if part is last:
+                piece = part[at + row:at + row + n]
+            else:
+                piece = part[row:row + n] if at is None else part[at, row:row + n]
+            t = piece.astype(F32) if t is None else t + piece.astype(F32)
         return t
 
     f, t, c = partial(total, fs), partial(total, ts), partial(total, cs)
@@ -877,8 +912,8 @@
             outside((TURNS, CD, WIDE), F32),
             outside((TURNS, 8, WIDE), F32),
             shape((1,), jnp.int32),
-            outside((SHARES, F_ROWS, 256), LOW),
-            outside((SHARES, F_ROWS, 256), LOW),
+            v((SHARES, F_ROWS, 256), LOW),
+            v((SHARES, F_ROWS, 256), LOW),
             shape((WORDS, WD // 2), LOW),
             shape((WORDS, WD // 2), LOW),
             shape((8, WD), F32),
@@ -888,7 +923,7 @@
             shape((WORDS, CD), LOW), shape((WORDS, CFF), LOW),
         ),
         in_specs=[ANYWHERE] * 22,
-        out_specs=(ANYWHERE,) * 4 + (SCALARS,) + (ANYWHERE,) * 2 + (INSIDE,) * 14,
+        out_specs=(ANYWHERE,) * 4 + (SCALARS,) + (INSIDE,) * 16,
         scratch_shapes=[
             v((1, WORDS), jnp.int32), v((1, WORDS * CPW), jnp.int32), v((1, WORDS), jnp.int32),
             v((CVOC, CD), LOW), v((CD,), LOW), v((CD, CD), LOW), v((CD, CD), LOW), v((CD, CD), LOW), v((CD, CD), LOW),
@@ -901,13 +936,11 @@
             v((WORDS + WINDOW, CFF), F32), v((WORDS + WINDOW, CD), F32), v((16, WORDS), LOW),
             v((8, 128), jnp.int32), pltpu.SMEM((8, 128), jnp.int32),
             v((CFF, WIDE), F32), v((CFF, WIDE), LOW), v((CHAR_HEADS * SPAN, WIDE), LOW), v((8, WIDE), F32),
-            v((CD, WIDE), LOW), v((CD, WIDE), LOW), v((8, WIDE), F32),
-            v((2, SHARES, F_ROWS, 256), LOW),
+            v((CD, WIDE), LOW), v((8, WIDE), F32), v((8, WIDE), F32),
             v((WORDS, WFF), LOW), v((WORDS, WFF), LOW),
             pltpu.SemaphoreType.DMA((15,)),
             pltpu.SemaphoreType.DMA((8,)),
             pltpu.SemaphoreType.DMA((4, 2)),
-            pltpu.SemaphoreType.DMA((2,)),
         ],
         compiler_params=params(44),
         cost_estimate=pl.CostEstimate(flops=200 * 10**9, bytes_accessed=60 * 10**6, transcendentals=10**6),
@@ -921,16 +954,12 @@
         kernel_a2,
         out_shape=(
             shape((CD, WORDS), LOW),
-            outside((SHARES, T_ROWS, 256), LOW),
-            outside((SHARES, T_ROWS, 256), LOW),
+            v((SHARES, T_ROWS, 256), LOW),
+            v((SHARES, T_ROWS, 256), LOW),
             shape((8, WD), F32),
         ),
         in_specs=[INSIDE] * 18,
-        out_specs=(INSIDE, ANYWHERE, ANYWHERE, INSIDE),
-        scratch_shapes=[
-            v((2, SHARES, T_ROWS, 256), LOW),
-            pltpu.SemaphoreType.DMA((2, 2)),
-        ],
+        out_specs=(INSIDE,) * 4,
         compiler_params=params(20),
         cost_estimate=pl.CostEstimate(flops=200 * 10**9, bytes_accessed=10 * 10**6, transcendentals=10**6),
         name="word_attention_backward",
@@ -942,20 +971,20 @@
     return pl.pallas_call(
         kernel_b1,
         out_shape=(outside((TURNS, CD, WIDE), LOW), shape((CD, CFF), LOW), shape((8, CD), F32), v((8, F_ROWS, 256), LOW)),
-        in_specs=[SCALARS] + [INSIDE] * 4 + [ANYWHERE] * 5,
+        in_specs=[SCALARS] + [INSIDE] * 4 + [ANYWHERE] * 3 + [INSIDE, ANYWHERE],
         out_specs=(ANYWHERE, INSIDE, INSIDE, INSIDE),
         scratch_shapes=[
             v((2, CFF, WIDE), LOW), v((2, CD, WIDE), F32), v((2, 8, WIDE), F32), v((2, CD, WIDE), LOW),
             v((CD, CFF), F32), v((CD, WIDE), F32), v((CFF, CD), LOW),
-            v((8, F_ROWS, 256), LOW), v((8, F_ROWS, 256), LOW),
+            v((8, F_ROWS, 256), LOW),
             pltpu.SemaphoreType.DMA((3, 2)),
             pltpu.SemaphoreType.DMA((2,)),
-            pltpu.SemaphoreType.DMA((2,)),
+            pltpu.SemaphoreType.DMA((1,)),
         ],
         compiler_params=params(18),
         cost_estimate=pl.CostEstimate(flops=200 * 10**9, bytes_accessed=20 * 10**6, transcendentals=10**6),
         name="character_backward_one",
-    )(turns, gw, gain, up, down, *kept_outside(kepts, keptm, kepti, f0, f1))
+    )(turns, gw, gain, up, down, *kept_outside(kepts, keptm, kepti), f0, *kept_outside(f1))
 
 
 def call_b2(turns, wgain1, wgain2, gain2, aup, weights, keptl, keptd, kepti, facc, f2, t0, t1):
@@ -965,22 +994,21 @@
         out_shape=(
             v((SHARES, C_ROWS, 128), LOW), v((SHARES, C_ROWS, 128), LOW), v((4, F_ROWS, 256), LOW), v((4, T_ROWS, 256), LOW)
         ),
-        in_specs=[SCALARS] + [INSIDE] * 9 + [ANYWHERE] * 3 + [INSIDE] + [ANYWHERE] * 3,
+        in_specs=[SCALARS] + [INSIDE] * 9 + [ANYWHERE] * 3 + [INSIDE, ANYWHERE] * 2,
         out_specs=(INSIDE,) * 4,
         scratch_shapes=[
             v((2, KEPT_LOW, WIDE), LOW), v((2, 8, WIDE), F32), v((2, CD, WIDE), LOW),
             v((CHAR_HEADS * SPAN, WIDE), LOW),
             v((CD, 3 * CD), LOW),
             v((CD, 3 * CD), F32), v((CD, CD), F32), v((CVOC, CD), F32), v((CD, WIDE), F32),
-            v((2, SHARES, C_ROWS, 128), LOW),
-            v((4, F_ROWS, 256), LOW), v((4, T_ROWS, 256), LOW), v((4, T_ROWS, 256), LOW),
+            v((4, F_ROWS, 256), LOW), v((4, T_ROWS, 256), LOW),
             pltpu.SemaphoreType.DMA((3, 2)),
-            pltpu.SemaphoreType.DMA((3,)),
+            pltpu.SemaphoreType.DMA((2,)),
         ],
         compiler_params=params(24),
         cost_estimate=pl.CostEstimate(flops=200 * 10**9, bytes_accessed=40 * 10**6, transcendentals=10**6),
         name="character_backward_two",
-    )(turns, wgain1, wgain2, gain2, aup, *weights, *kept_outside(keptl, keptd, kepti), facc, *kept_outside(f2, t0, t1))
+    )(turns, wgain1, wgain2, gain2, aup, *weights, *kept_outside(keptl, keptd, kepti), facc, *kept_outside(f2), t0, *kept_outside(t1))
 
 
 def call_add(kernel, name, outs, parts, specs, scratch):
@@ -990,7 +1018,7 @@
         out_shape=tuple(v(s, LOW) for s in outs),
         in_specs=specs,
         out_specs=(INSIDE,) * len(outs),
-        scratch_shapes=[v(s, LOW) for s in scratch] + [pltpu.SemaphoreType.DMA((len(scratch),))],
+        scratch_shapes=[v(s, LOW) for s in scratch] + [pltpu.SemaphoreType.DMA((4,))],
         compiler_params=params(12),
         name=name,
     )(*parts)
@@ -998,14 +1026,14 @@
 
 def add_one(f0, f1):
     half = (8, F_ROWS, 256)
-    return call_add(kernel_add_one, "add_one", (half,), kept_outside(f0, f1), [ANYWHERE] * 2, (half, half))[0]
+    return call_add(kernel_add_one, "add_one", (half,), (f0, *kept_outside(f1)), [INSIDE, ANYWHERE], (half,))[0]
 
 
 def add_two(facc, f2, t0, t1):
     fs, ts = (4, F_ROWS, 256), (4, T_ROWS, 256)
     return call_add(
-        kernel_add_two, "add_two", (fs, ts, ts, ts), (facc, *kept_outside(f2, t0, t1)), [INSIDE] + [ANYWHERE] * 3,
-        (fs, (3,) + ts, (3,) + ts),
+        kernel_add_two, "add_two", (fs, ts, ts, ts), (facc, *kept_outside(f2), t0, *kept_outside(t1)),
+        [INSIDE, ANYWHERE] * 2, (fs, (3,) + ts),
     )
 
 
@@ -1025,11 +1053,8 @@
     return pl.pallas_call(
         kernel_f,
         out_shape=(shape((2, 1, WORDS, WD // 2), LOW),) + tuple(shape(s, F32) for s in outs),
-        in_specs=[pl.BlockSpec(memory_space=pl.ANY)] * 13 + [INSIDE] * 2,
+        in_specs=[INSIDE] * 15,
         out_specs=(INSIDE,) * 19,
-        scratch_shapes=[
-            v((3, F_ROWS, 256), LOW), v((3, T_ROWS, 256), LOW), v((8, C_ROWS, 128), LOW), pltpu.SemaphoreType.DMA((3,)),
-        ],
         compiler_params=params(8),
         name="finish",
     )(*words, *c, outk, outg)

time: 105 us -> 100 us (0.952)
  Pallas kernels: 68.8 us -> 63.5 us
    pallas_call x1, Pallas kernels: 27.2 us -> 25.9 us  [call_a(): pl.pallas_call(kernel_a, out_shape=(outside((TURNS, KEPT_LOW, WIDE), LOW)...]
    pallas_call x1, Pallas kernels: 3.1 us -> 1.85 us  [call_f(): pl.pallas_call(kernel_f, out_shape=(shape((2, 1, WORDS, WD // 2), LOW),)...]
    pallas_call x1, Pallas kernels: 14.9 us -> 13.8 us  [call_b2(): pl.pallas_call(kernel_b2, out_shape=(v((SHARES, C_ROWS, 128), LOW), v((SH...]
where the time goes in v5:
time: 100 us; the launch traced here: 99.9 us
  Pallas kernels  63.5 us (64%)
  starting transfers between devices  21.8 us (22%)
  waiting for transfers between devices  12.4 us (12%)
  between operations  1.04 us (1%)
  other arithmetic  1.01 us (1%)
    pallas_call x1, Pallas kernels, call_a(): pl.pallas_call(kernel_a, out_shape=(outside((TURNS, KEPT_LOW, WIDE), LOW)...  25.9 us
    pallas_call x1, Pallas kernels, call_b2(): pl.pallas_call(kernel_b2, out_shape=(v((SHARES, C_ROWS, 128), LOW), v((SH...  13.8 us
    ppermute x13, starting transfers between devices, flip(): return lax.ppermute(value, axis, [(i, i ^ bits) for i in range(count)])  12 us
    pallas_call x1, Pallas kernels, call_b1(): pl.pallas_call(kernel_b1, out_shape=(outside((TURNS, CD, WIDE), LOW), sha...  11.3 us
    ppermute x5, starting transfers between devices, flip_both(): return lax.ppermute(value, ('phase', 'dp'), pairs)  9.8 us
    ppermute x13, waiting for transfers between devices, flip(): return lax.ppermute(value, axis, [(i, i ^ bits) for i in range(count)])  9.02 us
    pallas_call x3, Pallas kernels, call_add(): pl.pallas_call(kernel, out_shape=tuple((v(s, LOW) for s in outs)), in_spe...  6.4 us
    pallas_call x1, Pallas kernels, call_a2(): pl.pallas_call(kernel_a2, out_shape=(shape((CD, WORDS), LOW), v((SHARES,...  4.3 us
  transfers between devices with their start and end apart: 18, of which 9 were waited for; matrix products, arithmetic and copies ran while one was open for 1% of the time, Pallas kernels for 31%

profile of v5, /device:TPU:0, one launch (start us, length us, event | category | flops | bytes accessed | tf_op | source)
XLA Modules:
  0.0 99.9 jit_solution(3853361313727533077)
XLA Ops:
  0.7 25.9 %forward_and_words.1 = (bf16[9,2304,512]{2,1,0:T(8,128)(2,1)}, bf16[9,1024,512]{2,1,0:T(8,128)(2,1)}, f32[9,256,512]{2,1,0:T(8,128)}, f32[9,8,512]{2,1,0:T(8,128...) custom-call(s32[2,1,256]{2,1,0:T(1,128)} %counts_ref.1, ...), custom_call_target="tpu_custom_call" | custom-call | flops 199999995904 | bytes 60000000 | tf_op jit(solution)/shard_map/forward_and_words/pallas_call | solution.py:907
  26.6 0.5 collective-permute-start
  27.2 4.3 %word_attention_backward.1 = (bf16[256,256]{1,0:T(8,128)(2,1)S(1)}, bf16[16,176,256]{2,1,0:T(8,128)(2,1)S(1)}, bf16[16,176,256]{2,1,0:T(8,128)(2,1)}, f32[8,512]{1,0:T(8,128)S(1)}) custom-call(s32[2,1,256]{2,1,0:T(1,128)S(1)} %copy-done.11, bf16[256,512]{1,0:T(8,128)(2,1)S(1)} %get-tuple-element.84.q_ref, bf16[256,512]{1,0:T(8,128)(2,1)S(1)} %get-tuple-element.85.k_ref, ...), custom_call_target="tpu_custom_call" | custom-call | flops 199999995904 | bytes 10000000 | tf_op jit(solution)/shard_map/word_attention_backward/pallas_call | solution.py:953
  31.6 2.3 %add_one.1 = bf16[8,256,256]{2,1,0:T(8,128)(2,1)} custom-call(bf16[16,256,256]{2,1,0:T(8,128)(2,1)S(1)} %get-tuple-element.102.f0_ref, bf16[16,256,256]{2,1,0:T(8,128)(2,1)} %collective-permute-done.f1_hbm), custom_call_target="tpu_custom_call" | custom-call | tf_op jit(solution)/shard_map/add_one/pallas_call | solution.py:1016
  33.9 3.0 %collective-permute-start.2 = (bf16[8,256,256]{2,1,0:T(8,128)(2,1)}, bf16[8,256,256]{2,1,0:T(8,128)(2,1)}, u32[]{:S(2)}, u32[]{:S(2)}) collective-permute-start(bf16[8,256,256]{2,1,0:T(8,128)(2,1)} %add_one.1), channel_id=1, source_target_pairs={{0,1},{1,0},{2,3},{3,2},{4,5},{5,4},{6,7},{7,6},{8,9},{9,8},{10,11... | collective-permute-start | bytes 3145736 | tf_op jit(solution)/shard_map/ppermute | solution.py:1070
  36.9 11.3 %character_backward_one.1 = (bf16[9,256,512]{2,1,0:T(8,128)(2,1)}, bf16[256,1024]{1,0:T(8,128)(2,1)S(1)}, f32[8,256]{1,0:T(8,128)S(1)}, bf16[8,256,256]{2,1,0:T(8,128)(2,1)S(1)}) custom-call(s32[1]{0:T(128)} %get-tuple-element.83.turns_ref, bf16[256,256]{1,0:T(8,128)(2,1)S(1)} %get-tuple-element.104.gw_ref, bf16[256]{0:T(256)(128)(2,1)S(1)} %copy-done.13, ...), custom_call_target="tpu_custom_call" | custom-call | flops 199999995904 | bytes 20000000 | tf_op jit(solution)/shard_map/character_backward_one/pallas_call | solution.py:971
  48.2 1.7 %collective-permute-done.2.f2_hbm = bf16[8,256,256]{2,1,0:T(8,128)(2,1)} collective-permute-done((bf16[8,256,256]{2,1,0:T(8,128)(2,1)}, bf16[8,256,256]{2,1,0:T(8,128)(2,1)}, u32[]{:S(2)}, u32[]{:S(2)}) %collective-permute-start.2) | collective-permute-done | bytes 1048608 | tf_op jit(solution)/shard_map/ppermute | solution.py:1070
  50.0 2.6 %add_two.1 = (bf16[4,256,256]{2,1,0:T(8,128)(2,1)}, bf16[4,176,256]{2,1,0:T(8,128)(2,1)}, bf16[4,176,256]{2,1,0:T(8,128)(2,1)}, bf16[4,176,256]{2,1,0:T(8,128)(2,1)}) custom-call(bf16[8,256,256]{2,1,0:T(8,128)(2,1)S(1)} %get-tuple-element.115.facc_ref, bf16[8,256,256]{2,1,0:T(8,128)(2,1)} %collective-permute-done.2.f2_hbm, ...), custom_call_target="tpu_custom_call" | custom-call | tf_op jit(solution)/shard_map/add_two/pallas_call | solution.py:1016
  52.6 2.2 %collective-permute-start.4 = (bf16[4,256,256]{2,1,0:T(8,128)(2,1)}, bf16[4,256,256]{2,1,0:T(8,128)(2,1)}, u32[]{:S(2)}, u32[]{:S(2)}) collective-permute-start(bf16[4,256,256]{2,1,0:T(8,128)(2,1)} %get-tuple-element.127), channel_id=1, source_target_pairs={{0,4},{1,5},{2,6},{3,7},{4,0},{5,1},{6,2},{7,3},{8,12},{9,13},{10,... | collective-permute-start | bytes 1572872 | tf_op jit(solution)/shard_map/ppermute | solution.py:1070
  54.8 1.5 %collective-permute-start.5 = (bf16[4,176,256]{2,1,0:T(8,128)(2,1)}, bf16[4,176,256]{2,1,0:T(8,128)(2,1)}, u32[]{:S(2)}, u32[]{:S(2)}) collective-permute-start(bf16[4,176,256]{2,1,0:T(8,128)(2,1)} %get-tuple-element.128), channel_id=1, source_target_pairs={{0,1},{1,0},{2,3},{3,2},{4,5},{5,4},{6,7},{7,6},{8,9},{9,8},{10,11... | collective-permute-start | bytes 1081352 | tf_op jit(solution)/shard_map/ppermute | solution.py:1065
  56.3 1.5 %collective-permute-start.6 = (bf16[4,176,256]{2,1,0:T(8,128)(2,1)}, bf16[4,176,256]{2,1,0:T(8,128)(2,1)}, u32[]{:S(2)}, u32[]{:S(2)}) collective-permute-start(bf16[4,176,256]{2,1,0:T(8,128)(2,1)} %get-tuple-element.129), channel_id=1, source_target_pairs={{0,2},{1,3},{2,0},{3,1},{4,6},{5,7},{6,4},{7,5},{8,10},{9,11},{10,... | collective-permute-start | bytes 1081352 | tf_op jit(solution)/shard_map/ppermute | solution.py:1065
  57.8 0.5 collective-permute-start.7
  58.3 13.8 %character_backward_two.1 = (bf16[16,160,128]{2,1,0:T(8,128)(2,1)S(1)}, bf16[16,160,128]{2,1,0:T(8,128)(2,1)}, bf16[4,256,256]{2,1,0:T(8,128)(2,1)S(1)}, bf16[4,176,256]{2,1,0:T(8,128)(2,1)S(1)}) custom-call(s32[1]{0:T(128)} %get-tuple-element.83.turns_ref, f32[8,512]{1,0:T(8,128)S(1)} %get-tuple-element.95.wgain1_ref, ...), custom_call_target="tpu_custom_call" | custom-call | flops 199999995904 | bytes 40000000 | tf_op jit(solution)/shard_map/character_backward_two/pallas_call | solution.py:992
  72.1 1.2 %collective-permute-done.6.tg2_hbm = bf16[4,176,256]{2,1,0:T(8,128)(2,1)} collective-permute-done((bf16[4,176,256]{2,1,0:T(8,128)(2,1)}, bf16[4,176,256]{2,1,0:T(8,128)(2,1)}, u32[]{:S(2)}, u32[]{:S(2)}) %collective-permute-start.6) | collective-permute-done | bytes 360480 | tf_op jit(solution)/shard_map/ppermute | solution.py:1065
  73.3 1.5 %add_three.1 = (bf16[2,256,256]{2,1,0:T(8,128)(2,1)S(1)}, bf16[2,256,256]{2,1,0:T(8,128)(2,1)S(1)}, bf16[2,176,256]{2,1,0:T(8,128)(2,1)S(1)}, bf16[2,176,256]{2,1,0:T(8,128)(2,1)S(1)}) custom-call(bf16[4,256,256]{2,1,0:T(8,128)(2,1)S(1)} %get-tuple-element.131.facc_ref, bf16[4,256,256]{2,1,0:T(8,128)(2,1)} %collective-permute-done.4.f3_hbm, ...), custom_call_target="tpu_custom_call" | custom-call | tf_op jit(solution)/shard_map/add_three/pallas_call | solution.py:1016
  74.8 1.6 %collective-permute-start.8 = (bf16[2,256,256]{2,1,0:T(8,128)(2,1)S(1)}, bf16[2,256,256]{2,1,0:T(8,128)(2,1)S(1)}, u32[]{:S(2)}, u32[]{:S(2)}) collective-permute-start(bf16[2,256,256]{2,1,0:T(8,128)(2,1)S(1)} %get-tuple-element.138), channel_id=1, source_target_pairs={{0,2},{1,3},{2,0},{3,1},{4,6},{5,7},{6,4},{7,5},{8,10},{9,11},{10,... | collective-permute-start | bytes 786440 | tf_op jit(solution)/shard_map/ppermute | solution.py:1070
  76.8 0.8 fusion.2
  77.7 0.5 collective-permute-start.12
  78.2 1.2 %collective-permute-start.13 = (bf16[4,160,128]{2,1,0:T(8,128)(2,1)}, bf16[4,160,128]{2,1,0:T(8,128)(2,1)S(1)}, u32[]{:S(2)}, u32[]{:S(2)}) collective-permute-start(bf16[4,160,128]{2,1,0:T(8,128)(2,1)} %get-tuple-element.151), channel_id=1, source_target_pairs={{0,2},{1,3},{2,0},{3,1},{4,6},{5,7},{6,4},{7,5},{8,10},{9,11},{10,... | collective-permute-start | bytes 491528 | tf_op jit(solution)/shard_map/ppermute | solution.py:1065
  79.4 1.8 %collective-permute-start.14 = (bf16[4,160,128]{2,1,0:T(8,128)(2,1)S(1)}, bf16[4,160,128]{2,1,0:T(8,128)(2,1)S(1)}, u32[]{:S(2)}, u32[]{:S(2)}) collective-permute-start(bf16[4,160,128]{2,1,0:T(8,128)(2,1)S(1)} %get-tuple-element.150), channel_id=1, source_target_pairs={{0,3},{1,2},{2,1},{3,0},{4,7},{5,6},{6,5},{7,4},{8,11},{9,10},{10,... | collective-permute-start | bytes 491528 | tf_op jit(solution)/shard_map/ppermute | solution.py:1065
  81.2 0.6 collective-permute-done.8.f4
  81.8 1.0 %collective-permute-done.10.t3 = bf16[2,176,256]{2,1,0:T(8,128)(2,1)S(1)} collective-permute-done((bf16[2,176,256]{2,1,0:T(8,128)(2,1)S(1)}, bf16[2,176,256]{2,1,0:T(8,128)(2,1)S(1)}, u32[]{:S(2)}, u32[]{:S(2)}) %collective-permute-start.10) | collective-permute-done | bytes 180256 | tf_op jit(solution)/shard_map/ppermute | solution.py:1070
  82.9 2.6 %collective-permute-start.11 = (bf16[432,256]{1,0:T(8,128)(2,1)S(1)}, bf16[432,256]{1,0:T(8,128)(2,1)S(1)}, u32[]{:S(2)}, u32[]{:S(2)}) collective-permute-start(bf16[432,256]{1,0:T(8,128)(2,1)S(1)} %pad_maximum_fusion), channel_id=1, source_target_pairs={{0,8},{1,9},{2,10},{3,11},{4,12},{5,13},{6,14},{7,15},{8,0},{9,1},... | collective-permute-start | bytes 663560 | tf_op jit(solution)/shard_map/ppermute | solution.py:1070
  85.5 1.9 %collective-permute-done.13.c3 = bf16[4,160,128]{2,1,0:T(8,128)(2,1)S(1)} collective-permute-done((bf16[4,160,128]{2,1,0:T(8,128)(2,1)}, bf16[4,160,128]{2,1,0:T(8,128)(2,1)S(1)}, u32[]{:S(2)}, u32[]{:S(2)}) %collective-permute-start.13) | collective-permute-done | bytes 163872 | tf_op jit(solution)/shard_map/ppermute | solution.py:1065
  87.4 1.0 %collective-permute-done.14.c4 = bf16[4,160,128]{2,1,0:T(8,128)(2,1)S(1)} collective-permute-done((bf16[4,160,128]{2,1,0:T(8,128)(2,1)S(1)}, bf16[4,160,128]{2,1,0:T(8,128)(2,1)S(1)}, u32[]{:S(2)}, u32[]{:S(2)}) %collective-permute-start.14) | collective-permute-done | bytes 163872 | tf_op jit(solution)/shard_map/ppermute | solution.py:1065
  88.6 0.8 collective-permute-start.15
  89.4 2.6 %collective-permute-start.16 = (bf16[160,128]{1,0:T(8,128)(2,1)S(1)}, bf16[160,128]{1,0:T(8,128)(2,1)S(1)}, u32[]{:S(2)}, u32[]{:S(2)}) collective-permute-start(bf16[160,128]{1,0:T(8,128)(2,1)S(1)} %get-tuple-element.148), channel_id=1, source_target_pairs={{0,8},{1,9},{2,10},{3,11},{4,12},{5,13},{6,14},{7,15},{8,0},{9,1},... | collective-permute-start | bytes 122888 | tf_op jit(solution)/shard_map/ppermute | solution.py:1065
  92.0 1.0 %collective-permute-start.17 = (bf16[160,128]{1,0:T(8,128)(2,1)S(1)}, bf16[160,128]{1,0:T(8,128)(2,1)S(1)}, u32[]{:S(2)}, u32[]{:S(2)}) collective-permute-start(bf16[160,128]{1,0:T(8,128)(2,1)S(1)} %get-tuple-element.147), channel_id=1, source_target_pairs={{0,12},{1,13},{2,14},{3,15},{4,8},{5,9},{6,10},{7,11},{8,4},{9,5},... | collective-permute-start | bytes 122888 | tf_op jit(solution)/shard_map/ppermute | solution.py:1065
  93.0 2.3 %collective-permute-done.15.c5 = bf16[160,128]{1,0:T(8,128)(2,1)S(1)} collective-permute-done((bf16[160,128]{1,0:T(8,128)(2,1)S(1)}, bf16[160,128]{1,0:T(8,128)(2,1)S(1)}, u32[]{:S(2)}, u32[]{:S(2)}) %collective-permute-start.15) | collective-permute-done | bytes 40992 | tf_op jit(solution)/shard_map/ppermute | solution.py:1065
  95.3 1.9 %collective-permute-done.16.c6 = bf16[160,128]{1,0:T(8,128)(2,1)S(1)} collective-permute-done((bf16[160,128]{1,0:T(8,128)(2,1)S(1)}, bf16[160,128]{1,0:T(8,128)(2,1)S(1)}, u32[]{:S(2)}, u32[]{:S(2)}) %collective-permute-start.16) | collective-permute-done | bytes 40992 | tf_op jit(solution)/shard_map/ppermute | solution.py:1065
  97.2 0.7 collective-permute-done.17.c7
  97.9 1.9 %finish.1 = (bf16[2,1,256,256]{3,2,1,0:T(8,128)(2,1)}, f32[16,128]{1,0:T(8,128)}, f32[16]{0:T(128)}, f32[16,128]{1,0:T(8,128)}, f32[16,128]{1,0:T(8,128)}, /*ind...) custom-call(bf16[2,256,256]{2,1,0:T(8,128)(2,1)S(1)} %get-tuple-elem, ...), custom_call_target="tpu_custom_call" | custom-call | tf_op jit(solution)/shard_map/finish/pallas_call | solution.py:1053
  (47 shorter events, 0.8 us)
Async XLA Ops:
  0.7 26.5 %copy-start = (bf16[512,512]{1,0:T(8,128)(2,1)S(1)}, bf16[512,512]{1,0:T(8,128)(2,1)}, u32[]{:S(2)}) copy-start(bf16[512,512]{1,0:T(8,128)(2,1)} %wwq.1) | copy-start | bytes 1572868
  0.7 26.5 %copy-start.1 = (bf16[512,512]{1,0:T(8,128)(2,1)S(1)}, bf16[512,512]{1,0:T(8,128)(2,1)}, u32[]{:S(2)}) copy-start(bf16[512,512]{1,0:T(8,128)(2,1)} %wwk.1) | copy-start | bytes 1572868
  0.7 26.5 %copy-start.2 = (bf16[512,512]{1,0:T(8,128)(2,1)S(1)}, bf16[512,512]{1,0:T(8,128)(2,1)}, u32[]{:S(2)}) copy-start(bf16[512,512]{1,0:T(8,128)(2,1)} %wwv.1) | copy-start | bytes 1572868
  0.7 26.5 %copy-start.3 = (bf16[512,512]{1,0:T(8,128)(2,1)S(1)}, bf16[512,512]{1,0:T(8,128)(2,1)}, u32[]{:S(2)}) copy-start(bf16[512,512]{1,0:T(8,128)(2,1)} %wwo.1) | copy-start | bytes 1572868
  0.7 26.5 %copy-start.6 = (bf16[256,512]{1,0:T(8,128)(2,1)S(1)}, bf16[256,512]{1,0:T(8,128)(2,1)}, u32[]{:S(2)}) copy-start(bf16[256,512]{1,0:T(8,128)(2,1)} %proj_ref.1) | copy-start | bytes 786436
  0.7 26.5 %copy-start.11 = (s32[2,1,256]{2,1,0:T(1,128)S(1)}, s32[2,1,256]{2,1,0:T(1,128)}, u32[]{:S(2)}) copy-start(s32[2,1,256]{2,1,0:T(1,128)} %counts_ref.1) | copy-start | bytes 6148
  0.7 26.5 %copy-start.12 = (bf16[512]{0:T(512)(128)(2,1)S(1)}, bf16[512]{0:T(512)(128)(2,1)}, u32[]{:S(2)}) copy-start(bf16[512]{0:T(512)(128)(2,1)} %wg1_ref.1) | copy-start | bytes 3076
  26.6 5.0 %collective-permute-start = (bf16[16,256,256]{2,1,0:T(8,128)(2,1)}, bf16[16,256,256]{2,1,0:T(8,128)(2,1)}, u32[]{:S(2)}, u32[]{:S(2)}) collective-permute-start(bf16[16,256,256]{2,1,0:T(8,128)(2,1)} %get-tuple-element.99), channel_id=1, source_target_pairs={{0,16},{16,0},{1,17},{17,1},{2,18},{18,2},{3,19},{19,3},{4,20},{20... | collective-permute-start | bytes 6291464 | tf_op jit(solution)/shard_map/ppermute | solution.py:1065
  27.1 4.4 %collective-permute-start.1 = (bf16[256,256]{1,0:T(8,128)(2,1)}, bf16[256,256]{1,0:T(8,128)(2,1)}, u32[]{:S(2)}, u32[]{:S(2)}) collective-permute-start(bf16[256,256]{1,0:T(8,128)(2,1)} %get-tuple-element.100), channel_id=1, source_target_pairs={{0,16},{16,0},{1,17},{17,1},{2,18},{18,2},{3,19},{19,3},{4,20},{20... | collective-permute-start | bytes 393224 | tf_op jit(solution)/shard_map/ppermute | solution.py:1065
  31.6 5.3 %copy-start.4 = (bf16[256,1024]{1,0:T(8,128)(2,1)S(1)}, bf16[256,1024]{1,0:T(8,128)(2,1)}, u32[]{:S(2)}) copy-start(bf16[256,1024]{1,0:T(8,128)(2,1)} %up_ref.1) | copy-start | bytes 1572868
  31.6 5.3 %copy-start.5 = (bf16[1024,256]{1,0:T(8,128)(2,1)S(1)}, bf16[1024,256]{1,0:T(8,128)(2,1)}, u32[]{:S(2)}) copy-start(bf16[1024,256]{1,0:T(8,128)(2,1)} %down_ref.1) | copy-start | bytes 1572868
  33.9 16.1 %collective-permute-start.2 = (bf16[8,256,256]{2,1,0:T(8,128)(2,1)}, bf16[8,256,256]{2,1,0:T(8,128)(2,1)}, u32[]{:S(2)}, u32[]{:S(2)}) collective-permute-start(bf16[8,256,256]{2,1,0:T(8,128)(2,1)} %add_one.1), channel_id=1, source_target_pairs={{0,1},{1,0},{2,3},{3,2},{4,5},{5,4},{6,7},{7,6},{8,9},{9,8},{10,11... | collective-permute-start | bytes 3145736 | tf_op jit(solution)/shard_map/ppermute | solution.py:1070
  36.9 13.1 %collective-permute-start.3 = (bf16[16,176,256]{2,1,0:T(8,128)(2,1)}, bf16[16,176,256]{2,1,0:T(8,128)(2,1)}, u32[]{:S(2)}, u32[]{:S(2)}) collective-permute-start(bf16[16,176,256]{2,1,0:T(8,128)(2,1)} %get-tuple-element.113), channel_id=1, source_target_pairs={{0,16},{16,0},{1,17},{17,1},{2,18},{18,2},{3,19},{19,3},{4,20},{20... | collective-permute-start | bytes 4325384 | tf_op jit(solution)/shard_map/ppermute | solution.py:1065
  50.0 8.3 %copy-start.7 = (bf16[256,256]{1,0:T(8,128)(2,1)S(1)}, bf16[256,256]{1,0:T(8,128)(2,1)}, u32[]{:S(2)}) copy-start(bf16[256,256]{1,0:T(8,128)(2,1)} %wq_ref.1) | copy-start | bytes 393220
  50.0 8.3 %copy-start.8 = (bf16[256,256]{1,0:T(8,128)(2,1)S(1)}, bf16[256,256]{1,0:T(8,128)(2,1)}, u32[]{:S(2)}) copy-start(bf16[256,256]{1,0:T(8,128)(2,1)} %wk_ref.1) | copy-start | bytes 393220
  50.0 8.3 %copy-start.9 = (bf16[256,256]{1,0:T(8,128)(2,1)S(1)}, bf16[256,256]{1,0:T(8,128)(2,1)}, u32[]{:S(2)}) copy-start(bf16[256,256]{1,0:T(8,128)(2,1)} %wv_ref.1) | copy-start | bytes 393220
  50.0 8.3 %copy-start.10 = (bf16[256,256]{1,0:T(8,128)(2,1)S(1)}, bf16[256,256]{1,0:T(8,128)(2,1)}, u32[]{:S(2)}) copy-start(bf16[256,256]{1,0:T(8,128)(2,1)} %wo_ref.1) | copy-start | bytes 393220
  50.0 8.3 %copy-start.14 = (bf16[256]{0:T(256)(128)(2,1)S(1)}, bf16[256]{0:T(256)(128)(2,1)}, u32[]{:S(2)}) copy-start(bf16[256]{0:T(256)(128)(2,1)} %g1_ref.1) | copy-start | bytes 1540
  52.6 20.7 %collective-permute-start.4 = (bf16[4,256,256]{2,1,0:T(8,128)(2,1)}, bf16[4,256,256]{2,1,0:T(8,128)(2,1)}, u32[]{:S(2)}, u32[]{:S(2)}) collective-permute-start(bf16[4,256,256]{2,1,0:T(8,128)(2,1)} %get-tuple-element.127), channel_id=1, source_target_pairs={{0,4},{1,5},{2,6},{3,7},{4,0},{5,1},{6,2},{7,3},{8,12},{9,13},{10,... | collective-permute-start | bytes 1572872 | tf_op jit(solution)/shard_map/ppermute | solution.py:1070
  54.8 17.3 %collective-permute-start.5 = (bf16[4,176,256]{2,1,0:T(8,128)(2,1)}, bf16[4,176,256]{2,1,0:T(8,128)(2,1)}, u32[]{:S(2)}, u32[]{:S(2)}) collective-permute-start(bf16[4,176,256]{2,1,0:T(8,128)(2,1)} %get-tuple-element.128), channel_id=1, source_target_pairs={{0,1},{1,0},{2,3},{3,2},{4,5},{5,4},{6,7},{7,6},{8,9},{9,8},{10,11... | collective-permute-start | bytes 1081352 | tf_op jit(solution)/shard_map/ppermute | solution.py:1065
  56.3 17.0 %collective-permute-start.6 = (bf16[4,176,256]{2,1,0:T(8,128)(2,1)}, bf16[4,176,256]{2,1,0:T(8,128)(2,1)}, u32[]{:S(2)}, u32[]{:S(2)}) collective-permute-start(bf16[4,176,256]{2,1,0:T(8,128)(2,1)} %get-tuple-element.129), channel_id=1, source_target_pairs={{0,2},{1,3},{2,0},{3,1},{4,6},{5,7},{6,4},{7,5},{8,10},{9,11},{10,... | collective-permute-start | bytes 1081352 | tf_op jit(solution)/shard_map/ppermute | solution.py:1065
  57.8 15.5 %collective-permute-start.7 = (bf16[4,176,256]{2,1,0:T(8,128)(2,1)}, bf16[4,176,256]{2,1,0:T(8,128)(2,1)}, u32[]{:S(2)}, u32[]{:S(2)}) collective-permute-start(bf16[4,176,256]{2,1,0:T(8,128)(2,1)} %get-tuple-element.130), channel_id=1, source_target_pairs={{0,3},{1,2},{2,1},{3,0},{4,7},{5,6},{6,5},{7,4},{8,11},{9,10},{10,... | collective-permute-start | bytes 1081352 | tf_op jit(solution)/shard_map/ppermute | solution.py:1065
  73.3 3.5 %collective-permute-start.9 = (bf16[16,160,128]{2,1,0:T(8,128)(2,1)}, bf16[16,160,128]{2,1,0:T(8,128)(2,1)S(1)}, u32[]{:S(2)}, u32[]{:S(2)}) collective-permute-start(bf16[16,160,128]{2,1,0:T(8,128)(2,1)} %get-tuple-element.140), channel_id=1, source_target_pairs={{0,16},{16,0},{1,17},{17,1},{2,18},{18,2},{3,19},{19,3},{4,20},{20... | collective-permute-start | bytes 1966088 | tf_op jit(solution)/shard_map/ppermute | solution.py:1065
  74.8 7.0 %collective-permute-start.8 = (bf16[2,256,256]{2,1,0:T(8,128)(2,1)S(1)}, bf16[2,256,256]{2,1,0:T(8,128)(2,1)S(1)}, u32[]{:S(2)}, u32[]{:S(2)}) collective-permute-start(bf16[2,256,256]{2,1,0:T(8,128)(2,1)S(1)} %get-tuple-element.138), channel_id=1, source_target_pairs={{0,2},{1,3},{2,0},{3,1},{4,6},{5,7},{6,4},{7,5},{8,10},{9,11},{10,... | collective-permute-start | bytes 786440 | tf_op jit(solution)/shard_map/ppermute | solution.py:1070
  76.4 6.4 %collective-permute-start.10 = (bf16[2,176,256]{2,1,0:T(8,128)(2,1)S(1)}, bf16[2,176,256]{2,1,0:T(8,128)(2,1)S(1)}, u32[]{:S(2)}, u32[]{:S(2)}) collective-permute-start(bf16[2,176,256]{2,1,0:T(8,128)(2,1)S(1)} %get-tuple-element.143), channel_id=1, source_target_pairs={{0,4},{1,5},{2,6},{3,7},{4,0},{5,1},{6,2},{7,3},{8,12},{9,13},{10,... | collective-permute-start | bytes 540680 | tf_op jit(solution)/shard_map/ppermute | solution.py:1070
  77.7 7.8 %collective-permute-start.12 = (bf16[4,160,128]{2,1,0:T(8,128)(2,1)}, bf16[4,160,128]{2,1,0:T(8,128)(2,1)S(1)}, u32[]{:S(2)}, u32[]{:S(2)}) collective-permute-start(bf16[4,160,128]{2,1,0:T(8,128)(2,1)} %get-tuple-element.152), channel_id=1, source_target_pairs={{0,1},{1,0},{2,3},{3,2},{4,5},{5,4},{6,7},{7,6},{8,9},{9,8},{10,11... | collective-permute-start | bytes 491528 | tf_op jit(solution)/shard_map/ppermute | solution.py:1065
  78.2 9.2 %collective-permute-start.13 = (bf16[4,160,128]{2,1,0:T(8,128)(2,1)}, bf16[4,160,128]{2,1,0:T(8,128)(2,1)S(1)}, u32[]{:S(2)}, u32[]{:S(2)}) collective-permute-start(bf16[4,160,128]{2,1,0:T(8,128)(2,1)} %get-tuple-element.151), channel_id=1, source_target_pairs={{0,2},{1,3},{2,0},{3,1},{4,6},{5,7},{6,4},{7,5},{8,10},{9,11},{10,... | collective-permute-start | bytes 491528 | tf_op jit(solution)/shard_map/ppermute | solution.py:1065
  79.4 9.1 %collective-permute-start.14 = (bf16[4,160,128]{2,1,0:T(8,128)(2,1)S(1)}, bf16[4,160,128]{2,1,0:T(8,128)(2,1)S(1)}, u32[]{:S(2)}, u32[]{:S(2)}) collective-permute-start(bf16[4,160,128]{2,1,0:T(8,128)(2,1)S(1)} %get-tuple-element.150), channel_id=1, source_target_pairs={{0,3},{1,2},{2,1},{3,0},{4,7},{5,6},{6,5},{7,4},{8,11},{9,10},{10,... | collective-permute-start | bytes 491528 | tf_op jit(solution)/shard_map/ppermute | solution.py:1065
  82.9 15.0 %collective-permute-start.11 = (bf16[432,256]{1,0:T(8,128)(2,1)S(1)}, bf16[432,256]{1,0:T(8,128)(2,1)S(1)}, u32[]{:S(2)}, u32[]{:S(2)}) collective-permute-start(bf16[432,256]{1,0:T(8,128)(2,1)S(1)} %pad_maximum_fusion), channel_id=1, source_target_pairs={{0,8},{1,9},{2,10},{3,11},{4,12},{5,13},{6,14},{7,15},{8,0},{9,1},... | collective-permute-start | bytes 663560 | tf_op jit(solution)/shard_map/ppermute | solution.py:1070
  88.6 6.8 %collective-permute-start.15 = (bf16[160,128]{1,0:T(8,128)(2,1)S(1)}, bf16[160,128]{1,0:T(8,128)(2,1)S(1)}, u32[]{:S(2)}, u32[]{:S(2)}) collective-permute-start(bf16[160,128]{1,0:T(8,128)(2,1)S(1)} %get-tuple-element.149), channel_id=1, source_target_pairs={{0,4},{1,5},{2,6},{3,7},{4,0},{5,1},{6,2},{7,3},{8,12},{9,13},{10,... | collective-permute-start | bytes 122888 | tf_op jit(solution)/shard_map/ppermute | solution.py:1065
  89.4 7.8 %collective-permute-start.16 = (bf16[160,128]{1,0:T(8,128)(2,1)S(1)}, bf16[160,128]{1,0:T(8,128)(2,1)S(1)}, u32[]{:S(2)}, u32[]{:S(2)}) collective-permute-start(bf16[160,128]{1,0:T(8,128)(2,1)S(1)} %get-tuple-element.148), channel_id=1, source_target_pairs={{0,8},{1,9},{2,10},{3,11},{4,12},{5,13},{6,14},{7,15},{8,0},{9,1},... | collective-permute-start | bytes 122888 | tf_op jit(solution)/shard_map/ppermute | solution.py:1065
  92.0 5.9 %collective-permute-start.17 = (bf16[160,128]{1,0:T(8,128)(2,1)S(1)}, bf16[160,128]{1,0:T(8,128)(2,1)S(1)}, u32[]{:S(2)}, u32[]{:S(2)}) collective-permute-start(bf16[160,128]{1,0:T(8,128)(2,1)S(1)} %get-tuple-element.147), channel_id=1, source_target_pairs={{0,12},{1,13},{2,14},{3,15},{4,8},{5,9},{6,10},{7,11},{8,4},{9,5},... | collective-permute-start | bytes 122888 | tf_op jit(solution)/shard_map/ppermute | solution.py:1065
  (1 other events, 5.3 us)

commit v6 on v5

--- a/solution.py
+++ b/solution.py
@@ -33,7 +33,8 @@
 floor_score = -1e30
 log2_e = 1.4426950408889634
 
-R_EMB, R_Q, R_K, R_V, R_P, R_MIX = 0, 256, 512, 768, 1024, 2048
+R_V, R_P, R_EMB, R_Q, R_K, R_MIX = 0, 256, 1280, 1536, 1792, 2048
+KEPT_FIRST = 1280
 KEPT_LOW = 2304
 I_INV1, I_INV2, I_IDENT, I_WORD = 0, 1, 2, 3
 BAND = 144
@@ -194,7 +195,6 @@
     cot, wwq, wwk, wwv, wwo, wup, wdown,
     tab_t, wqkv_t, wo_t, up_t, ids_t, slow, sslope, smid, sinfo, pa, pm, rowinfo, firsts_v, firsts, before_s, act_s, prob_s, found_s,
     mid_s, word_s, old_s,
-    actw, slopew,
     csem, wsem, ksem,
 ):
     phase = lax.axis_index("phase")
@@ -494,34 +494,35 @@
     middle = x + nn(mixed_t.T, wwo[...])
     winv2 = lax.rsqrt(jnp.mean(middle * middle, axis=1, keepdims=True) + epsilon)
     normed_two = (middle * winv2 * wg2).astype(LOW)
+    cot_low = cot[...]
     result = middle
-    for c in range(WFF // 512):
-        cs = slice(c * 512, (c + 1) * 512)
-        act, slope = gelu_pair(nn(normed_two, wup[:, cs]))
+    n2d = jnp.zeros((WORDS, WD), F32)
+    n2_t = normed_two.T
+    held = {}
+    turns = (0, 2, 1, 3)
+    quarter = [slice(c * 512, (c + 1) * 512) for c in range(4)]
+    act, slope = gelu_pair(nn(normed_two, wup[:, quarter[0]]))
+    for i, c in enumerate(turns):
+        cs = quarter[c]
         act = act.astype(LOW)
-        actw[:, cs] = act
-        slopew[:, cs] = slope.astype(LOW)
+        bd = (nt(cot_low, wdown[cs, :]) * slope).astype(LOW)
+        if i < 3:
+            ahead = nn(normed_two, wup[:, quarter[turns[i + 1]]])
         result = result + nn(act, wdown[cs, :])
+        gd = nn(act.T, cot_low)
+        gu = nn(n2_t, bd).astype(LOW)
+        n2d = n2d + nt(bd, wup[:, cs])
+        if i < 3:
+            act, slope = gelu_pair(ahead)
+        put(keep_ref, send_ref, phase, lambda i, p: feed_order(c * 4 + i, p), F_DOWN, column_halves(gd), 128)
+        if c < 2:
+            held[c] = gu
+        else:
+            put(keep_ref, send_ref, phase, feed_order, F_UP + (c - 2) * 64, (held[c - 2], gu), 32)
     result = result.astype(LOW)
     front = phase == 0
     outk_ref[...] = jnp.where(front, result[:, :256], result[:, 256:])
     outs_ref[...] = jnp.where(front, result[:, 256:], result[:, :256])
-
-    cot_low = cot[...]
-    n2d = jnp.zeros((WORDS, WD), F32)
-    n2_t = normed_two.T
-    held = {}
-    for c in (0, 2, 1, 3):
-        cs = slice(c * 512, (c + 1) * 512)
-        gd = nn(actw[:, cs].T, cot_low)
-        put(keep_ref, send_ref, phase, lambda i, p: feed_order(c * 4 + i, p), F_DOWN, column_halves(gd), 128)
-        bd = (nt(cot_low, wdown[cs, :]) * slopew[:, cs].astype(F32)).astype(LOW)
-        gu = nn(n2_t, bd).astype(LOW)
-        if c < 2:
-            held[c] = gu
-        else:
-            put(keep_ref, send_ref, phase, feed_order, F_UP + (c - 2) * 64, (held[c - 2], gu), 32)
-        n2d = n2d + nt(bd, wup[:, cs])
     vhat = middle * winv2
     gain_ref[...] = jnp.broadcast_to(jnp.sum(n2d * vhat, axis=0, keepdims=True), (8, WD))
     lifted = n2d * wg2
@@ -598,9 +599,9 @@
 
 
 def kernel_b1(
-    turns_ref, gw_ref, g2_ref, up_ref, down_ref, kepts_hbm, keptm_hbm, kepti_hbm, f0_ref, f1_hbm,
-    keptd_hbm, aup_ref, gain_ref, facc_ref,
-    sslope, smid, sinfo, sdelta, aup, ag2, down, f1, ksem, dsem, fsem,
+    turns_ref, gw_ref, g2_ref, up_ref, down_ref, kepts_hbm, keptm_hbm, info_ref, f0_ref, f1_hbm,
+    delta_ref, aup_ref, gain_ref, facc_ref,
+    sslope, smid, given, aup, ag2, down, f1, ksem, fsem,
 ):
     n_turns = turns_ref[0]
 
@@ -608,11 +609,7 @@
         return (
             pltpu.make_async_copy(kepts_hbm.at[b], sslope.at[slot], ksem.at[0, slot]),
             pltpu.make_async_copy(keptm_hbm.at[b], smid.at[slot], ksem.at[1, slot]),
-            pltpu.make_async_copy(kepti_hbm.at[b], sinfo.at[slot], ksem.at[2, slot]),
         )
-
-    def delta_copy(b, slot):
-        return pltpu.make_async_copy(sdelta.at[slot], keptd_hbm.at[b], dsem.at[slot])
 
     for c in kept_copies(0, 0):
         c.start()
@@ -624,6 +621,11 @@
     aup[...] = jnp.zeros_like(aup)
     ag2[...] = jnp.zeros_like(ag2)
 
+    def give(b):
+        given[...] = nn(gw_ref[...], members(info_ref[b, I_WORD:I_WORD + 1], 0, WORDS)).astype(LOW)
+
+    give(0)
+
     def turn(b, carry):
         slot = lax.rem(b, 2)
 
@@ -632,27 +634,31 @@
             for c in kept_copies(b + 1, 1 - slot):
                 c.start()
 
-        @pl.when(b >= 2)
-        def _():
-            delta_copy(b - 2, slot).wait()
-
         for c in kept_copies(b, slot):
             c.wait()
-        inv2 = sinfo[slot, I_INV2:I_INV2 + 1]
-        g_low = nn(gw_ref[...], members(sinfo[slot, I_WORD:I_WORD + 1], 0, WORDS)).astype(LOW)
+        cuts = [slice(c * 256, (c + 1) * 256) for c in range(CFF // 256)]
+        inv2 = info_ref[b, I_INV2:I_INV2 + 1]
+        g_low = given[...]
         vhat = smid[slot] * inv2
         normed_two = (vhat * g2).astype(LOW)
         n2d = jnp.zeros((CD, WIDE), F32)
-        for c in range(CFF // 256):
-            cs = slice(c * 256, (c + 1) * 256)
-            bd = (nn(down[cs, :], g_low) * sslope[slot, cs].astype(F32)).astype(LOW)
-            aup[:, cs] += nt(normed_two, bd)
-            n2d = n2d + nn(up_ref[:, cs], bd)
+        ahead = nn(down[cuts[0], :], g_low)
+        bds = []
+        for c, cs in enumerate(cuts):
+            bds.append((ahead * sslope[slot, cs].astype(F32)).astype(LOW))
+            if c + 1 < len(cuts):
+                ahead = nn(down[cuts[c + 1], :], g_low)
+            n2d = n2d + nn(up_ref[:, cs], bds[c])
+        aup[:, cuts[0]] += nt(normed_two, bds[0])
         ag2[...] += n2d * vhat
         lifted = n2d * g2
-        md = g_low.astype(F32) + inv2 * (lifted - vhat * jnp.mean(lifted * vhat, axis=0, keepdims=True))
-        sdelta[slot] = md.astype(LOW)
-        delta_copy(b, slot).start()
+        aup[:, cuts[1]] += nt(normed_two, bds[1])
+        mean = jnp.mean(lifted * vhat, axis=0, keepdims=True)
+        aup[:, cuts[2]] += nt(normed_two, bds[2])
+        md = g_low.astype(F32) + inv2 * (lifted - vhat * mean)
+        delta_ref[b] = md.astype(LOW)
+        aup[:, cuts[3]] += nt(normed_two, bds[3])
+        give(jnp.minimum(b + 1, TURNS - 1))
         return carry
 
     lax.fori_loop(0, n_turns, turn, 0)
@@ -661,28 +667,21 @@
     add_up(facc_ref, f0_ref.at[pl.ds(a * 8, 8)], f1)
     gain_ref[...] = jnp.broadcast_to(jnp.sum(ag2[...], axis=1, keepdims=True), (CD, 8)).T
 
-    def drain(b, carry):
-        delta_copy(b, lax.rem(b, 2)).wait()
-        return carry
-
-    lax.fori_loop(jnp.maximum(n_turns - 2, 0), n_turns, drain, 0)
-
 
 def kernel_b2(
     turns_ref, wgain1_ref, wgain2_ref, gain2_ref, aup_ref, g1_ref, wq_ref, wk_ref, wv_ref, wo_ref,
-    keptl_hbm, keptd_hbm, kepti_hbm, facc_ref, f2_hbm, t0_ref, t1_hbm,
+    keptl_hbm, delta_ref, info_ref, facc_ref, f2_hbm, t0_ref, t1_hbm,
     keep_ref, send_ref, fnext_ref, tacc_ref,
-    slow, sinfo, sdelta, dscore, wqkv, aqkv, ao, atab, ag1, f2, t1, ksem, fsem,
+    slow, up_next, dscore, wqkv, aqkv, ao, atab, ag1, f2, t1, ksem, fsem,
 ):
     phase = lax.axis_index("phase")
     n_turns = turns_ref[0]
 
     def kept_copies(b, slot):
-        return (
-            pltpu.make_async_copy(keptl_hbm.at[b], slow.at[slot], ksem.at[0, slot]),
-            pltpu.make_async_copy(keptd_hbm.at[b], sdelta.at[slot], ksem.at[1, slot]),
-            pltpu.make_async_copy(kepti_hbm.at[b], sinfo.at[slot], ksem.at[2, slot]),
-        )
+        return [
+            pltpu.make_async_copy(keptl_hbm.at[b, rows], slow.at[slot, rows], ksem.at[i, slot])
+            for i, rows in enumerate((pl.ds(0, KEPT_FIRST), pl.ds(KEPT_FIRST, KEPT_LOW - KEPT_FIRST)))
+        ]
 
     for c in kept_copies(0, 0):
         c.start()
@@ -700,6 +699,11 @@
     for acc in (aqkv, ao, atab, ag1, dscore):
         acc[...] = jnp.zeros_like(acc)
 
+    def step(b):
+        up_next[...] = nn(wo_ref[...], delta_ref[b]).astype(LOW)
+
+    step(0)
+
     def turn(b, carry):
         slot = lax.rem(b, 2)
 
@@ -710,14 +714,7 @@
 
         for c in kept_copies(b, slot):
             c.wait()
-        inv1 = sinfo[slot, I_INV1:I_INV1 + 1]
-        ident = sinfo[slot, I_IDENT:I_IDENT + 1]
-        md_low = sdelta[slot]
-        do = nn(wo_ref[...], md_low).astype(LOW)
-        emb = slow[slot, R_EMB:R_EMB + CD].astype(F32)
-        ehat = emb * inv1
-        normed = (ehat * g1).astype(LOW)
-        hot = jnp.where(iota((CVOC, WIDE), 0).astype(F32) == ident, 1.0, 0.0).astype(LOW)
+        do = up_next[...]
         deltas = []
         for t in range(4):
             u, ks, ql = band(t)
@@ -740,6 +737,13 @@
                 h, v = (t % 2) * 2 + pair, t // 2
                 vs = slice(v * SPAN, (v + 1) * SPAN)
                 dv[h][v] = nt(do[h * HEAD:(h + 1) * HEAD, vs], slow[slot, R_P + h * SPAN:R_P + (h + 1) * SPAN, vs]).astype(LOW)
+        inv1 = info_ref[b, I_INV1:I_INV1 + 1]
+        ident = info_ref[b, I_IDENT:I_IDENT + 1]
+        md_low = delta_ref[b]
+        emb = slow[slot, R_EMB:R_EMB + CD].astype(F32)
+        ehat = emb * inv1
+        normed = (ehat * g1).astype(LOW)
+        hot = jnp.where(iota((CVOC, WIDE), 0).astype(F32) == ident, 1.0, 0.0).astype(LOW)
         for h in range(CHAR_HEADS):
             for u in range(2):
                 us = slice(u * SPAN, (u + 1) * SPAN)
@@ -755,6 +759,7 @@
         mean = jnp.mean(lifted * ehat, axis=0, keepdims=True)
         aqkv[:, 2 * CD:] += nt(normed, dqkv[2 * CD:])
         ed = md_low.astype(F32) + inv1 * (lifted - ehat * mean)
+        step(jnp.minimum(b + 1, TURNS - 1))
         ao[...] += nt(slow[slot, R_MIX:R_MIX + CD], md_low)
         atab[...] += nt(hot, ed.astype(LOW))
         return carry
@@ -799,20 +804,23 @@
         add_up(send_ref.at[at], f0_ref.at[pl.ds((1 - a) * 8 + i * 2, 2)], f1.at[at])
 
 
-def kernel_add_two(facc_ref, f2_hbm, t0_ref, t1_hbm, fsend_ref, ts1_ref, ts2_ref, ts3_ref, f2, t1, sem):
+def kernel_add_words(t0_ref, t1_hbm, ts1_ref, ts2_ref, ts3_ref, t1, sem):
+    places = [pl.ds(lax.bitwise_xor(own_plane(), k) * 4, 4) for k in range(1, 4)]
+    loads = [pltpu.make_async_copy(t1_hbm.at[at], t1.at[k], sem.at[k]) for k, at in enumerate(places)]
+    for load in loads:
+        load.start()
+    for k, out in enumerate((ts1_ref, ts2_ref, ts3_ref)):
+        loads[k].wait()
+        add_up(out, t0_ref.at[places[k]], t1.at[k])
+
+
+def kernel_add_two(facc_ref, f2_hbm, fsend_ref, f2, sem):
     _, _, low, _ = own_bits()
     half = pl.ds((1 - low) * 4, 4)
-    loads = [pltpu.make_async_copy(f2_hbm.at[half], f2, sem.at[0])]
-    places = [pl.ds(lax.bitwise_xor(own_plane(), k) * 4, 4) for k in range(1, 4)]
-    for k, at in enumerate(places):
-        loads.append(pltpu.make_async_copy(t1_hbm.at[at], t1.at[k], sem.at[1 + k]))
-    for load in loads:
-        load.start()
-    loads[0].wait()
+    load = pltpu.make_async_copy(f2_hbm.at[half], f2, sem.at[0])
+    load.start()
+    load.wait()
     add_up(fsend_ref, facc_ref.at[half], f2)
-    for k, out in enumerate((ts1_ref, ts2_ref, ts3_ref)):
-        loads[1 + k].wait()
-        add_up(out, t0_ref.at[places[k]], t1.at[k])
 
 
 def kernel_add_three(
@@ -937,7 +945,6 @@
             v((8, 128), jnp.int32), pltpu.SMEM((8, 128), jnp.int32),
             v((CFF, WIDE), F32), v((CFF, WIDE), LOW), v((CHAR_HEADS * SPAN, WIDE), LOW), v((8, WIDE), F32),
             v((CD, WIDE), LOW), v((8, WIDE), F32), v((8, WIDE), F32),
-            v((WORDS, WFF), LOW), v((WORDS, WFF), LOW),
             pltpu.SemaphoreType.DMA((15,)),
             pltpu.SemaphoreType.DMA((8,)),
             pltpu.SemaphoreType.DMA((4, 2)),
@@ -970,21 +977,20 @@
     v = pltpu.VMEM
     return pl.pallas_call(
         kernel_b1,
-        out_shape=(outside((TURNS, CD, WIDE), LOW), shape((CD, CFF), LOW), shape((8, CD), F32), v((8, F_ROWS, 256), LOW)),
-        in_specs=[SCALARS] + [INSIDE] * 4 + [ANYWHERE] * 3 + [INSIDE, ANYWHERE],
-        out_specs=(ANYWHERE, INSIDE, INSIDE, INSIDE),
+        out_shape=(v((TURNS, CD, WIDE), LOW), shape((CD, CFF), LOW), shape((8, CD), F32), v((8, F_ROWS, 256), LOW)),
+        in_specs=[SCALARS] + [INSIDE] * 4 + [ANYWHERE] * 2 + [INSIDE] * 2 + [ANYWHERE],
+        out_specs=(INSIDE,) * 4,
         scratch_shapes=[
-            v((2, CFF, WIDE), LOW), v((2, CD, WIDE), F32), v((2, 8, WIDE), F32), v((2, CD, WIDE), LOW),
+            v((2, CFF, WIDE), LOW), v((2, CD, WIDE), F32), v((CD, WIDE), LOW),
             v((CD, CFF), F32), v((CD, WIDE), F32), v((CFF, CD), LOW),
             v((8, F_ROWS, 256), LOW),
-            pltpu.SemaphoreType.DMA((3, 2)),
-            pltpu.SemaphoreType.DMA((2,)),
+            pltpu.SemaphoreType.DMA((2, 2)),
             pltpu.SemaphoreType.DMA((1,)),
         ],
         compiler_params=params(18),
         cost_estimate=pl.CostEstimate(flops=200 * 10**9, bytes_accessed=20 * 10**6, transcendentals=10**6),
         name="character_backward_one",
-    )(turns, gw, gain, up, down, *kept_outside(kepts, keptm, kepti), f0, *kept_outside(f1))
+    )(turns, gw, gain, up, down, *kept_outside(kepts, keptm), kepti, f0, *kept_outside(f1))
 
 
 def call_b2(turns, wgain1, wgain2, gain2, aup, weights, keptl, keptd, kepti, facc, f2, t0, t1):
@@ -994,10 +1000,10 @@
         out_shape=(
             v((SHARES, C_ROWS, 128), LOW), v((SHARES, C_ROWS, 128), LOW), v((4, F_ROWS, 256), LOW), v((4, T_ROWS, 256), LOW)
         ),
-        in_specs=[SCALARS] + [INSIDE] * 9 + [ANYWHERE] * 3 + [INSIDE, ANYWHERE] * 2,
+        in_specs=[SCALARS] + [INSIDE] * 9 + [ANYWHERE] + [INSIDE] * 3 + [ANYWHERE, INSIDE, ANYWHERE],
         out_specs=(INSIDE,) * 4,
         scratch_shapes=[
-            v((2, KEPT_LOW, WIDE), LOW), v((2, 8, WIDE), F32), v((2, CD, WIDE), LOW),
+            v((2, KEPT_LOW, WIDE), LOW), v((CD, WIDE), LOW),
             v((CHAR_HEADS * SPAN, WIDE), LOW),
             v((CD, 3 * CD), LOW),
             v((CD, 3 * CD), F32), v((CD, CD), F32), v((CVOC, CD), F32), v((CD, WIDE), F32),
@@ -1008,7 +1014,7 @@
         compiler_params=params(24),
         cost_estimate=pl.CostEstimate(flops=200 * 10**9, bytes_accessed=40 * 10**6, transcendentals=10**6),
         name="character_backward_two",
-    )(turns, wgain1, wgain2, gain2, aup, *weights, *kept_outside(keptl, keptd, kepti), facc, *kept_outside(f2), t0, *kept_outside(t1))
+    )(turns, wgain1, wgain2, gain2, aup, *weights, *kept_outside(keptl), keptd, kepti, facc, *kept_outside(f2), t0, *kept_outside(t1))
 
 
 def call_add(kernel, name, outs, parts, specs, scratch):
@@ -1029,12 +1035,16 @@
     return call_add(kernel_add_one, "add_one", (half,), (f0, *kept_outside(f1)), [INSIDE, ANYWHERE], (half,))[0]
 
 
-def add_two(facc, f2, t0, t1):
-    fs, ts = (4, F_ROWS, 256), (4, T_ROWS, 256)
+def add_words(t0, t1):
+    ts = (4, T_ROWS, 256)
     return call_add(
-        kernel_add_two, "add_two", (fs, ts, ts, ts), (facc, *kept_outside(f2), t0, *kept_outside(t1)),
-        [INSIDE, ANYWHERE] * 2, (fs, (3,) + ts),
+        kernel_add_words, "add_words", (ts, ts, ts), (t0, *kept_outside(t1)), [INSIDE, ANYWHERE], ((3,) + ts,)
     )
+
+
+def add_two(facc, f2):
+    fs = (4, F_ROWS, 256)
+    return call_add(kernel_add_two, "add_two", (fs,), (facc, *kept_outside(f2)), [INSIDE, ANYWHERE], (fs,))[0]
 
 
 def add_three(facc, f3, tacc, tgot):
@@ -1125,10 +1135,13 @@
     gw, fsend = together(gw, add_one(fkeep, fgot))
     f2, tgot = across(fsend, 0), flip(tsend, "phase", 1)
     keptd, aup, gain2, facc = call_b1(turns, gw, *one, fkeep, fgot)
-    keptd, f2, tgot = together(keptd, f2, tgot)
-    sends = add_two(facc, f2, tkeep, tgot)
-    keptd, fsend, *tsends = together(keptd, *sends)
-    f3, *tparts = across(fsend, 2), *(flip(send, "dp", k) for k, send in enumerate(tsends, 1))
+    keptd, tgot = together(keptd, tgot)
+    tsends = add_words(tkeep, tgot)
+    tparts = [flip(send, "dp", k) for k, send in enumerate(tsends, 1)]
+    f2 = after(f2, *tsends)
+    fsend = add_two(facc, f2)
+    keptd, fsend = together(keptd, fsend)
+    f3 = across(fsend, 2)
     ckeep, csend, facc, tacc = call_b2(
         turns, wgain1, wgain2, gain2, aup, two, keptl, keptd, kepti, facc, f2, tkeep, tgot
     )

time: 100 us -> 95.9 us (0.959)
  waiting for transfers between devices: 12.4 us -> 9.31 us
  Pallas kernels: 63.5 us -> 62.5 us
    ppermute x5, waiting for transfers between devices: 3.35 us -> 0.91 us  [flip_both(): return lax.ppermute(value, ('phase', 'dp'), pairs)]
    pallas_call x1, Pallas kernels: 11.3 us -> 9.42 us  [call_b1(): pl.pallas_call(kernel_b1, out_shape=(v((TURNS, CD, WIDE), LOW), shape((CD...]
    pallas_call x3 -> x4, Pallas kernels: 6.4 us -> 8.12 us  [call_add(): pl.pallas_call(kernel, out_shape=tuple((v(s, LOW) for s in outs)), in_spe...]
  transfers between devices with their start and end apart: 18 -> 18, of which waited for: 9 -> 8; matrix products, arithmetic and copies ran while one was open for 1% -> 1% of each run, Pallas kernels for 31% -> 35%
where the time goes in v6:
time: 95.9 us; the launch traced here: 95.6 us
  Pallas kernels  62.5 us (65%)
  starting transfers between devices  21.6 us (23%)
  waiting for transfers between devices  9.31 us (10%)
  between operations  1.09 us (1%)
  other arithmetic  1.02 us (1%)
    pallas_call x1, Pallas kernels, call_a(): pl.pallas_call(kernel_a, out_shape=(outside((TURNS, KEPT_LOW, WIDE), LOW)...  24.9 us
    pallas_call x1, Pallas kernels, call_b2(): pl.pallas_call(kernel_b2, out_shape=(v((SHARES, C_ROWS, 128), LOW), v((SH...  14 us
    ppermute x13, starting transfers between devices, flip(): return lax.ppermute(value, axis, [(i, i ^ bits) for i in range(count)])  12.7 us
    pallas_call x1, Pallas kernels, call_b1(): pl.pallas_call(kernel_b1, out_shape=(v((TURNS, CD, WIDE), LOW), shape((CD...  9.42 us
    ppermute x5, starting transfers between devices, flip_both(): return lax.ppermute(value, ('phase', 'dp'), pairs)  8.9 us
    ppermute x13, waiting for transfers between devices, flip(): return lax.ppermute(value, axis, [(i, i ^ bits) for i in range(count)])  8.4 us
    pallas_call x4, Pallas kernels, call_add(): pl.pallas_call(kernel, out_shape=tuple((v(s, LOW) for s in outs)), in_spe...  8.12 us
    pallas_call x1, Pallas kernels, call_a2(): pl.pallas_call(kernel_a2, out_shape=(shape((CD, WORDS), LOW), v((SHARES,...  4.28 us
  transfers between devices with their start and end apart: 18, of which 8 were waited for; matrix products, arithmetic and copies ran while one was open for 1% of the time, Pallas kernels for 35%

profile of v6, /device:TPU:0, one launch (start us, length us, event | category | flops | bytes accessed | tf_op | source)
XLA Modules:
  0.0 95.6 jit_solution(6123925164589642910)
XLA Ops:
  0.7 24.9 %forward_and_words.1 = (bf16[9,2304,512]{2,1,0:T(8,128)(2,1)}, bf16[9,1024,512]{2,1,0:T(8,128)(2,1)}, f32[9,256,512]{2,1,0:T(8,128)}, f32[9,8,512]{2,1,0:T(8,128...) custom-call(s32[2,1,256]{2,1,0:T(1,128)} %counts_ref.1, ...), custom_call_target="tpu_custom_call" | custom-call | flops 199999995904 | bytes 60000000 | tf_op jit(solution)/shard_map/forward_and_words/pallas_call | solution.py:915
  25.6 0.5 collective-permute-start
  26.3 4.3 %word_attention_backward.1 = (bf16[256,256]{1,0:T(8,128)(2,1)S(1)}, bf16[16,176,256]{2,1,0:T(8,128)(2,1)S(1)}, bf16[16,176,256]{2,1,0:T(8,128)(2,1)}, f32[8,512]{1,0:T(8,128)S(1)}) custom-call(s32[2,1,256]{2,1,0:T(1,128)S(1)} %copy-done.11, bf16[256,512]{1,0:T(8,128)(2,1)S(1)} %get-tuple-element.80.q_ref, bf16[256,512]{1,0:T(8,128)(2,1)S(1)} %get-tuple-element.81.k_ref, ...), custom_call_target="tpu_custom_call" | custom-call | flops 199999995904 | bytes 10000000 | tf_op jit(solution)/shard_map/word_attention_backward/pallas_call | solution.py:960
  30.6 2.4 %add_one.1 = bf16[8,256,256]{2,1,0:T(8,128)(2,1)} custom-call(bf16[16,256,256]{2,1,0:T(8,128)(2,1)S(1)} %get-tuple-element.98.f0_ref, bf16[16,256,256]{2,1,0:T(8,128)(2,1)} %collective-permute-done.f1_hbm), custom_call_target="tpu_custom_call" | custom-call | tf_op jit(solution)/shard_map/add_one/pallas_call | solution.py:1022
  32.9 0.5 collective-permute-start.2
  33.4 2.5 %collective-permute-start.3 = (bf16[8,256,256]{2,1,0:T(8,128)(2,1)}, bf16[8,256,256]{2,1,0:T(8,128)(2,1)}, u32[]{:S(2)}, u32[]{:S(2)}) collective-permute-start(bf16[8,256,256]{2,1,0:T(8,128)(2,1)} %add_one.1), channel_id=1, source_target_pairs={{0,1},{1,0},{2,3},{3,2},{4,5},{5,4},{6,7},{7,6},{8,9},{9,8},{10,11... | collective-permute-start | bytes 3145736 | tf_op jit(solution)/shard_map/ppermute | solution.py:1080
  36.0 9.4 %character_backward_one.1 = (bf16[9,256,512]{2,1,0:T(8,128)(2,1)S(1)}, bf16[256,1024]{1,0:T(8,128)(2,1)S(1)}, f32[8,256]{1,0:T(8,128)S(1)}, bf16[8,256,256]{2,1,0:T(8,128)(2,1)S(1)}) custom-call(s32[1]{0:T(128)} %get-tuple-element.79.turns_ref, bf16[256,256]{1,0:T(8,128)(2,1)S(1)} %get-tuple-element.100.gw_ref, bf16[256]{0:T(256)(128)(2,1)S(1)} %copy-done.13, ...), custom_call_target="tpu_custom_call" | custom-call | flops 199999995904 | bytes 20000000 | tf_op jit(solution)/shard_map/character_backward_one/pallas_call | solution.py:978
  45.5 2.4 %add_words.1 = (bf16[4,176,256]{2,1,0:T(8,128)(2,1)}, bf16[4,176,256]{2,1,0:T(8,128)(2,1)}, bf16[4,176,256]{2,1,0:T(8,128)(2,1)}) custom-call(bf16[16,176,256]{2,1,0:T(8,128)(2,1)S(1)} %get-tuple-element.112.t0_ref, bf16[16,176,256]{2,1,0:T(8,128)(2,1)} %collective-permute-done.2.t1_hbm), custom_call_target="tpu_custom_call" | custom-call | tf_op jit(solution)/shard_map/add_words/pallas_call | solution.py:1022
  48.0 2.0 %collective-permute-start.6 = (bf16[4,176,256]{2,1,0:T(8,128)(2,1)}, bf16[4,176,256]{2,1,0:T(8,128)(2,1)}, u32[]{:S(2)}, u32[]{:S(2)}) collective-permute-start(bf16[4,176,256]{2,1,0:T(8,128)(2,1)} %get-tuple-element.115), channel_id=1, source_target_pairs={{0,2},{1,3},{2,0},{3,1},{4,6},{5,7},{6,4},{7,5},{8,10},{9,11},{10,... | collective-permute-start | bytes 1081352 | tf_op jit(solution)/shard_map/ppermute | solution.py:1075
  50.0 1.4 %collective-permute-start.7 = (bf16[4,176,256]{2,1,0:T(8,128)(2,1)}, bf16[4,176,256]{2,1,0:T(8,128)(2,1)}, u32[]{:S(2)}, u32[]{:S(2)}) collective-permute-start(bf16[4,176,256]{2,1,0:T(8,128)(2,1)} %get-tuple-element.116), channel_id=1, source_target_pairs={{0,3},{1,2},{2,1},{3,0},{4,7},{5,6},{6,5},{7,4},{8,11},{9,10},{10,... | collective-permute-start | bytes 1081352 | tf_op jit(solution)/shard_map/ppermute | solution.py:1075
  51.4 1.9 %add_two.1 = bf16[4,256,256]{2,1,0:T(8,128)(2,1)} custom-call(bf16[8,256,256]{2,1,0:T(8,128)(2,1)S(1)} %get-tuple-element.110.facc_ref, bf16[8,256,256]{2,1,0:T(8,128)(2,1)} %collective-permute-done.3.f2_hbm), custom_call_target="tpu_custom_call" | custom-call | tf_op jit(solution)/shard_map/add_two/pallas_call | solution.py:1022
  53.4 1.6 %collective-permute-start.4 = (bf16[4,256,256]{2,1,0:T(8,128)(2,1)}, bf16[4,256,256]{2,1,0:T(8,128)(2,1)}, u32[]{:S(2)}, u32[]{:S(2)}) collective-permute-start(bf16[4,256,256]{2,1,0:T(8,128)(2,1)} %add_two.1), channel_id=1, source_target_pairs={{0,4},{1,5},{2,6},{3,7},{4,0},{5,1},{6,2},{7,3},{8,12},{9,13},{10,... | collective-permute-start | bytes 1572872 | tf_op jit(solution)/shard_map/ppermute | solution.py:1080
  55.0 14.0 %character_backward_two.1 = (bf16[16,160,128]{2,1,0:T(8,128)(2,1)S(1)}, bf16[16,160,128]{2,1,0:T(8,128)(2,1)}, bf16[4,256,256]{2,1,0:T(8,128)(2,1)S(1)}, bf16[4,176,256]{2,1,0:T(8,128)(2,1)S(1)}) custom-call(s32[1]{0:T(128)} %get-tuple-element.79.turns_ref, f32[8,512]{1,0:T(8,128)S(1)} %get-tuple-element.91.wgain1_ref, ...), custom_call_target="tpu_custom_call" | custom-call | flops 199999995904 | bytes 40000000 | tf_op jit(solution)/shard_map/character_backward_two/pallas_call | solution.py:998
  69.1 1.5 %add_three.1 = (bf16[2,256,256]{2,1,0:T(8,128)(2,1)S(1)}, bf16[2,256,256]{2,1,0:T(8,128)(2,1)S(1)}, bf16[2,176,256]{2,1,0:T(8,128)(2,1)S(1)}, bf16[2,176,256]{2,1,0:T(8,128)(2,1)S(1)}) custom-call(bf16[4,256,256]{2,1,0:T(8,128)(2,1)S(1)} %get-tuple-element.123.facc_ref, bf16[4,256,256]{2,1,0:T(8,128)(2,1)} %collective-permute-done.4.f3_hbm, ...), custom_call_target="tpu_custom_call" | custom-call | tf_op jit(solution)/shard_map/add_three/pallas_call | solution.py:1022
  70.6 1.6 %collective-permute-start.8 = (bf16[2,256,256]{2,1,0:T(8,128)(2,1)S(1)}, bf16[2,256,256]{2,1,0:T(8,128)(2,1)S(1)}, u32[]{:S(2)}, u32[]{:S(2)}) collective-permute-start(bf16[2,256,256]{2,1,0:T(8,128)(2,1)S(1)} %get-tuple-element.130), channel_id=1, source_target_pairs={{0,2},{1,3},{2,0},{3,1},{4,6},{5,7},{6,4},{7,5},{8,10},{9,11},{10,... | collective-permute-start | bytes 786440 | tf_op jit(solution)/shard_map/ppermute | solution.py:1080
  72.2 0.4 collective-permute-start.10
  72.7 0.8 fusion.2
  73.5 0.5 collective-permute-start.12
  74.0 0.5 collective-permute-start.13
  74.5 2.5 %collective-permute-start.14 = (bf16[4,160,128]{2,1,0:T(8,128)(2,1)S(1)}, bf16[4,160,128]{2,1,0:T(8,128)(2,1)S(1)}, u32[]{:S(2)}, u32[]{:S(2)}) collective-permute-start(bf16[4,160,128]{2,1,0:T(8,128)(2,1)S(1)} %get-tuple-element.142), channel_id=1, source_target_pairs={{0,3},{1,2},{2,1},{3,0},{4,7},{5,6},{6,5},{7,4},{8,11},{9,10},{10,... | collective-permute-start | bytes 491528 | tf_op jit(solution)/shard_map/ppermute | solution.py:1075
  77.0 0.6 collective-permute-done.8.f4
  77.6 0.3 collective-permute-done.10.t3
  78.0 2.7 %collective-permute-start.11 = (bf16[432,256]{1,0:T(8,128)(2,1)S(1)}, bf16[432,256]{1,0:T(8,128)(2,1)S(1)}, u32[]{:S(2)}, u32[]{:S(2)}) collective-permute-start(bf16[432,256]{1,0:T(8,128)(2,1)S(1)} %pad_maximum_fusion), channel_id=1, source_target_pairs={{0,8},{1,9},{2,10},{3,11},{4,12},{5,13},{6,14},{7,15},{8,0},{9,1},... | collective-permute-start | bytes 663560 | tf_op jit(solution)/shard_map/ppermute | solution.py:1080
  80.9 2.4 %collective-permute-done.13.c3 = bf16[4,160,128]{2,1,0:T(8,128)(2,1)S(1)} collective-permute-done((bf16[4,160,128]{2,1,0:T(8,128)(2,1)}, bf16[4,160,128]{2,1,0:T(8,128)(2,1)S(1)}, u32[]{:S(2)}, u32[]{:S(2)}) %collective-permute-start.13) | collective-permute-done | bytes 163872 | tf_op jit(solution)/shard_map/ppermute | solution.py:1075
  83.3 1.0 %collective-permute-done.14.c4 = bf16[4,160,128]{2,1,0:T(8,128)(2,1)S(1)} collective-permute-done((bf16[4,160,128]{2,1,0:T(8,128)(2,1)S(1)}, bf16[4,160,128]{2,1,0:T(8,128)(2,1)S(1)}, u32[]{:S(2)}, u32[]{:S(2)}) %collective-permute-start.14) | collective-permute-done | bytes 163872 | tf_op jit(solution)/shard_map/ppermute | solution.py:1075
  84.4 0.8 collective-permute-start.15
  85.2 2.6 %collective-permute-start.16 = (bf16[160,128]{1,0:T(8,128)(2,1)S(1)}, bf16[160,128]{1,0:T(8,128)(2,1)S(1)}, u32[]{:S(2)}, u32[]{:S(2)}) collective-permute-start(bf16[160,128]{1,0:T(8,128)(2,1)S(1)} %get-tuple-element.140), channel_id=1, source_target_pairs={{0,8},{1,9},{2,10},{3,11},{4,12},{5,13},{6,14},{7,15},{8,0},{9,1},... | collective-permute-start | bytes 122888 | tf_op jit(solution)/shard_map/ppermute | solution.py:1075
  87.8 1.0 %collective-permute-start.17 = (bf16[160,128]{1,0:T(8,128)(2,1)S(1)}, bf16[160,128]{1,0:T(8,128)(2,1)S(1)}, u32[]{:S(2)}, u32[]{:S(2)}) collective-permute-start(bf16[160,128]{1,0:T(8,128)(2,1)S(1)} %get-tuple-element.139), channel_id=1, source_target_pairs={{0,12},{1,13},{2,14},{3,15},{4,8},{5,9},{6,10},{7,11},{8,4},{9,5},... | collective-permute-start | bytes 122888 | tf_op jit(solution)/shard_map/ppermute | solution.py:1075
  88.8 2.3 %collective-permute-done.15.c5 = bf16[160,128]{1,0:T(8,128)(2,1)S(1)} collective-permute-done((bf16[160,128]{1,0:T(8,128)(2,1)S(1)}, bf16[160,128]{1,0:T(8,128)(2,1)S(1)}, u32[]{:S(2)}, u32[]{:S(2)}) %collective-permute-start.15) | collective-permute-done | bytes 40992 | tf_op jit(solution)/shard_map/ppermute | solution.py:1075
  91.2 0.9 collective-permute-done.16.c6
  92.1 1.6 %collective-permute-done.17.c7 = bf16[160,128]{1,0:T(8,128)(2,1)S(1)} collective-permute-done((bf16[160,128]{1,0:T(8,128)(2,1)S(1)}, bf16[160,128]{1,0:T(8,128)(2,1)S(1)}, u32[]{:S(2)}, u32[]{:S(2)}) %collective-permute-start.17) | collective-permute-done | bytes 40992 | tf_op jit(solution)/shard_map/ppermute | solution.py:1075
  93.6 1.9 %finish.1 = (bf16[2,1,256,256]{3,2,1,0:T(8,128)(2,1)}, f32[16,128]{1,0:T(8,128)}, f32[16]{0:T(128)}, f32[16,128]{1,0:T(8,128)}, f32[16,128]{1,0:T(8,128)}, /*ind...) custom-call(bf16[2,256,256]{2,1,0:T(8,128)(2,1)S(1)} %get-tuple-elem, ...), custom_call_target="tpu_custom_call" | custom-call | tf_op jit(solution)/shard_map/finish/pallas_call | solution.py:1063
  (50 shorter events, 0.7 us)
Async XLA Ops:
  0.7 25.6 %copy-start = (bf16[512,512]{1,0:T(8,128)(2,1)S(1)}, bf16[512,512]{1,0:T(8,128)(2,1)}, u32[]{:S(2)}) copy-start(bf16[512,512]{1,0:T(8,128)(2,1)} %wwq.1) | copy-start | bytes 1572868
  0.7 25.6 %copy-start.1 = (bf16[512,512]{1,0:T(8,128)(2,1)S(1)}, bf16[512,512]{1,0:T(8,128)(2,1)}, u32[]{:S(2)}) copy-start(bf16[512,512]{1,0:T(8,128)(2,1)} %wwk.1) | copy-start | bytes 1572868
  0.7 25.5 %copy-start.2 = (bf16[512,512]{1,0:T(8,128)(2,1)S(1)}, bf16[512,512]{1,0:T(8,128)(2,1)}, u32[]{:S(2)}) copy-start(bf16[512,512]{1,0:T(8,128)(2,1)} %wwv.1) | copy-start | bytes 1572868
  0.7 25.5 %copy-start.3 = (bf16[512,512]{1,0:T(8,128)(2,1)S(1)}, bf16[512,512]{1,0:T(8,128)(2,1)}, u32[]{:S(2)}) copy-start(bf16[512,512]{1,0:T(8,128)(2,1)} %wwo.1) | copy-start | bytes 1572868
  0.7 25.5 %copy-start.6 = (bf16[256,512]{1,0:T(8,128)(2,1)S(1)}, bf16[256,512]{1,0:T(8,128)(2,1)}, u32[]{:S(2)}) copy-start(bf16[256,512]{1,0:T(8,128)(2,1)} %proj_ref.1) | copy-start | bytes 786436
  0.7 25.5 %copy-start.11 = (s32[2,1,256]{2,1,0:T(1,128)S(1)}, s32[2,1,256]{2,1,0:T(1,128)}, u32[]{:S(2)}) copy-start(s32[2,1,256]{2,1,0:T(1,128)} %counts_ref.1) | copy-start | bytes 6148
  0.7 25.5 %copy-start.12 = (bf16[512]{0:T(512)(128)(2,1)S(1)}, bf16[512]{0:T(512)(128)(2,1)}, u32[]{:S(2)}) copy-start(bf16[512]{0:T(512)(128)(2,1)} %wg1_ref.1) | copy-start | bytes 3076
  25.6 4.9 %collective-permute-start = (bf16[16,256,256]{2,1,0:T(8,128)(2,1)}, bf16[16,256,256]{2,1,0:T(8,128)(2,1)}, u32[]{:S(2)}, u32[]{:S(2)}) collective-permute-start(bf16[16,256,256]{2,1,0:T(8,128)(2,1)} %get-tuple-element.95), channel_id=1, source_target_pairs={{0,16},{16,0},{1,17},{17,1},{2,18},{18,2},{3,19},{19,3},{4,20},{20... | collective-permute-start | bytes 6291464 | tf_op jit(solution)/shard_map/ppermute | solution.py:1075
  26.1 4.4 %collective-permute-start.1 = (bf16[256,256]{1,0:T(8,128)(2,1)}, bf16[256,256]{1,0:T(8,128)(2,1)}, u32[]{:S(2)}, u32[]{:S(2)}) collective-permute-start(bf16[256,256]{1,0:T(8,128)(2,1)} %get-tuple-element.96), channel_id=1, source_target_pairs={{0,16},{16,0},{1,17},{17,1},{2,18},{18,2},{3,19},{19,3},{4,20},{20... | collective-permute-start | bytes 393224 | tf_op jit(solution)/shard_map/ppermute | solution.py:1075
  30.5 5.4 %copy-start.4 = (bf16[256,1024]{1,0:T(8,128)(2,1)S(1)}, bf16[256,1024]{1,0:T(8,128)(2,1)}, u32[]{:S(2)}) copy-start(bf16[256,1024]{1,0:T(8,128)(2,1)} %up_ref.1) | copy-start | bytes 1572868
  30.6 5.4 %copy-start.5 = (bf16[1024,256]{1,0:T(8,128)(2,1)S(1)}, bf16[1024,256]{1,0:T(8,128)(2,1)}, u32[]{:S(2)}) copy-start(bf16[1024,256]{1,0:T(8,128)(2,1)} %down_ref.1) | copy-start | bytes 1572868
  32.9 12.5 %collective-permute-start.2 = (bf16[16,176,256]{2,1,0:T(8,128)(2,1)}, bf16[16,176,256]{2,1,0:T(8,128)(2,1)}, u32[]{:S(2)}, u32[]{:S(2)}) collective-permute-start(bf16[16,176,256]{2,1,0:T(8,128)(2,1)} %get-tuple-element.108), channel_id=1, source_target_pairs={{0,16},{16,0},{1,17},{17,1},{2,18},{18,2},{3,19},{19,3},{4,20},{20... | collective-permute-start | bytes 4325384 | tf_op jit(solution)/shard_map/ppermute | solution.py:1075
  33.4 18.0 %collective-permute-start.3 = (bf16[8,256,256]{2,1,0:T(8,128)(2,1)}, bf16[8,256,256]{2,1,0:T(8,128)(2,1)}, u32[]{:S(2)}, u32[]{:S(2)}) collective-permute-start(bf16[8,256,256]{2,1,0:T(8,128)(2,1)} %add_one.1), channel_id=1, source_target_pairs={{0,1},{1,0},{2,3},{3,2},{4,5},{5,4},{6,7},{7,6},{8,9},{9,8},{10,11... | collective-permute-start | bytes 3145736 | tf_op jit(solution)/shard_map/ppermute | solution.py:1080
  45.4 9.6 %copy-start.7 = (bf16[256,256]{1,0:T(8,128)(2,1)S(1)}, bf16[256,256]{1,0:T(8,128)(2,1)}, u32[]{:S(2)}) copy-start(bf16[256,256]{1,0:T(8,128)(2,1)} %wq_ref.1) | copy-start | bytes 393220
  45.5 9.6 %copy-start.8 = (bf16[256,256]{1,0:T(8,128)(2,1)S(1)}, bf16[256,256]{1,0:T(8,128)(2,1)}, u32[]{:S(2)}) copy-start(bf16[256,256]{1,0:T(8,128)(2,1)} %wk_ref.1) | copy-start | bytes 393220
  45.5 9.6 %copy-start.9 = (bf16[256,256]{1,0:T(8,128)(2,1)S(1)}, bf16[256,256]{1,0:T(8,128)(2,1)}, u32[]{:S(2)}) copy-start(bf16[256,256]{1,0:T(8,128)(2,1)} %wv_ref.1) | copy-start | bytes 393220
  45.5 9.5 %copy-start.10 = (bf16[256,256]{1,0:T(8,128)(2,1)S(1)}, bf16[256,256]{1,0:T(8,128)(2,1)}, u32[]{:S(2)}) copy-start(bf16[256,256]{1,0:T(8,128)(2,1)} %wo_ref.1) | copy-start | bytes 393220
  45.5 9.5 %copy-start.14 = (bf16[256]{0:T(256)(128)(2,1)S(1)}, bf16[256]{0:T(256)(128)(2,1)}, u32[]{:S(2)}) copy-start(bf16[256]{0:T(256)(128)(2,1)} %g1_ref.1) | copy-start | bytes 1540
  47.9 21.2 %collective-permute-start.5 = (bf16[4,176,256]{2,1,0:T(8,128)(2,1)}, bf16[4,176,256]{2,1,0:T(8,128)(2,1)}, u32[]{:S(2)}, u32[]{:S(2)}) collective-permute-start(bf16[4,176,256]{2,1,0:T(8,128)(2,1)} %get-tuple-element.114), channel_id=1, source_target_pairs={{0,1},{1,0},{2,3},{3,2},{4,5},{5,4},{6,7},{7,6},{8,9},{9,8},{10,11... | collective-permute-start | bytes 1081352 | tf_op jit(solution)/shard_map/ppermute | solution.py:1075
  48.0 21.1 %collective-permute-start.6 = (bf16[4,176,256]{2,1,0:T(8,128)(2,1)}, bf16[4,176,256]{2,1,0:T(8,128)(2,1)}, u32[]{:S(2)}, u32[]{:S(2)}) collective-permute-start(bf16[4,176,256]{2,1,0:T(8,128)(2,1)} %get-tuple-element.115), channel_id=1, source_target_pairs={{0,2},{1,3},{2,0},{3,1},{4,6},{5,7},{6,4},{7,5},{8,10},{9,11},{10,... | collective-permute-start | bytes 1081352 | tf_op jit(solution)/shard_map/ppermute | solution.py:1075
  50.0 19.0 %collective-permute-start.7 = (bf16[4,176,256]{2,1,0:T(8,128)(2,1)}, bf16[4,176,256]{2,1,0:T(8,128)(2,1)}, u32[]{:S(2)}, u32[]{:S(2)}) collective-permute-start(bf16[4,176,256]{2,1,0:T(8,128)(2,1)} %get-tuple-element.116), channel_id=1, source_target_pairs={{0,3},{1,2},{2,1},{3,0},{4,7},{5,6},{6,5},{7,4},{8,11},{9,10},{10,... | collective-permute-start | bytes 1081352 | tf_op jit(solution)/shard_map/ppermute | solution.py:1075
  53.4 15.7 %collective-permute-start.4 = (bf16[4,256,256]{2,1,0:T(8,128)(2,1)}, bf16[4,256,256]{2,1,0:T(8,128)(2,1)}, u32[]{:S(2)}, u32[]{:S(2)}) collective-permute-start(bf16[4,256,256]{2,1,0:T(8,128)(2,1)} %add_two.1), channel_id=1, source_target_pairs={{0,4},{1,5},{2,6},{3,7},{4,0},{5,1},{6,2},{7,3},{8,12},{9,13},{10,... | collective-permute-start | bytes 1572872 | tf_op jit(solution)/shard_map/ppermute | solution.py:1080
  69.1 3.6 %collective-permute-start.9 = (bf16[16,160,128]{2,1,0:T(8,128)(2,1)}, bf16[16,160,128]{2,1,0:T(8,128)(2,1)S(1)}, u32[]{:S(2)}, u32[]{:S(2)}) collective-permute-start(bf16[16,160,128]{2,1,0:T(8,128)(2,1)} %get-tuple-element.132), channel_id=1, source_target_pairs={{0,16},{16,0},{1,17},{17,1},{2,18},{18,2},{3,19},{19,3},{4,20},{20... | collective-permute-start | bytes 1966088 | tf_op jit(solution)/shard_map/ppermute | solution.py:1075
  70.6 7.0 %collective-permute-start.8 = (bf16[2,256,256]{2,1,0:T(8,128)(2,1)S(1)}, bf16[2,256,256]{2,1,0:T(8,128)(2,1)S(1)}, u32[]{:S(2)}, u32[]{:S(2)}) collective-permute-start(bf16[2,256,256]{2,1,0:T(8,128)(2,1)S(1)} %get-tuple-element.130), channel_id=1, source_target_pairs={{0,2},{1,3},{2,0},{3,1},{4,6},{5,7},{6,4},{7,5},{8,10},{9,11},{10,... | collective-permute-start | bytes 786440 | tf_op jit(solution)/shard_map/ppermute | solution.py:1080
  72.2 5.7 %collective-permute-start.10 = (bf16[2,176,256]{2,1,0:T(8,128)(2,1)S(1)}, bf16[2,176,256]{2,1,0:T(8,128)(2,1)S(1)}, u32[]{:S(2)}, u32[]{:S(2)}) collective-permute-start(bf16[2,176,256]{2,1,0:T(8,128)(2,1)S(1)} %get-tuple-element.135), channel_id=1, source_target_pairs={{0,4},{1,5},{2,6},{3,7},{4,0},{5,1},{6,2},{7,3},{8,12},{9,13},{10,... | collective-permute-start | bytes 540680 | tf_op jit(solution)/shard_map/ppermute | solution.py:1080
  73.5 7.3 %collective-permute-start.12 = (bf16[4,160,128]{2,1,0:T(8,128)(2,1)}, bf16[4,160,128]{2,1,0:T(8,128)(2,1)S(1)}, u32[]{:S(2)}, u32[]{:S(2)}) collective-permute-start(bf16[4,160,128]{2,1,0:T(8,128)(2,1)} %get-tuple-element.144), channel_id=1, source_target_pairs={{0,1},{1,0},{2,3},{3,2},{4,5},{5,4},{6,7},{7,6},{8,9},{9,8},{10,11... | collective-permute-start | bytes 491528 | tf_op jit(solution)/shard_map/ppermute | solution.py:1075
  74.0 9.2 %collective-permute-start.13 = (bf16[4,160,128]{2,1,0:T(8,128)(2,1)}, bf16[4,160,128]{2,1,0:T(8,128)(2,1)S(1)}, u32[]{:S(2)}, u32[]{:S(2)}) collective-permute-start(bf16[4,160,128]{2,1,0:T(8,128)(2,1)} %get-tuple-element.143), channel_id=1, source_target_pairs={{0,2},{1,3},{2,0},{3,1},{4,6},{5,7},{6,4},{7,5},{8,10},{9,11},{10,... | collective-permute-start | bytes 491528 | tf_op jit(solution)/shard_map/ppermute | solution.py:1075
  74.5 9.8 %collective-permute-start.14 = (bf16[4,160,128]{2,1,0:T(8,128)(2,1)S(1)}, bf16[4,160,128]{2,1,0:T(8,128)(2,1)S(1)}, u32[]{:S(2)}, u32[]{:S(2)}) collective-permute-start(bf16[4,160,128]{2,1,0:T(8,128)(2,1)S(1)} %get-tuple-element.142), channel_id=1, source_target_pairs={{0,3},{1,2},{2,1},{3,0},{4,7},{5,6},{6,5},{7,4},{8,11},{9,10},{10,... | collective-permute-start | bytes 491528 | tf_op jit(solution)/shard_map/ppermute | solution.py:1075
  78.0 15.6 %collective-permute-start.11 = (bf16[432,256]{1,0:T(8,128)(2,1)S(1)}, bf16[432,256]{1,0:T(8,128)(2,1)S(1)}, u32[]{:S(2)}, u32[]{:S(2)}) collective-permute-start(bf16[432,256]{1,0:T(8,128)(2,1)S(1)} %pad_maximum_fusion), channel_id=1, source_target_pairs={{0,8},{1,9},{2,10},{3,11},{4,12},{5,13},{6,14},{7,15},{8,0},{9,1},... | collective-permute-start | bytes 663560 | tf_op jit(solution)/shard_map/ppermute | solution.py:1080
  84.4 6.8 %collective-permute-start.15 = (bf16[160,128]{1,0:T(8,128)(2,1)S(1)}, bf16[160,128]{1,0:T(8,128)(2,1)S(1)}, u32[]{:S(2)}, u32[]{:S(2)}) collective-permute-start(bf16[160,128]{1,0:T(8,128)(2,1)S(1)} %get-tuple-element.141), channel_id=1, source_target_pairs={{0,4},{1,5},{2,6},{3,7},{4,0},{5,1},{6,2},{7,3},{8,12},{9,13},{10,... | collective-permute-start | bytes 122888 | tf_op jit(solution)/shard_map/ppermute | solution.py:1075
  85.2 6.8 %collective-permute-start.16 = (bf16[160,128]{1,0:T(8,128)(2,1)S(1)}, bf16[160,128]{1,0:T(8,128)(2,1)S(1)}, u32[]{:S(2)}, u32[]{:S(2)}) collective-permute-start(bf16[160,128]{1,0:T(8,128)(2,1)S(1)} %get-tuple-element.140), channel_id=1, source_target_pairs={{0,8},{1,9},{2,10},{3,11},{4,12},{5,13},{6,14},{7,15},{8,0},{9,1},... | collective-permute-start | bytes 122888 | tf_op jit(solution)/shard_map/ppermute | solution.py:1075
  87.8 5.8 %collective-permute-start.17 = (bf16[160,128]{1,0:T(8,128)(2,1)S(1)}, bf16[160,128]{1,0:T(8,128)(2,1)S(1)}, u32[]{:S(2)}, u32[]{:S(2)}) collective-permute-start(bf16[160,128]{1,0:T(8,128)(2,1)S(1)} %get-tuple-element.139), channel_id=1, source_target_pairs={{0,12},{1,13},{2,14},{3,15},{4,8},{5,9},{6,10},{7,11},{8,4},{9,5},... | collective-permute-start | bytes 122888 | tf_op jit(solution)/shard_map/ppermute | solution.py:1075
  (2 other events, 10.9 us)

commit v7 on v6

--- a/solution.py
+++ b/solution.py
@@ -189,12 +189,13 @@
     wg1_hbm, wwq_hbm, wwk_hbm, wwv_hbm, wwo_hbm, wg2_hbm, wup_hbm, wdown_hbm,
     keptl_hbm, kepts_hbm, keptm_hbm, kepti_hbm, turns_ref,
     keep_ref, send_ref, outk_ref, outs_ref, gain_ref,
+    first_low_ref, first_slope_ref, first_mid_ref,
     q_ref, k_ref, v_ref, probs_ref, mixt_ref, normed_ref, xhat_ref, winv_ref, md_ref, pooled_ref, pa_ref,
     counts_ref, ids_ref, segs_ref,
     table_ref, g1_ref, wq_ref, wk_ref, wv_ref, wo_ref, g2_ref, up_ref, down_ref, proj_ref, wg1_ref, wg2_ref,
     cot, wwq, wwk, wwv, wwo, wup, wdown,
     tab_t, wqkv_t, wo_t, up_t, ids_t, slow, sslope, smid, sinfo, pa, pm, rowinfo, firsts_v, firsts, before_s, act_s, prob_s, found_s,
-    mid_s, word_s, old_s,
+    mid_s, word_s, old_s, back_s,
     csem, wsem, ksem,
 ):
     phase = lax.axis_index("phase")
@@ -422,6 +423,8 @@
     run("a" * 28, attend(jnp.int32(0)), None)
     more_one(jnp.int32(0))
     start(copies_one(jnp.int32(0)))
+    first_low_ref[...] = slow[0]
+    first_mid_ref[...] = smid[0]
 
     def turn(b, carry):
         @pl.when(b >= 2)
@@ -435,6 +438,11 @@
         run(SCHEDULE, attend(b), feed(b - 1))
         more_one(b)
         more_two(b - 1, old_s)
+
+        @pl.when(b == 1)
+        def _():
+            first_slope_ref[...] = sslope[0]
+
         start(copies_one(b))
         start(copies_two(b - 1))
         return carry
@@ -445,8 +453,20 @@
     def _():
         wait(copies_two(n_turns - 3))
 
-    run("f" * 4, None, feed(n_turns - 1))
+    for load in loads:
+        load.wait()
+    cot_low = cot[...]
+    last = feed(n_turns - 1)
+    for c in range(4):
+        cs = slice(c * 512, (c + 1) * 512)
+        back_s[:, cs] = nt(cot_low, wdown[cs, :])
+        next(last)
     more_two(n_turns - 1, word_s)
+
+    @pl.when(n_turns == 1)
+    def _():
+        first_slope_ref[...] = sslope[0]
+
     start(copies_two(n_turns - 1))
 
     pa_hi = pa[0:WORDS].astype(LOW)
@@ -456,8 +476,6 @@
     pooled_ref[...] = pooled_low
     pa_ref[...] = pa_hi
     x = nn(pooled_low, proj_ref[...]).astype(LOW).astype(F32)
-    for load in loads:
-        load.wait()
     wg1 = wg1_ref[...].astype(F32)[None, :]
     wg2 = wg2_ref[...].astype(F32)[None, :]
     winv1 = lax.rsqrt(jnp.mean(x * x, axis=1, keepdims=True) + epsilon)
@@ -494,7 +512,6 @@
     middle = x + nn(mixed_t.T, wwo[...])
     winv2 = lax.rsqrt(jnp.mean(middle * middle, axis=1, keepdims=True) + epsilon)
     normed_two = (middle * winv2 * wg2).astype(LOW)
-    cot_low = cot[...]
     result = middle
     n2d = jnp.zeros((WORDS, WD), F32)
     n2_t = normed_two.T
@@ -505,7 +522,7 @@
     for i, c in enumerate(turns):
         cs = quarter[c]
         act = act.astype(LOW)
-        bd = (nt(cot_low, wdown[cs, :]) * slope).astype(LOW)
+        bd = (back_s[:, cs] * slope).astype(LOW)
         if i < 3:
             ahead = nn(normed_two, wup[:, quarter[turns[i + 1]]])
         result = result + nn(act, wdown[cs, :])
@@ -599,7 +616,7 @@
 
 
 def kernel_b1(
-    turns_ref, gw_ref, g2_ref, up_ref, down_ref, kepts_hbm, keptm_hbm, info_ref, f0_ref, f1_hbm,
+    turns_ref, gw_ref, g2_ref, up_ref, down_ref, kepts_hbm, keptm_hbm, info_ref, f0_ref, f1_hbm, first_slope_ref, first_mid_ref,
     delta_ref, aup_ref, gain_ref, facc_ref,
     sslope, smid, given, aup, ag2, down, f1, ksem, fsem,
 ):
@@ -611,8 +628,8 @@
             pltpu.make_async_copy(keptm_hbm.at[b], smid.at[slot], ksem.at[1, slot]),
         )
 
-    for c in kept_copies(0, 0):
-        c.start()
+    sslope[0] = first_slope_ref[...]
+    smid[0] = first_mid_ref[...]
     a, _, _, _ = own_bits()
     load = pltpu.make_async_copy(f1_hbm.at[pl.ds(a * 8, 8)], f1, fsem.at[0])
     load.start()
@@ -634,8 +651,11 @@
             for c in kept_copies(b + 1, 1 - slot):
                 c.start()
 
-        for c in kept_copies(b, slot):
-            c.wait()
+        @pl.when(b > 0)
+        def _():
+            for c in kept_copies(b, slot):
+                c.wait()
+
         cuts = [slice(c * 256, (c + 1) * 256) for c in range(CFF // 256)]
         inv2 = info_ref[b, I_INV2:I_INV2 + 1]
         g_low = given[...]
@@ -670,7 +690,7 @@
 
 def kernel_b2(
     turns_ref, wgain1_ref, wgain2_ref, gain2_ref, aup_ref, g1_ref, wq_ref, wk_ref, wv_ref, wo_ref,
-    keptl_hbm, delta_ref, info_ref, facc_ref, f2_hbm, t0_ref, t1_hbm,
+    keptl_hbm, first_low_ref, delta_ref, info_ref, facc_ref, f2_hbm, t0_ref, t1_hbm,
     keep_ref, send_ref, fnext_ref, tacc_ref,
     slow, up_next, dscore, wqkv, aqkv, ao, atab, ag1, f2, t1, ksem, fsem,
 ):
@@ -683,8 +703,7 @@
             for i, rows in enumerate((pl.ds(0, KEPT_FIRST), pl.ds(KEPT_FIRST, KEPT_LOW - KEPT_FIRST)))
         ]
 
-    for c in kept_copies(0, 0):
-        c.start()
+    slow[0] = first_low_ref[...]
     _, _, low, _ = own_bits()
     quarter = pl.ds(own_plane() * 4, 4)
     loads = [
@@ -712,8 +731,11 @@
             for c in kept_copies(b + 1, 1 - slot):
                 c.start()
 
-        for c in kept_copies(b, slot):
-            c.wait()
+        @pl.when(b > 0)
+        def _():
+            for c in kept_copies(b, slot):
+                c.wait()
+
         do = up_next[...]
         deltas = []
         for t in range(4):
@@ -925,13 +947,14 @@
             shape((WORDS, WD // 2), LOW),
             shape((WORDS, WD // 2), LOW),
             shape((8, WD), F32),
+            v((KEPT_LOW, WIDE), LOW), v((CFF, WIDE), LOW), v((CD, WIDE), F32),
             shape((WORDS, WD), LOW), shape((WORDS, WD), LOW), shape((WORDS, WD), LOW),
             shape((WORD_HEADS, WORDS, WORDS), LOW), shape((WD, WORDS), LOW), shape((WORDS, WD), LOW),
             shape((WORDS, WD), F32), shape((WORDS, 128), F32), shape((WORDS, WD), F32),
             shape((WORDS, CD), LOW), shape((WORDS, CFF), LOW),
         ),
         in_specs=[ANYWHERE] * 22,
-        out_specs=(ANYWHERE,) * 4 + (SCALARS,) + (INSIDE,) * 16,
+        out_specs=(ANYWHERE,) * 4 + (SCALARS,) + (INSIDE,) * 19,
         scratch_shapes=[
             v((1, WORDS), jnp.int32), v((1, WORDS * CPW), jnp.int32), v((1, WORDS), jnp.int32),
             v((CVOC, CD), LOW), v((CD,), LOW), v((CD, CD), LOW), v((CD, CD), LOW), v((CD, CD), LOW), v((CD, CD), LOW),
@@ -944,12 +967,12 @@
             v((WORDS + WINDOW, CFF), F32), v((WORDS + WINDOW, CD), F32), v((16, WORDS), LOW),
             v((8, 128), jnp.int32), pltpu.SMEM((8, 128), jnp.int32),
             v((CFF, WIDE), F32), v((CFF, WIDE), LOW), v((CHAR_HEADS * SPAN, WIDE), LOW), v((8, WIDE), F32),
-            v((CD, WIDE), LOW), v((8, WIDE), F32), v((8, WIDE), F32),
+            v((CD, WIDE), LOW), v((8, WIDE), F32), v((8, WIDE), F32), v((WORDS, WFF), F32),
             pltpu.SemaphoreType.DMA((15,)),
             pltpu.SemaphoreType.DMA((8,)),
             pltpu.SemaphoreType.DMA((4, 2)),
         ],
-        compiler_params=params(44),
+        compiler_params=params(38),
         cost_estimate=pl.CostEstimate(flops=200 * 10**9, bytes_accessed=60 * 10**6, transcendentals=10**6),
         name="forward_and_words",
     )(*kept_outside(char_counts, char_ids, segment_ids, out_cotangent, *weights))
@@ -973,12 +996,12 @@
     )(char_counts, *kept, gain, project, *weights)
 
 
-def call_b1(turns, gw, gain, up, down, kepts, keptm, kepti, f0, f1):
+def call_b1(turns, gw, gain, up, down, kepts, keptm, kepti, f0, f1, first):
     v = pltpu.VMEM
     return pl.pallas_call(
         kernel_b1,
         out_shape=(v((TURNS, CD, WIDE), LOW), shape((CD, CFF), LOW), shape((8, CD), F32), v((8, F_ROWS, 256), LOW)),
-        in_specs=[SCALARS] + [INSIDE] * 4 + [ANYWHERE] * 2 + [INSIDE] * 2 + [ANYWHERE],
+        in_specs=[SCALARS] + [INSIDE] * 4 + [ANYWHERE] * 2 + [INSIDE] * 2 + [ANYWHERE] + [INSIDE] * 2,
         out_specs=(INSIDE,) * 4,
         scratch_shapes=[
             v((2, CFF, WIDE), LOW), v((2, CD, WIDE), F32), v((CD, WIDE), LOW),
@@ -990,17 +1013,17 @@
         compiler_params=params(18),
         cost_estimate=pl.CostEstimate(flops=200 * 10**9, bytes_accessed=20 * 10**6, transcendentals=10**6),
         name="character_backward_one",
-    )(turns, gw, gain, up, down, *kept_outside(kepts, keptm), kepti, f0, *kept_outside(f1))
-
-
-def call_b2(turns, wgain1, wgain2, gain2, aup, weights, keptl, keptd, kepti, facc, f2, t0, t1):
+    )(turns, gw, gain, up, down, *kept_outside(kepts, keptm), kepti, f0, *kept_outside(f1), *first)
+
+
+def call_b2(turns, wgain1, wgain2, gain2, aup, weights, keptl, first, keptd, kepti, facc, f2, t0, t1):
     v = pltpu.VMEM
     return pl.pallas_call(
         kernel_b2,
         out_shape=(
             v((SHARES, C_ROWS, 128), LOW), v((SHARES, C_ROWS, 128), LOW), v((4, F_ROWS, 256), LOW), v((4, T_ROWS, 256), LOW)
         ),
-        in_specs=[SCALARS] + [INSIDE] * 9 + [ANYWHERE] + [INSIDE] * 3 + [ANYWHERE, INSIDE, ANYWHERE],
+        in_specs=[SCALARS] + [INSIDE] * 9 + [ANYWHERE] + [INSIDE] * 4 + [ANYWHERE, INSIDE, ANYWHERE],
         out_specs=(INSIDE,) * 4,
         scratch_shapes=[
             v((2, KEPT_LOW, WIDE), LOW), v((CD, WIDE), LOW),
@@ -1014,7 +1037,7 @@
         compiler_params=params(24),
         cost_estimate=pl.CostEstimate(flops=200 * 10**9, bytes_accessed=40 * 10**6, transcendentals=10**6),
         name="character_backward_two",
-    )(turns, wgain1, wgain2, gain2, aup, *weights, *kept_outside(keptl), keptd, kepti, facc, *kept_outside(f2), t0, *kept_outside(t1))
+    )(turns, wgain1, wgain2, gain2, aup, *weights, *kept_outside(keptl), first, keptd, kepti, facc, *kept_outside(f2), t0, *kept_outside(t1))
 
 
 def call_add(kernel, name, outs, parts, specs, scratch):
@@ -1113,7 +1136,7 @@
     char_project,
     word_gain_one, word_query, word_key, word_value, word_output, word_gain_two, word_up, word_down,
 ):
-    keptl, kepts, keptm, kepti, turns, fkeep, fsend, outk, outs, wgain2, *words = call_a(
+    keptl, kepts, keptm, kepti, turns, fkeep, fsend, outk, outs, wgain2, flow, fslope, fmid, *words = call_a(
         char_counts, char_ids, segment_ids, out_cotangent,
         (char_table, char_gain_one, char_query, char_key, char_value, char_output, char_gain_two, char_up, char_down,
          char_project,
@@ -1127,14 +1150,14 @@
     one = (char_gain_two, char_up, char_down, kepts, keptm, kepti)
     two = (char_gain_one, char_query, char_key, char_value, char_output)
     if lax.axis_size("dp") != SHARES:
-        keptd, aup, gain2, facc = call_b1(turns, gw, *one, fkeep, fgot)
+        keptd, aup, gain2, facc = call_b1(turns, gw, *one, fkeep, fgot, (fslope, fmid))
         tgot = flip(tsend, "phase", 1)
-        ckeep, csend, _, _ = call_b2(turns, wgain1, wgain2, gain2, aup, two, keptl, keptd, kepti, facc, facc, tkeep, tgot)
+        ckeep, csend, _, _ = call_b2(turns, wgain1, wgain2, gain2, aup, two, keptl, flow, keptd, kepti, facc, facc, tkeep, tgot)
         return general_sums(outk, outg, (fkeep, fgot), (tkeep, tgot), (ckeep, flip(csend, "phase", 1)))
     gw, tsend, fgot, outg = together(gw, tsend, fgot, outg)
     gw, fsend = together(gw, add_one(fkeep, fgot))
     f2, tgot = across(fsend, 0), flip(tsend, "phase", 1)
-    keptd, aup, gain2, facc = call_b1(turns, gw, *one, fkeep, fgot)
+    keptd, aup, gain2, facc = call_b1(turns, gw, *one, fkeep, fgot, (fslope, fmid))
     keptd, tgot = together(keptd, tgot)
     tsends = add_words(tkeep, tgot)
     tparts = [flip(send, "dp", k) for k, send in enumerate(tsends, 1)]
@@ -1143,7 +1166,7 @@
     keptd, fsend = together(keptd, fsend)
     f3 = across(fsend, 2)
     ckeep, csend, facc, tacc = call_b2(
-        turns, wgain1, wgain2, gain2, aup, two, keptl, keptd, kepti, facc, f2, tkeep, tgot
+        turns, wgain1, wgain2, gain2, aup, two, keptl, flow, keptd, kepti, facc, f2, tkeep, tgot
     )
     ckeep, csend, facc, f3, *tparts = together(ckeep, csend, facc, f3, *tparts)
     _, _, low, high = own_bits()

time: 95.9 us -> 94.2 us (0.982)
  Pallas kernels: 62.5 us -> 60.3 us
    pallas_call x1, Pallas kernels: 14 us -> 12.7 us  [call_b2(): pl.pallas_call(kernel_b2, out_shape=(v((SHARES, C_ROWS, 128), LOW), v((SH...]
  transfers between devices with their start and end apart: 18 -> 18, of which waited for: 8 -> 7; matrix products, arithmetic and copies ran while one was open for 1% -> 1% of each run, Pallas kernels for 35% -> 33%
where the time goes in v7:
time: 94.2 us; the launch traced here: 93.8 us
  Pallas kernels  60.3 us (64%)
  starting transfers between devices  21.6 us (23%)
  waiting for transfers between devices  9.74 us (10%)
  between operations  1.09 us (1%)
  other arithmetic  1.02 us (1%)
    pallas_call x1, Pallas kernels, call_a(): pl.pallas_call(kernel_a, out_shape=(outside((TURNS, KEPT_LOW, WIDE), LOW)...  24.8 us
    pallas_call x1, Pallas kernels, call_b2(): pl.pallas_call(kernel_b2, out_shape=(v((SHARES, C_ROWS, 128), LOW), v((SH...  12.7 us
    ppermute x13, starting transfers between devices, flip(): return lax.ppermute(value, axis, [(i, i ^ bits) for i in range(count)])  12.7 us
    ppermute x5, starting transfers between devices, flip_both(): return lax.ppermute(value, ('phase', 'dp'), pairs)  8.92 us
    ppermute x13, waiting for transfers between devices, flip(): return lax.ppermute(value, axis, [(i, i ^ bits) for i in range(count)])  8.79 us
    pallas_call x1, Pallas kernels, call_b1(): pl.pallas_call(kernel_b1, out_shape=(v((TURNS, CD, WIDE), LOW), shape((CD...  8.5 us
    pallas_call x4, Pallas kernels, call_add(): pl.pallas_call(kernel, out_shape=tuple((v(s, LOW) for s in outs)), in_spe...  8.12 us
    pallas_call x1, Pallas kernels, call_a2(): pl.pallas_call(kernel_a2, out_shape=(shape((CD, WORDS), LOW), v((SHARES,...  4.28 us
  transfers between devices with their start and end apart: 18, of which 7 were waited for; matrix products, arithmetic and copies ran while one was open for 1% of the time, Pallas kernels for 33%

profile of v7, /device:TPU:0, one launch (start us, length us, event | category | flops | bytes accessed | tf_op | source)
XLA Modules:
  0.0 93.8 jit_solution(390507545061674753)
XLA Ops:
  0.7 24.8 %forward_and_words.1 = (bf16[9,2304,512]{2,1,0:T(8,128)(2,1)}, bf16[9,1024,512]{2,1,0:T(8,128)(2,1)}, f32[9,256,512]{2,1,0:T(8,128)}, f32[9,8,512]{2,1,0:T(8,128...) custom-call(s32[2,1,256]{2,1,0:T(1,128)} %counts_ref.1, ...), custom_call_target="tpu_custom_call" | custom-call | flops 199999995904 | bytes 60000000 | tf_op jit(solution)/shard_map/forward_and_words/pallas_call | solution.py:937
  25.6 0.5 collective-permute-start
  26.2 4.3 %word_attention_backward.1 = (bf16[256,256]{1,0:T(8,128)(2,1)S(1)}, bf16[16,176,256]{2,1,0:T(8,128)(2,1)S(1)}, bf16[16,176,256]{2,1,0:T(8,128)(2,1)}, f32[8,512]{1,0:T(8,128)S(1)}) custom-call(s32[2,1,256]{2,1,0:T(1,128)S(1)} %copy-done.11, bf16[256,512]{1,0:T(8,128)(2,1)S(1)} %get-tuple-element.83.q_ref, bf16[256,512]{1,0:T(8,128)(2,1)S(1)} %get-tuple-element.84.k_ref, ...), custom_call_target="tpu_custom_call" | custom-call | flops 199999995904 | bytes 10000000 | tf_op jit(solution)/shard_map/word_attention_backward/pallas_call | solution.py:983
  30.6 2.4 %add_one.1 = bf16[8,256,256]{2,1,0:T(8,128)(2,1)} custom-call(bf16[16,256,256]{2,1,0:T(8,128)(2,1)S(1)} %get-tuple-element.101.f0_ref, bf16[16,256,256]{2,1,0:T(8,128)(2,1)} %collective-permute-done.f1_hbm), custom_call_target="tpu_custom_call" | custom-call | tf_op jit(solution)/shard_map/add_one/pallas_call | solution.py:1045
  32.9 0.5 collective-permute-start.2
  33.4 2.6 %collective-permute-start.3 = (bf16[8,256,256]{2,1,0:T(8,128)(2,1)}, bf16[8,256,256]{2,1,0:T(8,128)(2,1)}, u32[]{:S(2)}, u32[]{:S(2)}) collective-permute-start(bf16[8,256,256]{2,1,0:T(8,128)(2,1)} %add_one.1), channel_id=1, source_target_pairs={{0,1},{1,0},{2,3},{3,2},{4,5},{5,4},{6,7},{7,6},{8,9},{9,8},{10,11... | collective-permute-start | bytes 3145736 | tf_op jit(solution)/shard_map/ppermute | solution.py:1103
  36.0 8.5 %character_backward_one.1 = (bf16[9,256,512]{2,1,0:T(8,128)(2,1)S(1)}, bf16[256,1024]{1,0:T(8,128)(2,1)S(1)}, f32[8,256]{1,0:T(8,128)S(1)}, bf16[8,256,256]{2,1,0:T(8,128)(2,1)S(1)}) custom-call(s32[1]{0:T(128)} %get-tuple-element.82.turns_ref, bf16[256,256]{1,0:T(8,128)(2,1)S(1)} %get-tuple-element.103.gw_ref, bf16[256]{0:T(256)(128)(2,1)S(1)} %copy-done.13, ...), custom_call_target="tpu_custom_call" | custom-call | flops 199999995904 | bytes 20000000 | tf_op jit(solution)/shard_map/character_backward_one/pallas_call | solution.py:1001
  44.6 2.4 %add_words.1 = (bf16[4,176,256]{2,1,0:T(8,128)(2,1)}, bf16[4,176,256]{2,1,0:T(8,128)(2,1)}, bf16[4,176,256]{2,1,0:T(8,128)(2,1)}) custom-call(bf16[16,176,256]{2,1,0:T(8,128)(2,1)S(1)} %get-tuple-element.118.t0_ref, bf16[16,176,256]{2,1,0:T(8,128)(2,1)} %collective-permute-done.2.t1_hbm), custom_call_target="tpu_custom_call" | custom-call | tf_op jit(solution)/shard_map/add_words/pallas_call | solution.py:1045
  47.1 2.0 %collective-permute-start.6 = (bf16[4,176,256]{2,1,0:T(8,128)(2,1)}, bf16[4,176,256]{2,1,0:T(8,128)(2,1)}, u32[]{:S(2)}, u32[]{:S(2)}) collective-permute-start(bf16[4,176,256]{2,1,0:T(8,128)(2,1)} %get-tuple-element.121), channel_id=1, source_target_pairs={{0,2},{1,3},{2,0},{3,1},{4,6},{5,7},{6,4},{7,5},{8,10},{9,11},{10,... | collective-permute-start | bytes 1081352 | tf_op jit(solution)/shard_map/ppermute | solution.py:1098
  49.1 1.4 %collective-permute-start.7 = (bf16[4,176,256]{2,1,0:T(8,128)(2,1)}, bf16[4,176,256]{2,1,0:T(8,128)(2,1)}, u32[]{:S(2)}, u32[]{:S(2)}) collective-permute-start(bf16[4,176,256]{2,1,0:T(8,128)(2,1)} %get-tuple-element.122), channel_id=1, source_target_pairs={{0,3},{1,2},{2,1},{3,0},{4,7},{5,6},{6,5},{7,4},{8,11},{9,10},{10,... | collective-permute-start | bytes 1081352 | tf_op jit(solution)/shard_map/ppermute | solution.py:1098
  50.5 1.9 %add_two.1 = bf16[4,256,256]{2,1,0:T(8,128)(2,1)} custom-call(bf16[8,256,256]{2,1,0:T(8,128)(2,1)S(1)} %get-tuple-element.116.facc_ref, bf16[8,256,256]{2,1,0:T(8,128)(2,1)} %collective-permute-done.3.f2_hbm), custom_call_target="tpu_custom_call" | custom-call | tf_op jit(solution)/shard_map/add_two/pallas_call | solution.py:1045
  52.5 1.6 %collective-permute-start.4 = (bf16[4,256,256]{2,1,0:T(8,128)(2,1)}, bf16[4,256,256]{2,1,0:T(8,128)(2,1)}, u32[]{:S(2)}, u32[]{:S(2)}) collective-permute-start(bf16[4,256,256]{2,1,0:T(8,128)(2,1)} %add_two.1), channel_id=1, source_target_pairs={{0,4},{1,5},{2,6},{3,7},{4,0},{5,1},{6,2},{7,3},{8,12},{9,13},{10,... | collective-permute-start | bytes 1572872 | tf_op jit(solution)/shard_map/ppermute | solution.py:1103
  54.1 12.7 %character_backward_two.1 = (bf16[16,160,128]{2,1,0:T(8,128)(2,1)S(1)}, bf16[16,160,128]{2,1,0:T(8,128)(2,1)}, bf16[4,256,256]{2,1,0:T(8,128)(2,1)S(1)}, bf16[4,176,256]{2,1,0:T(8,128)(2,1)S(1)}) custom-call(s32[1]{0:T(128)} %get-tuple-element.82.turns_ref, f32[8,512]{1,0:T(8,128)S(1)} %get-tuple-element.94.wgain1_ref, ...), custom_call_target="tpu_custom_call" | custom-call | flops 199999995904 | bytes 40000000 | tf_op jit(solution)/shard_map/character_backward_two/pallas_call | solution.py:1021
  66.9 1.5 %add_three.1 = (bf16[2,256,256]{2,1,0:T(8,128)(2,1)S(1)}, bf16[2,256,256]{2,1,0:T(8,128)(2,1)S(1)}, bf16[2,176,256]{2,1,0:T(8,128)(2,1)S(1)}, bf16[2,176,256]{2,1,0:T(8,128)(2,1)S(1)}) custom-call(bf16[4,256,256]{2,1,0:T(8,128)(2,1)S(1)} %get-tuple-element.129.facc_ref, bf16[4,256,256]{2,1,0:T(8,128)(2,1)} %collective-permute-done.4.f3_hbm, ...), custom_call_target="tpu_custom_call" | custom-call | tf_op jit(solution)/shard_map/add_three/pallas_call | solution.py:1045
  68.4 1.6 %collective-permute-start.8 = (bf16[2,256,256]{2,1,0:T(8,128)(2,1)S(1)}, bf16[2,256,256]{2,1,0:T(8,128)(2,1)S(1)}, u32[]{:S(2)}, u32[]{:S(2)}) collective-permute-start(bf16[2,256,256]{2,1,0:T(8,128)(2,1)S(1)} %get-tuple-element.136), channel_id=1, source_target_pairs={{0,2},{1,3},{2,0},{3,1},{4,6},{5,7},{6,4},{7,5},{8,10},{9,11},{10,... | collective-permute-start | bytes 786440 | tf_op jit(solution)/shard_map/ppermute | solution.py:1103
  70.0 0.5 collective-permute-start.10
  70.5 0.8 fusion.2
  71.3 1.1 %collective-permute-start.12 = (bf16[4,160,128]{2,1,0:T(8,128)(2,1)}, bf16[4,160,128]{2,1,0:T(8,128)(2,1)S(1)}, u32[]{:S(2)}, u32[]{:S(2)}) collective-permute-start(bf16[4,160,128]{2,1,0:T(8,128)(2,1)} %get-tuple-element.150), channel_id=1, source_target_pairs={{0,1},{1,0},{2,3},{3,2},{4,5},{5,4},{6,7},{7,6},{8,9},{9,8},{10,11... | collective-permute-start | bytes 491528 | tf_op jit(solution)/shard_map/ppermute | solution.py:1098
  72.4 1.1 %collective-permute-start.13 = (bf16[4,160,128]{2,1,0:T(8,128)(2,1)}, bf16[4,160,128]{2,1,0:T(8,128)(2,1)S(1)}, u32[]{:S(2)}, u32[]{:S(2)}) collective-permute-start(bf16[4,160,128]{2,1,0:T(8,128)(2,1)} %get-tuple-element.149), channel_id=1, source_target_pairs={{0,2},{1,3},{2,0},{3,1},{4,6},{5,7},{6,4},{7,5},{8,10},{9,11},{10,... | collective-permute-start | bytes 491528 | tf_op jit(solution)/shard_map/ppermute | solution.py:1098
  73.5 1.3 %collective-permute-start.14 = (bf16[4,160,128]{2,1,0:T(8,128)(2,1)S(1)}, bf16[4,160,128]{2,1,0:T(8,128)(2,1)S(1)}, u32[]{:S(2)}, u32[]{:S(2)}) collective-permute-start(bf16[4,160,128]{2,1,0:T(8,128)(2,1)S(1)} %get-tuple-element.148), channel_id=1, source_target_pairs={{0,3},{1,2},{2,1},{3,0},{4,7},{5,6},{6,5},{7,4},{8,11},{9,10},{10,... | collective-permute-start | bytes 491528 | tf_op jit(solution)/shard_map/ppermute | solution.py:1098
  74.8 0.9 collective-permute-done.10.t3
  75.8 2.7 %collective-permute-start.11 = (bf16[432,256]{1,0:T(8,128)(2,1)S(1)}, bf16[432,256]{1,0:T(8,128)(2,1)S(1)}, u32[]{:S(2)}, u32[]{:S(2)}) collective-permute-start(bf16[432,256]{1,0:T(8,128)(2,1)S(1)} %pad_maximum_fusion), channel_id=1, source_target_pairs={{0,8},{1,9},{2,10},{3,11},{4,12},{5,13},{6,14},{7,15},{8,0},{9,1},... | collective-permute-start | bytes 663560 | tf_op jit(solution)/shard_map/ppermute | solution.py:1103
  78.5 0.1 collective-permute-done.12.c2
  78.7 2.4 %collective-permute-done.13.c3 = bf16[4,160,128]{2,1,0:T(8,128)(2,1)S(1)} collective-permute-done((bf16[4,160,128]{2,1,0:T(8,128)(2,1)}, bf16[4,160,128]{2,1,0:T(8,128)(2,1)S(1)}, u32[]{:S(2)}, u32[]{:S(2)}) %collective-permute-start.13) | collective-permute-done | bytes 163872 | tf_op jit(solution)/shard_map/ppermute | solution.py:1098
  81.1 1.3 %collective-permute-done.14.c4 = bf16[4,160,128]{2,1,0:T(8,128)(2,1)S(1)} collective-permute-done((bf16[4,160,128]{2,1,0:T(8,128)(2,1)S(1)}, bf16[4,160,128]{2,1,0:T(8,128)(2,1)S(1)}, u32[]{:S(2)}, u32[]{:S(2)}) %collective-permute-start.14) | collective-permute-done | bytes 163872 | tf_op jit(solution)/shard_map/ppermute | solution.py:1098
  82.4 1.0 %collective-permute-start.15 = (bf16[160,128]{1,0:T(8,128)(2,1)S(1)}, bf16[160,128]{1,0:T(8,128)(2,1)S(1)}, u32[]{:S(2)}, u32[]{:S(2)}) collective-permute-start(bf16[160,128]{1,0:T(8,128)(2,1)S(1)} %get-tuple-element.147), channel_id=1, source_target_pairs={{0,4},{1,5},{2,6},{3,7},{4,0},{5,1},{6,2},{7,3},{8,12},{9,13},{10,... | collective-permute-start | bytes 122888 | tf_op jit(solution)/shard_map/ppermute | solution.py:1098
  83.5 2.6 %collective-permute-start.16 = (bf16[160,128]{1,0:T(8,128)(2,1)S(1)}, bf16[160,128]{1,0:T(8,128)(2,1)S(1)}, u32[]{:S(2)}, u32[]{:S(2)}) collective-permute-start(bf16[160,128]{1,0:T(8,128)(2,1)S(1)} %get-tuple-element.146), channel_id=1, source_target_pairs={{0,8},{1,9},{2,10},{3,11},{4,12},{5,13},{6,14},{7,15},{8,0},{9,1},... | collective-permute-start | bytes 122888 | tf_op jit(solution)/shard_map/ppermute | solution.py:1098
  86.0 0.9 collective-permute-start.17
  86.9 0.8 collective-permute-done.15.c5
  87.7 2.6 %collective-permute-done.16.c6 = bf16[160,128]{1,0:T(8,128)(2,1)S(1)} collective-permute-done((bf16[160,128]{1,0:T(8,128)(2,1)S(1)}, bf16[160,128]{1,0:T(8,128)(2,1)S(1)}, u32[]{:S(2)}, u32[]{:S(2)}) %collective-permute-start.16) | collective-permute-done | bytes 40992 | tf_op jit(solution)/shard_map/ppermute | solution.py:1098
  90.3 1.6 %collective-permute-done.17.c7 = bf16[160,128]{1,0:T(8,128)(2,1)S(1)} collective-permute-done((bf16[160,128]{1,0:T(8,128)(2,1)S(1)}, bf16[160,128]{1,0:T(8,128)(2,1)S(1)}, u32[]{:S(2)}, u32[]{:S(2)}) %collective-permute-start.17) | collective-permute-done | bytes 40992 | tf_op jit(solution)/shard_map/ppermute | solution.py:1098
  91.8 1.9 %finish.1 = (bf16[2,1,256,256]{3,2,1,0:T(8,128)(2,1)}, f32[16,128]{1,0:T(8,128)}, f32[16]{0:T(128)}, f32[16,128]{1,0:T(8,128)}, f32[16,128]{1,0:T(8,128)}, /*ind...) custom-call(bf16[2,256,256]{2,1,0:T(8,128)(2,1)S(1)} %get-tuple-elem, ...), custom_call_target="tpu_custom_call" | custom-call | tf_op jit(solution)/shard_map/finish/pallas_call | solution.py:1086
  (50 shorter events, 0.6 us)
Async XLA Ops:
  0.7 25.5 %copy-start = (bf16[512,512]{1,0:T(8,128)(2,1)S(1)}, bf16[512,512]{1,0:T(8,128)(2,1)}, u32[]{:S(2)}) copy-start(bf16[512,512]{1,0:T(8,128)(2,1)} %wwq.1) | copy-start | bytes 1572868
  0.7 25.5 %copy-start.1 = (bf16[512,512]{1,0:T(8,128)(2,1)S(1)}, bf16[512,512]{1,0:T(8,128)(2,1)}, u32[]{:S(2)}) copy-start(bf16[512,512]{1,0:T(8,128)(2,1)} %wwk.1) | copy-start | bytes 1572868
  0.7 25.5 %copy-start.2 = (bf16[512,512]{1,0:T(8,128)(2,1)S(1)}, bf16[512,512]{1,0:T(8,128)(2,1)}, u32[]{:S(2)}) copy-start(bf16[512,512]{1,0:T(8,128)(2,1)} %wwv.1) | copy-start | bytes 1572868
  0.7 25.5 %copy-start.3 = (bf16[512,512]{1,0:T(8,128)(2,1)S(1)}, bf16[512,512]{1,0:T(8,128)(2,1)}, u32[]{:S(2)}) copy-start(bf16[512,512]{1,0:T(8,128)(2,1)} %wwo.1) | copy-start | bytes 1572868
  0.7 25.5 %copy-start.6 = (bf16[256,512]{1,0:T(8,128)(2,1)S(1)}, bf16[256,512]{1,0:T(8,128)(2,1)}, u32[]{:S(2)}) copy-start(bf16[256,512]{1,0:T(8,128)(2,1)} %proj_ref.1) | copy-start | bytes 786436
  0.7 25.5 %copy-start.11 = (s32[2,1,256]{2,1,0:T(1,128)S(1)}, s32[2,1,256]{2,1,0:T(1,128)}, u32[]{:S(2)}) copy-start(s32[2,1,256]{2,1,0:T(1,128)} %counts_ref.1) | copy-start | bytes 6148
  0.7 25.5 %copy-start.12 = (bf16[512]{0:T(512)(128)(2,1)S(1)}, bf16[512]{0:T(512)(128)(2,1)}, u32[]{:S(2)}) copy-start(bf16[512]{0:T(512)(128)(2,1)} %wg1_ref.1) | copy-start | bytes 3076
  25.6 4.9 %collective-permute-start = (bf16[16,256,256]{2,1,0:T(8,128)(2,1)}, bf16[16,256,256]{2,1,0:T(8,128)(2,1)}, u32[]{:S(2)}, u32[]{:S(2)}) collective-permute-start(bf16[16,256,256]{2,1,0:T(8,128)(2,1)} %get-tuple-element.98), channel_id=1, source_target_pairs={{0,16},{16,0},{1,17},{17,1},{2,18},{18,2},{3,19},{19,3},{4,20},{20... | collective-permute-start | bytes 6291464 | tf_op jit(solution)/shard_map/ppermute | solution.py:1098
  26.1 4.4 %collective-permute-start.1 = (bf16[256,256]{1,0:T(8,128)(2,1)}, bf16[256,256]{1,0:T(8,128)(2,1)}, u32[]{:S(2)}, u32[]{:S(2)}) collective-permute-start(bf16[256,256]{1,0:T(8,128)(2,1)} %get-tuple-element.99), channel_id=1, source_target_pairs={{0,16},{16,0},{1,17},{17,1},{2,18},{18,2},{3,19},{19,3},{4,20},{20... | collective-permute-start | bytes 393224 | tf_op jit(solution)/shard_map/ppermute | solution.py:1098
  30.5 5.5 %copy-start.4 = (bf16[256,1024]{1,0:T(8,128)(2,1)S(1)}, bf16[256,1024]{1,0:T(8,128)(2,1)}, u32[]{:S(2)}) copy-start(bf16[256,1024]{1,0:T(8,128)(2,1)} %up_ref.1) | copy-start | bytes 1572868
  30.5 5.5 %copy-start.5 = (bf16[1024,256]{1,0:T(8,128)(2,1)S(1)}, bf16[1024,256]{1,0:T(8,128)(2,1)}, u32[]{:S(2)}) copy-start(bf16[1024,256]{1,0:T(8,128)(2,1)} %down_ref.1) | copy-start | bytes 1572868
  32.9 11.6 %collective-permute-start.2 = (bf16[16,176,256]{2,1,0:T(8,128)(2,1)}, bf16[16,176,256]{2,1,0:T(8,128)(2,1)}, u32[]{:S(2)}, u32[]{:S(2)}) collective-permute-start(bf16[16,176,256]{2,1,0:T(8,128)(2,1)} %get-tuple-element.114), channel_id=1, source_target_pairs={{0,16},{16,0},{1,17},{17,1},{2,18},{18,2},{3,19},{19,3},{4,20},{20... | collective-permute-start | bytes 4325384 | tf_op jit(solution)/shard_map/ppermute | solution.py:1098
  33.4 17.1 %collective-permute-start.3 = (bf16[8,256,256]{2,1,0:T(8,128)(2,1)}, bf16[8,256,256]{2,1,0:T(8,128)(2,1)}, u32[]{:S(2)}, u32[]{:S(2)}) collective-permute-start(bf16[8,256,256]{2,1,0:T(8,128)(2,1)} %add_one.1), channel_id=1, source_target_pairs={{0,1},{1,0},{2,3},{3,2},{4,5},{5,4},{6,7},{7,6},{8,9},{9,8},{10,11... | collective-permute-start | bytes 3145736 | tf_op jit(solution)/shard_map/ppermute | solution.py:1103
  44.5 9.6 %copy-start.7 = (bf16[256,256]{1,0:T(8,128)(2,1)S(1)}, bf16[256,256]{1,0:T(8,128)(2,1)}, u32[]{:S(2)}) copy-start(bf16[256,256]{1,0:T(8,128)(2,1)} %wq_ref.1) | copy-start | bytes 393220
  44.5 9.5 %copy-start.8 = (bf16[256,256]{1,0:T(8,128)(2,1)S(1)}, bf16[256,256]{1,0:T(8,128)(2,1)}, u32[]{:S(2)}) copy-start(bf16[256,256]{1,0:T(8,128)(2,1)} %wk_ref.1) | copy-start | bytes 393220
  44.5 9.5 %copy-start.9 = (bf16[256,256]{1,0:T(8,128)(2,1)S(1)}, bf16[256,256]{1,0:T(8,128)(2,1)}, u32[]{:S(2)}) copy-start(bf16[256,256]{1,0:T(8,128)(2,1)} %wv_ref.1) | copy-start | bytes 393220
  44.6 9.5 %copy-start.10 = (bf16[256,256]{1,0:T(8,128)(2,1)S(1)}, bf16[256,256]{1,0:T(8,128)(2,1)}, u32[]{:S(2)}) copy-start(bf16[256,256]{1,0:T(8,128)(2,1)} %wo_ref.1) | copy-start | bytes 393220
  44.6 9.5 %copy-start.14 = (bf16[256]{0:T(256)(128)(2,1)S(1)}, bf16[256]{0:T(256)(128)(2,1)}, u32[]{:S(2)}) copy-start(bf16[256]{0:T(256)(128)(2,1)} %g1_ref.1) | copy-start | bytes 1540
  46.9 19.9 %collective-permute-start.5 = (bf16[4,176,256]{2,1,0:T(8,128)(2,1)}, bf16[4,176,256]{2,1,0:T(8,128)(2,1)}, u32[]{:S(2)}, u32[]{:S(2)}) collective-permute-start(bf16[4,176,256]{2,1,0:T(8,128)(2,1)} %get-tuple-element.120), channel_id=1, source_target_pairs={{0,1},{1,0},{2,3},{3,2},{4,5},{5,4},{6,7},{7,6},{8,9},{9,8},{10,11... | collective-permute-start | bytes 1081352 | tf_op jit(solution)/shard_map/ppermute | solution.py:1098
  47.1 19.8 %collective-permute-start.6 = (bf16[4,176,256]{2,1,0:T(8,128)(2,1)}, bf16[4,176,256]{2,1,0:T(8,128)(2,1)}, u32[]{:S(2)}, u32[]{:S(2)}) collective-permute-start(bf16[4,176,256]{2,1,0:T(8,128)(2,1)} %get-tuple-element.121), channel_id=1, source_target_pairs={{0,2},{1,3},{2,0},{3,1},{4,6},{5,7},{6,4},{7,5},{8,10},{9,11},{10,... | collective-permute-start | bytes 1081352 | tf_op jit(solution)/shard_map/ppermute | solution.py:1098
  49.1 17.8 %collective-permute-start.7 = (bf16[4,176,256]{2,1,0:T(8,128)(2,1)}, bf16[4,176,256]{2,1,0:T(8,128)(2,1)}, u32[]{:S(2)}, u32[]{:S(2)}) collective-permute-start(bf16[4,176,256]{2,1,0:T(8,128)(2,1)} %get-tuple-element.122), channel_id=1, source_target_pairs={{0,3},{1,2},{2,1},{3,0},{4,7},{5,6},{6,5},{7,4},{8,11},{9,10},{10,... | collective-permute-start | bytes 1081352 | tf_op jit(solution)/shard_map/ppermute | solution.py:1098
  52.5 14.4 %collective-permute-start.4 = (bf16[4,256,256]{2,1,0:T(8,128)(2,1)}, bf16[4,256,256]{2,1,0:T(8,128)(2,1)}, u32[]{:S(2)}, u32[]{:S(2)}) collective-permute-start(bf16[4,256,256]{2,1,0:T(8,128)(2,1)} %add_two.1), channel_id=1, source_target_pairs={{0,4},{1,5},{2,6},{3,7},{4,0},{5,1},{6,2},{7,3},{8,12},{9,13},{10,... | collective-permute-start | bytes 1572872 | tf_op jit(solution)/shard_map/ppermute | solution.py:1103
  66.8 3.6 %collective-permute-start.9 = (bf16[16,160,128]{2,1,0:T(8,128)(2,1)}, bf16[16,160,128]{2,1,0:T(8,128)(2,1)S(1)}, u32[]{:S(2)}, u32[]{:S(2)}) collective-permute-start(bf16[16,160,128]{2,1,0:T(8,128)(2,1)} %get-tuple-element.138), channel_id=1, source_target_pairs={{0,16},{16,0},{1,17},{17,1},{2,18},{18,2},{3,19},{19,3},{4,20},{20... | collective-permute-start | bytes 1966088 | tf_op jit(solution)/shard_map/ppermute | solution.py:1098
  68.4 6.4 %collective-permute-start.8 = (bf16[2,256,256]{2,1,0:T(8,128)(2,1)S(1)}, bf16[2,256,256]{2,1,0:T(8,128)(2,1)S(1)}, u32[]{:S(2)}, u32[]{:S(2)}) collective-permute-start(bf16[2,256,256]{2,1,0:T(8,128)(2,1)S(1)} %get-tuple-element.136), channel_id=1, source_target_pairs={{0,2},{1,3},{2,0},{3,1},{4,6},{5,7},{6,4},{7,5},{8,10},{9,11},{10,... | collective-permute-start | bytes 786440 | tf_op jit(solution)/shard_map/ppermute | solution.py:1103
  70.0 5.7 %collective-permute-start.10 = (bf16[2,176,256]{2,1,0:T(8,128)(2,1)S(1)}, bf16[2,176,256]{2,1,0:T(8,128)(2,1)S(1)}, u32[]{:S(2)}, u32[]{:S(2)}) collective-permute-start(bf16[2,176,256]{2,1,0:T(8,128)(2,1)S(1)} %get-tuple-element.141), channel_id=1, source_target_pairs={{0,4},{1,5},{2,6},{3,7},{4,0},{5,1},{6,2},{7,3},{8,12},{9,13},{10,... | collective-permute-start | bytes 540680 | tf_op jit(solution)/shard_map/ppermute | solution.py:1103
  71.3 7.4 %collective-permute-start.12 = (bf16[4,160,128]{2,1,0:T(8,128)(2,1)}, bf16[4,160,128]{2,1,0:T(8,128)(2,1)S(1)}, u32[]{:S(2)}, u32[]{:S(2)}) collective-permute-start(bf16[4,160,128]{2,1,0:T(8,128)(2,1)} %get-tuple-element.150), channel_id=1, source_target_pairs={{0,1},{1,0},{2,3},{3,2},{4,5},{5,4},{6,7},{7,6},{8,9},{9,8},{10,11... | collective-permute-start | bytes 491528 | tf_op jit(solution)/shard_map/ppermute | solution.py:1098
  72.4 8.7 %collective-permute-start.13 = (bf16[4,160,128]{2,1,0:T(8,128)(2,1)}, bf16[4,160,128]{2,1,0:T(8,128)(2,1)S(1)}, u32[]{:S(2)}, u32[]{:S(2)}) collective-permute-start(bf16[4,160,128]{2,1,0:T(8,128)(2,1)} %get-tuple-element.149), channel_id=1, source_target_pairs={{0,2},{1,3},{2,0},{3,1},{4,6},{5,7},{6,4},{7,5},{8,10},{9,11},{10,... | collective-permute-start | bytes 491528 | tf_op jit(solution)/shard_map/ppermute | solution.py:1098
  73.5 8.8 %collective-permute-start.14 = (bf16[4,160,128]{2,1,0:T(8,128)(2,1)S(1)}, bf16[4,160,128]{2,1,0:T(8,128)(2,1)S(1)}, u32[]{:S(2)}, u32[]{:S(2)}) collective-permute-start(bf16[4,160,128]{2,1,0:T(8,128)(2,1)S(1)} %get-tuple-element.148), channel_id=1, source_target_pairs={{0,3},{1,2},{2,1},{3,0},{4,7},{5,6},{6,5},{7,4},{8,11},{9,10},{10,... | collective-permute-start | bytes 491528 | tf_op jit(solution)/shard_map/ppermute | solution.py:1098
  75.8 16.0 %collective-permute-start.11 = (bf16[432,256]{1,0:T(8,128)(2,1)S(1)}, bf16[432,256]{1,0:T(8,128)(2,1)S(1)}, u32[]{:S(2)}, u32[]{:S(2)}) collective-permute-start(bf16[432,256]{1,0:T(8,128)(2,1)S(1)} %pad_maximum_fusion), channel_id=1, source_target_pairs={{0,8},{1,9},{2,10},{3,11},{4,12},{5,13},{6,14},{7,15},{8,0},{9,1},... | collective-permute-start | bytes 663560 | tf_op jit(solution)/shard_map/ppermute | solution.py:1103
  82.4 5.2 %collective-permute-start.15 = (bf16[160,128]{1,0:T(8,128)(2,1)S(1)}, bf16[160,128]{1,0:T(8,128)(2,1)S(1)}, u32[]{:S(2)}, u32[]{:S(2)}) collective-permute-start(bf16[160,128]{1,0:T(8,128)(2,1)S(1)} %get-tuple-element.147), channel_id=1, source_target_pairs={{0,4},{1,5},{2,6},{3,7},{4,0},{5,1},{6,2},{7,3},{8,12},{9,13},{10,... | collective-permute-start | bytes 122888 | tf_op jit(solution)/shard_map/ppermute | solution.py:1098
  83.5 6.8 %collective-permute-start.16 = (bf16[160,128]{1,0:T(8,128)(2,1)S(1)}, bf16[160,128]{1,0:T(8,128)(2,1)S(1)}, u32[]{:S(2)}, u32[]{:S(2)}) collective-permute-start(bf16[160,128]{1,0:T(8,128)(2,1)S(1)} %get-tuple-element.146), channel_id=1, source_target_pairs={{0,8},{1,9},{2,10},{3,11},{4,12},{5,13},{6,14},{7,15},{8,0},{9,1},... | collective-permute-start | bytes 122888 | tf_op jit(solution)/shard_map/ppermute | solution.py:1098
  86.0 5.8 %collective-permute-start.17 = (bf16[160,128]{1,0:T(8,128)(2,1)S(1)}, bf16[160,128]{1,0:T(8,128)(2,1)S(1)}, u32[]{:S(2)}, u32[]{:S(2)}) collective-permute-start(bf16[160,128]{1,0:T(8,128)(2,1)S(1)} %get-tuple-element.145), channel_id=1, source_target_pairs={{0,12},{1,13},{2,14},{3,15},{4,8},{5,9},{6,10},{7,11},{8,4},{9,5},... | collective-permute-start | bytes 122888 | tf_op jit(solution)/shard_map/ppermute | solution.py:1098
  (2 other events, 10.9 us)

commit v8 on v7

--- a/solution.py
+++ b/solution.py
@@ -21,7 +21,7 @@
 WORD_HEADS = 8
 WORDS = 256
 
-SCHEDULE = "aaaafaaaaaaaaafaaaaaaaaafaaaaafa"
+SCHEDULE = "aaafaaaaaaaaaafaaaaaaaaafaaaaafa"
 SPAN = 256
 STEP = 241
 WIDE = 2 * SPAN
@@ -194,7 +194,7 @@
     counts_ref, ids_ref, segs_ref,
     table_ref, g1_ref, wq_ref, wk_ref, wv_ref, wo_ref, g2_ref, up_ref, down_ref, proj_ref, wg1_ref, wg2_ref,
     cot, wwq, wwk, wwv, wwo, wup, wdown,
-    tab_t, wqkv_t, wo_t, up_t, ids_t, slow, sslope, smid, sinfo, pa, pm, rowinfo, firsts_v, firsts, before_s, act_s, prob_s, found_s,
+    tab_t, wqkv_t, wo_t, up_t, ids_t, slow, sslope, smid, sinfo, pa, pm, rowinfo, firsts_v, firsts, before_s, act_s, found_s,
     mid_s, word_s, old_s, back_s,
     csem, wsem, ksem,
 ):
@@ -224,7 +224,6 @@
     ]
     pa[...] = jnp.zeros_like(pa)
     pm[...] = jnp.zeros_like(pm)
-    prob_s[...] = jnp.zeros_like(prob_s)
     for slot in range(2):
         slow[slot, R_P:R_P + CHAR_HEADS * SPAN] = jnp.zeros((CHAR_HEADS * SPAN, WIDE), LOW)
     for load in tiny:
@@ -347,7 +346,6 @@
                 for i in range(2):
                     p = softmax_keys(s[:, i * 128:i * 128 + 128] + bias)
                     row = (pair * 2 + i) * SPAN
-                    prob_s[row + ks.start:row + ks.stop, ql] = p
                     slow[slot, R_P + row + ks.start:R_P + row + ks.stop, ql] = p
         yield
         mixed = [[], []]
@@ -355,7 +353,7 @@
             us = slice(u * SPAN, (u + 1) * SPAN)
             for h in range(CHAR_HEADS):
                 hs = slice(h * HEAD, (h + 1) * HEAD)
-                mixed[u].append(nn(value_t[hs, us], prob_s[h * SPAN:(h + 1) * SPAN, us]).astype(LOW))
+                mixed[u].append(nn(value_t[hs, us], slow[slot, R_P + h * SPAN:R_P + (h + 1) * SPAN, us]).astype(LOW))
                 yield
         mixed = jnp.concatenate([jnp.concatenate(part, axis=0) for part in mixed], axis=1)
         slow[slot, R_MIX:R_MIX + CD] = mixed
@@ -966,7 +964,7 @@
             v((2, KEPT_LOW, WIDE), LOW), v((2, CFF, WIDE), LOW), v((2, CD, WIDE), F32), v((2, 8, WIDE), F32),
             v((WORDS + WINDOW, CFF), F32), v((WORDS + WINDOW, CD), F32), v((16, WORDS), LOW),
             v((8, 128), jnp.int32), pltpu.SMEM((8, 128), jnp.int32),
-            v((CFF, WIDE), F32), v((CFF, WIDE), LOW), v((CHAR_HEADS * SPAN, WIDE), LOW), v((8, WIDE), F32),
+            v((CFF, WIDE), F32), v((CFF, WIDE), LOW), v((8, WIDE), F32),
             v((CD, WIDE), LOW), v((8, WIDE), F32), v((8, WIDE), F32), v((WORDS, WFF), F32),
             pltpu.SemaphoreType.DMA((15,)),
             pltpu.SemaphoreType.DMA((8,)),

time: 94.2 us -> 93.5 us (level)
  transfers between devices with their start and end apart: 18 -> 18, of which waited for: 7 -> 8; matrix products, arithmetic and copies ran while one was open for 1% -> 1% of each run, Pallas kernels for 33% -> 34%
where the time goes in v8:
time: 93.5 us; the launch traced here: 93.1 us
  Pallas kernels  59.6 us (64%)
  starting transfers between devices  21.6 us (23%)
  waiting for transfers between devices  9.76 us (10%)
  between operations  1.09 us (1%)
  other arithmetic  1.02 us (1%)
    pallas_call x1, Pallas kernels, call_a(): pl.pallas_call(kernel_a, out_shape=(outside((TURNS, KEPT_LOW, WIDE), LOW)...  24.2 us
    pallas_call x1, Pallas kernels, call_b2(): pl.pallas_call(kernel_b2, out_shape=(v((SHARES, C_ROWS, 128), LOW), v((SH...  12.7 us
    ppermute x13, starting transfers between devices, flip(): return lax.ppermute(value, axis, [(i, i ^ bits) for i in range(count)])  12.7 us
    ppermute x5, starting transfers between devices, flip_both(): return lax.ppermute(value, ('phase', 'dp'), pairs)  8.9 us
    ppermute x13, waiting for transfers between devices, flip(): return lax.ppermute(value, axis, [(i, i ^ bits) for i in range(count)])  8.8 us
    pallas_call x1, Pallas kernels, call_b1(): pl.pallas_call(kernel_b1, out_shape=(v((TURNS, CD, WIDE), LOW), shape((CD...  8.5 us
    pallas_call x4, Pallas kernels, call_add(): pl.pallas_call(kernel, out_shape=tuple((v(s, LOW) for s in outs)), in_spe...  8.12 us
    pallas_call x1, Pallas kernels, call_a2(): pl.pallas_call(kernel_a2, out_shape=(shape((CD, WORDS), LOW), v((SHARES,...  4.28 us
  transfers between devices with their start and end apart: 18, of which 8 were waited for; matrix products, arithmetic and copies ran while one was open for 1% of the time, Pallas kernels for 34%

profile of v8, /device:TPU:0, one launch (start us, length us, event | category | flops | bytes accessed | tf_op | source)
XLA Modules:
  0.0 93.1 jit_solution(15386730652168652165)
XLA Ops:
  0.7 24.2 %forward_and_words.1 = (bf16[9,2304,512]{2,1,0:T(8,128)(2,1)}, bf16[9,1024,512]{2,1,0:T(8,128)(2,1)}, f32[9,256,512]{2,1,0:T(8,128)}, f32[9,8,512]{2,1,0:T(8,128...) custom-call(s32[2,1,256]{2,1,0:T(1,128)} %counts_ref.1, ...), custom_call_target="tpu_custom_call" | custom-call | flops 199999995904 | bytes 60000000 | tf_op jit(solution)/shard_map/forward_and_words/pallas_call | solution.py:935
  24.9 0.5 collective-permute-start
  25.6 4.3 %word_attention_backward.1 = (bf16[256,256]{1,0:T(8,128)(2,1)S(1)}, bf16[16,176,256]{2,1,0:T(8,128)(2,1)S(1)}, bf16[16,176,256]{2,1,0:T(8,128)(2,1)}, f32[8,512]{1,0:T(8,128)S(1)}) custom-call(s32[2,1,256]{2,1,0:T(1,128)S(1)} %copy-done.11, bf16[256,512]{1,0:T(8,128)(2,1)S(1)} %get-tuple-element.83.q_ref, bf16[256,512]{1,0:T(8,128)(2,1)S(1)} %get-tuple-element.84.k_ref, ...), custom_call_target="tpu_custom_call" | custom-call | flops 199999995904 | bytes 10000000 | tf_op jit(solution)/shard_map/word_attention_backward/pallas_call | solution.py:981
  29.9 2.4 %add_one.1 = bf16[8,256,256]{2,1,0:T(8,128)(2,1)} custom-call(bf16[16,256,256]{2,1,0:T(8,128)(2,1)S(1)} %get-tuple-element.101.f0_ref, bf16[16,256,256]{2,1,0:T(8,128)(2,1)} %collective-permute-done.f1_hbm), custom_call_target="tpu_custom_call" | custom-call | tf_op jit(solution)/shard_map/add_one/pallas_call | solution.py:1043
  32.2 0.5 collective-permute-start.2
  32.7 2.6 %collective-permute-start.3 = (bf16[8,256,256]{2,1,0:T(8,128)(2,1)}, bf16[8,256,256]{2,1,0:T(8,128)(2,1)}, u32[]{:S(2)}, u32[]{:S(2)}) collective-permute-start(bf16[8,256,256]{2,1,0:T(8,128)(2,1)} %add_one.1), channel_id=1, source_target_pairs={{0,1},{1,0},{2,3},{3,2},{4,5},{5,4},{6,7},{7,6},{8,9},{9,8},{10,11... | collective-permute-start | bytes 3145736 | tf_op jit(solution)/shard_map/ppermute | solution.py:1101
  35.3 8.5 %character_backward_one.1 = (bf16[9,256,512]{2,1,0:T(8,128)(2,1)S(1)}, bf16[256,1024]{1,0:T(8,128)(2,1)S(1)}, f32[8,256]{1,0:T(8,128)S(1)}, bf16[8,256,256]{2,1,0:T(8,128)(2,1)S(1)}) custom-call(s32[1]{0:T(128)} %get-tuple-element.82.turns_ref, bf16[256,256]{1,0:T(8,128)(2,1)S(1)} %get-tuple-element.103.gw_ref, bf16[256]{0:T(256)(128)(2,1)S(1)} %copy-done.13, ...), custom_call_target="tpu_custom_call" | custom-call | flops 199999995904 | bytes 20000000 | tf_op jit(solution)/shard_map/character_backward_one/pallas_call | solution.py:999
  43.9 2.4 %add_words.1 = (bf16[4,176,256]{2,1,0:T(8,128)(2,1)}, bf16[4,176,256]{2,1,0:T(8,128)(2,1)}, bf16[4,176,256]{2,1,0:T(8,128)(2,1)}) custom-call(bf16[16,176,256]{2,1,0:T(8,128)(2,1)S(1)} %get-tuple-element.118.t0_ref, bf16[16,176,256]{2,1,0:T(8,128)(2,1)} %collective-permute-done.2.t1_hbm), custom_call_target="tpu_custom_call" | custom-call | tf_op jit(solution)/shard_map/add_words/pallas_call | solution.py:1043
  46.4 2.0 %collective-permute-start.6 = (bf16[4,176,256]{2,1,0:T(8,128)(2,1)}, bf16[4,176,256]{2,1,0:T(8,128)(2,1)}, u32[]{:S(2)}, u32[]{:S(2)}) collective-permute-start(bf16[4,176,256]{2,1,0:T(8,128)(2,1)} %get-tuple-element.121), channel_id=1, source_target_pairs={{0,2},{1,3},{2,0},{3,1},{4,6},{5,7},{6,4},{7,5},{8,10},{9,11},{10,... | collective-permute-start | bytes 1081352 | tf_op jit(solution)/shard_map/ppermute | solution.py:1096
  48.4 1.4 %collective-permute-start.7 = (bf16[4,176,256]{2,1,0:T(8,128)(2,1)}, bf16[4,176,256]{2,1,0:T(8,128)(2,1)}, u32[]{:S(2)}, u32[]{:S(2)}) collective-permute-start(bf16[4,176,256]{2,1,0:T(8,128)(2,1)} %get-tuple-element.122), channel_id=1, source_target_pairs={{0,3},{1,2},{2,1},{3,0},{4,7},{5,6},{6,5},{7,4},{8,11},{9,10},{10,... | collective-permute-start | bytes 1081352 | tf_op jit(solution)/shard_map/ppermute | solution.py:1096
  49.8 1.9 %add_two.1 = bf16[4,256,256]{2,1,0:T(8,128)(2,1)} custom-call(bf16[8,256,256]{2,1,0:T(8,128)(2,1)S(1)} %get-tuple-element.116.facc_ref, bf16[8,256,256]{2,1,0:T(8,128)(2,1)} %collective-permute-done.3.f2_hbm), custom_call_target="tpu_custom_call" | custom-call | tf_op jit(solution)/shard_map/add_two/pallas_call | solution.py:1043
  51.8 1.6 %collective-permute-start.4 = (bf16[4,256,256]{2,1,0:T(8,128)(2,1)}, bf16[4,256,256]{2,1,0:T(8,128)(2,1)}, u32[]{:S(2)}, u32[]{:S(2)}) collective-permute-start(bf16[4,256,256]{2,1,0:T(8,128)(2,1)} %add_two.1), channel_id=1, source_target_pairs={{0,4},{1,5},{2,6},{3,7},{4,0},{5,1},{6,2},{7,3},{8,12},{9,13},{10,... | collective-permute-start | bytes 1572872 | tf_op jit(solution)/shard_map/ppermute | solution.py:1101
  53.4 12.7 %character_backward_two.1 = (bf16[16,160,128]{2,1,0:T(8,128)(2,1)S(1)}, bf16[16,160,128]{2,1,0:T(8,128)(2,1)}, bf16[4,256,256]{2,1,0:T(8,128)(2,1)S(1)}, bf16[4,176,256]{2,1,0:T(8,128)(2,1)S(1)}) custom-call(s32[1]{0:T(128)} %get-tuple-element.82.turns_ref, f32[8,512]{1,0:T(8,128)S(1)} %get-tuple-element.94.wgain1_ref, ...), custom_call_target="tpu_custom_call" | custom-call | flops 199999995904 | bytes 40000000 | tf_op jit(solution)/shard_map/character_backward_two/pallas_call | solution.py:1019
  66.2 1.5 %add_three.1 = (bf16[2,256,256]{2,1,0:T(8,128)(2,1)S(1)}, bf16[2,256,256]{2,1,0:T(8,128)(2,1)S(1)}, bf16[2,176,256]{2,1,0:T(8,128)(2,1)S(1)}, bf16[2,176,256]{2,1,0:T(8,128)(2,1)S(1)}) custom-call(bf16[4,256,256]{2,1,0:T(8,128)(2,1)S(1)} %get-tuple-element.129.facc_ref, bf16[4,256,256]{2,1,0:T(8,128)(2,1)} %collective-permute-done.4.f3_hbm, ...), custom_call_target="tpu_custom_call" | custom-call | tf_op jit(solution)/shard_map/add_three/pallas_call | solution.py:1043
  67.7 1.6 %collective-permute-start.8 = (bf16[2,256,256]{2,1,0:T(8,128)(2,1)S(1)}, bf16[2,256,256]{2,1,0:T(8,128)(2,1)S(1)}, u32[]{:S(2)}, u32[]{:S(2)}) collective-permute-start(bf16[2,256,256]{2,1,0:T(8,128)(2,1)S(1)} %get-tuple-element.136), channel_id=1, source_target_pairs={{0,2},{1,3},{2,0},{3,1},{4,6},{5,7},{6,4},{7,5},{8,10},{9,11},{10,... | collective-permute-start | bytes 786440 | tf_op jit(solution)/shard_map/ppermute | solution.py:1101
  69.3 0.5 collective-permute-start.10
  69.8 0.8 fusion.2
  70.6 1.1 %collective-permute-start.12 = (bf16[4,160,128]{2,1,0:T(8,128)(2,1)}, bf16[4,160,128]{2,1,0:T(8,128)(2,1)S(1)}, u32[]{:S(2)}, u32[]{:S(2)}) collective-permute-start(bf16[4,160,128]{2,1,0:T(8,128)(2,1)} %get-tuple-element.150), channel_id=1, source_target_pairs={{0,1},{1,0},{2,3},{3,2},{4,5},{5,4},{6,7},{7,6},{8,9},{9,8},{10,11... | collective-permute-start | bytes 491528 | tf_op jit(solution)/shard_map/ppermute | solution.py:1096
  71.7 1.1 %collective-permute-start.13 = (bf16[4,160,128]{2,1,0:T(8,128)(2,1)}, bf16[4,160,128]{2,1,0:T(8,128)(2,1)S(1)}, u32[]{:S(2)}, u32[]{:S(2)}) collective-permute-start(bf16[4,160,128]{2,1,0:T(8,128)(2,1)} %get-tuple-element.149), channel_id=1, source_target_pairs={{0,2},{1,3},{2,0},{3,1},{4,6},{5,7},{6,4},{7,5},{8,10},{9,11},{10,... | collective-permute-start | bytes 491528 | tf_op jit(solution)/shard_map/ppermute | solution.py:1096
  72.8 1.3 %collective-permute-start.14 = (bf16[4,160,128]{2,1,0:T(8,128)(2,1)S(1)}, bf16[4,160,128]{2,1,0:T(8,128)(2,1)S(1)}, u32[]{:S(2)}, u32[]{:S(2)}) collective-permute-start(bf16[4,160,128]{2,1,0:T(8,128)(2,1)S(1)} %get-tuple-element.148), channel_id=1, source_target_pairs={{0,3},{1,2},{2,1},{3,0},{4,7},{5,6},{6,5},{7,4},{8,11},{9,10},{10,... | collective-permute-start | bytes 491528 | tf_op jit(solution)/shard_map/ppermute | solution.py:1096
  74.2 0.9 collective-permute-done.10.t3
  75.2 2.7 %collective-permute-start.11 = (bf16[432,256]{1,0:T(8,128)(2,1)S(1)}, bf16[432,256]{1,0:T(8,128)(2,1)S(1)}, u32[]{:S(2)}, u32[]{:S(2)}) collective-permute-start(bf16[432,256]{1,0:T(8,128)(2,1)S(1)} %pad_maximum_fusion), channel_id=1, source_target_pairs={{0,8},{1,9},{2,10},{3,11},{4,12},{5,13},{6,14},{7,15},{8,0},{9,1},... | collective-permute-start | bytes 663560 | tf_op jit(solution)/shard_map/ppermute | solution.py:1101
  77.8 0.1 collective-permute-done.12.c2
  78.0 2.4 %collective-permute-done.13.c3 = bf16[4,160,128]{2,1,0:T(8,128)(2,1)S(1)} collective-permute-done((bf16[4,160,128]{2,1,0:T(8,128)(2,1)}, bf16[4,160,128]{2,1,0:T(8,128)(2,1)S(1)}, u32[]{:S(2)}, u32[]{:S(2)}) %collective-permute-start.13) | collective-permute-done | bytes 163872 | tf_op jit(solution)/shard_map/ppermute | solution.py:1096
  80.4 1.3 %collective-permute-done.14.c4 = bf16[4,160,128]{2,1,0:T(8,128)(2,1)S(1)} collective-permute-done((bf16[4,160,128]{2,1,0:T(8,128)(2,1)S(1)}, bf16[4,160,128]{2,1,0:T(8,128)(2,1)S(1)}, u32[]{:S(2)}, u32[]{:S(2)}) %collective-permute-start.14) | collective-permute-done | bytes 163872 | tf_op jit(solution)/shard_map/ppermute | solution.py:1096
  81.8 1.0 %collective-permute-start.15 = (bf16[160,128]{1,0:T(8,128)(2,1)S(1)}, bf16[160,128]{1,0:T(8,128)(2,1)S(1)}, u32[]{:S(2)}, u32[]{:S(2)}) collective-permute-start(bf16[160,128]{1,0:T(8,128)(2,1)S(1)} %get-tuple-element.147), channel_id=1, source_target_pairs={{0,4},{1,5},{2,6},{3,7},{4,0},{5,1},{6,2},{7,3},{8,12},{9,13},{10,... | collective-permute-start | bytes 122888 | tf_op jit(solution)/shard_map/ppermute | solution.py:1096
  82.8 2.6 %collective-permute-start.16 = (bf16[160,128]{1,0:T(8,128)(2,1)S(1)}, bf16[160,128]{1,0:T(8,128)(2,1)S(1)}, u32[]{:S(2)}, u32[]{:S(2)}) collective-permute-start(bf16[160,128]{1,0:T(8,128)(2,1)S(1)} %get-tuple-element.146), channel_id=1, source_target_pairs={{0,8},{1,9},{2,10},{3,11},{4,12},{5,13},{6,14},{7,15},{8,0},{9,1},... | collective-permute-start | bytes 122888 | tf_op jit(solution)/shard_map/ppermute | solution.py:1096
  85.4 0.9 collective-permute-start.17
  86.2 0.8 collective-permute-done.15.c5
  87.0 2.6 %collective-permute-done.16.c6 = bf16[160,128]{1,0:T(8,128)(2,1)S(1)} collective-permute-done((bf16[160,128]{1,0:T(8,128)(2,1)S(1)}, bf16[160,128]{1,0:T(8,128)(2,1)S(1)}, u32[]{:S(2)}, u32[]{:S(2)}) %collective-permute-start.16) | collective-permute-done | bytes 40992 | tf_op jit(solution)/shard_map/ppermute | solution.py:1096
  89.6 1.6 %collective-permute-done.17.c7 = bf16[160,128]{1,0:T(8,128)(2,1)S(1)} collective-permute-done((bf16[160,128]{1,0:T(8,128)(2,1)S(1)}, bf16[160,128]{1,0:T(8,128)(2,1)S(1)}, u32[]{:S(2)}, u32[]{:S(2)}) %collective-permute-start.17) | collective-permute-done | bytes 40992 | tf_op jit(solution)/shard_map/ppermute | solution.py:1096
  91.2 1.9 %finish.1 = (bf16[2,1,256,256]{3,2,1,0:T(8,128)(2,1)}, f32[16,128]{1,0:T(8,128)}, f32[16]{0:T(128)}, f32[16,128]{1,0:T(8,128)}, f32[16,128]{1,0:T(8,128)}, /*ind...) custom-call(bf16[2,256,256]{2,1,0:T(8,128)(2,1)S(1)} %get-tuple-elem, ...), custom_call_target="tpu_custom_call" | custom-call | tf_op jit(solution)/shard_map/finish/pallas_call | solution.py:1084
  (50 shorter events, 0.6 us)
Async XLA Ops:
  0.7 24.9 %copy-start = (bf16[512,512]{1,0:T(8,128)(2,1)S(1)}, bf16[512,512]{1,0:T(8,128)(2,1)}, u32[]{:S(2)}) copy-start(bf16[512,512]{1,0:T(8,128)(2,1)} %wwq.1) | copy-start | bytes 1572868
  0.7 24.9 %copy-start.1 = (bf16[512,512]{1,0:T(8,128)(2,1)S(1)}, bf16[512,512]{1,0:T(8,128)(2,1)}, u32[]{:S(2)}) copy-start(bf16[512,512]{1,0:T(8,128)(2,1)} %wwk.1) | copy-start | bytes 1572868
  0.7 24.8 %copy-start.2 = (bf16[512,512]{1,0:T(8,128)(2,1)S(1)}, bf16[512,512]{1,0:T(8,128)(2,1)}, u32[]{:S(2)}) copy-start(bf16[512,512]{1,0:T(8,128)(2,1)} %wwv.1) | copy-start | bytes 1572868
  0.7 24.8 %copy-start.3 = (bf16[512,512]{1,0:T(8,128)(2,1)S(1)}, bf16[512,512]{1,0:T(8,128)(2,1)}, u32[]{:S(2)}) copy-start(bf16[512,512]{1,0:T(8,128)(2,1)} %wwo.1) | copy-start | bytes 1572868
  0.7 24.8 %copy-start.6 = (bf16[256,512]{1,0:T(8,128)(2,1)S(1)}, bf16[256,512]{1,0:T(8,128)(2,1)}, u32[]{:S(2)}) copy-start(bf16[256,512]{1,0:T(8,128)(2,1)} %proj_ref.1) | copy-start | bytes 786436
  0.7 24.8 %copy-start.11 = (s32[2,1,256]{2,1,0:T(1,128)S(1)}, s32[2,1,256]{2,1,0:T(1,128)}, u32[]{:S(2)}) copy-start(s32[2,1,256]{2,1,0:T(1,128)} %counts_ref.1) | copy-start | bytes 6148
  0.7 24.8 %copy-start.12 = (bf16[512]{0:T(512)(128)(2,1)S(1)}, bf16[512]{0:T(512)(128)(2,1)}, u32[]{:S(2)}) copy-start(bf16[512]{0:T(512)(128)(2,1)} %wg1_ref.1) | copy-start | bytes 3076
  24.9 4.9 %collective-permute-start = (bf16[16,256,256]{2,1,0:T(8,128)(2,1)}, bf16[16,256,256]{2,1,0:T(8,128)(2,1)}, u32[]{:S(2)}, u32[]{:S(2)}) collective-permute-start(bf16[16,256,256]{2,1,0:T(8,128)(2,1)} %get-tuple-element.98), channel_id=1, source_target_pairs={{0,16},{16,0},{1,17},{17,1},{2,18},{18,2},{3,19},{19,3},{4,20},{20... | collective-permute-start | bytes 6291464 | tf_op jit(solution)/shard_map/ppermute | solution.py:1096
  25.4 4.4 %collective-permute-start.1 = (bf16[256,256]{1,0:T(8,128)(2,1)}, bf16[256,256]{1,0:T(8,128)(2,1)}, u32[]{:S(2)}, u32[]{:S(2)}) collective-permute-start(bf16[256,256]{1,0:T(8,128)(2,1)} %get-tuple-element.99), channel_id=1, source_target_pairs={{0,16},{16,0},{1,17},{17,1},{2,18},{18,2},{3,19},{19,3},{4,20},{20... | collective-permute-start | bytes 393224 | tf_op jit(solution)/shard_map/ppermute | solution.py:1096
  29.8 5.5 %copy-start.4 = (bf16[256,1024]{1,0:T(8,128)(2,1)S(1)}, bf16[256,1024]{1,0:T(8,128)(2,1)}, u32[]{:S(2)}) copy-start(bf16[256,1024]{1,0:T(8,128)(2,1)} %up_ref.1) | copy-start | bytes 1572868
  29.9 5.5 %copy-start.5 = (bf16[1024,256]{1,0:T(8,128)(2,1)S(1)}, bf16[1024,256]{1,0:T(8,128)(2,1)}, u32[]{:S(2)}) copy-start(bf16[1024,256]{1,0:T(8,128)(2,1)} %down_ref.1) | copy-start | bytes 1572868
  32.2 11.6 %collective-permute-start.2 = (bf16[16,176,256]{2,1,0:T(8,128)(2,1)}, bf16[16,176,256]{2,1,0:T(8,128)(2,1)}, u32[]{:S(2)}, u32[]{:S(2)}) collective-permute-start(bf16[16,176,256]{2,1,0:T(8,128)(2,1)} %get-tuple-element.114), channel_id=1, source_target_pairs={{0,16},{16,0},{1,17},{17,1},{2,18},{18,2},{3,19},{19,3},{4,20},{20... | collective-permute-start | bytes 4325384 | tf_op jit(solution)/shard_map/ppermute | solution.py:1096
  32.7 17.1 %collective-permute-start.3 = (bf16[8,256,256]{2,1,0:T(8,128)(2,1)}, bf16[8,256,256]{2,1,0:T(8,128)(2,1)}, u32[]{:S(2)}, u32[]{:S(2)}) collective-permute-start(bf16[8,256,256]{2,1,0:T(8,128)(2,1)} %add_one.1), channel_id=1, source_target_pairs={{0,1},{1,0},{2,3},{3,2},{4,5},{5,4},{6,7},{7,6},{8,9},{9,8},{10,11... | collective-permute-start | bytes 3145736 | tf_op jit(solution)/shard_map/ppermute | solution.py:1101
  43.8 9.6 %copy-start.7 = (bf16[256,256]{1,0:T(8,128)(2,1)S(1)}, bf16[256,256]{1,0:T(8,128)(2,1)}, u32[]{:S(2)}) copy-start(bf16[256,256]{1,0:T(8,128)(2,1)} %wq_ref.1) | copy-start | bytes 393220
  43.9 9.6 %copy-start.8 = (bf16[256,256]{1,0:T(8,128)(2,1)S(1)}, bf16[256,256]{1,0:T(8,128)(2,1)}, u32[]{:S(2)}) copy-start(bf16[256,256]{1,0:T(8,128)(2,1)} %wk_ref.1) | copy-start | bytes 393220
  43.9 9.5 %copy-start.9 = (bf16[256,256]{1,0:T(8,128)(2,1)S(1)}, bf16[256,256]{1,0:T(8,128)(2,1)}, u32[]{:S(2)}) copy-start(bf16[256,256]{1,0:T(8,128)(2,1)} %wv_ref.1) | copy-start | bytes 393220
  43.9 9.5 %copy-start.10 = (bf16[256,256]{1,0:T(8,128)(2,1)S(1)}, bf16[256,256]{1,0:T(8,128)(2,1)}, u32[]{:S(2)}) copy-start(bf16[256,256]{1,0:T(8,128)(2,1)} %wo_ref.1) | copy-start | bytes 393220
  43.9 9.5 %copy-start.14 = (bf16[256]{0:T(256)(128)(2,1)S(1)}, bf16[256]{0:T(256)(128)(2,1)}, u32[]{:S(2)}) copy-start(bf16[256]{0:T(256)(128)(2,1)} %g1_ref.1) | copy-start | bytes 1540
  46.3 19.9 %collective-permute-start.5 = (bf16[4,176,256]{2,1,0:T(8,128)(2,1)}, bf16[4,176,256]{2,1,0:T(8,128)(2,1)}, u32[]{:S(2)}, u32[]{:S(2)}) collective-permute-start(bf16[4,176,256]{2,1,0:T(8,128)(2,1)} %get-tuple-element.120), channel_id=1, source_target_pairs={{0,1},{1,0},{2,3},{3,2},{4,5},{5,4},{6,7},{7,6},{8,9},{9,8},{10,11... | collective-permute-start | bytes 1081352 | tf_op jit(solution)/shard_map/ppermute | solution.py:1096
  46.4 19.8 %collective-permute-start.6 = (bf16[4,176,256]{2,1,0:T(8,128)(2,1)}, bf16[4,176,256]{2,1,0:T(8,128)(2,1)}, u32[]{:S(2)}, u32[]{:S(2)}) collective-permute-start(bf16[4,176,256]{2,1,0:T(8,128)(2,1)} %get-tuple-element.121), channel_id=1, source_target_pairs={{0,2},{1,3},{2,0},{3,1},{4,6},{5,7},{6,4},{7,5},{8,10},{9,11},{10,... | collective-permute-start | bytes 1081352 | tf_op jit(solution)/shard_map/ppermute | solution.py:1096
  48.4 17.8 %collective-permute-start.7 = (bf16[4,176,256]{2,1,0:T(8,128)(2,1)}, bf16[4,176,256]{2,1,0:T(8,128)(2,1)}, u32[]{:S(2)}, u32[]{:S(2)}) collective-permute-start(bf16[4,176,256]{2,1,0:T(8,128)(2,1)} %get-tuple-element.122), channel_id=1, source_target_pairs={{0,3},{1,2},{2,1},{3,0},{4,7},{5,6},{6,5},{7,4},{8,11},{9,10},{10,... | collective-permute-start | bytes 1081352 | tf_op jit(solution)/shard_map/ppermute | solution.py:1096
  51.8 14.4 %collective-permute-start.4 = (bf16[4,256,256]{2,1,0:T(8,128)(2,1)}, bf16[4,256,256]{2,1,0:T(8,128)(2,1)}, u32[]{:S(2)}, u32[]{:S(2)}) collective-permute-start(bf16[4,256,256]{2,1,0:T(8,128)(2,1)} %add_two.1), channel_id=1, source_target_pairs={{0,4},{1,5},{2,6},{3,7},{4,0},{5,1},{6,2},{7,3},{8,12},{9,13},{10,... | collective-permute-start | bytes 1572872 | tf_op jit(solution)/shard_map/ppermute | solution.py:1101
  66.2 3.6 %collective-permute-start.9 = (bf16[16,160,128]{2,1,0:T(8,128)(2,1)}, bf16[16,160,128]{2,1,0:T(8,128)(2,1)S(1)}, u32[]{:S(2)}, u32[]{:S(2)}) collective-permute-start(bf16[16,160,128]{2,1,0:T(8,128)(2,1)} %get-tuple-element.138), channel_id=1, source_target_pairs={{0,16},{16,0},{1,17},{17,1},{2,18},{18,2},{3,19},{19,3},{4,20},{20... | collective-permute-start | bytes 1966088 | tf_op jit(solution)/shard_map/ppermute | solution.py:1096
  67.7 6.4 %collective-permute-start.8 = (bf16[2,256,256]{2,1,0:T(8,128)(2,1)S(1)}, bf16[2,256,256]{2,1,0:T(8,128)(2,1)S(1)}, u32[]{:S(2)}, u32[]{:S(2)}) collective-permute-start(bf16[2,256,256]{2,1,0:T(8,128)(2,1)S(1)} %get-tuple-element.136), channel_id=1, source_target_pairs={{0,2},{1,3},{2,0},{3,1},{4,6},{5,7},{6,4},{7,5},{8,10},{9,11},{10,... | collective-permute-start | bytes 786440 | tf_op jit(solution)/shard_map/ppermute | solution.py:1101
  69.3 5.7 %collective-permute-start.10 = (bf16[2,176,256]{2,1,0:T(8,128)(2,1)S(1)}, bf16[2,176,256]{2,1,0:T(8,128)(2,1)S(1)}, u32[]{:S(2)}, u32[]{:S(2)}) collective-permute-start(bf16[2,176,256]{2,1,0:T(8,128)(2,1)S(1)} %get-tuple-element.141), channel_id=1, source_target_pairs={{0,4},{1,5},{2,6},{3,7},{4,0},{5,1},{6,2},{7,3},{8,12},{9,13},{10,... | collective-permute-start | bytes 540680 | tf_op jit(solution)/shard_map/ppermute | solution.py:1101
  70.6 7.3 %collective-permute-start.12 = (bf16[4,160,128]{2,1,0:T(8,128)(2,1)}, bf16[4,160,128]{2,1,0:T(8,128)(2,1)S(1)}, u32[]{:S(2)}, u32[]{:S(2)}) collective-permute-start(bf16[4,160,128]{2,1,0:T(8,128)(2,1)} %get-tuple-element.150), channel_id=1, source_target_pairs={{0,1},{1,0},{2,3},{3,2},{4,5},{5,4},{6,7},{7,6},{8,9},{9,8},{10,11... | collective-permute-start | bytes 491528 | tf_op jit(solution)/shard_map/ppermute | solution.py:1096
  71.7 8.7 %collective-permute-start.13 = (bf16[4,160,128]{2,1,0:T(8,128)(2,1)}, bf16[4,160,128]{2,1,0:T(8,128)(2,1)S(1)}, u32[]{:S(2)}, u32[]{:S(2)}) collective-permute-start(bf16[4,160,128]{2,1,0:T(8,128)(2,1)} %get-tuple-element.149), channel_id=1, source_target_pairs={{0,2},{1,3},{2,0},{3,1},{4,6},{5,7},{6,4},{7,5},{8,10},{9,11},{10,... | collective-permute-start | bytes 491528 | tf_op jit(solution)/shard_map/ppermute | solution.py:1096
  72.8 8.8 %collective-permute-start.14 = (bf16[4,160,128]{2,1,0:T(8,128)(2,1)S(1)}, bf16[4,160,128]{2,1,0:T(8,128)(2,1)S(1)}, u32[]{:S(2)}, u32[]{:S(2)}) collective-permute-start(bf16[4,160,128]{2,1,0:T(8,128)(2,1)S(1)} %get-tuple-element.148), channel_id=1, source_target_pairs={{0,3},{1,2},{2,1},{3,0},{4,7},{5,6},{6,5},{7,4},{8,11},{9,10},{10,... | collective-permute-start | bytes 491528 | tf_op jit(solution)/shard_map/ppermute | solution.py:1096
  75.2 16.0 %collective-permute-start.11 = (bf16[432,256]{1,0:T(8,128)(2,1)S(1)}, bf16[432,256]{1,0:T(8,128)(2,1)S(1)}, u32[]{:S(2)}, u32[]{:S(2)}) collective-permute-start(bf16[432,256]{1,0:T(8,128)(2,1)S(1)} %pad_maximum_fusion), channel_id=1, source_target_pairs={{0,8},{1,9},{2,10},{3,11},{4,12},{5,13},{6,14},{7,15},{8,0},{9,1},... | collective-permute-start | bytes 663560 | tf_op jit(solution)/shard_map/ppermute | solution.py:1101
  81.8 5.2 %collective-permute-start.15 = (bf16[160,128]{1,0:T(8,128)(2,1)S(1)}, bf16[160,128]{1,0:T(8,128)(2,1)S(1)}, u32[]{:S(2)}, u32[]{:S(2)}) collective-permute-start(bf16[160,128]{1,0:T(8,128)(2,1)S(1)} %get-tuple-element.147), channel_id=1, source_target_pairs={{0,4},{1,5},{2,6},{3,7},{4,0},{5,1},{6,2},{7,3},{8,12},{9,13},{10,... | collective-permute-start | bytes 122888 | tf_op jit(solution)/shard_map/ppermute | solution.py:1096
  82.8 6.8 %collective-permute-start.16 = (bf16[160,128]{1,0:T(8,128)(2,1)S(1)}, bf16[160,128]{1,0:T(8,128)(2,1)S(1)}, u32[]{:S(2)}, u32[]{:S(2)}) collective-permute-start(bf16[160,128]{1,0:T(8,128)(2,1)S(1)} %get-tuple-element.146), channel_id=1, source_target_pairs={{0,8},{1,9},{2,10},{3,11},{4,12},{5,13},{6,14},{7,15},{8,0},{9,1},... | collective-permute-start | bytes 122888 | tf_op jit(solution)/shard_map/ppermute | solution.py:1096
  85.4 5.8 %collective-permute-start.17 = (bf16[160,128]{1,0:T(8,128)(2,1)S(1)}, bf16[160,128]{1,0:T(8,128)(2,1)S(1)}, u32[]{:S(2)}, u32[]{:S(2)}) collective-permute-start(bf16[160,128]{1,0:T(8,128)(2,1)S(1)} %get-tuple-element.145), channel_id=1, source_target_pairs={{0,12},{1,13},{2,14},{3,15},{4,8},{5,9},{6,10},{7,11},{8,4},{9,5},... | collective-permute-start | bytes 122888 | tf_op jit(solution)/shard_map/ppermute | solution.py:1096
  (2 other events, 10.9 us)
